TPU v7x, 256 devices: a whole 4x4x8 slice. The times are simulated.
256 devices in a mesh: users: 32 (over y, z), items: 8 (over x, core).
Axes of the slice: x: 4, y: 4, z: 8, core: 2. Of those that a mesh axis runs over, the one named last changes fastest.
Arguments:
- item_ids: int32 [2048, 8, 128], P(('users', 'items')), may hold values from 0 to 65535, as said below
- clicks: int32 [2048, 8, 128], P(('users', 'items')), may hold values from 1 to 8
- block_counts: int32 [2048], P(('users', 'items')), may hold values from 1 to 8, as said below
- user_shape0: float32 [2048, 128], P(('users', 'items')), may hold values from 0.5 to 5
- user_rate0: float32 [2048, 128], P(('users', 'items')), may hold values from 0.5 to 5
- item_shape: float32 [65536, 128], P('users'), may hold values from 0.1 to 3
- item_rate: float32 [65536, 128], P('users'), may hold values from 0.5 to 5
- beta_totals: float32 [128], replicated, may hold values from 5 to 50
- covariates: float32 [512, 65536], P('items', 'users'), may hold values from -6 to 6
- cov_weight: float32 [512, 128], P('items'), may hold values from -0.125 to 0.125
Outputs:
- user_shape: float32 [2048, 128], P(('users', 'items'))
- user_rate: float32 [2048, 128], P(('users', 'items'))
- activity_rate: float32 [2048], P(('users', 'items'))
- item_shape_new: float32 [65536, 128], P(('users', 'items'))
- cov_grad: float32 [512, 128], P('items')
Inputs may be any that keep to these rules, and one draw needn't show every extreme that they name: `item_ids`: item i belongs to owner i // 2048. In each aligned block of 8 users (one device's users), the slots name items of every owner exactly 256 times; items may repeat. `block_counts`: some user in every draw has 8 live blocks; blocks at or after a user's count are padding. Counts are skewed; about half of all block slots are live.
All inputs are finite; a program needn't handle non-finite values.
Results may differ from a plain program's by a relative error of at most 0.0001.
Values sent between devices are 32-bit elements; how exact they have to be, the bound alone decides.
No kernel may reach another device: no remote copies, remote signals or barrier semaphores. Data moves between devices by JAX's collectives and lax.ppermute only.
A program may use at most 64 MiB of HBM per device.

v0:
```python
import jax
import jax.numpy as jnp
from jax import lax
from jax.sharding import PartitionSpec as P

ITERS = 3
USER_RATIO = 4


user_prior = 0.3
activity_prior = 0.3
activity_base = 1.0
item_prior = 0.3
step_weight = 0.5


def expect_log(shapes, rates):
    return lax.digamma(shapes) - jnp.log(rates)


def ascend(shape_start, rate_start, blocks_log, weights, totals):
    factors = shape_start.shape[1]
    activity_shape = activity_prior + factors * user_prior
    activity = activity_base + jnp.sum(shape_start / rate_start, axis=-1)
    shapes, rates = (shape_start, rate_start)
    alloc = None
    for iteration in range(ITERS):
        log_terms = expect_log(shapes, rates)[:, None, :] + blocks_log
        exp_terms = jnp.exp(log_terms)
        alloc = exp_terms / jnp.sum(exp_terms, axis=-1, keepdims=True)
        shapes = user_prior + jnp.sum(weights[:, :, None] * alloc, axis=1)
        rates = (activity_shape / activity)[:, None] + totals[None, :]
        activity = activity_base + jnp.sum(shapes / rates, axis=-1)
    return (shapes, rates, activity, weights[:, :, None] * alloc)


def prior_part(covariates, cov_weight):
    return lax.dot_general(
        covariates,
        cov_weight,
        (((0,), (0,)), ((), ())),
        precision=lax.Precision.HIGHEST,
        preferred_element_type=jnp.float32,
    )


def shards(
    item_ids,
    clicks,
    block_counts,
    user_shape0,
    user_rate0,
    item_shape,
    item_rate,
    beta_totals,
    covariates,
    cov_weight,
):
    owners = lax.axis_size("users")
    item_rows, factors = item_shape.shape
    users_here, blocks, block_width = item_ids.shape
    slot_count = users_here * blocks * block_width
    capacity = slot_count // owners
    flat_ids = item_ids.reshape(slot_count)
    owner_of = flat_ids // item_rows
    local_row = flat_ids - owner_of * item_rows
    owner_marks = (owner_of[:, None] == jnp.arange(owners, dtype=jnp.int32)[None, :]).astype(
        jnp.int32
    )
    earlier_marks = jnp.cumsum(owner_marks, axis=0) - owner_marks
    slot_rank = jnp.sum(earlier_marks * owner_marks, axis=1)
    position = owner_of * capacity + slot_rank
    requests = (
        jnp.zeros((owners * capacity,), jnp.int32)
        .at[position]
        .set(local_row)
        .reshape(owners, capacity)
    )
    wanted = lax.all_to_all(requests, "users", split_axis=0, concat_axis=0, tiled=True)
    wanted_flat = wanted.reshape(owners * capacity)
    elog_items = expect_log(item_shape, item_rate)
    answer = elog_items[wanted_flat].reshape(owners, capacity, factors)
    split_count = lax.axis_size("items")
    share_rows = item_rows // split_count
    first_row = lax.axis_index("items") * share_rows
    prior_log = lax.psum(prior_part(covariates, cov_weight), "items")
    returned = lax.all_to_all(answer, "users", split_axis=0, concat_axis=0, tiled=True)
    fetched = returned.reshape(owners * capacity, factors)[position].reshape(
        users_here, blocks * block_width, factors
    )
    live_mask = (jnp.arange(blocks, dtype=jnp.int32)[None, :] < block_counts[:, None]).astype(
        jnp.float32
    )
    weights = (clicks.astype(jnp.float32) * live_mask[:, :, None]).reshape(
        users_here, blocks * block_width
    )
    user_shape, user_rate, activity_rate, item_stats = ascend(
        user_shape0, user_rate0, fetched, weights, beta_totals
    )
    outgoing = (
        jnp.zeros((owners * capacity, factors), jnp.float32)
        .at[position]
        .set(item_stats.reshape(slot_count, factors))
    )
    incoming = lax.all_to_all(
        outgoing.reshape(owners, capacity, factors),
        "users",
        split_axis=0,
        concat_axis=0,
        tiled=True,
    )
    local_stats = (
        jnp.zeros((item_rows, factors), jnp.float32)
        .at[wanted_flat]
        .add(incoming.reshape(owners * capacity, factors))
    )
    totals = lax.psum(local_stats, "items")
    new_shape = (1.0 - step_weight) * item_shape + step_weight * (item_prior + USER_RATIO * totals)
    item_score = item_prior - jnp.exp(prior_log) * new_shape / item_rate
    partial_grad = jnp.dot(
        covariates, item_score, precision=lax.Precision.HIGHEST, preferred_element_type=jnp.float32
    )
    shape_out = lax.dynamic_slice_in_dim(new_shape, first_row, share_rows, 0)
    total_items = item_rows * owners
    cov_grad = lax.psum(partial_grad, "users") / jnp.sqrt(jnp.float32(total_items))
    return (user_shape, user_rate, activity_rate, shape_out, cov_grad)


def solution(mesh):
    return jax.shard_map(
        shards,
        mesh=mesh,
        in_specs=(
            P(("users", "items"), None, None),
            P(("users", "items"), None, None),
            P(("users", "items")),
            P(("users", "items"), None),
            P(("users", "items"), None),
            P("users", None),
            P("users", None),
            P(),
            P("items", "users"),
            P("items", None),
        ),
        out_specs=(
            P(("users", "items"), None),
            P(("users", "items"), None),
            P(("users", "items")),
            P(("users", "items"), None),
            P("items", None),
        ),
        check_vma=False,
    )
```

profile of v0, /device:TPU:2, one launch (start us, length us, event | category | flops | bytes accessed | tf_op | source)
XLA Modules:
  0.0 672.6 jit_solution(6749224644218447751)
XLA Ops:
  7.2 0.0 copy-start
  7.2 0.0 copy-start.4
  7.2 0.0 copy-start.2
  7.2 0.9 add_select_fusion
  8.1 0.8 bitcast_subtract_fusion
  8.9 1.1 fusion.22
  10.0 17.1 %reduce-window.6 = s32[32,64,128]{2,1,0:T(8,128)S(1)} reduce-window(s32[32,64,128]{2,1,0:T(8,128)} %fusion.22, s32[]{:T(128)} %constant.25.clone.1), window={size=1x1x128 pad=0_0x0_0x127_0}, to_apply=%region_0.1 | reduce-window | flops 33292288 | bytes 2097156 | tf_op jit(solution)/shard_map/reduce-window
  27.1 0.9 slice_reduce_fusion
  28.1 0.2 reduce-window.9
  28.3 0.3 broadcast_add_fusion
  28.6 0.8 fusion.17
  29.4 0.2 compare_select_fusion.1
  29.6 31.0 %scatter_custom_fusion = s32[8192]{0:T(1024)} fusion(s32[8192]{0:T(1024)S(1)} %bitcast.104, s32[8192]{0:T(1024)S(1)} %get-tuple-element.12, s32[]{:T(128)} %constant.25.clone.1), kind=kCustom, calls=%fused_computation.81 | custom fusion | bytes 32772 | tf_op jit(solution)/shard_map/scatter | solution.py:76
  60.7 11.5 %all-to-all-start = ((s32[32,1,256]{2,1,0:T(1,128)}), s32[32,1,256]{2,1,0:T(1,128)S(1)}, u32[]{:S(2)}, u32[]{:S(2)}) async-start(s32[32,1,256]{2,1,0:T(1,128)} %bitcast.6), calls=%async_computation | async-start | bytes 65536 | tf_op jit(solution)/shard_map/all_to_all | solution.py:79
  72.2 0.0 copy-done.2
  72.2 8.3 %fusion.14 = f32[2048,128]{1,0:T(8,128)S(1)} fusion(f32[2048,128]{1,0:T(8,128)} %param.16, f32[2048,128]{1,0:T(8,128)S(1)} %copy-done.2), kind=kLoop, calls=%fused_computation.29 | loop fusion | flops 19922944 | bytes 3145728 | tf_op jit(solution)/shard_map/sub | solution.py:18
  80.5 1.6 all-to-all-done
  82.1 27.7 %gather_fusion = f32[8192,128]{1,0:T(8,128)} fusion(f32[2048,128]{1,0:T(8,128)S(1)} %fusion.14, s32[8192]{0:T(1024)S(1)} %broadcast_clamp_fusion.1), kind=kCustom, calls=%fused_computation | custom fusion | bytes 8421376 | tf_op jit(solution)/shard_map/gather | solution.py:82
  109.8 8.6 %all-to-all-start.1 = ((f32[32,256,128]{2,1,0:T(8,128)}), f32[32,256,128]{2,1,0:T(8,128)}, u32[]{:S(2)}, u32[]{:S(2)}) async-start(f32[32,256,128]{2,1,0:T(8,128)} %bitcast.95), calls=%async_computation.1 | async-start | bytes 8388608 | tf_op jit(solution)/shard_map/all_to_all | solution.py:87
  118.5 0.1 fusion.48
  118.6 0.1 fusion.33
  118.7 0.1 divide_reduce_fusion.1
  118.8 96.0 %all-to-all-done.1 = f32[32,256,128]{2,1,0:T(8,128)} async-done(((f32[32,256,128]{2,1,0:T(8,128)}), f32[32,256,128]{2,1,0:T(8,128)}, u32[]{:S(2)}, u32[]{:S(2)}) %all-to-all-start.1) | async-done | bytes 4194336 | tf_op jit(solution)/shard_map/all_to_all | solution.py:87
  214.8 29.9 %gather_fusion.1 = f32[8192,128]{1,0:T(8,128)} fusion(f32[8192,128]{1,0:T(8,128)} %bitcast.10, s32[8192]{0:T(1024)S(1)} %broadcast_clamp_fusion), kind=kCustom, calls=%fused_computation.1 | custom fusion | bytes 8421376 | tf_op jit(solution)/shard_map/gather | solution.py:88
  244.7 17.7 %multiply_reduce_fusion.2 = f32[8,128]{1,0:T(8,128)S(1)} fusion(f32[8,128]{1,0:T(8,128)S(1)} %get-tuple-element.15, f32[8,1024]{1,0:T(8,128)S(1)} %bitcast.99, f32[8192,128]{1,0:T(8,128)} %gather_fusion.1, f32[8,1024,128]{2,1,0:T(8,128)} %bitcast.91), kind=kOutput, calls=%fused_computation.15 | output fusion | flops 5250175 | bytes 8429568 | tf_op jit(solution)/shard_map/div | solution.py:30
  262.4 0.2 fusion.46
  262.6 0.0 copy-done.1
  262.6 14.4 %multiply_reduce_fusion.1 = f32[8,128]{1,0:T(8,128)S(1)} fusion(f32[8,128]{1,0:T(8,128)S(1)} %get-tuple-element.19, f32[8,1024]{1,0:T(8,128)S(1)} %bitcast.100, f32[8192,128]{1,0:T(8,128)S(1)} %copy-done.1, f32[8,1024,128]{2,1,0:T(8,128)S(1)} %bitcast.92), kind=kOutput, calls=%fused_computation.13 | output fusion | flops 5250175 | bytes 8429568 | tf_op jit(solution)/shard_map/div | solution.py:30
  277.0 0.2 fusion.38
  277.2 1.2 fusion.5
  278.4 3.8 fusion.4
  282.2 23.0 %scatter_custom_fusion.1 = f32[8192,128]{1,0:T(8,128)} fusion(s32[8192]{0:T(1024)S(1)} %bitcast.106, f32[8192,128]{1,0:T(8,128)} %fusion.4, f32[]{:T(128)} %constant.39.clone.1), kind=kCustom, calls=%fused_computation.20 | custom fusion | bytes 4194816 | tf_op jit(solution)/shard_map/scatter | solution.py:103
  305.2 5.2 all-to-all-start.2
  310.4 0.3 all-reduce.3.cloned.1.call-start
  310.7 2.9 fusion.53
  313.6 94.1 %all-to-all-done.2 = f32[32,256,128]{2,1,0:T(8,128)} async-done(((f32[32,256,128]{2,1,0:T(8,128)}), f32[32,256,128]{2,1,0:T(8,128)}, u32[]{:S(2)}, u32[]{:S(2)}) %all-to-all-start.2) | async-done | bytes 4194336 | tf_op jit(solution)/shard_map/all_to_all | solution.py:105
  407.6 45.4 %scatter_custom_fusion.2 = f32[2048,128]{1,0:T(8,128)} fusion(s32[8192]{0:T(1024)S(1)} %bitcast.108, f32[8192,128]{1,0:T(8,128)} %bitcast.15, f32[]{:T(128)} %constant.39.clone.1), kind=kCustom, calls=%fused_computation.46 | custom fusion | flops 1048576 | bytes 1049088 | tf_op jit(solution)/shard_map/scatter-add | solution.py:115
  453.0 0.0 all-reduce.3.cloned.1.call-update
  453.1 0.0 copy-start.3
  453.1 5.5 multiply_reduce_fusion
  458.6 0.8 divide_reduce_fusion
  459.4 0.5 broadcast_add_fusion.3
  459.9 57.8 %all-reduce.3.cloned.1.call-done = (f32[2048,128]{1,0:T(8,128)}, f32[2048,128]{1,0:T(8,128)}) async-done(((f32[2048,128]{1,0:T(8,128)}, f32[2048,128]{1,0:T(8,128)}), (f32[2048,128]{1,0:T(8,128)}, f32[2048,128]{1,0:T(8,128)})) %all-reduce.3.cloned.1.call-update) | async-done | bytes 2097168 | tf_op jit(solution)/shard_map/psum | solution.py:117
  517.7 1.4 add_multiply_fusion
  519.1 0.7 constant_dynamic-slice_fusion
  519.8 2.2 convolution_bitcast_fusion
  522.0 143.1 %psum.23 = f32[64,128]{1,0:T(8,128)S(1)} all-reduce(f32[64,128]{1,0:T(8,128)S(1)} %convolution_bitcast_fusion), channel_id=1, replica_groups=mesh['users'=32,'items'=8] {'users'}, use_global_device_ids=true, to_apply=%region_18.19 | all-reduce | flops 8192 | bytes 65536 | tf_op jit(solution)/shard_map/psum | solution.py:125
  665.2 0.6 broadcast_multiply_fusion
  (24 shorter events, 0.1 us)
Async XLA Ops:
  7.2 303.5 %copy-start = (f32[64,2048]{1,0:T(8,128)S(1)}, f32[64,2048]{1,0:T(8,128)}, u32[]{:S(2)}) copy-start(f32[64,2048]{1,0:T(8,128)} %param.18) | copy-start | bytes 1572868
  7.2 22.2 %copy-start.4 = (s32[8,8,128]{2,1,0:T(8,128)S(1)}, s32[8,8,128]{2,1,0:T(8,128)}, u32[]{:S(2)}) copy-start(s32[8,8,128]{2,1,0:T(8,128)} %param.10) | copy-start | bytes 98308
  7.2 65.0 %copy-start.2 = (f32[2048,128]{1,0:T(8,128)S(1)}, f32[2048,128]{1,0:T(8,128)}, u32[]{:S(2)}) copy-start(f32[2048,128]{1,0:T(8,128)} %param.15) | copy-start | bytes 3145732
  60.7 21.4 %all-to-all-start = ((s32[32,1,256]{2,1,0:T(1,128)}), s32[32,1,256]{2,1,0:T(1,128)S(1)}, u32[]{:S(2)}, u32[]{:S(2)}) async-start(s32[32,1,256]{2,1,0:T(1,128)} %bitcast.6), calls=%async_computation | async-start | bytes 65536 | tf_op jit(solution)/shard_map/all_to_all | solution.py:79
  109.8 8.7 %copy-start.10 = (s32[8]{0:T(128)S(1)}, s32[8]{0:T(128)}, u32[]{:S(2)}) copy-start(s32[8]{0:T(128)} %param.12) | copy-start | bytes 100
  109.8 8.8 %copy-start.5 = (s32[8,8,128]{2,1,0:T(8,128)S(1)}, s32[8,8,128]{2,1,0:T(8,128)}, u32[]{:S(2)}) copy-start(s32[8,8,128]{2,1,0:T(8,128)} %param.11) | copy-start | bytes 98308
  109.8 8.8 %copy-start.8 = (f32[8,128]{1,0:T(8,128)S(1)}, f32[8,128]{1,0:T(8,128)}, u32[]{:S(2)}) copy-start(f32[8,128]{1,0:T(8,128)} %param.13) | copy-start | bytes 12292
  109.8 8.8 %copy-start.9 = (f32[8,128]{1,0:T(8,128)S(1)}, f32[8,128]{1,0:T(8,128)}, u32[]{:S(2)}) copy-start(f32[8,128]{1,0:T(8,128)} %param.14) | copy-start | bytes 12292
  109.8 105.0 %all-to-all-start.1 = ((f32[32,256,128]{2,1,0:T(8,128)}), f32[32,256,128]{2,1,0:T(8,128)}, u32[]{:S(2)}, u32[]{:S(2)}) async-start(f32[32,256,128]{2,1,0:T(8,128)} %bitcast.95), calls=%async_computation.1 | async-start | bytes 8388608 | tf_op jit(solution)/shard_map/all_to_all | solution.py:87
  244.7 17.7 %copy-start.7 = (f32[128]{0:T(128)S(1)}, f32[128]{0:T(128)}, u32[]{:S(2)}) copy-start(f32[128]{0:T(128)} %param.17) | copy-start | bytes 1540
  244.7 17.9 %copy-start.1 = (f32[8192,128]{1,0:T(8,128)S(1)}, f32[8192,128]{1,0:T(8,128)}, u32[]{:S(2)}) copy-start(f32[8192,128]{1,0:T(8,128)} %gather_fusion.1) | copy-start | bytes 12582916
  305.2 5.5 copy-start.6
  305.2 102.4 %all-to-all-start.2 = ((f32[32,256,128]{2,1,0:T(8,128)}), f32[32,256,128]{2,1,0:T(8,128)}, u32[]{:S(2)}, u32[]{:S(2)}) async-start(f32[32,256,128]{2,1,0:T(8,128)} %bitcast.94), calls=%async_computation.2 | async-start | bytes 8388608 | tf_op jit(solution)/shard_map/all_to_all | solution.py:105
  310.4 207.3 %all-reduce.3.cloned.1.call-start = ((), (), s32[]{:S(2)}) async-start(), calls=%async_computation.3 | async-start | bytes 4194304 | tf_op jit(solution)/shard_map/psum | solution.py:117
  453.1 66.8 %copy-start.3 = (f32[2048,128]{1,0:T(8,128)S(1)}, f32[2048,128]{1,0:T(8,128)}, u32[]{:S(2)}) copy-start(f32[2048,128]{1,0:T(8,128)} %param.16) | copy-start | bytes 3145732
Sparse Core Ops, SparseCore 0:
  453.2 64.5 all-reduce.2
where the time goes:
time: 676 us; the launch traced here: 673 us
  waiting for transfers between devices  250 us (37%)
  blocking collectives  143 us (21%)
  other arithmetic  122 us (18%)
  local copies, waits for them, and re-layouts  113 us (17%)
  starting transfers between devices  25.6 us (4%)
  between operations  14.3 us (2%)
    psum x1, blocking collectives, shards(): lax.psum(partial_grad, 'users') / jnp.sqrt(jnp.float32(total_items))  143 us
    all_to_all x1, waiting for transfers between devices, shards(): lax.all_to_all(answer, 'users', split_axis=0, concat_axis=0, tiled=True)  96 us
    all_to_all x1, waiting for transfers between devices, shards(): lax.all_to_all(outgoing.reshape(owners, capacity, factors), 'users', spli...  94.1 us
    psum x1, waiting for transfers between devices, shards(): totals = lax.psum(local_stats, 'items')  57.8 us
    scatter-add x1, other arithmetic, shards(): local_stats = jnp.zeros((item_rows, factors), jnp.float32).at[wanted_flat...  45.4 us
    div x2, other arithmetic, ascend(): alloc = exp_terms / jnp.sum(exp_terms, axis=-1, keepdims=True)  32 us
    scatter x1, local copies, waits for them, and re-layouts, shards(): requests = jnp.zeros((owners * capacity,), jnp.int32).at[position].set(lo...  31 us
    gather x1, local copies, waits for them, and re-layouts, shards(): returned.reshape(owners * capacity, factors)[position]  29.9 us
  transfers between devices with their start and end apart: 4, of which 4 were waited for; matrix products, arithmetic and copies ran while one was open for 3% of the time, Pallas kernels for 0%

commit v1 on v0

v1 whole, which is shorter than its diff:
```python
import functools

import jax
import jax.numpy as jnp
from jax import lax
from jax.experimental import pallas as pl
from jax.experimental.pallas import tpu as pltpu
from jax.sharding import Mesh
from jax.sharding import PartitionSpec as P

ITERS = 3
USER_RATIO = 4

user_prior = 0.3
activity_prior = 0.3
activity_base = 1.0
item_prior = 0.3
step_weight = 0.5

F32 = jnp.float32
BF16 = jnp.bfloat16
HIGHEST = lax.Precision.HIGHEST
NT = (((1,), (1,)), ((), ()))
NN = (((1,), (0,)), ((), ()))
TN = (((0,), (0,)), ((), ()))
LANES = 128
VMEM_LIMIT = 48 * 1024 * 1024


def exp_digamma_over(x, rate):
    pair = x * (x + 5.0)
    low = pair + 4.0
    high = pair + 6.0
    steps = (2.0 * x + 5.0) * (low * high + pair * (low + high)) / (pair * low * high)
    y = x + 6.0
    inv = 1.0 / y
    sq = inv * inv
    tail = 0.5 * inv + sq * (1.0 / 12.0 - sq * (1.0 / 120.0 - sq * (1.0 / 252.0)))
    return y * jnp.exp(-steps - tail) / rate


def kernel_call(kernel, out_shape, **specs):
    return pl.pallas_call(
        kernel,
        out_shape=out_shape,
        compiler_params=pltpu.CompilerParams(vmem_limit_bytes=VMEM_LIMIT),
        **specs,
    )


def shape_of(*dims):
    return jax.ShapeDtypeStruct(dims, F32)


def prep_kernel(owners, counts_ref, ids_ref, clicks_ref, shape_ref, rate_ref, send_ref, theta_ref):
    rows = ids_ref.shape[0]
    blocks = 8
    width = 2 * LANES
    capacity = rows * LANES // owners
    before = (
        lax.broadcasted_iota(jnp.int32, (width, width), 0)
        < lax.broadcasted_iota(jnp.int32, (width, width), 1)
    )
    before = jnp.where(before, 1.0, 0.0).astype(BF16)
    owner_iota = lax.broadcasted_iota(jnp.int32, (owners, width), 0)
    rank_iota = lax.broadcasted_iota(jnp.int32, (capacity, width), 0).astype(F32)
    carry = jnp.zeros((owners, 1), F32)
    lists = jnp.zeros((3 * owners, capacity), F32)
    for chunk in range(rows // 2):
        user = 2 * chunk // blocks
        ids = jnp.concatenate(
            [ids_ref[2 * chunk : 2 * chunk + 1, :], ids_ref[2 * chunk + 1 : 2 * chunk + 2, :]], axis=1
        )
        weights = []
        for row in (2 * chunk, 2 * chunk + 1):
            live = jnp.where(row % blocks < counts_ref[user], 1.0, 0.0)
            weights.append(clicks_ref[row : row + 1, :].astype(F32) * live)
        weight = jnp.concatenate(weights, axis=1)
        marks = jnp.where(owner_iota == (ids >> 11), 1.0, 0.0)
        earlier = lax.dot_general(marks.astype(BF16), before, NN, preferred_element_type=F32)
        rank = jnp.sum(marks * (earlier + carry), axis=0, keepdims=True)
        carry = carry + jnp.sum(marks, axis=1, keepdims=True)
        place = jnp.where(rank_iota == rank, 1.0, 0.0).astype(BF16)
        high = (((ids >> 7) & 15) * 8 + user).astype(F32)
        low = (ids & 127).astype(F32)
        payload = jnp.concatenate([marks * high, marks * low, marks * weight], axis=0).astype(BF16)
        lists = lists + lax.dot_general(payload, place, NT, preferred_element_type=F32)
    theta = exp_digamma_over(shape_ref[...], rate_ref[...])
    theta_ref[...] = theta
    zeros = jnp.zeros((2, LANES), F32)
    for owner in range(owners):
        for part in range(3):
            line = lists[part * owners + owner : part * owners + owner + 1, :]
            send_ref[owner, 2 * part : 2 * part + 1, :] = line[:, :LANES]
            send_ref[owner, 2 * part + 1 : 2 * part + 2, :] = line[:, LANES:]
        send_ref[owner, 6:8, :] = zeros
        send_ref[owner, 8:16, :] = theta


def table_kernel(shape_ref, rate_ref, table_ref):
    table_ref[...] = exp_digamma_over(shape_ref[...], rate_ref[...])


def ascend_block(theta, marks, table):
    share = lax.dot_general(theta, table, NT, precision=HIGHEST, preferred_element_type=F32)
    ratio = marks / share
    return ratio, lax.dot_general(ratio, table, NN, precision=HIGHEST, preferred_element_type=F32)


def build_kernel(recv_ref, table_ref, marks_ref, partial_ref):
    owners = recv_ref.shape[0]
    highs = marks_ref.shape[0]
    line_iota = lax.broadcasted_iota(jnp.int32, (LANES, 2 * LANES), 0).astype(F32)

    def wide(source, part):
        return jnp.concatenate(
            [recv_ref[source, 2 * part : 2 * part + 1, :], recv_ref[source, 2 * part + 1 : 2 * part + 2, :]],
            axis=1,
        )

    for source in range(owners):
        left = jnp.where(line_iota == wide(source, 0), wide(source, 2), 0.0).astype(BF16)
        right = jnp.where(line_iota == wide(source, 1), 1.0, 0.0).astype(BF16)
        tile = lax.dot_general(left, right, NT, preferred_element_type=F32)
        for high in range(highs):
            marks_ref[high, 8 * source : 8 * source + 8, :] = tile[8 * high : 8 * high + 8, :]
    theta = jnp.concatenate([recv_ref[source, 8:16, :] for source in range(owners)], axis=0)
    total = jnp.zeros(theta.shape, F32)
    for high in range(highs):
        table = table_ref[high * LANES : (high + 1) * LANES, :]
        total = total + ascend_block(theta, marks_ref[high], table)[1]
    partial_ref[...] = total


def ascend_kernel(theta_ref, marks_ref, table_ref, partial_ref):
    theta = theta_ref[...]
    total = jnp.zeros(theta.shape, F32)
    for high in range(marks_ref.shape[0]):
        table = table_ref[high * LANES : (high + 1) * LANES, :]
        total = total + ascend_block(theta, marks_ref[high], table)[1]
    partial_ref[...] = total


def last_kernel(theta_ref, marks_ref, table_ref, partial_ref, stats_ref):
    theta = theta_ref[...]
    total = jnp.zeros(theta.shape, F32)
    for high in range(marks_ref.shape[0]):
        table = table_ref[high * LANES : (high + 1) * LANES, :]
        ratio, part = ascend_block(theta, marks_ref[high], table)
        total = total + part
        spread = lax.dot_general(ratio, theta, TN, precision=HIGHEST, preferred_element_type=F32)
        stats_ref[high * LANES : (high + 1) * LANES, :] = table * spread
    partial_ref[...] = total


def update_kernel(
    activity_shape, recv_ref, theta_ref, activity_ref, totals_ref, shapes_ref, rates_ref, active_ref, next_ref, send_ref
):
    total = jnp.sum(recv_ref[...], axis=0)
    shapes = user_prior + theta_ref[...] * total
    rates = activity_shape / activity_ref[...] + totals_ref[...]
    shapes_ref[...] = shapes
    rates_ref[...] = rates
    active = activity_base + jnp.sum(shapes / rates, axis=1, keepdims=True)
    active_ref[...] = jnp.broadcast_to(active, shapes.shape)
    theta = exp_digamma_over(shapes, rates)
    next_ref[...] = theta
    send_ref[...] = jnp.broadcast_to(theta[None], send_ref.shape)


def shards(
    item_ids,
    clicks,
    block_counts,
    user_shape0,
    user_rate0,
    item_shape,
    item_rate,
    beta_totals,
    covariates,
    cov_weight,
):
    y_size, z_size = lax.axis_size("y"), lax.axis_size("z")
    owners = y_size * z_size
    item_rows, factors = item_shape.shape
    users_here, blocks, block_width = item_ids.shape
    slot_rows = users_here * blocks
    highs = item_rows // LANES
    split_count = lax.axis_size(("x", "core"))
    share_rows = item_rows // split_count
    first_row = lax.axis_index(("x", "core")) * share_rows
    activity_shape = activity_prior + factors * user_prior
    user_axes = ("y", "z")
    item_axes = ("x", "core")

    def exchange(array, axes):
        return lax.all_to_all(array, axes, split_axis=0, concat_axis=0, tiled=True)

    cov_full = lax.all_gather(covariates, item_axes, axis=0, tiled=True)
    weight_full = lax.all_gather(cov_weight, item_axes, axis=0, tiled=True)

    smem = pl.BlockSpec(memory_space=pltpu.SMEM)
    vmem = pl.BlockSpec(memory_space=pltpu.VMEM)
    send, theta = kernel_call(
        functools.partial(prep_kernel, owners),
        (shape_of(owners, 16, LANES), shape_of(users_here, factors)),
        in_specs=[smem, vmem, vmem, vmem, vmem],
    )(
        block_counts,
        item_ids.reshape(slot_rows, block_width),
        clicks.reshape(slot_rows, block_width),
        user_shape0,
        user_rate0,
    )
    recv = exchange(send, user_axes)
    table = kernel_call(table_kernel, shape_of(item_rows, factors))(item_shape, item_rate)
    marks, partial = kernel_call(
        build_kernel, (shape_of(highs, owners * users_here, LANES), shape_of(owners * users_here, factors))
    )(recv, table)
    active = jnp.broadcast_to(
        activity_base + jnp.sum(user_shape0 / user_rate0, axis=1, keepdims=True), user_shape0.shape
    )
    totals = beta_totals[None, :]
    small = shape_of(users_here, factors)
    for iteration in range(ITERS - 1):
        parts = exchange(partial.reshape(owners, users_here, factors), user_axes)
        _, _, active, theta, spread = kernel_call(
            functools.partial(update_kernel, activity_shape),
            (small, small, small, small, shape_of(owners, users_here, factors)),
        )(parts, theta, active, totals)
        theta_all = exchange(spread, user_axes).reshape(owners * users_here, factors)
        if iteration < ITERS - 2:
            partial = kernel_call(ascend_kernel, shape_of(owners * users_here, factors))(
                theta_all, marks, table
            )
    partial, stats = kernel_call(
        last_kernel, (shape_of(owners * users_here, factors), shape_of(item_rows, factors))
    )(theta_all, marks, table)

    stats_here = jnp.sum(
        exchange(stats, item_axes).reshape(split_count, share_rows, factors), axis=0
    )
    shape_here = lax.dynamic_slice_in_dim(item_shape, first_row, share_rows, 0)
    rate_here = lax.dynamic_slice_in_dim(item_rate, first_row, share_rows, 0)
    cov_here = lax.dynamic_slice_in_dim(cov_full, first_row, share_rows, 1)
    prior_log = lax.dot_general(cov_here, weight_full, TN, precision=HIGHEST, preferred_element_type=F32)
    scale = jnp.exp(prior_log) / rate_here
    new_shape = (1.0 - step_weight) * shape_here + step_weight * (item_prior + USER_RATIO * stats_here)
    item_score = item_prior - scale * new_shape
    grad_part = jnp.dot(cov_here, item_score, precision=HIGHEST, preferred_element_type=F32)
    cov_rows = covariates.shape[0]
    grad_part = jnp.sum(
        exchange(grad_part, item_axes).reshape(split_count, cov_rows, factors), axis=0
    )

    by_z = partial.reshape(y_size, z_size, users_here, factors).transpose(1, 0, 2, 3)
    by_z = by_z.reshape(z_size, y_size * users_here, factors)
    both = jnp.concatenate(
        [by_z, jnp.broadcast_to(grad_part[None], (z_size, cov_rows, factors))], axis=1
    )
    both = jnp.sum(exchange(both, ("z",)), axis=0)
    user_part = both[: y_size * users_here].reshape(y_size, users_here, factors)
    grad_part = both[y_size * users_here :]
    both = jnp.concatenate(
        [user_part, jnp.broadcast_to(grad_part[None], (y_size, cov_rows, factors))], axis=1
    )
    both = jnp.sum(exchange(both, ("y",)), axis=0)
    user_shape = user_prior + theta * both[:users_here]
    user_rate = activity_shape / active + totals
    activity_rate = activity_base + jnp.sum(user_shape / user_rate, axis=1)
    cov_grad = both[users_here:] / jnp.sqrt(jnp.float32(item_rows * owners))
    return (user_shape, user_rate, activity_rate, new_shape, cov_grad)


def solution(mesh):
    fine = Mesh(mesh.devices.reshape(4, 8, 4, 2), ("y", "z", "x", "core"))
    users, items = ("y", "z"), ("x", "core")
    both = users + items
    return jax.shard_map(
        shards,
        mesh=fine,
        in_specs=(
            P(both, None, None),
            P(both, None, None),
            P(both),
            P(both, None),
            P(both, None),
            P(users, None),
            P(users, None),
            P(),
            P(items, users),
            P(items, None),
        ),
        out_specs=(
            P(both, None),
            P(both, None),
            P(both),
            P(both, None),
            P(items, None),
        ),
        check_vma=False,
    )
```

time: 676 us -> 193 us (0.29)
  waiting for transfers between devices: 250 us -> 25.9 us
  other arithmetic: 122 us -> 3.06 us
  local copies, waits for them, and re-layouts: 113 us -> 7.09 us
  blocking collectives: 143 us -> 87.9 us
  Pallas kernels: 0 us -> 24.7 us
    all_to_all x3 -> x4, waiting for transfers between devices: 192 us -> 25.2 us  [exchange(): return lax.all_to_all(array, axes, split_axis=0, concat_axis=0, tiled=True)]
    psum x1 -> x0, blocking collectives: 143 us -> none  [shards(): lax.psum(partial_grad, 'users') / jnp.sqrt(jnp.float32(total_items))]
    all_to_all x0 -> x5, blocking collectives: none -> 67 us  [exchange(): return lax.all_to_all(array, axes, split_axis=0, concat_axis=0, tiled=True)]
    psum x1 -> x0, waiting for transfers between devices: 57.8 us -> none  [shards(): totals = lax.psum(local_stats, 'items')]
    gather x2 -> x0, local copies, waits for them, and re-layouts: 57.6 us -> none  [the longest x1 29.9 us: shards(): returned.reshape(owners * capacity, factors)[position]]
    scatter x2 -> x0, local copies, waits for them, and re-layouts: 54 us -> none  [the longest x1 31 us: shards(): requests = jnp.zeros((owners * capacity,), jnp.int32).at[position].set(lo...]
    scatter-add x1 -> x0, other arithmetic: 45.4 us -> none  [shards(): local_stats = jnp.zeros((item_rows, factors), jnp.float32).at[wanted_flat...]
    div x6 -> x1, other arithmetic: 32.7 us -> 0.62 us  [shards(): cov_grad = both[users_here:] / jnp.sqrt(jnp.float32(item_rows * owners))]
  transfers between devices with their start and end apart: 4 -> 5, of which waited for: 4 -> 3; matrix products, arithmetic and copies ran while one was open for 3% -> 1% of each run, Pallas kernels for 0% -> 13%
where the time goes in v1:
time: 193 us
  blocking collectives  87.9 us (46%)
  waiting for transfers between devices  25.9 us (13%)
  starting transfers between devices  25.3 us (13%)
  Pallas kernels  24.7 us (13%)
  between operations  14.2 us (7%)
  local copies, waits for them, and re-layouts  7.09 us (4%)
  matrix products  4.42 us (2%)
  other arithmetic  3.06 us (2%)
    all_to_all x5, blocking collectives, exchange(): return lax.all_to_all(array, axes, split_axis=0, concat_axis=0, tiled=True)  67 us
    all_to_all x4, starting transfers between devices, exchange(): return lax.all_to_all(array, axes, split_axis=0, concat_axis=0, tiled=True)  25.2 us
    all_to_all x4, waiting for transfers between devices, exchange(): return lax.all_to_all(array, axes, split_axis=0, concat_axis=0, tiled=True)  25.2 us
    all_gather x1, blocking collectives, shards(): weight_full = lax.all_gather(cov_weight, item_axes, axis=0, tiled=True)  20.9 us
    pallas_call x1, Pallas kernels, shards(): kernel_call(last_kernel, (shape_of(owners * users_here, factors), shape_o...  8.22 us
    unnamed x26, local copies, waits for them, and re-layouts  6.98 us
    pallas_call x1, Pallas kernels, shards(): kernel_call(build_kernel, (shape_of(highs, owners * users_here, LANES), s...  5.15 us
    pallas_call x1, Pallas kernels, shards(): kernel_call(functools.partial(prep_kernel, owners), (shape_of(owners, 16,...  5.08 us
  transfers between devices with their start and end apart: 5, of which 3 were waited for; matrix products, arithmetic and copies ran while one was open for 1% of the time, Pallas kernels for 13%

profile of v1, /device:TPU:2, one launch (start us, length us, event | category | flops | bytes accessed | tf_op | source)
XLA Modules:
  0.0 192.5 jit_solution(10155827591344732621)
XLA Ops:
  7.2 0.0 all-gather.2.cloned.1.call-start
  7.2 0.7 all-gather.2.cloned.1.call-update
  7.9 0.0 copy-start.3
  7.9 0.7 copy-done.3
  8.7 0.8 copy-done.4
  9.5 0.7 copy-done.5
  10.1 0.7 copy-done.7
  10.8 0.7 copy-done.10
  11.5 5.1 %shard_map.137 = (f32[32,16,128]{2,1,0:T(8,128)}, f32[8,128]{1,0:T(8,128)S(1)}) custom-call(s32[8]{0:T(128)S(1)} %copy-done.10, s32[64,128]{1,0:T(8,128)S(1)} %bitcast.24, s32[64,128]{1,0:T(8,128)S(1)} %bitcast.25, f32[8,128]{1,0:T(8,128)S(1)} %copy-done.5, f32[8,128]{1,0:T(8,128)S(1)} %copy-done.7), custom_call_target="tpu_custom_call" | custom-call | tf_op jit(solution)/shard_map/pallas_call | solution.py:204
  16.6 11.5 %all-to-all-start = ((f32[32,16,128]{2,1,0:T(8,128)}), f32[32,16,128]{2,1,0:T(8,128)S(1)}, u32[]{:S(2)}, u32[]{:S(2)}) async-start(f32[32,16,128]{2,1,0:T(8,128)} %get-tuple-element.17), calls=%async_computation | async-start | bytes 524288 | tf_op jit(solution)/shard_map/all_to_all | solution.py:197
  28.0 0.0 copy-start
  28.1 1.2 copy-done
  29.3 1.2 copy-done.1
  30.5 1.1 shard_map.138.table_ref
  31.6 8.9 %all-to-all-done.recv_ref = f32[32,16,128]{2,1,0:T(8,128)S(1)} async-done(((f32[32,16,128]{2,1,0:T(8,128)}), f32[32,16,128]{2,1,0:T(8,128)S(1)}, u32[]{:S(2)}, u32[]{:S(2)}) %all-to-all-start) | async-done | bytes 262176 | tf_op jit(solution)/shard_map/all_to_all | solution.py:197
  40.5 5.1 %shard_map.139 = (f32[16,256,128]{2,1,0:T(8,128)S(1)}, f32[256,128]{1,0:T(8,128)}) custom-call(f32[32,16,128]{2,1,0:T(8,128)S(1)} %all-to-all-done.recv_ref, f32[2048,128]{1,0:T(8,128)S(1)} %shard_map.138.table_ref), custom_call_target="tpu_custom_call" | custom-call | tf_op jit(solution)/shard_map/pallas_call | solution.py:217
  45.7 4.4 %all-to-all-start.1 = ((f32[32,8,128]{2,1,0:T(8,128)}), f32[32,8,128]{2,1,0:T(8,128)S(1)}, u32[]{:S(2)}, u32[]{:S(2)}) async-start(f32[32,8,128]{2,1,0:T(8,128)} %bitcast.2), calls=%async_computation.1 | async-start | bytes 262144 | tf_op jit(solution)/shard_map/all_to_all | solution.py:197
  50.1 0.0 copy-done.6
  50.1 0.0 copy-done.8
  50.1 0.1 divide_reduce_fusion.1
  50.2 10.2 %all-to-all-done.1.recv_ref = f32[32,8,128]{2,1,0:T(8,128)S(1)} async-done(((f32[32,8,128]{2,1,0:T(8,128)}), f32[32,8,128]{2,1,0:T(8,128)S(1)}, u32[]{:S(2)}, u32[]{:S(2)}) %all-to-all-start.1) | async-done | bytes 131104 | tf_op jit(solution)/shard_map/all_to_all | solution.py:197
  60.4 0.1 broadcast_in_dim.8.activity_ref
  60.5 0.0 copy-done.9
  60.5 0.6 shard_map.140
  61.1 13.8 %all_to_all.53 = f32[32,8,128]{2,1,0:T(8,128)S(1)} all-to-all(f32[32,8,128]{2,1,0:T(8,128)S(1)} %get-tuple-element.20), channel_id=1, replica_groups=mesh['y'=4,'z'=8,'x'=4,'core'=2] {'y','z'}, dimensions={0} | all-to-all | bytes 262144 | tf_op jit(solution)/shard_map/all_to_all | solution.py:197
  75.0 3.9 %shard_map.141 = f32[256,128]{1,0:T(8,128)S(1)} custom-call(f32[256,128]{1,0:T(8,128)S(1)} %bitcast.21, f32[16,256,128]{2,1,0:T(8,128)S(1)} %get-tuple-element.21.marks_ref, f32[2048,128]{1,0:T(8,128)S(1)} %shard_map.138.table_ref), custom_call_target="tpu_custom_call" | custom-call | tf_op jit(solution)/shard_map/pallas_call | solution.py:233
  78.9 13.8 %all_to_all.54.recv_ref = f32[32,8,128]{2,1,0:T(8,128)S(1)} all-to-all(f32[32,8,128]{2,1,0:T(8,128)S(1)} %bitcast.22), channel_id=1, replica_groups=mesh['y'=4,'z'=8,'x'=4,'core'=2] {'y','z'}, dimensions={0} | all-to-all | bytes 262144 | tf_op jit(solution)/shard_map/all_to_all | solution.py:197
  92.7 0.6 shard_map.142
  93.3 13.8 %all_to_all.55 = f32[32,8,128]{2,1,0:T(8,128)S(1)} all-to-all(f32[32,8,128]{2,1,0:T(8,128)S(1)} %get-tuple-element.25), channel_id=1, replica_groups=mesh['y'=4,'z'=8,'x'=4,'core'=2] {'y','z'}, dimensions={0} | all-to-all | bytes 262144 | tf_op jit(solution)/shard_map/all_to_all | solution.py:197
  107.1 8.2 %shard_map.143 = (f32[256,128]{1,0:T(8,128)S(1)}, f32[2048,128]{1,0:T(8,128)S(1)}) custom-call(f32[256,128]{1,0:T(8,128)S(1)} %bitcast.20, f32[16,256,128]{2,1,0:T(8,128)S(1)} %get-tuple-element.21.marks_ref, f32[2048,128]{1,0:T(8,128)S(1)} %shard_map.138.table_ref), custom_call_target="tpu_custom_call" | custom-call | tf_op jit(solution)/shard_map/pallas_call | solution.py:236
  115.4 1.0 copy-done.2
  116.3 4.8 %all-to-all-start.5 = ((f32[8,256,128]{2,1,0:T(8,128)}), f32[8,256,128]{2,1,0:T(8,128)S(1)}, u32[]{:S(2)}, u32[]{:S(2)}) async-start(f32[8,256,128]{2,1,0:T(8,128)} %bitcast.19), calls=%async_computation.5 | async-start | bytes 2097152 | tf_op jit(solution)/shard_map/all_to_all | solution.py:197
  121.1 0.0 copy-done.12
  121.1 20.9 %all_gather.7 = f32[512,128]{1,0:T(8,128)S(1)} all-gather(f32[64,128]{1,0:T(8,128)S(1)} %copy-done.12), channel_id=1, replica_groups=mesh['y'=4,'z'=8,'x'=4,'core'=2] {'x','core'}, dimensions={0}, use_global_device_ids=true | all-gather | bytes 294912 | tf_op jit(solution)/shard_map/all_gather | solution.py:200
  142.0 0.0 all-to-all-done.5
  142.0 0.1 reduce_sum.55
  142.1 0.9 add_multiply_fusion
  143.0 0.0 copy-start.11
  143.0 0.0 all-gather.2.cloned.1.call-done
  143.1 2.1 %fusion.2 = f32[256,128]{1,0:T(8,128)S(1)} fusion(f32[256,128]{1,0:T(8,128)S(1)} %add_multiply_fusion, f32[512,128]{1,0:T(8,128)S(1)} %all_gather.7, f32[512,2048]{1,0:T(8,128)} %all-gather.2.cloned.1.call-done, s32[]{:T(128)S(6)} %select_n.2, f32[2048,128]{1,0:T(8,128)} %rate_ref.3), kind=kOutput, calls=%fused_computation.3 | convolution fusion | flops 201424896 | bytes 1180672 | tf_op jit(solution)/shard_map/dot_general | solution.py:246
  145.2 2.3 %fusion.3 = f32[512,128]{1,0:T(8,128)} fusion(f32[256,128]{1,0:T(8,128)S(1)} %fusion.2, f32[512,2048]{1,0:T(8,128)} %all-gather.2.cloned.1.call-done, s32[]{:T(128)S(6)} %select_n.2), kind=kOutput, calls=%fused_computation.4 | convolution fusion | flops 201326592 | bytes 917508 | tf_op jit(solution)/shard_map/dot_general | solution.py:250
  147.5 4.5 %all-to-all-start.6 = ((f32[8,64,128]{2,1,0:T(8,128)}), f32[8,64,128]{2,1,0:T(8,128)S(1)}, u32[]{:S(2)}, u32[]{:S(2)}) async-start(f32[8,64,128]{2,1,0:T(8,128)} %bitcast.11), calls=%async_computation.6 | async-start | bytes 524288 | tf_op jit(solution)/shard_map/all_to_all | solution.py:197
  152.0 6.1 %all-to-all-done.6 = f32[8,64,128]{2,1,0:T(8,128)S(1)} async-done(((f32[8,64,128]{2,1,0:T(8,128)}), f32[8,64,128]{2,1,0:T(8,128)S(1)}, u32[]{:S(2)}, u32[]{:S(2)}) %all-to-all-start.6) | async-done | bytes 262176 | tf_op jit(solution)/shard_map/all_to_all | solution.py:197
  158.2 17.0 %all_to_all.56 = f32[8,96,128]{2,1,0:T(8,128)S(1)} all-to-all(f32[8,96,128]{2,1,0:T(8,128)S(1)} %pad_maximum_fusion), channel_id=1, replica_groups=mesh['y'=4,'z'=8,'x'=4,'core'=2] {'z'}, dimensions={0} | all-to-all | bytes 786432 | tf_op jit(solution)/shard_map/all_to_all | solution.py:197
  175.3 8.5 %all_to_all.57 = f32[4,72,128]{2,1,0:T(8,128)S(1)} all-to-all(f32[4,72,128]{2,1,0:T(8,128)S(1)} %pad_maximum_fusion.1), channel_id=1, replica_groups=mesh['y'=4,'z'=8,'x'=4,'core'=2] {'y'}, dimensions={0} | all-to-all | bytes 294912 | tf_op jit(solution)/shard_map/all_to_all | solution.py:197
  183.8 0.6 slice_multiply_fusion
  184.4 0.7 divide_reduce_fusion
  185.2 0.5 broadcast_add_fusion
  (22 shorter events, 0.2 us)
Async XLA Ops:
  7.2 42.9 %copy-start.6 = (f32[8,128]{1,0:T(8,128)S(1)}, f32[8,128]{1,0:T(8,128)}, u32[]{:S(2)}) copy-start(f32[8,128]{1,0:T(8,128)} %shape_ref.2) | copy-start | bytes 12292
  7.2 42.9 %copy-start.8 = (f32[8,128]{1,0:T(8,128)S(1)}, f32[8,128]{1,0:T(8,128)}, u32[]{:S(2)}) copy-start(f32[8,128]{1,0:T(8,128)} %rate_ref.2) | copy-start | bytes 12292
  7.2 53.3 %copy-start.9 = (f32[128]{0:T(128)S(1)}, f32[128]{0:T(128)}, u32[]{:S(2)}) copy-start(f32[128]{0:T(128)} %param.17) | copy-start | bytes 1540
  7.2 135.9 %all-gather.2.cloned.1.call-start = ((), (), s32[]{:S(2)}) async-start(), calls=%async_computation.9 | async-start | bytes 4718592 | tf_op jit(solution)/shard_map/all_gather | solution.py:199
  7.9 0.8 copy-start.3
  8.7 0.8 copy-start.4
  9.4 0.7 copy-start.5
  10.1 0.7 copy-start.7
  10.8 0.7 copy-start.10
  16.6 23.9 %all-to-all-start = ((f32[32,16,128]{2,1,0:T(8,128)}), f32[32,16,128]{2,1,0:T(8,128)S(1)}, u32[]{:S(2)}, u32[]{:S(2)}) async-start(f32[32,16,128]{2,1,0:T(8,128)} %get-tuple-element.17), calls=%async_computation | async-start | bytes 524288 | tf_op jit(solution)/shard_map/all_to_all | solution.py:197
  28.0 1.2 copy-start
  29.3 1.2 copy-start.1
  45.7 14.8 %all-to-all-start.1 = ((f32[32,8,128]{2,1,0:T(8,128)}), f32[32,8,128]{2,1,0:T(8,128)S(1)}, u32[]{:S(2)}, u32[]{:S(2)}) async-start(f32[32,8,128]{2,1,0:T(8,128)} %bitcast.2), calls=%async_computation.1 | async-start | bytes 262144 | tf_op jit(solution)/shard_map/all_to_all | solution.py:197
  75.0 46.2 %copy-start.12 = (f32[64,128]{1,0:T(8,128)S(1)}, f32[64,128]{1,0:T(8,128)}, u32[]{:S(2)}) copy-start(f32[64,128]{1,0:T(8,128)} %param.19) | copy-start | bytes 98308
  115.3 1.0 copy-start.2
  116.3 25.7 %all-to-all-start.5 = ((f32[8,256,128]{2,1,0:T(8,128)}), f32[8,256,128]{2,1,0:T(8,128)S(1)}, u32[]{:S(2)}, u32[]{:S(2)}) async-start(f32[8,256,128]{2,1,0:T(8,128)} %bitcast.19), calls=%async_computation.5 | async-start | bytes 2097152 | tf_op jit(solution)/shard_map/all_to_all | solution.py:197
  143.0 42.6 %copy-start.11 = (f32[256,128]{1,0:T(8,128)}, f32[256,128]{1,0:T(8,128)S(1)}, u32[]{:S(2)}) copy-start(f32[256,128]{1,0:T(8,128)S(1)} %add_multiply_fusion) | copy-start | bytes 393220
  147.5 10.6 %all-to-all-start.6 = ((f32[8,64,128]{2,1,0:T(8,128)}), f32[8,64,128]{2,1,0:T(8,128)S(1)}, u32[]{:S(2)}, u32[]{:S(2)}) async-start(f32[8,64,128]{2,1,0:T(8,128)} %bitcast.11), calls=%async_computation.6 | async-start | bytes 524288 | tf_op jit(solution)/shard_map/all_to_all | solution.py:197
Sparse Core Ops, SparseCore 0:
  9.9 36.5 all-gather.1

commit v2 on v1

--- a/solution.py
+++ b/solution.py
@@ -1,4 +1,5 @@
 import functools
+import math
 
 import jax
 import jax.numpy as jnp
@@ -101,10 +102,38 @@
     table_ref[...] = exp_digamma_over(shape_ref[...], rate_ref[...])
 
 
-def ascend_block(theta, marks, table):
-    share = lax.dot_general(theta, table, NT, precision=HIGHEST, preferred_element_type=F32)
-    ratio = marks / share
-    return ratio, lax.dot_general(ratio, table, NN, precision=HIGHEST, preferred_element_type=F32)
+def split(x):
+    high = x.astype(BF16)
+    return high, (x - high.astype(F32)).astype(BF16)
+
+
+def dot(left, right, dims):
+    return lax.dot_general(left, right, dims, preferred_element_type=F32)
+
+
+def ascend(theta, marks_ref, table_ref, stats_ref=None):
+    factors = theta.shape[1]
+    theta_high, theta_low = split(theta)
+    theta_both = jnp.concatenate([theta_high, theta_low], axis=1)
+    total = jnp.zeros(theta.shape, F32)
+    width = 2 * LANES
+    for pair in range(marks_ref.shape[0] // 2):
+        rows = slice(pair * width, (pair + 1) * width)
+        table = table_ref[rows, :]
+        table_high, table_low = split(table)
+        share = dot(theta_both, jnp.concatenate([table_high, table_high], axis=1), NT) + dot(
+            theta_high, table_low, NT
+        )
+        marks = jnp.concatenate([marks_ref[2 * pair], marks_ref[2 * pair + 1]], axis=1)
+        ratio = marks / share
+        ratio_high, ratio_low = split(ratio)
+        wide = dot(ratio_high, jnp.concatenate([table_high, table_low], axis=1), NN)
+        total = total + (wide[:, :factors] + wide[:, factors:]) + dot(ratio_low, table_high, NN)
+        if stats_ref is not None:
+            wide = dot(ratio_high, theta_both, TN)
+            spread = wide[:, :factors] + wide[:, factors:] + dot(ratio_low, theta_high, TN)
+            stats_ref[rows, :] = table * spread
+    return total
 
 
 def build_kernel(recv_ref, table_ref, marks_ref, partial_ref):
@@ -125,32 +154,15 @@
         for high in range(highs):
             marks_ref[high, 8 * source : 8 * source + 8, :] = tile[8 * high : 8 * high + 8, :]
     theta = jnp.concatenate([recv_ref[source, 8:16, :] for source in range(owners)], axis=0)
-    total = jnp.zeros(theta.shape, F32)
-    for high in range(highs):
-        table = table_ref[high * LANES : (high + 1) * LANES, :]
-        total = total + ascend_block(theta, marks_ref[high], table)[1]
-    partial_ref[...] = total
+    partial_ref[...] = ascend(theta, marks_ref, table_ref)
 
 
 def ascend_kernel(theta_ref, marks_ref, table_ref, partial_ref):
-    theta = theta_ref[...]
-    total = jnp.zeros(theta.shape, F32)
-    for high in range(marks_ref.shape[0]):
-        table = table_ref[high * LANES : (high + 1) * LANES, :]
-        total = total + ascend_block(theta, marks_ref[high], table)[1]
-    partial_ref[...] = total
+    partial_ref[...] = ascend(theta_ref[...], marks_ref, table_ref)
 
 
 def last_kernel(theta_ref, marks_ref, table_ref, partial_ref, stats_ref):
-    theta = theta_ref[...]
-    total = jnp.zeros(theta.shape, F32)
-    for high in range(marks_ref.shape[0]):
-        table = table_ref[high * LANES : (high + 1) * LANES, :]
-        ratio, part = ascend_block(theta, marks_ref[high], table)
-        total = total + part
-        spread = lax.dot_general(ratio, theta, TN, precision=HIGHEST, preferred_element_type=F32)
-        stats_ref[high * LANES : (high + 1) * LANES, :] = table * spread
-    partial_ref[...] = total
+    partial_ref[...] = ascend(theta_ref[...], marks_ref, table_ref, stats_ref)
 
 
 def update_kernel(
@@ -166,6 +178,52 @@
     theta = exp_digamma_over(shapes, rates)
     next_ref[...] = theta
     send_ref[...] = jnp.broadcast_to(theta[None], send_ref.shape)
+
+
+def score_kernel(stats_ref, shape_ref, scale_ref, cov_ref, new_ref, grad_ref):
+    stats = jnp.sum(stats_ref[...], axis=0)
+    new_shape = (1.0 - step_weight) * shape_ref[...] + step_weight * (item_prior + USER_RATIO * stats)
+    new_ref[...] = new_shape
+    score = item_prior - scale_ref[...] * new_shape
+    parts, rows, _ = grad_ref.shape
+    share = score.shape[0]
+    for part in range(parts):
+        grad_ref[part] = lax.dot_general(
+            cov_ref[part, :, :share], score, NN, precision=HIGHEST, preferred_element_type=F32
+        )
+
+
+def join_kernel(grad_ref, partial_ref, send_ref):
+    parts, rows, _ = send_ref.shape
+    half = rows // 2
+    grad = jnp.sum(grad_ref[...], axis=0)
+    for part in range(parts):
+        send_ref[part, :half, :] = partial_ref[part * half : (part + 1) * half, :]
+        send_ref[part, half:, :] = grad
+
+
+def fan_kernel(recv_ref, send_ref):
+    parts, rows, _ = send_ref.shape
+    total = jnp.sum(recv_ref[...], axis=0)
+    half = total.shape[0] // 2
+    users = half // parts
+    for part in range(parts):
+        send_ref[part, :users, :] = total[part * users : (part + 1) * users, :]
+        send_ref[part, users:, :] = total[half:, :]
+
+
+def finish_kernel(
+    activity_shape, root, recv_ref, theta_ref, activity_ref, totals_ref, shapes_ref, rates_ref, active_ref, grad_ref
+):
+    total = jnp.sum(recv_ref[...], axis=0)
+    users = theta_ref.shape[0]
+    shapes = user_prior + theta_ref[...] * total[:users]
+    rates = activity_shape / activity_ref[...] + totals_ref[...]
+    shapes_ref[...] = shapes
+    rates_ref[...] = rates
+    active = activity_base + jnp.sum(shapes / rates, axis=1, keepdims=True)
+    active_ref[...] = jnp.broadcast_to(active, shapes.shape)
+    grad_ref[...] = total[users:] / root
 
 
 def shards(
@@ -196,8 +254,22 @@
     def exchange(array, axes):
         return lax.all_to_all(array, axes, split_axis=0, concat_axis=0, tiled=True)
 
-    cov_full = lax.all_gather(covariates, item_axes, axis=0, tiled=True)
-    weight_full = lax.all_gather(cov_weight, item_axes, axis=0, tiled=True)
+    cov_rows = covariates.shape[0]
+    cov_send = jnp.concatenate(
+        [
+            covariates.reshape(cov_rows, split_count, share_rows).transpose(1, 0, 2),
+            jnp.broadcast_to(cov_weight[None], (split_count, cov_rows, factors)),
+        ],
+        axis=2,
+    )
+    cov_recv = exchange(cov_send, item_axes)
+    shape_here = lax.dynamic_slice_in_dim(item_shape, first_row, share_rows, 0)
+    rate_here = lax.dynamic_slice_in_dim(item_rate, first_row, share_rows, 0)
+    flat = cov_recv.reshape(split_count * cov_rows, share_rows + factors)
+    prior_log = lax.dot_general(
+        flat[:, :share_rows], flat[:, share_rows:], TN, precision=HIGHEST, preferred_element_type=F32
+    )
+    scale = jnp.exp(prior_log) / rate_here
 
     smem = pl.BlockSpec(memory_space=pltpu.SMEM)
     vmem = pl.BlockSpec(memory_space=pltpu.VMEM)
@@ -237,39 +309,21 @@
         last_kernel, (shape_of(owners * users_here, factors), shape_of(item_rows, factors))
     )(theta_all, marks, table)
 
-    stats_here = jnp.sum(
-        exchange(stats, item_axes).reshape(split_count, share_rows, factors), axis=0
-    )
-    shape_here = lax.dynamic_slice_in_dim(item_shape, first_row, share_rows, 0)
-    rate_here = lax.dynamic_slice_in_dim(item_rate, first_row, share_rows, 0)
-    cov_here = lax.dynamic_slice_in_dim(cov_full, first_row, share_rows, 1)
-    prior_log = lax.dot_general(cov_here, weight_full, TN, precision=HIGHEST, preferred_element_type=F32)
-    scale = jnp.exp(prior_log) / rate_here
-    new_shape = (1.0 - step_weight) * shape_here + step_weight * (item_prior + USER_RATIO * stats_here)
-    item_score = item_prior - scale * new_shape
-    grad_part = jnp.dot(cov_here, item_score, precision=HIGHEST, preferred_element_type=F32)
-    cov_rows = covariates.shape[0]
-    grad_part = jnp.sum(
-        exchange(grad_part, item_axes).reshape(split_count, cov_rows, factors), axis=0
-    )
-
-    by_z = partial.reshape(y_size, z_size, users_here, factors).transpose(1, 0, 2, 3)
-    by_z = by_z.reshape(z_size, y_size * users_here, factors)
-    both = jnp.concatenate(
-        [by_z, jnp.broadcast_to(grad_part[None], (z_size, cov_rows, factors))], axis=1
-    )
-    both = jnp.sum(exchange(both, ("z",)), axis=0)
-    user_part = both[: y_size * users_here].reshape(y_size, users_here, factors)
-    grad_part = both[y_size * users_here :]
-    both = jnp.concatenate(
-        [user_part, jnp.broadcast_to(grad_part[None], (y_size, cov_rows, factors))], axis=1
-    )
-    both = jnp.sum(exchange(both, ("y",)), axis=0)
-    user_shape = user_prior + theta * both[:users_here]
-    user_rate = activity_shape / active + totals
-    activity_rate = activity_base + jnp.sum(user_shape / user_rate, axis=1)
-    cov_grad = both[users_here:] / jnp.sqrt(jnp.float32(item_rows * owners))
-    return (user_shape, user_rate, activity_rate, new_shape, cov_grad)
+    parts = exchange(stats, item_axes).reshape(split_count, share_rows, factors)
+    new_shape, grad = kernel_call(
+        score_kernel, (shape_of(share_rows, factors), shape_of(split_count, cov_rows, factors))
+    )(parts, shape_here, scale, cov_recv)
+    grad = exchange(grad, item_axes)
+    lines = z_size * users_here + cov_rows
+    both = kernel_call(join_kernel, shape_of(y_size, lines, factors))(grad, partial)
+    both = exchange(both, ("y",))
+    both = kernel_call(fan_kernel, shape_of(z_size, users_here + cov_rows, factors))(both)
+    both = exchange(both, ("z",))
+    user_shape, user_rate, active, cov_grad = kernel_call(
+        functools.partial(finish_kernel, activity_shape, math.sqrt(item_rows * owners)),
+        (small, small, small, shape_of(cov_rows, factors)),
+    )(both, theta, active, totals)
+    return (user_shape, user_rate, active[:, 0], new_shape, cov_grad)
 
 
 def solution(mesh):

time: 193 us -> 168 us (0.87)
  blocking collectives: 87.9 us -> 60.3 us
  waiting for transfers between devices: 25.9 us -> 46.5 us
  between operations: 14.2 us -> 0.77 us
  Pallas kernels: 24.7 us -> 17.4 us
  starting transfers between devices: 25.3 us -> 29.5 us
  local copies, waits for them, and re-layouts: 7.09 us -> 9.69 us
  matrix products: 4.42 us -> 2.15 us
  other arithmetic: 3.06 us -> 1.05 us
    all_to_all x4 -> x5, waiting for transfers between devices: 25.2 us -> 46.5 us  [exchange(): return lax.all_to_all(array, axes, split_axis=0, concat_axis=0, tiled=True)]
    all_gather x1 -> x0, blocking collectives: 20.9 us -> none  [shards(): weight_full = lax.all_gather(cov_weight, item_axes, axis=0, tiled=True)]
    all_to_all x5, blocking collectives: 67 us -> 60.3 us  [exchange(): return lax.all_to_all(array, axes, split_axis=0, concat_axis=0, tiled=True)]
    pallas_call x1, Pallas kernels: 8.22 us -> 3.16 us  [shards(): kernel_call(last_kernel, (shape_of(owners * users_here, factors), shape_o...]
    all_to_all x4 -> x5, starting transfers between devices: 25.2 us -> 29.5 us  [exchange(): return lax.all_to_all(array, axes, split_axis=0, concat_axis=0, tiled=True)]
    pallas_call x0 -> x4, Pallas kernels: none -> 2.56 us  [the longest x1 1.88 us: shards(): kernel_call(score_kernel, (shape_of(share_rows, factors), shape_of(split_...]
    pallas_call x1, Pallas kernels: 5.15 us -> 2.68 us  [shards(): kernel_call(build_kernel, (shape_of(highs, owners * users_here, LANES), s...]
    pallas_call x1, Pallas kernels: 3.89 us -> 1.46 us  [shards(): kernel_call(ascend_kernel, shape_of(owners * users_here, factors))]
  transfers between devices with their start and end apart: 5 -> 5, of which waited for: 3 -> 5; matrix products, arithmetic and copies ran while one was open for 1% -> 3% of each run, Pallas kernels for 13% -> 3%
where the time goes in v2:
time: 168 us; the launch traced here: 167 us
  blocking collectives  60.3 us (36%)
  waiting for transfers between devices  46.5 us (28%)
  starting transfers between devices  29.5 us (18%)
  Pallas kernels  17.4 us (10%)
  local copies, waits for them, and re-layouts  9.69 us (6%)
  matrix products  2.15 us (1%)
    all_to_all x5, blocking collectives, exchange(): return lax.all_to_all(array, axes, split_axis=0, concat_axis=0, tiled=True)  60.3 us
    all_to_all x5, waiting for transfers between devices, exchange(): return lax.all_to_all(array, axes, split_axis=0, concat_axis=0, tiled=True)  46.5 us
    all_to_all x5, starting transfers between devices, exchange(): return lax.all_to_all(array, axes, split_axis=0, concat_axis=0, tiled=True)  29.5 us
    unnamed x24, local copies, waits for them, and re-layouts  6.98 us
    pallas_call x1, Pallas kernels, shards(): kernel_call(functools.partial(prep_kernel, owners), (shape_of(owners, 16,...  5.08 us
  transfers between devices with their start and end apart: 5, of which 5 were waited for; matrix products, arithmetic and copies ran while one was open for 3% of the time, Pallas kernels for 3%

profile of v2, /device:TPU:2, one launch (start us, length us, event | category | flops | bytes accessed | tf_op | source)
XLA Modules:
  0.0 167.3 jit_solution(8321452882094610341)
XLA Ops:
  0.6 0.0 copy-start.3
  0.6 0.7 copy-done.3
  1.4 0.0 copy-start.4
  1.4 0.8 copy-done.4
  2.1 0.0 copy-start.5
  2.2 0.7 copy-done.5
  2.8 0.7 copy-done.7
  3.5 0.7 copy-done.10
  4.2 5.1 %shard_map.137 = (f32[32,16,128]{2,1,0:T(8,128)}, f32[8,128]{1,0:T(8,128)S(1)}) custom-call(s32[8]{0:T(128)S(1)} %copy-done.10, s32[64,128]{1,0:T(8,128)S(1)} %bitcast.20, s32[64,128]{1,0:T(8,128)S(1)} %bitcast.21, f32[8,128]{1,0:T(8,128)S(1)} %copy-done.5, f32[8,128]{1,0:T(8,128)S(1)} %copy-done.7), custom_call_target="tpu_custom_call" | custom-call | tf_op jit(solution)/shard_map/pallas_call | solution.py:276
  9.3 11.5 %all-to-all-start = ((f32[32,16,128]{2,1,0:T(8,128)}), f32[32,16,128]{2,1,0:T(8,128)S(1)}, u32[]{:S(2)}, u32[]{:S(2)}) async-start(f32[32,16,128]{2,1,0:T(8,128)} %get-tuple-element.23), calls=%async_computation | async-start | bytes 524288 | tf_op jit(solution)/shard_map/all_to_all | solution.py:255
  20.7 0.0 copy-start
  20.8 1.2 copy-done
  22.0 1.2 copy-done.1
  23.2 1.1 shard_map.138.table_ref
  24.3 8.9 %all-to-all-done.recv_ref = f32[32,16,128]{2,1,0:T(8,128)S(1)} async-done(((f32[32,16,128]{2,1,0:T(8,128)}), f32[32,16,128]{2,1,0:T(8,128)S(1)}, u32[]{:S(2)}, u32[]{:S(2)}) %all-to-all-start) | async-done | bytes 262176 | tf_op jit(solution)/shard_map/all_to_all | solution.py:255
  33.2 2.7 %shard_map.139 = (f32[16,256,128]{2,1,0:T(8,128)S(1)}, f32[256,128]{1,0:T(8,128)}) custom-call(f32[32,16,128]{2,1,0:T(8,128)S(1)} %all-to-all-done.recv_ref, f32[2048,128]{1,0:T(8,128)S(1)} %shard_map.138.table_ref), custom_call_target="tpu_custom_call" | custom-call | tf_op jit(solution)/shard_map/pallas_call | solution.py:289
  35.9 4.4 %all-to-all-start.1 = ((f32[32,8,128]{2,1,0:T(8,128)}), f32[32,8,128]{2,1,0:T(8,128)S(1)}, u32[]{:S(2)}, u32[]{:S(2)}) async-start(f32[32,8,128]{2,1,0:T(8,128)} %bitcast.2), calls=%async_computation.1 | async-start | bytes 262144 | tf_op jit(solution)/shard_map/all_to_all | solution.py:255
  40.3 0.0 copy-done.6
  40.3 0.0 copy-done.8
  40.3 0.1 divide_reduce_fusion
  40.4 10.2 %all-to-all-done.1.recv_ref = f32[32,8,128]{2,1,0:T(8,128)S(1)} async-done(((f32[32,8,128]{2,1,0:T(8,128)}), f32[32,8,128]{2,1,0:T(8,128)S(1)}, u32[]{:S(2)}, u32[]{:S(2)}) %all-to-all-start.1) | async-done | bytes 131104 | tf_op jit(solution)/shard_map/all_to_all | solution.py:255
  50.7 0.1 broadcast_in_dim.6.activity_ref
  50.7 0.0 copy-done.9
  50.7 0.6 shard_map.140
  51.4 13.8 %all_to_all.54 = f32[32,8,128]{2,1,0:T(8,128)S(1)} all-to-all(f32[32,8,128]{2,1,0:T(8,128)S(1)} %get-tuple-element.26), channel_id=1, replica_groups=mesh['y'=4,'z'=8,'x'=4,'core'=2] {'y','z'}, dimensions={0} | all-to-all | bytes 262144 | tf_op jit(solution)/shard_map/all_to_all | solution.py:255
  65.2 1.5 shard_map.141
  66.7 13.8 %all_to_all.55.recv_ref = f32[32,8,128]{2,1,0:T(8,128)S(1)} all-to-all(f32[32,8,128]{2,1,0:T(8,128)S(1)} %bitcast.19), channel_id=1, replica_groups=mesh['y'=4,'z'=8,'x'=4,'core'=2] {'y','z'}, dimensions={0} | all-to-all | bytes 262144 | tf_op jit(solution)/shard_map/all_to_all | solution.py:255
  80.4 0.7 shard_map.142
  81.2 3.9 %all-to-all-start.4 = ((f32[32,8,128]{2,1,0:T(8,128)}), f32[32,8,128]{2,1,0:T(8,128)S(1)}, u32[]{:S(2)}, u32[]{:S(2)}) async-start(f32[32,8,128]{2,1,0:T(8,128)} %get-tuple-element.30), calls=%async_computation.4 | async-start | bytes 262144 | tf_op jit(solution)/shard_map/all_to_all | solution.py:255
  85.0 1.1 copy.18
  86.1 0.0 copy-done.11
  86.2 0.9 pad_maximum_fusion
  87.1 8.2 %all-to-all-done.4 = f32[32,8,128]{2,1,0:T(8,128)S(1)} async-done(((f32[32,8,128]{2,1,0:T(8,128)}), f32[32,8,128]{2,1,0:T(8,128)S(1)}, u32[]{:S(2)}, u32[]{:S(2)}) %all-to-all-start.4) | async-done | bytes 131104 | tf_op jit(solution)/shard_map/all_to_all | solution.py:255
  95.3 4.8 %all-to-all-start.6 = ((f32[8,64,384]{2,1,0:T(8,128)}), f32[8,64,384]{2,1,0:T(8,128)}, u32[]{:S(2)}, u32[]{:S(2)}) async-start(f32[8,64,384]{2,1,0:T(8,128)} %pad_maximum_fusion), calls=%async_computation.6 | async-start | bytes 1572864 | tf_op jit(solution)/shard_map/all_to_all | solution.py:255
  100.2 3.2 %shard_map.143 = (f32[256,128]{1,0:T(8,128)S(1)}, f32[2048,128]{1,0:T(8,128)S(1)}) custom-call(f32[256,128]{1,0:T(8,128)S(1)} %bitcast.17, f32[16,256,128]{2,1,0:T(8,128)S(1)} %get-tuple-element.27.marks_ref, f32[2048,128]{1,0:T(8,128)S(1)} %shard_map.138.table_ref), custom_call_target="tpu_custom_call" | custom-call | tf_op jit(solution)/shard_map/pallas_call | solution.py:308
  103.3 0.0 copy-start.2
  103.3 1.0 copy-done.2
  104.3 7.6 %all-to-all-done.6.cov_ref = f32[8,64,384]{2,1,0:T(8,128)} async-done(((f32[8,64,384]{2,1,0:T(8,128)}), f32[8,64,384]{2,1,0:T(8,128)}, u32[]{:S(2)}, u32[]{:S(2)}) %all-to-all-start.6) | async-done | bytes 786464 | tf_op jit(solution)/shard_map/all_to_all | solution.py:255
  112.0 4.9 %all-to-all-start.5 = ((f32[8,256,128]{2,1,0:T(8,128)}), f32[8,256,128]{2,1,0:T(8,128)S(1)}, u32[]{:S(2)}, u32[]{:S(2)}) async-start(f32[8,256,128]{2,1,0:T(8,128)} %bitcast.16), calls=%async_computation.5 | async-start | bytes 2097152 | tf_op jit(solution)/shard_map/all_to_all | solution.py:255
  116.9 0.9 constant_dynamic-slice_fusion.shape_ref
  117.8 2.2 %fusion.scale_ref = f32[256,128]{1,0:T(8,128)S(1)} fusion(f32[512,384]{1,0:T(8,128)} %bitcast.9, f32[2048,128]{1,0:T(8,128)} %rate_ref.3, s32[]{:T(128)S(6)} %select_n.4), kind=kOutput, calls=%fused_computation.1 | convolution fusion | flops 201359360 | bytes 1048580 | tf_op jit(solution)/shard_map/dot_general | solution.py:269
  120.0 11.5 %all-to-all-done.5.stats_ref = f32[8,256,128]{2,1,0:T(8,128)S(1)} async-done(((f32[8,256,128]{2,1,0:T(8,128)}), f32[8,256,128]{2,1,0:T(8,128)S(1)}, u32[]{:S(2)}, u32[]{:S(2)}) %all-to-all-start.5) | async-done | bytes 1048608 | tf_op jit(solution)/shard_map/all_to_all | solution.py:255
  131.4 1.9 %shard_map.144 = (f32[256,128]{1,0:T(8,128)}, f32[8,64,128]{2,1,0:T(8,128)S(1)}) custom-call(f32[8,256,128]{2,1,0:T(8,128)S(1)} %all-to-all-done.5.stats_ref, f32[256,128]{1,0:T(8,128)S(1)} %constant_dynamic-slice_fusion.shape_ref, f32[256,128]{1,0:T(8,128)S(1)} %fusion.scale_ref, f32[8,64,384]{2,1,0:T(8,128)} %all-to-all-done.6.cov_ref), custom_call_target="tpu_custom_call" | custom-call | tf_op jit(solution)/shard_map/pallas_call | solution.py:313
  133.3 9.9 %all_to_all.56.grad_ref = f32[8,64,128]{2,1,0:T(8,128)S(1)} all-to-all(f32[8,64,128]{2,1,0:T(8,128)S(1)} %get-tuple-element.32), channel_id=1, replica_groups=mesh['y'=4,'z'=8,'x'=4,'core'=2] {'x','core'}, dimensions={0} | all-to-all | bytes 524288 | tf_op jit(solution)/shard_map/all_to_all | solution.py:255
  143.3 9.2 %all_to_all.57.recv_ref = f32[4,128,128]{2,1,0:T(8,128)S(1)} all-to-all(f32[4,128,128]{2,1,0:T(8,128)S(1)} %shard_map.145), channel_id=1, replica_groups=mesh['y'=4,'z'=8,'x'=4,'core'=2] {'y'}, dimensions={0} | all-to-all | bytes 524288 | tf_op jit(solution)/shard_map/all_to_all | solution.py:255
  152.5 13.6 %all_to_all.58.recv_ref = f32[8,72,128]{2,1,0:T(8,128)S(1)} all-to-all(f32[8,72,128]{2,1,0:T(8,128)S(1)} %shard_map.146), channel_id=1, replica_groups=mesh['y'=4,'z'=8,'x'=4,'core'=2] {'z'}, dimensions={0} | all-to-all | bytes 589824 | tf_op jit(solution)/shard_map/all_to_all | solution.py:255
  166.1 0.6 shard_map.147
  166.7 0.6 slice_reduce_fusion
  (11 shorter events, 0.1 us)
Async XLA Ops:
  0.6 0.8 copy-start.3
  1.4 0.8 copy-start.4
  2.1 0.7 copy-start.5
  2.8 0.7 copy-start.7
  3.5 0.7 copy-start.10
  9.3 23.9 %all-to-all-start = ((f32[32,16,128]{2,1,0:T(8,128)}), f32[32,16,128]{2,1,0:T(8,128)S(1)}, u32[]{:S(2)}, u32[]{:S(2)}) async-start(f32[32,16,128]{2,1,0:T(8,128)} %get-tuple-element.23), calls=%async_computation | async-start | bytes 524288 | tf_op jit(solution)/shard_map/all_to_all | solution.py:255
  20.7 1.2 copy-start
  22.0 1.2 copy-start.1
  23.2 17.1 %copy-start.6 = (f32[8,128]{1,0:T(8,128)S(1)}, f32[8,128]{1,0:T(8,128)}, u32[]{:S(2)}) copy-start(f32[8,128]{1,0:T(8,128)} %shape_ref.2) | copy-start | bytes 12292
  23.2 17.1 %copy-start.8 = (f32[8,128]{1,0:T(8,128)S(1)}, f32[8,128]{1,0:T(8,128)}, u32[]{:S(2)}) copy-start(f32[8,128]{1,0:T(8,128)} %rate_ref.2) | copy-start | bytes 12292
  23.2 27.5 %copy-start.9 = (f32[128]{0:T(128)S(1)}, f32[128]{0:T(128)}, u32[]{:S(2)}) copy-start(f32[128]{0:T(128)} %param.17) | copy-start | bytes 1540
  35.9 14.8 %all-to-all-start.1 = ((f32[32,8,128]{2,1,0:T(8,128)}), f32[32,8,128]{2,1,0:T(8,128)S(1)}, u32[]{:S(2)}, u32[]{:S(2)}) async-start(f32[32,8,128]{2,1,0:T(8,128)} %bitcast.2), calls=%async_computation.1 | async-start | bytes 262144 | tf_op jit(solution)/shard_map/all_to_all | solution.py:255
  65.2 20.9 %copy-start.11 = (f32[64,128]{1,0:T(8,128)S(1)}, f32[64,128]{1,0:T(8,128)}, u32[]{:S(2)}) copy-start(f32[64,128]{1,0:T(8,128)} %param.19) | copy-start | bytes 98308
  81.2 14.2 %all-to-all-start.4 = ((f32[32,8,128]{2,1,0:T(8,128)}), f32[32,8,128]{2,1,0:T(8,128)S(1)}, u32[]{:S(2)}, u32[]{:S(2)}) async-start(f32[32,8,128]{2,1,0:T(8,128)} %get-tuple-element.30), calls=%async_computation.4 | async-start | bytes 262144 | tf_op jit(solution)/shard_map/all_to_all | solution.py:255
  95.3 16.6 %all-to-all-start.6 = ((f32[8,64,384]{2,1,0:T(8,128)}), f32[8,64,384]{2,1,0:T(8,128)}, u32[]{:S(2)}, u32[]{:S(2)}) async-start(f32[8,64,384]{2,1,0:T(8,128)} %pad_maximum_fusion), calls=%async_computation.6 | async-start | bytes 1572864 | tf_op jit(solution)/shard_map/all_to_all | solution.py:255
  103.3 1.0 copy-start.2
  112.0 19.5 %all-to-all-start.5 = ((f32[8,256,128]{2,1,0:T(8,128)}), f32[8,256,128]{2,1,0:T(8,128)S(1)}, u32[]{:S(2)}, u32[]{:S(2)}) async-start(f32[8,256,128]{2,1,0:T(8,128)} %bitcast.16), calls=%async_computation.5 | async-start | bytes 2097152 | tf_op jit(solution)/shard_map/all_to_all | solution.py:255

commit v3 on v2

v3 whole, which is shorter than its diff:
```python
import functools
import math

import jax
import jax.numpy as jnp
from jax import lax
from jax.experimental import pallas as pl
from jax.experimental.pallas import tpu as pltpu
from jax.sharding import Mesh
from jax.sharding import PartitionSpec as P

ITERS = 3
USER_RATIO = 4

user_prior = 0.3
activity_prior = 0.3
activity_base = 1.0
item_prior = 0.3
step_weight = 0.5

F32 = jnp.float32
BF16 = jnp.bfloat16
HIGHEST = lax.Precision.HIGHEST
NT = (((1,), (1,)), ((), ()))
NN = (((1,), (0,)), ((), ()))
TN = (((0,), (0,)), ((), ()))
LANES = 128
VMEM_LIMIT = 48 * 1024 * 1024


def exp_digamma_over(x, rate):
    pair = x * (x + 5.0)
    low = pair + 4.0
    high = pair + 6.0
    steps = (2.0 * x + 5.0) * (low * high + pair * (low + high)) / (pair * low * high)
    y = x + 6.0
    inv = 1.0 / y
    sq = inv * inv
    tail = 0.5 * inv + sq * (1.0 / 12.0 - sq * (1.0 / 120.0 - sq * (1.0 / 252.0)))
    return y * jnp.exp(-steps - tail) / rate


def kernel_call(kernel, out_shape, **specs):
    return pl.pallas_call(
        kernel,
        out_shape=out_shape,
        compiler_params=pltpu.CompilerParams(vmem_limit_bytes=VMEM_LIMIT),
        **specs,
    )


def shape_of(*dims):
    return jax.ShapeDtypeStruct(dims, F32)


def prep_kernel(
    owners,
    counts_hbm,
    ids_hbm,
    clicks_hbm,
    shape_hbm,
    rate_hbm,
    send_ref,
    counts_ref,
    ids_ref,
    clicks_ref,
    shape_ref,
    rate_ref,
    sems,
):
    copies = [
        pltpu.make_async_copy(source, target, sems.at[place])
        for place, (source, target) in enumerate(
            (
                (counts_hbm, counts_ref),
                (ids_hbm, ids_ref),
                (clicks_hbm, clicks_ref),
                (shape_hbm, shape_ref),
                (rate_hbm, rate_ref),
            )
        )
    ]
    for copy in copies:
        copy.start()
    for copy in copies:
        copy.wait()
    rows = ids_ref.shape[0]
    blocks = 8
    width = 2 * LANES
    capacity = rows * LANES // owners
    before = (
        lax.broadcasted_iota(jnp.int32, (width, width), 0)
        < lax.broadcasted_iota(jnp.int32, (width, width), 1)
    )
    before = jnp.where(before, 1.0, 0.0).astype(BF16)
    owner_iota = lax.broadcasted_iota(jnp.int32, (owners, width), 0)
    rank_iota = lax.broadcasted_iota(jnp.int32, (capacity, width), 0).astype(F32)
    carry = jnp.zeros((owners, 1), F32)
    lists = jnp.zeros((4 * owners, capacity), F32)
    for chunk in range(rows // 2):
        user = 2 * chunk // blocks
        ids = jnp.concatenate(
            [ids_ref[2 * chunk : 2 * chunk + 1, :], ids_ref[2 * chunk + 1 : 2 * chunk + 2, :]], axis=1
        )
        weights = []
        for row in (2 * chunk, 2 * chunk + 1):
            live = jnp.where(row % blocks < counts_ref[user], 1.0, 0.0)
            weights.append(clicks_ref[row : row + 1, :].astype(F32) * live)
        weight = jnp.concatenate(weights, axis=1)
        marks = jnp.where(owner_iota == (ids >> 11), 1.0, 0.0)
        earlier = lax.dot_general(marks.astype(BF16), before, NN, preferred_element_type=F32)
        rank = jnp.sum(marks * (earlier + carry), axis=0, keepdims=True)
        carry = carry + jnp.sum(marks, axis=1, keepdims=True)
        place = jnp.where(rank_iota == rank, 1.0, 0.0).astype(BF16)
        high = ((ids >> 7) & 15).astype(F32)
        low = (ids & 127).astype(F32)
        payload = jnp.concatenate(
            [marks * high, marks * low, marks * float(user), marks * weight], axis=0
        ).astype(BF16)
        lists = lists + lax.dot_general(payload, place, NT, preferred_element_type=F32)
    theta = exp_digamma_over(shape_ref[...], rate_ref[...])
    active = activity_base + jnp.sum(shape_ref[...] / rate_ref[...], axis=1, keepdims=True)
    eye = lax.broadcasted_iota(jnp.int32, theta.shape, 0) == lax.broadcasted_iota(jnp.int32, theta.shape, 1)
    active = jnp.sum(jnp.where(eye, active, 0.0), axis=0, keepdims=True)
    item_line = lists[:owners] * float(LANES) + lists[owners : 2 * owners]
    lines = (item_line, lists[2 * owners : 3 * owners], lists[3 * owners :])
    for owner in range(owners):
        for part in range(3):
            line = lines[part][owner : owner + 1, :]
            send_ref[owner, 2 * part : 2 * part + 1, :] = line[:, :LANES]
            send_ref[owner, 2 * part + 1 : 2 * part + 2, :] = line[:, LANES:]
        send_ref[owner, 6:7, :] = active
        send_ref[owner, 7:8, :] = jnp.zeros((1, LANES), F32)
        send_ref[owner, 8:16, :] = theta


def table_kernel(spot_ref, shape_ref, rate_ref, table_ref, shape_here_ref, rate_here_ref):
    table_ref[...] = exp_digamma_over(shape_ref[...], rate_ref[...])
    share = shape_here_ref.shape[0]
    here = pl.ds(pl.multiple_of(spot_ref[2] * share, share), share)
    shape_here_ref[...] = shape_ref[here, :]
    rate_here_ref[...] = rate_ref[here, :]


def split(x):
    high = x.astype(BF16)
    return high, (x - high.astype(F32)).astype(BF16)


def dot(left, right, dims):
    return lax.dot_general(left, right, dims, preferred_element_type=F32)


def ascend(theta, marks_ref, table_ref, stats_ref=None):
    factors = theta.shape[1]
    theta_high, theta_low = split(theta)
    theta_both = jnp.concatenate([theta_high, theta_low], axis=1)
    total = jnp.zeros(theta.shape, F32)
    width = 2 * LANES
    for pair in range(marks_ref.shape[0] // 2):
        rows = slice(pair * width, (pair + 1) * width)
        table = table_ref[rows, :]
        table_high, table_low = split(table)
        share = dot(theta_both, jnp.concatenate([table_high, table_high], axis=1), NT) + dot(
            theta_high, table_low, NT
        )
        marks = jnp.concatenate([marks_ref[2 * pair], marks_ref[2 * pair + 1]], axis=1)
        ratio = marks / share
        ratio_high, ratio_low = split(ratio)
        wide = dot(ratio_high, jnp.concatenate([table_high, table_low], axis=1), NN)
        total = total + (wide[:, :factors] + wide[:, factors:]) + dot(ratio_low, table_high, NN)
        if stats_ref is not None:
            wide = dot(ratio_high, theta_both, TN)
            spread = wide[:, :factors] + wide[:, factors:] + dot(ratio_low, theta_high, TN)
            stats_ref[pair, :width, :] = table * spread
    return total


def build_kernel(y_size, spot_ref, recv_ref, table_ref, marks_ref, partial_ref, theta_ref, active_ref):
    owners = recv_ref.shape[0]
    z_size = owners // y_size
    highs = marks_ref.shape[0]
    line_iota = lax.broadcasted_iota(jnp.int32, (LANES, 2 * LANES), 0).astype(F32)

    def wide(source, part):
        return jnp.concatenate(
            [recv_ref[source, 2 * part : 2 * part + 1, :], recv_ref[source, 2 * part + 1 : 2 * part + 2, :]],
            axis=1,
        )

    order = [y * z_size + z for z in range(z_size) for y in range(y_size)]
    for place, source in enumerate(order):
        item = wide(source, 0).astype(jnp.int32)
        low = (item & (LANES - 1)).astype(F32)
        high = (item >> 7).astype(F32) * 8.0 + wide(source, 1)
        left = jnp.where(line_iota == high, wide(source, 2), 0.0).astype(BF16)
        right = jnp.where(line_iota == low, 1.0, 0.0).astype(BF16)
        tile = dot(left, right, NT)
        for high in range(highs):
            marks_ref[high, 8 * place : 8 * place + 8, :] = tile[8 * high : 8 * high + 8, :]
    theta = jnp.concatenate([recv_ref[source, 8:16, :] for source in order], axis=0)
    partial_ref[...] = ascend(theta, marks_ref, table_ref)
    eye = lax.broadcasted_iota(jnp.int32, (8, LANES), 0) == lax.broadcasted_iota(jnp.int32, (8, LANES), 1)
    for y in range(y_size):
        source = y * z_size + spot_ref[1]
        theta_ref[8 * y : 8 * y + 8, :] = recv_ref[source, 8:16, :]
        active = jnp.sum(jnp.where(eye, recv_ref[source, 6:7, :], 0.0), axis=1, keepdims=True)
        active_ref[8 * y : 8 * y + 8, :] = jnp.broadcast_to(active, (8, LANES))


def ascend_kernel(theta_ref, marks_ref, table_ref, partial_ref):
    partial_ref[...] = ascend(theta_ref[...], marks_ref, table_ref)


def last_kernel(theta_ref, marks_ref, table_ref, cov_ref, weight_ref, partial_ref, send_ref):
    width = 2 * LANES
    rows = weight_ref.shape[0]
    for part in range(send_ref.shape[0]):
        for half in range(2):
            start = part * width + half * LANES
            send_ref[part, width + half * rows : width + (half + 1) * rows, :] = cov_ref[:, start : start + LANES]
        send_ref[part, width + 2 * rows :, :] = weight_ref[...]
    partial_ref[...] = ascend(theta_ref[...], marks_ref, table_ref, send_ref)


def sum_kernel(recv_ref, send_ref):
    total = jnp.sum(recv_ref[...], axis=0)
    send_ref[...] = jnp.broadcast_to(total[None], send_ref.shape)


def update_kernel(activity_shape, recv_ref, theta_ref, activity_ref, totals_ref, active_ref, next_ref, send_ref):
    total = jnp.sum(recv_ref[...], axis=0)
    shapes = user_prior + theta_ref[...] * total
    rates = activity_shape / activity_ref[...] + totals_ref[...]
    active = activity_base + jnp.sum(shapes / rates, axis=1, keepdims=True)
    active_ref[...] = jnp.broadcast_to(active, shapes.shape)
    theta = exp_digamma_over(shapes, rates)
    next_ref[...] = theta
    send_ref[...] = jnp.broadcast_to(theta[None], send_ref.shape)


def score_kernel(recv_ref, shape_ref, rate_ref, new_ref, grad_ref):
    share = shape_ref.shape[0]
    parts, rows, _ = grad_ref.shape
    stats = jnp.sum(recv_ref[:, :share, :], axis=0)
    new_shape = (1.0 - step_weight) * shape_ref[...] + step_weight * (item_prior + USER_RATIO * stats)
    new_ref[...] = new_shape
    cov = jnp.concatenate(
        [
            jnp.concatenate(
                [recv_ref[part, share : share + rows, :], recv_ref[part, share + rows : share + 2 * rows, :]],
                axis=1,
            )
            for part in range(parts)
        ],
        axis=0,
    )
    weight = jnp.concatenate([recv_ref[part, share + 2 * rows :, :] for part in range(parts)], axis=0)
    prior_log = lax.dot_general(cov, weight, TN, precision=HIGHEST, preferred_element_type=F32)
    score = item_prior - jnp.exp(prior_log) * new_shape / rate_ref[...]
    grad = lax.dot_general(cov, score, NN, precision=HIGHEST, preferred_element_type=F32)
    for part in range(parts):
        grad_ref[part] = grad[part * rows : (part + 1) * rows]


def join_kernel(users, grad_ref, partial_ref, send_ref):
    y_size, rows, _ = send_ref.shape
    grad = jnp.sum(grad_ref[...], axis=0)
    z_size = partial_ref.shape[0] // (y_size * users)
    for y in range(y_size):
        for z in range(z_size):
            place = (z * y_size + y) * users
            send_ref[y, z * users : (z + 1) * users, :] = partial_ref[place : place + users, :]
        send_ref[y, z_size * users :, :] = grad


def fan_kernel(users, recv_ref, send_ref):
    z_size, rows, _ = send_ref.shape
    total = jnp.sum(recv_ref[...], axis=0)
    for z in range(z_size):
        send_ref[z, :users, :] = total[z * users : (z + 1) * users, :]
        send_ref[z, users:, :] = total[z_size * users :, :]


def finish_kernel(
    activity_shape, root, spot_ref, recv_ref, theta_ref, activity_ref, totals_ref, shapes_ref, rates_ref, active_ref, grad_ref
):
    total = jnp.sum(recv_ref[...], axis=0)
    users = shapes_ref.shape[0]
    here = pl.ds(pl.multiple_of(spot_ref[0] * users, users), users)
    shapes = user_prior + theta_ref[here, :] * total[:users]
    rates = activity_shape / activity_ref[here, :] + totals_ref[...]
    shapes_ref[...] = shapes
    rates_ref[...] = rates
    active = activity_base + jnp.sum(shapes / rates, axis=1, keepdims=True)
    active_ref[...] = jnp.broadcast_to(active, shapes.shape)
    grad_ref[...] = total[users:] / root


def shards(
    item_ids,
    clicks,
    block_counts,
    user_shape0,
    user_rate0,
    item_shape,
    item_rate,
    beta_totals,
    covariates,
    cov_weight,
):
    y_size, z_size = lax.axis_size("y"), lax.axis_size("z")
    owners = y_size * z_size
    item_rows, factors = item_shape.shape
    users_here, blocks, block_width = item_ids.shape
    cov_rows = covariates.shape[0]
    slot_rows = users_here * blocks
    highs = item_rows // LANES
    user_axes, item_axes = ("y", "z"), ("x", "core")
    split_count = lax.axis_size(item_axes)
    share_rows = item_rows // split_count
    group = y_size * users_here
    everyone = owners * users_here
    activity_shape = activity_prior + factors * user_prior

    def exchange(array, axes):
        return lax.all_to_all(array, axes, split_axis=0, concat_axis=0, tiled=True)

    spot = jnp.stack([lax.axis_index("y"), lax.axis_index("z"), lax.axis_index(item_axes)]).astype(jnp.int32)
    totals = beta_totals[None, :]
    smem = pl.BlockSpec(memory_space=pltpu.SMEM)
    vmem = pl.BlockSpec(memory_space=pltpu.VMEM)
    hbm = pl.BlockSpec(memory_space=pltpu.HBM)
    send = kernel_call(
        functools.partial(prep_kernel, owners),
        shape_of(owners, 16, LANES),
        in_specs=[hbm] * 5,
        scratch_shapes=[
            pltpu.SMEM((users_here,), jnp.int32),
            pltpu.VMEM((slot_rows, block_width), jnp.int32),
            pltpu.VMEM((slot_rows, block_width), jnp.int32),
            pltpu.VMEM((users_here, factors), F32),
            pltpu.VMEM((users_here, factors), F32),
            pltpu.SemaphoreType.DMA((5,)),
        ],
    )(
        block_counts,
        item_ids.reshape(slot_rows, block_width),
        clicks.reshape(slot_rows, block_width),
        user_shape0,
        user_rate0,
    )
    recv = exchange(send, user_axes)
    share = shape_of(share_rows, factors)
    table, shape_here, rate_here = kernel_call(
        table_kernel, (shape_of(item_rows, factors), share, share), in_specs=[smem, vmem, vmem]
    )(spot, item_shape, item_rate)
    local = shape_of(group, factors)
    marks, partial, theta, active = kernel_call(
        functools.partial(build_kernel, y_size),
        (shape_of(highs, everyone, LANES), shape_of(everyone, factors), local, local),
        in_specs=[smem, vmem, vmem],
    )(spot, recv, table)
    for iteration in range(ITERS - 1):
        parts = exchange(partial.reshape(z_size, group, factors), ("z",))
        parts = kernel_call(sum_kernel, shape_of(y_size, group, factors))(parts)
        parts = exchange(parts, ("y",))
        active, theta, spread = kernel_call(
            functools.partial(update_kernel, activity_shape),
            (local, local, shape_of(z_size, group, factors)),
        )(parts, theta, active, totals)
        theta_all = exchange(spread, ("z",)).reshape(everyone, factors)
        if iteration < ITERS - 2:
            partial = kernel_call(ascend_kernel, shape_of(everyone, factors))(theta_all, marks, table)
    partial, send = kernel_call(
        last_kernel, (shape_of(everyone, factors), shape_of(split_count, share_rows + 3 * cov_rows, factors))
    )(theta_all, marks, table, covariates, cov_weight)
    recv = exchange(send, item_axes)
    new_shape, grad = kernel_call(score_kernel, (share, shape_of(split_count, cov_rows, factors)))(
        recv, shape_here, rate_here
    )
    grad = exchange(grad, item_axes)
    both = kernel_call(
        functools.partial(join_kernel, users_here), shape_of(y_size, z_size * users_here + cov_rows, factors)
    )(grad, partial)
    both = exchange(both, ("y",))
    both = kernel_call(
        functools.partial(fan_kernel, users_here), shape_of(z_size, users_here + cov_rows, factors)
    )(both)
    both = exchange(both, ("z",))
    small = shape_of(users_here, factors)
    user_shape, user_rate, active, cov_grad = kernel_call(
        functools.partial(finish_kernel, activity_shape, math.sqrt(item_rows * owners)),
        (small, small, small, shape_of(cov_rows, factors)),
        in_specs=[smem, vmem, vmem, vmem, vmem],
    )(spot, both, theta, active, totals)
    return (user_shape, user_rate, active[:, 0], new_shape, cov_grad)


def solution(mesh):
    fine = Mesh(mesh.devices.reshape(4, 8, 4, 2), ("y", "z", "x", "core"))
    users, items = ("y", "z"), ("x", "core")
    both = users + items
    return jax.shard_map(
        shards,
        mesh=fine,
        in_specs=(
            P(both, None, None),
            P(both, None, None),
            P(both),
            P(both, None),
            P(both, None),
            P(users, None),
            P(users, None),
            P(),
            P(items, users),
            P(items, None),
        ),
        out_specs=(
            P(both, None),
            P(both, None),
            P(both),
            P(both, None),
            P(items, None),
        ),
        check_vma=False,
    )
```

time: 168 us -> 168 us (level)
  blocking collectives: 60.3 us -> 123 us
  waiting for transfers between devices: 46.5 us -> 8.28 us
  starting transfers between devices: 29.5 us -> 11.5 us
  local copies, waits for them, and re-layouts: 9.69 us -> 6.62 us
  matrix products: 2.15 us -> 0 us
    all_to_all x5 -> x10, blocking collectives: 60.3 us -> 123 us  [exchange(): return lax.all_to_all(array, axes, split_axis=0, concat_axis=0, tiled=True)]
    all_to_all x5 -> x1, waiting for transfers between devices: 46.5 us -> 8.28 us  [exchange(): return lax.all_to_all(array, axes, split_axis=0, concat_axis=0, tiled=True)]
    all_to_all x5 -> x1, starting transfers between devices: 29.5 us -> 11.5 us  [exchange(): return lax.all_to_all(array, axes, split_axis=0, concat_axis=0, tiled=True)]
    dot_general x1 -> x0, matrix products: 2.15 us -> none  [shards(): lax.dot_general(flat[:, :share_rows], flat[:, share_rows:], TN, precision...]
    unnamed x24 -> x20, local copies, waits for them, and re-layouts: 6.98 us -> 6 us
    pallas_call x10 -> x12, Pallas kernels: 16.7 us -> 16.1 us  [the longest x1 5.14 us: shards(): kernel_call(functools.partial(prep_kernel, owners), shape_of(owners, 16,...]
  transfers between devices with their start and end apart: 5 -> 1, of which waited for: 5 -> 1; matrix products, arithmetic and copies ran while one was open for 3% -> 0% of each run, Pallas kernels for 3% -> 1%
where the time goes in v3:
time: 168 us
  blocking collectives  123 us (73%)
  Pallas kernels  17.3 us (10%)
  starting transfers between devices  11.5 us (7%)
  waiting for transfers between devices  8.28 us (5%)
  local copies, waits for them, and re-layouts  6.62 us (4%)
    all_to_all x10, blocking collectives, exchange(): return lax.all_to_all(array, axes, split_axis=0, concat_axis=0, tiled=True)  123 us
    all_to_all x1, starting transfers between devices, exchange(): return lax.all_to_all(array, axes, split_axis=0, concat_axis=0, tiled=True)  11.5 us
    all_to_all x1, waiting for transfers between devices, exchange(): return lax.all_to_all(array, axes, split_axis=0, concat_axis=0, tiled=True)  8.28 us
    unnamed x20, local copies, waits for them, and re-layouts  6 us
    pallas_call x1, Pallas kernels, shards(): kernel_call(functools.partial(prep_kernel, owners), shape_of(owners, 16,...  5.14 us
  transfers between devices with their start and end apart: 1, of which 1 were waited for; matrix products, arithmetic and copies ran while one was open for 0% of the time, Pallas kernels for 1%

profile of v3, /device:TPU:2, one launch (start us, length us, event | category | flops | bytes accessed | tf_op | source)
XLA Modules:
  0.0 167.5 jit_solution(10739210244401134638)
XLA Ops:
  0.6 0.0 copy-start.4
  0.6 0.7 copy-done.4
  1.4 0.0 copy-start.5
  1.4 0.8 copy-done.5
  2.1 0.0 copy-start.7
  2.2 0.7 copy-done.7
  2.8 0.0 copy-start.8
  2.8 0.7 copy-done.8
  3.5 0.0 copy-start.9
  3.5 0.7 copy-done.9
  4.2 5.1 %shard_map.137 = f32[32,16,128]{2,1,0:T(8,128)} custom-call(s32[8]{0:T(128)S(1)} %copy-done.9, s32[64,128]{1,0:T(8,128)S(1)} %bitcast.14, s32[64,128]{1,0:T(8,128)S(1)} %bitcast.15, f32[8,128]{1,0:T(8,128)S(1)} %copy-done.7, f32[8,128]{1,0:T(8,128)S(1)} %copy-done.8), custom_call_target="tpu_custom_call" | custom-call | tf_op jit(solution)/shard_map/pallas_call | solution.py:334
  9.3 11.5 %all-to-all-start = ((f32[32,16,128]{2,1,0:T(8,128)}), f32[32,16,128]{2,1,0:T(8,128)S(1)}, u32[]{:S(2)}, u32[]{:S(2)}) async-start(f32[32,16,128]{2,1,0:T(8,128)} %shard_map.137), calls=%async_computation | async-start | bytes 524288 | tf_op jit(solution)/shard_map/all_to_all | solution.py:327
  20.8 0.1 pad_add_fusion.spot_ref
  20.9 0.0 copy-start
  20.9 1.2 copy-done
  22.1 0.0 copy-start.1
  22.1 1.2 copy-done.1
  23.4 0.0 copy-start.6
  23.4 1.6 shard_map.138
  25.0 8.3 %all-to-all-done.recv_ref = f32[32,16,128]{2,1,0:T(8,128)S(1)} async-done(((f32[32,16,128]{2,1,0:T(8,128)}), f32[32,16,128]{2,1,0:T(8,128)S(1)}, u32[]{:S(2)}, u32[]{:S(2)}) %all-to-all-start) | async-done | bytes 262176 | tf_op jit(solution)/shard_map/all_to_all | solution.py:327
  33.3 2.5 %shard_map.139 = (f32[16,256,128]{2,1,0:T(8,128)S(1)}, f32[256,128]{1,0:T(8,128)S(1)}, f32[32,128]{1,0:T(8,128)S(1)}, f32[32,128]{1,0:T(8,128)S(1)}) custom-call(s32[3]{0:T(128)S(1)} %pad_add_fusion.spot_ref, f32[32,16,128]{2,1,0:T(8,128)S(1)} %all-to-all-done.recv_ref, f32[2048,128]{1,0:T(8,128)S(1)} %get-tuple-element.26.table_ref), custom_call_target="tpu_custom_call" | custom-call | tf_op jit(solution)/shard_map/pallas_call | solution.py:359
  35.8 12.1 %all_to_all.55.recv_ref = f32[8,32,128]{2,1,0:T(8,128)S(1)} all-to-all(f32[8,32,128]{2,1,0:T(8,128)S(1)} %bitcast.13), channel_id=1, replica_groups=mesh['y'=4,'z'=8,'x'=4,'core'=2] {'z'}, dimensions={0} | all-to-all | bytes 262144 | tf_op jit(solution)/shard_map/all_to_all | solution.py:327
  47.9 8.1 %all_to_all.56.recv_ref = f32[4,32,128]{2,1,0:T(8,128)S(1)} all-to-all(f32[4,32,128]{2,1,0:T(8,128)S(1)} %shard_map.140), channel_id=1, replica_groups=mesh['y'=4,'z'=8,'x'=4,'core'=2] {'y'}, dimensions={0} | all-to-all | bytes 131072 | tf_op jit(solution)/shard_map/all_to_all | solution.py:327
  56.0 0.0 copy-done.6
  56.0 0.1 shard_map.141
  56.1 11.5 %all_to_all.57 = f32[8,32,128]{2,1,0:T(8,128)S(1)} all-to-all(f32[8,32,128]{2,1,0:T(8,128)S(1)} %get-tuple-element.30), channel_id=1, replica_groups=mesh['y'=4,'z'=8,'x'=4,'core'=2] {'z'}, dimensions={0} | all-to-all | bytes 262144 | tf_op jit(solution)/shard_map/all_to_all | solution.py:327
  67.5 0.0 copy-start.2
  67.5 0.0 copy-start.3
  67.5 1.4 shard_map.142
  69.0 11.5 %all_to_all.58.recv_ref = f32[8,32,128]{2,1,0:T(8,128)S(1)} all-to-all(f32[8,32,128]{2,1,0:T(8,128)S(1)} %bitcast.11), channel_id=1, replica_groups=mesh['y'=4,'z'=8,'x'=4,'core'=2] {'z'}, dimensions={0} | all-to-all | bytes 262144 | tf_op jit(solution)/shard_map/all_to_all | solution.py:327
  80.5 8.0 %all_to_all.59.recv_ref = f32[4,32,128]{2,1,0:T(8,128)S(1)} all-to-all(f32[4,32,128]{2,1,0:T(8,128)S(1)} %shard_map.143), channel_id=1, replica_groups=mesh['y'=4,'z'=8,'x'=4,'core'=2] {'y'}, dimensions={0} | all-to-all | bytes 131072 | tf_op jit(solution)/shard_map/all_to_all | solution.py:327
  88.5 0.1 shard_map.144
  88.6 11.5 %all_to_all.60 = f32[8,32,128]{2,1,0:T(8,128)S(1)} all-to-all(f32[8,32,128]{2,1,0:T(8,128)S(1)} %get-tuple-element.34), channel_id=1, replica_groups=mesh['y'=4,'z'=8,'x'=4,'core'=2] {'z'}, dimensions={0} | all-to-all | bytes 262144 | tf_op jit(solution)/shard_map/all_to_all | solution.py:327
  100.0 0.0 copy-done.2
  100.0 0.0 copy-done.3
  100.0 3.2 %shard_map.145 = (f32[256,128]{1,0:T(8,128)S(1)}, f32[8,448,128]{2,1,0:T(8,128)S(1)}) custom-call(f32[256,128]{1,0:T(8,128)S(1)} %bitcast.12, f32[16,256,128]{2,1,0:T(8,128)S(1)} %get-tuple-element.31.marks_ref, f32[2048,128]{1,0:T(8,128)S(1)} %get-tuple-element.26.table_ref, f32[64,2048]{1,0:T(8,128)S(1)} %copy-done.2, f32[64,128]{1,0:T(8,128)S(1)} %copy-done.3), custom_call_target="tpu_custom_call" | custom-call | tf_op jit(solution)/shard_map/pallas_call | solution.py:375
  103.2 27.8 %all_to_all.61.recv_ref = f32[8,448,128]{2,1,0:T(8,128)S(1)} all-to-all(f32[8,448,128]{2,1,0:T(8,128)S(1)} %get-tuple-element.35), channel_id=1, replica_groups=mesh['y'=4,'z'=8,'x'=4,'core'=2] {'x','core'}, dimensions={0} | all-to-all | bytes 3670016 | tf_op jit(solution)/shard_map/all_to_all | solution.py:327
  131.0 1.9 %shard_map.146 = (f32[256,128]{1,0:T(8,128)}, f32[8,64,128]{2,1,0:T(8,128)S(1)}) custom-call(f32[8,448,128]{2,1,0:T(8,128)S(1)} %all_to_all.61.recv_ref, f32[256,128]{1,0:T(8,128)S(1)} %get-tuple-element.36.shape_ref, f32[256,128]{1,0:T(8,128)S(1)} %get-tuple-element.37.rate_ref), custom_call_target="tpu_custom_call" | custom-call | tf_op jit(solution)/shard_map/pallas_call | solution.py:379
  132.9 10.0 %all_to_all.62.grad_ref = f32[8,64,128]{2,1,0:T(8,128)S(1)} all-to-all(f32[8,64,128]{2,1,0:T(8,128)S(1)} %get-tuple-element.38), channel_id=1, replica_groups=mesh['y'=4,'z'=8,'x'=4,'core'=2] {'x','core'}, dimensions={0} | all-to-all | bytes 524288 | tf_op jit(solution)/shard_map/all_to_all | solution.py:327
  142.9 9.1 %all_to_all.63.recv_ref = f32[4,128,128]{2,1,0:T(8,128)S(1)} all-to-all(f32[4,128,128]{2,1,0:T(8,128)S(1)} %shard_map.147), channel_id=1, replica_groups=mesh['y'=4,'z'=8,'x'=4,'core'=2] {'y'}, dimensions={0} | all-to-all | bytes 524288 | tf_op jit(solution)/shard_map/all_to_all | solution.py:327
  152.0 13.7 %all_to_all.64.recv_ref = f32[8,72,128]{2,1,0:T(8,128)S(1)} all-to-all(f32[8,72,128]{2,1,0:T(8,128)S(1)} %shard_map.148), channel_id=1, replica_groups=mesh['y'=4,'z'=8,'x'=4,'core'=2] {'z'}, dimensions={0} | all-to-all | bytes 589824 | tf_op jit(solution)/shard_map/all_to_all | solution.py:327
  165.7 1.2 shard_map.149
  166.9 0.6 slice_reduce_fusion
  (4 shorter events, 0.1 us)
Async XLA Ops:
  0.6 0.8 copy-start.4
  1.4 0.8 copy-start.5
  2.1 0.7 copy-start.7
  2.8 0.7 copy-start.8
  3.5 0.7 copy-start.9
  9.3 24.0 %all-to-all-start = ((f32[32,16,128]{2,1,0:T(8,128)}), f32[32,16,128]{2,1,0:T(8,128)S(1)}, u32[]{:S(2)}, u32[]{:S(2)}) async-start(f32[32,16,128]{2,1,0:T(8,128)} %shard_map.137), calls=%async_computation | async-start | bytes 524288 | tf_op jit(solution)/shard_map/all_to_all | solution.py:327
  20.9 1.2 copy-start
  22.1 1.2 copy-start.1
  23.4 32.6 %copy-start.6 = (f32[128]{0:T(128)S(1)}, f32[128]{0:T(128)}, u32[]{:S(2)}) copy-start(f32[128]{0:T(128)} %param.17) | copy-start | bytes 1540
  67.5 32.5 %copy-start.2 = (f32[64,2048]{1,0:T(8,128)S(1)}, f32[64,2048]{1,0:T(8,128)}, u32[]{:S(2)}) copy-start(f32[64,2048]{1,0:T(8,128)} %cov_ref.1) | copy-start | bytes 1572868
  67.5 32.5 %copy-start.3 = (f32[64,128]{1,0:T(8,128)S(1)}, f32[64,128]{1,0:T(8,128)}, u32[]{:S(2)}) copy-start(f32[64,128]{1,0:T(8,128)} %weight_ref.1) | copy-start | bytes 98308

commit v4 on v3

--- a/solution.py
+++ b/solution.py
@@ -49,6 +49,13 @@
     )
 
 
+def behind(kernel, inputs):
+    def wrapped(*refs):
+        kernel(*refs[:inputs], *refs[inputs + 1 :])
+
+    return wrapped
+
+
 def shape_of(*dims):
     return jax.ShapeDtypeStruct(dims, F32)
 
@@ -61,6 +68,8 @@
     shape_hbm,
     rate_hbm,
     send_ref,
+    theta_ref,
+    active_ref,
     counts_ref,
     ids_ref,
     clicks_ref,
@@ -120,8 +129,8 @@
         lists = lists + lax.dot_general(payload, place, NT, preferred_element_type=F32)
     theta = exp_digamma_over(shape_ref[...], rate_ref[...])
     active = activity_base + jnp.sum(shape_ref[...] / rate_ref[...], axis=1, keepdims=True)
-    eye = lax.broadcasted_iota(jnp.int32, theta.shape, 0) == lax.broadcasted_iota(jnp.int32, theta.shape, 1)
-    active = jnp.sum(jnp.where(eye, active, 0.0), axis=0, keepdims=True)
+    theta_ref[...] = theta
+    active_ref[...] = jnp.broadcast_to(active, theta.shape)
     item_line = lists[:owners] * float(LANES) + lists[owners : 2 * owners]
     lines = (item_line, lists[2 * owners : 3 * owners], lists[3 * owners :])
     for owner in range(owners):
@@ -129,8 +138,7 @@
             line = lines[part][owner : owner + 1, :]
             send_ref[owner, 2 * part : 2 * part + 1, :] = line[:, :LANES]
             send_ref[owner, 2 * part + 1 : 2 * part + 2, :] = line[:, LANES:]
-        send_ref[owner, 6:7, :] = active
-        send_ref[owner, 7:8, :] = jnp.zeros((1, LANES), F32)
+        send_ref[owner, 6:8, :] = jnp.zeros((2, LANES), F32)
         send_ref[owner, 8:16, :] = theta
 
 
@@ -176,9 +184,8 @@
     return total
 
 
-def build_kernel(y_size, spot_ref, recv_ref, table_ref, marks_ref, partial_ref, theta_ref, active_ref):
+def build_kernel(recv_ref, table_ref, marks_ref, partial_ref):
     owners = recv_ref.shape[0]
-    z_size = owners // y_size
     highs = marks_ref.shape[0]
     line_iota = lax.broadcasted_iota(jnp.int32, (LANES, 2 * LANES), 0).astype(F32)
 
@@ -188,8 +195,7 @@
             axis=1,
         )
 
-    order = [y * z_size + z for z in range(z_size) for y in range(y_size)]
-    for place, source in enumerate(order):
+    for source in range(owners):
         item = wide(source, 0).astype(jnp.int32)
         low = (item & (LANES - 1)).astype(F32)
         high = (item >> 7).astype(F32) * 8.0 + wide(source, 1)
@@ -197,35 +203,68 @@
         right = jnp.where(line_iota == low, 1.0, 0.0).astype(BF16)
         tile = dot(left, right, NT)
         for high in range(highs):
-            marks_ref[high, 8 * place : 8 * place + 8, :] = tile[8 * high : 8 * high + 8, :]
-    theta = jnp.concatenate([recv_ref[source, 8:16, :] for source in order], axis=0)
+            marks_ref[high, 8 * source : 8 * source + 8, :] = tile[8 * high : 8 * high + 8, :]
+    theta = jnp.concatenate([recv_ref[source, 8:16, :] for source in range(owners)], axis=0)
     partial_ref[...] = ascend(theta, marks_ref, table_ref)
-    eye = lax.broadcasted_iota(jnp.int32, (8, LANES), 0) == lax.broadcasted_iota(jnp.int32, (8, LANES), 1)
-    for y in range(y_size):
-        source = y * z_size + spot_ref[1]
-        theta_ref[8 * y : 8 * y + 8, :] = recv_ref[source, 8:16, :]
-        active = jnp.sum(jnp.where(eye, recv_ref[source, 6:7, :], 0.0), axis=1, keepdims=True)
-        active_ref[8 * y : 8 * y + 8, :] = jnp.broadcast_to(active, (8, LANES))
 
 
 def ascend_kernel(theta_ref, marks_ref, table_ref, partial_ref):
     partial_ref[...] = ascend(theta_ref[...], marks_ref, table_ref)
 
 
-def last_kernel(theta_ref, marks_ref, table_ref, cov_ref, weight_ref, partial_ref, send_ref):
-    width = 2 * LANES
-    rows = weight_ref.shape[0]
-    for part in range(send_ref.shape[0]):
-        for half in range(2):
-            start = part * width + half * LANES
-            send_ref[part, width + half * rows : width + (half + 1) * rows, :] = cov_ref[:, start : start + LANES]
-        send_ref[part, width + 2 * rows :, :] = weight_ref[...]
-    partial_ref[...] = ascend(theta_ref[...], marks_ref, table_ref, send_ref)
-
-
-def sum_kernel(recv_ref, send_ref):
-    total = jnp.sum(recv_ref[...], axis=0)
-    send_ref[...] = jnp.broadcast_to(total[None], send_ref.shape)
+def last_kernel(theta_ref, marks_ref, table_ref, partial_ref, stats_ref):
+    partial_ref[...] = ascend(theta_ref[...], marks_ref, table_ref, stats_ref)
+
+
+def core_kernel(spot_ref, cov_ref, weight_ref, send_ref, keep_ref):
+    pairs, _, width = keep_ref.shape
+    core = spot_ref[2] & 1
+    for pair in range(pairs):
+        other = pl.multiple_of((2 * pair + 1 - core) * width, width)
+        own = pl.multiple_of((2 * pair + core) * width, width)
+        send_ref[pair] = cov_ref[:, pl.ds(other, width)]
+        keep_ref[pair] = cov_ref[:, pl.ds(own, width)]
+    send_ref[pairs, :, :LANES] = weight_ref[...]
+    send_ref[pairs, :, LANES:] = weight_ref[...]
+
+
+def near_kernel(spot_ref, recv_ref, held_ref, weight_ref, send_ref, keep_ref):
+    low = (spot_ref[2] >> 1) & 1
+    for high in range(2):
+        other = 2 * high + 1 - low
+        own = 2 * high + low
+        send_ref[2 * high] = held_ref[other]
+        send_ref[2 * high + 1] = recv_ref[other]
+        keep_ref[2 * high] = held_ref[own]
+        keep_ref[2 * high + 1] = recv_ref[own]
+    for target in (send_ref, keep_ref):
+        target[4, :, :LANES] = weight_ref[...]
+        target[4, :, LANES:] = recv_ref[4, :, :LANES]
+
+
+def far_kernel(spot_ref, recv_ref, held_ref, send_ref, keep_ref):
+    high = spot_ref[2] >> 2
+    for core in range(2):
+        other = 2 * (1 - high) + core
+        own = 2 * high + core
+        send_ref[core] = held_ref[other]
+        send_ref[2 + core] = recv_ref[other]
+        keep_ref[core] = held_ref[own]
+        keep_ref[2 + core] = recv_ref[own]
+    for target in (send_ref, keep_ref):
+        target[4] = held_ref[4]
+        target[5] = recv_ref[4]
+
+
+def scale_kernel(held_ref, recv_ref, rate_ref, scale_ref):
+    total = jnp.zeros(rate_ref.shape, F32)
+    for source in (held_ref, recv_ref):
+        cov = jnp.concatenate([source[place] for place in range(4)], axis=0)
+        weight = jnp.concatenate(
+            [source[4 + place // 2, :, (place % 2) * LANES : (place % 2 + 1) * LANES] for place in range(4)], axis=0
+        )
+        total = total + lax.dot_general(cov, weight, TN, precision=HIGHEST, preferred_element_type=F32)
+    scale_ref[...] = jnp.exp(total) / rate_ref[...]
 
 
 def update_kernel(activity_shape, recv_ref, theta_ref, activity_ref, totals_ref, active_ref, next_ref, send_ref):
@@ -239,39 +278,26 @@
     send_ref[...] = jnp.broadcast_to(theta[None], send_ref.shape)
 
 
-def score_kernel(recv_ref, shape_ref, rate_ref, new_ref, grad_ref):
-    share = shape_ref.shape[0]
-    parts, rows, _ = grad_ref.shape
-    stats = jnp.sum(recv_ref[:, :share, :], axis=0)
+def score_kernel(spot_ref, stats_ref, shape_ref, scale_ref, held_ref, recv_ref, new_ref, grad_ref):
+    stats = jnp.sum(stats_ref[...], axis=0)
     new_shape = (1.0 - step_weight) * shape_ref[...] + step_weight * (item_prior + USER_RATIO * stats)
     new_ref[...] = new_shape
-    cov = jnp.concatenate(
-        [
-            jnp.concatenate(
-                [recv_ref[part, share : share + rows, :], recv_ref[part, share + rows : share + 2 * rows, :]],
-                axis=1,
-            )
-            for part in range(parts)
-        ],
-        axis=0,
-    )
-    weight = jnp.concatenate([recv_ref[part, share + 2 * rows :, :] for part in range(parts)], axis=0)
-    prior_log = lax.dot_general(cov, weight, TN, precision=HIGHEST, preferred_element_type=F32)
-    score = item_prior - jnp.exp(prior_log) * new_shape / rate_ref[...]
-    grad = lax.dot_general(cov, score, NN, precision=HIGHEST, preferred_element_type=F32)
-    for part in range(parts):
-        grad_ref[part] = grad[part * rows : (part + 1) * rows]
-
-
-def join_kernel(users, grad_ref, partial_ref, send_ref):
+    score = item_prior - scale_ref[...] * new_shape
+    rows = grad_ref.shape[1]
+    for part, source in enumerate((held_ref, recv_ref)):
+        cov = jnp.concatenate([source[place] for place in range(4)], axis=0)
+        grad = lax.dot_general(cov, score, NN, precision=HIGHEST, preferred_element_type=F32)
+        for place in range(4):
+            grad_ref[spot_ref[2] ^ (4 * part + place)] = grad[place * rows : (place + 1) * rows]
+
+
+def join_kernel(grad_ref, partial_ref, send_ref):
     y_size, rows, _ = send_ref.shape
     grad = jnp.sum(grad_ref[...], axis=0)
-    z_size = partial_ref.shape[0] // (y_size * users)
+    users = partial_ref.shape[0] // y_size
     for y in range(y_size):
-        for z in range(z_size):
-            place = (z * y_size + y) * users
-            send_ref[y, z * users : (z + 1) * users, :] = partial_ref[place : place + users, :]
-        send_ref[y, z_size * users :, :] = grad
+        send_ref[y, :users, :] = partial_ref[y * users : (y + 1) * users, :]
+        send_ref[y, users:, :] = grad
 
 
 def fan_kernel(users, recv_ref, send_ref):
@@ -283,13 +309,12 @@
 
 
 def finish_kernel(
-    activity_shape, root, spot_ref, recv_ref, theta_ref, activity_ref, totals_ref, shapes_ref, rates_ref, active_ref, grad_ref
+    activity_shape, root, recv_ref, theta_ref, activity_ref, totals_ref, shapes_ref, rates_ref, active_ref, grad_ref
 ):
     total = jnp.sum(recv_ref[...], axis=0)
     users = shapes_ref.shape[0]
-    here = pl.ds(pl.multiple_of(spot_ref[0] * users, users), users)
-    shapes = user_prior + theta_ref[here, :] * total[:users]
-    rates = activity_shape / activity_ref[here, :] + totals_ref[...]
+    shapes = user_prior + theta_ref[...] * total[:users]
+    rates = activity_shape / activity_ref[...] + totals_ref[...]
     shapes_ref[...] = shapes
     rates_ref[...] = rates
     active = activity_base + jnp.sum(shapes / rates, axis=1, keepdims=True)
@@ -319,7 +344,6 @@
     user_axes, item_axes = ("y", "z"), ("x", "core")
     split_count = lax.axis_size(item_axes)
     share_rows = item_rows // split_count
-    group = y_size * users_here
     everyone = owners * users_here
     activity_shape = activity_prior + factors * user_prior
 
@@ -330,10 +354,12 @@
     totals = beta_totals[None, :]
     smem = pl.BlockSpec(memory_space=pltpu.SMEM)
     vmem = pl.BlockSpec(memory_space=pltpu.VMEM)
-    hbm = pl.BlockSpec(memory_space=pltpu.HBM)
-    send = kernel_call(
+    hbm = pl.BlockSpec(memory_space=pl.ANY)
+    small = shape_of(users_here, factors)
+    share = shape_of(share_rows, factors)
+    send, theta, active = kernel_call(
         functools.partial(prep_kernel, owners),
-        shape_of(owners, 16, LANES),
+        (shape_of(owners, 16, LANES), small, small),
         in_specs=[hbm] * 5,
         scratch_shapes=[
             pltpu.SMEM((users_here,), jnp.int32),
@@ -351,49 +377,61 @@
         user_rate0,
     )
     recv = exchange(send, user_axes)
-    share = shape_of(share_rows, factors)
     table, shape_here, rate_here = kernel_call(
         table_kernel, (shape_of(item_rows, factors), share, share), in_specs=[smem, vmem, vmem]
     )(spot, item_shape, item_rate)
-    local = shape_of(group, factors)
-    marks, partial, theta, active = kernel_call(
-        functools.partial(build_kernel, y_size),
-        (shape_of(highs, everyone, LANES), shape_of(everyone, factors), local, local),
-        in_specs=[smem, vmem, vmem],
-    )(spot, recv, table)
+
+    swap_core = [(place, place ^ 1) for place in range(lax.axis_size("core"))]
+    swap_near = [(place, place ^ 1) for place in range(lax.axis_size("x"))]
+    swap_far = [(place, place ^ 2) for place in range(lax.axis_size("x"))]
+    block = (cov_rows, share_rows)
+    moved, held = kernel_call(
+        behind(core_kernel, 3), (shape_of(5, *block), shape_of(4, *block)), in_specs=[smem, vmem, vmem, hbm]
+    )(spot, covariates, cov_weight, send)
+    moved = lax.ppermute(moved, "core", swap_core)
+    marks, partial = kernel_call(build_kernel, (shape_of(highs, everyone, LANES), shape_of(everyone, factors)))(
+        recv, table
+    )
+    moved, held = kernel_call(
+        behind(near_kernel, 4), (shape_of(5, *block), shape_of(5, *block)), in_specs=[smem, vmem, vmem, vmem, hbm]
+    )(spot, moved, held, cov_weight, partial)
+    moved = lax.ppermute(moved, "x", swap_near)
     for iteration in range(ITERS - 1):
-        parts = exchange(partial.reshape(z_size, group, factors), ("z",))
-        parts = kernel_call(sum_kernel, shape_of(y_size, group, factors))(parts)
-        parts = exchange(parts, ("y",))
+        parts = exchange(partial.reshape(owners, users_here, factors), user_axes)
         active, theta, spread = kernel_call(
             functools.partial(update_kernel, activity_shape),
-            (local, local, shape_of(z_size, group, factors)),
+            (small, small, shape_of(owners, users_here, factors)),
         )(parts, theta, active, totals)
-        theta_all = exchange(spread, ("z",)).reshape(everyone, factors)
+        theta_all = exchange(spread, user_axes).reshape(everyone, factors)
+        if iteration == 0:
+            moved, held = kernel_call(
+                behind(far_kernel, 3), (shape_of(6, *block), shape_of(6, *block)), in_specs=[smem, vmem, vmem, hbm]
+            )(spot, moved, held, spread)
+            moved = lax.ppermute(moved, "x", swap_far)
+        else:
+            scale = kernel_call(behind(scale_kernel, 3), share, in_specs=[vmem, vmem, vmem, hbm])(
+                held, moved, rate_here, spread
+            )
         if iteration < ITERS - 2:
             partial = kernel_call(ascend_kernel, shape_of(everyone, factors))(theta_all, marks, table)
-    partial, send = kernel_call(
-        last_kernel, (shape_of(everyone, factors), shape_of(split_count, share_rows + 3 * cov_rows, factors))
-    )(theta_all, marks, table, covariates, cov_weight)
-    recv = exchange(send, item_axes)
-    new_shape, grad = kernel_call(score_kernel, (share, shape_of(split_count, cov_rows, factors)))(
-        recv, shape_here, rate_here
-    )
+    partial, stats = kernel_call(
+        last_kernel, (shape_of(everyone, factors), shape_of(split_count, share_rows, factors))
+    )(theta_all, marks, table)
+    stats = exchange(stats, item_axes)
+    new_shape, grad = kernel_call(
+        score_kernel, (share, shape_of(split_count, cov_rows, factors)), in_specs=[smem] + [vmem] * 5
+    )(spot, stats, shape_here, scale, held, moved)
     grad = exchange(grad, item_axes)
-    both = kernel_call(
-        functools.partial(join_kernel, users_here), shape_of(y_size, z_size * users_here + cov_rows, factors)
-    )(grad, partial)
+    both = kernel_call(join_kernel, shape_of(y_size, z_size * users_here + cov_rows, factors))(grad, partial)
     both = exchange(both, ("y",))
     both = kernel_call(
         functools.partial(fan_kernel, users_here), shape_of(z_size, users_here + cov_rows, factors)
     )(both)
     both = exchange(both, ("z",))
-    small = shape_of(users_here, factors)
     user_shape, user_rate, active, cov_grad = kernel_call(
         functools.partial(finish_kernel, activity_shape, math.sqrt(item_rows * owners)),
         (small, small, small, shape_of(cov_rows, factors)),
-        in_specs=[smem, vmem, vmem, vmem, vmem],
-    )(spot, both, theta, active, totals)
+    )(both, theta, active, totals)
     return (user_shape, user_rate, active[:, 0], new_shape, cov_grad)
 
 

time: 168 us -> 175 us (1.042)
  blocking collectives: 123 us -> 76.2 us
  waiting for transfers between devices: 8.28 us -> 42 us
  starting transfers between devices: 11.5 us -> 23.1 us
  local copies, waits for them, and re-layouts: 6.62 us -> 12 us
  Pallas kernels: 17.3 us -> 19.8 us
    all_to_all x10 -> x6, blocking collectives: 123 us -> 76.2 us  [exchange(): return lax.all_to_all(array, axes, split_axis=0, concat_axis=0, tiled=True)]
    ppermute x0 -> x3, waiting for transfers between devices: none -> 28.6 us  [the longest x1 18.7 us: shards(): moved = lax.ppermute(moved, 'x', swap_near)]
    all_to_all x1 -> x3, starting transfers between devices: 11.5 us -> 20.3 us  [exchange(): return lax.all_to_all(array, axes, split_axis=0, concat_axis=0, tiled=True)]
    unnamed x20 -> x40, local copies, waits for them, and re-layouts: 6 us -> 11.4 us
    all_to_all x1 -> x3, waiting for transfers between devices: 8.28 us -> 13.5 us  [exchange(): return lax.all_to_all(array, axes, split_axis=0, concat_axis=0, tiled=True)]
    pallas_call x8 -> x10, Pallas kernels: 9.84 us -> 12.9 us  [the longest x1 5.14 us: shards(): kernel_call(functools.partial(prep_kernel, owners), (shape_of(owners, 16,...]
    ppermute x0 -> x3, starting transfers between devices: none -> 2.75 us  [the longest x1 2.65 us: shards(): moved = lax.ppermute(moved, 'x', swap_far)]
  transfers between devices with their start and end apart: 1 -> 6, of which waited for: 1 -> 4; matrix products, arithmetic and copies ran while one was open for 0% -> 0% of each run, Pallas kernels for 1% -> 5%
where the time goes in v4:
time: 175 us; the launch traced here: 174 us
  blocking collectives  76.2 us (44%)
  waiting for transfers between devices  42 us (24%)
  starting transfers between devices  23.1 us (13%)
  Pallas kernels  19.8 us (11%)
  local copies, waits for them, and re-layouts  12 us (7%)
    all_to_all x6, blocking collectives, exchange(): return lax.all_to_all(array, axes, split_axis=0, concat_axis=0, tiled=True)  76.2 us
    all_to_all x3, starting transfers between devices, exchange(): return lax.all_to_all(array, axes, split_axis=0, concat_axis=0, tiled=True)  20.3 us
    ppermute x1, waiting for transfers between devices, shards(): moved = lax.ppermute(moved, 'x', swap_near)  18.7 us
    all_to_all x3, waiting for transfers between devices, exchange(): return lax.all_to_all(array, axes, split_axis=0, concat_axis=0, tiled=True)  13.5 us
    unnamed x40, local copies, waits for them, and re-layouts  11.4 us
    ppermute x1, waiting for transfers between devices, shards(): moved = lax.ppermute(moved, 'x', swap_far)  9.89 us
    pallas_call x1, Pallas kernels, shards(): kernel_call(functools.partial(prep_kernel, owners), (shape_of(owners, 16,...  5.14 us
  transfers between devices with their start and end apart: 6, of which 4 were waited for; matrix products, arithmetic and copies ran while one was open for 0% of the time, Pallas kernels for 5%

profile of v4, /device:TPU:2, one launch (start us, length us, event | category | flops | bytes accessed | tf_op | source)
XLA Modules:
  0.0 174.0 jit_solution(14395688094984189587)
XLA Ops:
  0.6 0.7 copy-done.14
  1.4 0.8 copy-done.15
  2.2 0.7 copy-done.17
  2.8 0.7 copy-done.18
  3.5 0.7 copy-done.19
  4.2 5.1 %shard_map.137 = (f32[32,16,128]{2,1,0:T(8,128)}, f32[8,128]{1,0:T(8,128)S(1)}, f32[8,128]{1,0:T(8,128)S(1)}) custom-call(s32[8]{0:T(128)S(1)} %copy-done.19, s32[64,128]{1,0:T(8,128)S(1)} %bitcast.14, s32[64,128]{1,0:T(8,128)S(1)} %bitcast.15, f32[8,128]{1,0:T(8,128)S(1)} %copy-done.17, f32[8,128]{1,0:T(8,128)S(1)} %copy-done.18), custom_call_target="tpu_custom_call" | custom-call | tf_op jit(solution)/shard_map/pallas_call | solution.py:360
  9.3 0.0 copy-start.16
  9.3 11.5 %all-to-all-start = ((f32[32,16,128]{2,1,0:T(8,128)}), f32[32,16,128]{2,1,0:T(8,128)S(1)}, u32[]{:S(2)}, u32[]{:S(2)}) async-start(f32[32,16,128]{2,1,0:T(8,128)} %get-tuple-element.33.refs_3_), calls=%async_computation | async-start | bytes 524288 | tf_op jit(solution)/shard_map/all_to_all | solution.py:351
  20.9 0.1 pad_add_fusion.spot_ref.refs_0_
  20.9 1.2 copy-done
  22.2 1.2 copy-done.1
  23.4 1.6 shard_map.138
  25.0 0.6 copy-done.6
  25.7 0.6 copy-done.8
  26.3 7.0 %all-to-all-done.recv_ref = f32[32,16,128]{2,1,0:T(8,128)S(1)} async-done(((f32[32,16,128]{2,1,0:T(8,128)}), f32[32,16,128]{2,1,0:T(8,128)S(1)}, u32[]{:S(2)}, u32[]{:S(2)}) %all-to-all-start) | async-done | bytes 262176 | tf_op jit(solution)/shard_map/all_to_all | solution.py:351
  33.3 2.0 %shard_map.139 = (f32[16,256,128]{2,1,0:T(8,128)S(1)}, f32[256,128]{1,0:T(8,128)S(1)}) custom-call(f32[32,16,128]{2,1,0:T(8,128)S(1)} %all-to-all-done.recv_ref, f32[2048,128]{1,0:T(8,128)S(1)} %get-tuple-element.34.table_ref), custom_call_target="tpu_custom_call" | custom-call | tf_op jit(solution)/shard_map/pallas_call | solution.py:392
  35.3 14.6 %all_to_all.45.recv_ref = f32[32,8,128]{2,1,0:T(8,128)S(1)} all-to-all(f32[32,8,128]{2,1,0:T(8,128)S(1)} %bitcast.10), channel_id=1, replica_groups=mesh['y'=4,'z'=8,'x'=4,'core'=2] {'y','z'}, dimensions={0} | all-to-all | bytes 262144 | tf_op jit(solution)/shard_map/all_to_all | solution.py:351
  49.9 0.1 shard_map.140
  50.0 13.8 %all_to_all.46 = f32[32,8,128]{2,1,0:T(8,128)S(1)} all-to-all(f32[32,8,128]{2,1,0:T(8,128)S(1)} %get-tuple-element.38.refs_3_), channel_id=1, replica_groups=mesh['y'=4,'z'=8,'x'=4,'core'=2] {'y','z'}, dimensions={0} | all-to-all | bytes 262144 | tf_op jit(solution)/shard_map/all_to_all | solution.py:351
  63.8 1.4 shard_map.141
  65.3 13.8 %all_to_all.47.recv_ref = f32[32,8,128]{2,1,0:T(8,128)S(1)} all-to-all(f32[32,8,128]{2,1,0:T(8,128)S(1)} %bitcast.13), channel_id=1, replica_groups=mesh['y'=4,'z'=8,'x'=4,'core'=2] {'y','z'}, dimensions={0} | all-to-all | bytes 262144 | tf_op jit(solution)/shard_map/all_to_all | solution.py:351
  79.1 0.7 shard_map.142
  79.8 3.9 %all-to-all-start.4 = ((f32[32,8,128]{2,1,0:T(8,128)}), f32[32,8,128]{2,1,0:T(8,128)S(1)}, u32[]{:S(2)}, u32[]{:S(2)}) async-start(f32[32,8,128]{2,1,0:T(8,128)} %get-tuple-element.42.refs_3_), calls=%async_computation.4 | async-start | bytes 262144 | tf_op jit(solution)/shard_map/all_to_all | solution.py:351
  83.6 0.0 copy-start.3
  83.7 1.0 copy-done.3
  84.7 0.8 copy-done.12
  85.5 1.3 shard_map.144
  86.8 0.7 copy-done.4
  87.4 0.0 collective-permute-start
  87.4 6.5 %all-to-all-done.4 = f32[32,8,128]{2,1,0:T(8,128)S(1)} async-done(((f32[32,8,128]{2,1,0:T(8,128)}), f32[32,8,128]{2,1,0:T(8,128)S(1)}, u32[]{:S(2)}, u32[]{:S(2)}) %all-to-all-start.4) | async-done | bytes 131104 | tf_op jit(solution)/shard_map/all_to_all | solution.py:351
  93.9 3.1 %shard_map.143 = (f32[256,128]{1,0:T(8,128)S(1)}, f32[8,256,128]{2,1,0:T(8,128)S(1)}) custom-call(f32[256,128]{1,0:T(8,128)S(1)} %bitcast.11, f32[16,256,128]{2,1,0:T(8,128)S(1)} %get-tuple-element.39.marks_ref, f32[2048,128]{1,0:T(8,128)S(1)} %get-tuple-element.34.table_ref), custom_call_target="tpu_custom_call" | custom-call | tf_op jit(solution)/shard_map/pallas_call | solution.py:417
  97.1 1.0 copy-done.2
  98.0 0.6 copy-done.10
  98.7 5.0 %all-to-all-start.5 = ((f32[8,256,128]{2,1,0:T(8,128)}), f32[8,256,128]{2,1,0:T(8,128)S(1)}, u32[]{:S(2)}, u32[]{:S(2)}) async-start(f32[8,256,128]{2,1,0:T(8,128)} %copy-done.2), calls=%async_computation.5 | async-start | bytes 2097152 | tf_op jit(solution)/shard_map/all_to_all | solution.py:351
  103.7 0.0 collective-permute-done.refs_1_
  103.7 1.0 shard_map.145
  104.7 0.1 collective-permute-start.1
  104.8 18.7 %collective-permute-done.1.refs_1_ = f32[5,64,256]{2,1,0:T(8,128)S(1)} collective-permute-done((f32[5,64,256]{2,1,0:T(8,128)S(1)}, f32[5,64,256]{2,1,0:T(8,128)S(1)}, u32[]{:S(2)}, u32[]{:S(2)}) %collective-permute-start.1) | collective-permute-done | bytes 327712 | tf_op jit(solution)/shard_map/ppermute | solution.py:398
  123.5 0.6 shard_map.146
  124.1 2.7 %collective-permute-start.2 = (f32[6,64,256]{2,1,0:T(8,128)S(1)}, f32[6,64,256]{2,1,0:T(8,128)S(1)}, u32[]{:S(2)}, u32[]{:S(2)}) collective-permute-start(f32[6,64,256]{2,1,0:T(8,128)S(1)} %get-tuple-element.50), channel_id=1, source_target_pairs={{0,4},{2,6},{4,0},{6,2},{1,5},{3,7},{5,1},{7,3},{8,12},{10,14},{12... | collective-permute-start | bytes 1179656 | tf_op jit(solution)/shard_map/ppermute | solution.py:410
  126.8 9.9 %collective-permute-done.2.refs_1_.recv_ref = f32[6,64,256]{2,1,0:T(8,128)S(1)} collective-permute-done((f32[6,64,256]{2,1,0:T(8,128)S(1)}, f32[6,64,256]{2,1,0:T(8,128)S(1)}, u32[]{:S(2)}, u32[]{:S(2)}) %collective-permute-start.2) | collective-permute-done | bytes 393248 | tf_op jit(solution)/shard_map/ppermute | solution.py:410
  136.6 0.7 shard_map.147.scale_ref
  137.4 1.3 shard_map.148
  138.7 11.2 %all_to_all.48.grad_ref = f32[8,64,128]{2,1,0:T(8,128)S(1)} all-to-all(f32[8,64,128]{2,1,0:T(8,128)S(1)} %get-tuple-element.52), channel_id=1, replica_groups=mesh['y'=4,'z'=8,'x'=4,'core'=2] {'x','core'}, dimensions={0} | all-to-all | bytes 524288 | tf_op jit(solution)/shard_map/all_to_all | solution.py:351
  149.9 9.2 %all_to_all.49.recv_ref = f32[4,128,128]{2,1,0:T(8,128)S(1)} all-to-all(f32[4,128,128]{2,1,0:T(8,128)S(1)} %shard_map.149), channel_id=1, replica_groups=mesh['y'=4,'z'=8,'x'=4,'core'=2] {'y'}, dimensions={0} | all-to-all | bytes 524288 | tf_op jit(solution)/shard_map/all_to_all | solution.py:351
  159.1 13.6 %all_to_all.50.recv_ref = f32[8,72,128]{2,1,0:T(8,128)S(1)} all-to-all(f32[8,72,128]{2,1,0:T(8,128)S(1)} %shard_map.150), channel_id=1, replica_groups=mesh['y'=4,'z'=8,'x'=4,'core'=2] {'z'}, dimensions={0} | all-to-all | bytes 589824 | tf_op jit(solution)/shard_map/all_to_all | solution.py:351
  172.7 0.6 shard_map.151
  173.3 0.6 slice_reduce_fusion
  (27 shorter events, 0.1 us)
Async XLA Ops:
  0.6 0.8 copy-start.14
  1.4 0.8 copy-start.15
  2.1 0.7 copy-start.17
  2.8 0.7 copy-start.18
  3.5 0.7 copy-start.19
  9.3 40.6 %copy-start.16 = (f32[128]{0:T(128)S(1)}, f32[128]{0:T(128)}, u32[]{:S(2)}) copy-start(f32[128]{0:T(128)} %param.17) | copy-start | bytes 1540
  9.3 24.0 %all-to-all-start = ((f32[32,16,128]{2,1,0:T(8,128)}), f32[32,16,128]{2,1,0:T(8,128)S(1)}, u32[]{:S(2)}, u32[]{:S(2)}) async-start(f32[32,16,128]{2,1,0:T(8,128)} %get-tuple-element.33.refs_3_), calls=%async_computation | async-start | bytes 524288 | tf_op jit(solution)/shard_map/all_to_all | solution.py:351
  20.9 1.2 copy-start
  22.2 1.2 copy-start.1
  25.0 0.6 copy-start.6
  25.7 0.6 copy-start.8
  79.8 14.2 %all-to-all-start.4 = ((f32[32,8,128]{2,1,0:T(8,128)}), f32[32,8,128]{2,1,0:T(8,128)S(1)}, u32[]{:S(2)}, u32[]{:S(2)}) async-start(f32[32,8,128]{2,1,0:T(8,128)} %get-tuple-element.42.refs_3_), calls=%async_computation.4 | async-start | bytes 262144 | tf_op jit(solution)/shard_map/all_to_all | solution.py:351
  83.6 1.0 copy-start.3
  84.7 0.8 copy-start.12
  86.7 0.7 copy-start.4
  87.4 16.2 %collective-permute-start = (f32[5,64,256]{2,1,0:T(8,128)}, f32[5,64,256]{2,1,0:T(8,128)}, u32[]{:S(2)}, u32[]{:S(2)}) collective-permute-start(f32[5,64,256]{2,1,0:T(8,128)} %get-tuple-element.45), channel_id=1, source_target_pairs={{0,1},{1,0},{2,3},{3,2},{4,5},{5,4},{6,7},{7,6},{8,9},{9,8},{10,11... | collective-permute-start | bytes 983048 | tf_op jit(solution)/shard_map/ppermute | solution.py:391
  97.1 1.0 copy-start.2
  98.0 0.6 copy-start.10
  98.7 5.0 %copy-start.5 = (f32[4,64,256]{2,1,0:T(8,128)S(1)}, f32[4,64,256]{2,1,0:T(8,128)}, u32[]{:S(2)}) copy-start(f32[4,64,256]{2,1,0:T(8,128)} %copy-done.4) | copy-start | bytes 786436
  98.7 5.0 %copy-start.13 = (f32[64,128]{1,0:T(8,128)S(1)}, f32[64,128]{1,0:T(8,128)}, u32[]{:S(2)}) copy-start(f32[64,128]{1,0:T(8,128)} %refs_3_.1) | copy-start | bytes 98308
  98.7 38.0 %copy-start.9 = (f32[256,128]{1,0:T(8,128)S(1)}, f32[256,128]{1,0:T(8,128)}, u32[]{:S(2)}) copy-start(f32[256,128]{1,0:T(8,128)} %copy-done.8) | copy-start | bytes 393220
  98.7 38.7 %copy-start.7 = (f32[256,128]{1,0:T(8,128)S(1)}, f32[256,128]{1,0:T(8,128)}, u32[]{:S(2)}) copy-start(f32[256,128]{1,0:T(8,128)} %copy-done.6) | copy-start | bytes 393220
  98.7 38.7 %all-to-all-start.5 = ((f32[8,256,128]{2,1,0:T(8,128)}), f32[8,256,128]{2,1,0:T(8,128)S(1)}, u32[]{:S(2)}, u32[]{:S(2)}) async-start(f32[8,256,128]{2,1,0:T(8,128)} %copy-done.2), calls=%async_computation.5 | async-start | bytes 2097152 | tf_op jit(solution)/shard_map/all_to_all | solution.py:351
  104.7 18.8 %collective-permute-start.1 = (f32[5,64,256]{2,1,0:T(8,128)S(1)}, f32[5,64,256]{2,1,0:T(8,128)S(1)}, u32[]{:S(2)}, u32[]{:S(2)}) collective-permute-start(f32[5,64,256]{2,1,0:T(8,128)S(1)} %get-tuple-element.47), channel_id=1, source_target_pairs={{0,2},{2,0},{4,6},{6,4},{1,3},{3,1},{5,7},{7,5},{8,10},{10,8},{12,... | collective-permute-start | bytes 983048 | tf_op jit(solution)/shard_map/ppermute | solution.py:398
  124.1 25.8 %copy-start.11 = (f32[256,128]{1,0:T(8,128)S(1)}, f32[256,128]{1,0:T(8,128)}, u32[]{:S(2)}) copy-start(f32[256,128]{1,0:T(8,128)} %copy-done.10) | copy-start | bytes 393220
  124.1 12.5 %collective-permute-start.2 = (f32[6,64,256]{2,1,0:T(8,128)S(1)}, f32[6,64,256]{2,1,0:T(8,128)S(1)}, u32[]{:S(2)}, u32[]{:S(2)}) collective-permute-start(f32[6,64,256]{2,1,0:T(8,128)S(1)} %get-tuple-element.50), channel_id=1, source_target_pairs={{0,4},{2,6},{4,0},{6,2},{1,5},{3,7},{5,1},{7,3},{8,12},{10,14},{12... | collective-permute-start | bytes 1179656 | tf_op jit(solution)/shard_map/ppermute | solution.py:410

commit v5 on v4

--- a/solution.py
+++ b/solution.py
@@ -26,6 +26,7 @@
 TN = (((0,), (0,)), ((), ()))
 LANES = 128
 VMEM_LIMIT = 48 * 1024 * 1024
+WHOLE_VMEM = 60 * 1024 * 1024
 
 
 def exp_digamma_over(x, rate):
@@ -40,18 +41,18 @@
     return y * jnp.exp(-steps - tail) / rate
 
 
-def kernel_call(kernel, out_shape, **specs):
+def kernel_call(kernel, out_shape, vmem=VMEM_LIMIT, **specs):
     return pl.pallas_call(
         kernel,
         out_shape=out_shape,
-        compiler_params=pltpu.CompilerParams(vmem_limit_bytes=VMEM_LIMIT),
+        compiler_params=pltpu.CompilerParams(vmem_limit_bytes=vmem),
         **specs,
     )
 
 
-def behind(kernel, inputs):
+def behind(kernel, inputs, awaited=1):
     def wrapped(*refs):
-        kernel(*refs[:inputs], *refs[inputs + 1 :])
+        kernel(*refs[:inputs], *refs[inputs + awaited :])
 
     return wrapped
 
@@ -318,7 +319,9 @@
     shapes_ref[...] = shapes
     rates_ref[...] = rates
     active = activity_base + jnp.sum(shapes / rates, axis=1, keepdims=True)
-    active_ref[...] = jnp.broadcast_to(active, shapes.shape)
+    eye = lax.broadcasted_iota(jnp.int32, shapes.shape, 0) == lax.broadcasted_iota(jnp.int32, shapes.shape, 1)
+    row = jnp.sum(jnp.where(eye, active, 0.0), axis=0, keepdims=True)
+    active_ref[...] = row[:, :users]
     grad_ref[...] = total[users:] / root
 
 
@@ -360,6 +363,7 @@
     send, theta, active = kernel_call(
         functools.partial(prep_kernel, owners),
         (shape_of(owners, 16, LANES), small, small),
+        vmem=WHOLE_VMEM,
         in_specs=[hbm] * 5,
         scratch_shapes=[
             pltpu.SMEM((users_here,), jnp.int32),
@@ -388,32 +392,38 @@
     moved, held = kernel_call(
         behind(core_kernel, 3), (shape_of(5, *block), shape_of(4, *block)), in_specs=[smem, vmem, vmem, hbm]
     )(spot, covariates, cov_weight, send)
-    moved = lax.ppermute(moved, "core", swap_core)
-    marks, partial = kernel_call(build_kernel, (shape_of(highs, everyone, LANES), shape_of(everyone, factors)))(
-        recv, table
-    )
-    moved, held = kernel_call(
-        behind(near_kernel, 4), (shape_of(5, *block), shape_of(5, *block)), in_specs=[smem, vmem, vmem, vmem, hbm]
-    )(spot, moved, held, cov_weight, partial)
-    moved = lax.ppermute(moved, "x", swap_near)
+    marks, partial = kernel_call(
+        behind(build_kernel, 2),
+        (shape_of(highs, everyone, LANES), shape_of(everyone, factors)),
+        in_specs=[vmem, vmem, hbm],
+    )(recv, table, moved)
     for iteration in range(ITERS - 1):
+        first = iteration == 0
+        if first:
+            moved = lax.ppermute(moved, "core", swap_core)
+            moved, held = kernel_call(
+                behind(near_kernel, 4), (shape_of(5, *block), shape_of(5, *block)), in_specs=[smem, vmem, vmem, vmem, hbm]
+            )(spot, moved, held, cov_weight, partial)
+        else:
+            moved = lax.ppermute(moved, "x", swap_far)
+            scale = kernel_call(behind(scale_kernel, 3), share, in_specs=[vmem, vmem, vmem, hbm])(
+                held, moved, rate_here, partial
+            )
         parts = exchange(partial.reshape(owners, users_here, factors), user_axes)
         active, theta, spread = kernel_call(
-            functools.partial(update_kernel, activity_shape),
+            behind(functools.partial(update_kernel, activity_shape), 4),
             (small, small, shape_of(owners, users_here, factors)),
-        )(parts, theta, active, totals)
+            in_specs=[vmem] * 4 + [hbm],
+        )(parts, theta, active, totals, moved if first else scale)
         theta_all = exchange(spread, user_axes).reshape(everyone, factors)
-        if iteration == 0:
+        if first:
+            moved = lax.ppermute(moved, "x", swap_near)
             moved, held = kernel_call(
                 behind(far_kernel, 3), (shape_of(6, *block), shape_of(6, *block)), in_specs=[smem, vmem, vmem, hbm]
             )(spot, moved, held, spread)
-            moved = lax.ppermute(moved, "x", swap_far)
-        else:
-            scale = kernel_call(behind(scale_kernel, 3), share, in_specs=[vmem, vmem, vmem, hbm])(
-                held, moved, rate_here, spread
-            )
-        if iteration < ITERS - 2:
-            partial = kernel_call(ascend_kernel, shape_of(everyone, factors))(theta_all, marks, table)
+            partial = kernel_call(
+                behind(ascend_kernel, 3), shape_of(everyone, factors), in_specs=[vmem, vmem, vmem, hbm]
+            )(theta_all, marks, table, moved)
     partial, stats = kernel_call(
         last_kernel, (shape_of(everyone, factors), shape_of(split_count, share_rows, factors))
     )(theta_all, marks, table)
@@ -430,9 +440,9 @@
     both = exchange(both, ("z",))
     user_shape, user_rate, active, cov_grad = kernel_call(
         functools.partial(finish_kernel, activity_shape, math.sqrt(item_rows * owners)),
-        (small, small, small, shape_of(cov_rows, factors)),
+        (small, small, shape_of(1, users_here), shape_of(cov_rows, factors)),
     )(both, theta, active, totals)
-    return (user_shape, user_rate, active[:, 0], new_shape, cov_grad)
+    return (user_shape, user_rate, active.reshape(users_here), new_shape, cov_grad)
 
 
 def solution(mesh):

time: 175 us -> 158 us (0.903)
  waiting for transfers between devices: 42 us -> 21.9 us
  blocking collectives: 76.2 us -> 65.8 us
  starting transfers between devices: 23.1 us -> 29.7 us
  Pallas kernels: 19.8 us -> 26 us
    ppermute x1, waiting for transfers between devices: 18.7 us -> 0.01 us  [shards(): moved = lax.ppermute(moved, 'x', swap_near)]
    all_to_all x6 -> x5, blocking collectives: 76.2 us -> 65.8 us  [exchange(): return lax.all_to_all(array, axes, split_axis=0, concat_axis=0, tiled=True)]
    ppermute x1, waiting for transfers between devices: 9.89 us -> 0.01 us  [shards(): moved = lax.ppermute(moved, 'x', swap_far)]
    all_to_all x3 -> x4, waiting for transfers between devices: 13.5 us -> 21.9 us  [exchange(): return lax.all_to_all(array, axes, split_axis=0, concat_axis=0, tiled=True)]
    all_to_all x3 -> x4, starting transfers between devices: 20.3 us -> 27 us  [exchange(): return lax.all_to_all(array, axes, split_axis=0, concat_axis=0, tiled=True)]
    pallas_call x4, Pallas kernels: 4.27 us -> 6.74 us  [the longest x1 2.65 us: shards(): kernel_call(behind(build_kernel, 2), (shape_of(highs, everyone, LANES), s...]
    unnamed x40 -> x44, local copies, waits for them, and re-layouts: 11.4 us -> 12.7 us
  transfers between devices with their start and end apart: 6 -> 7, of which waited for: 4 -> 4; matrix products, arithmetic and copies ran while one was open for 0% -> 0% of each run, Pallas kernels for 5% -> 9%
where the time goes in v5:
time: 158 us; the launch traced here: 157 us
  blocking collectives  65.8 us (42%)
  starting transfers between devices  29.7 us (19%)
  Pallas kernels  26 us (16%)
  waiting for transfers between devices  21.9 us (14%)
  local copies, waits for them, and re-layouts  12.7 us (8%)
    all_to_all x5, blocking collectives, exchange(): return lax.all_to_all(array, axes, split_axis=0, concat_axis=0, tiled=True)  65.8 us
    all_to_all x4, starting transfers between devices, exchange(): return lax.all_to_all(array, axes, split_axis=0, concat_axis=0, tiled=True)  27 us
    all_to_all x4, waiting for transfers between devices, exchange(): return lax.all_to_all(array, axes, split_axis=0, concat_axis=0, tiled=True)  21.9 us
    unnamed x44, local copies, waits for them, and re-layouts  12.7 us
    pallas_call x1, Pallas kernels, shards(): kernel_call(functools.partial(prep_kernel, owners), (shape_of(owners, 16,...  5.49 us
  transfers between devices with their start and end apart: 7, of which 4 were waited for; matrix products, arithmetic and copies ran while one was open for 0% of the time, Pallas kernels for 9%

profile of v5, /device:TPU:2, one launch (start us, length us, event | category | flops | bytes accessed | tf_op | source)
XLA Modules:
  0.0 157.0 jit_solution(7386755385308944921)
XLA Ops:
  0.6 5.5 %shard_map.137 = (f32[32,16,128]{2,1,0:T(8,128)}, f32[8,128]{1,0:T(8,128)}, f32[8,128]{1,0:T(8,128)}) custom-call(s32[8]{0:T(128)} %counts_hbm.1, s32[64,128]{1,0:T(8,128)} %bitcast.16, s32[64,128]{1,0:T(8,128)} %bitcast.17, f32[8,128]{1,0:T(8,128)} %shape_hbm.1, f32[8,128]{1,0:T(8,128)} %rate_hbm.1), custom_call_target="tpu_custom_call" | custom-call | tf_op jit(solution)/shard_map/pallas_call | solution.py:363
  6.1 11.5 %all-to-all-start = ((f32[32,16,128]{2,1,0:T(8,128)}), f32[32,16,128]{2,1,0:T(8,128)S(1)}, u32[]{:S(2)}, u32[]{:S(2)}) async-start(f32[32,16,128]{2,1,0:T(8,128)} %get-tuple-element.33.refs_3_), calls=%async_computation | async-start | bytes 524288 | tf_op jit(solution)/shard_map/all_to_all | solution.py:354
  17.7 0.1 pad_add_fusion.spot_ref.refs_0_
  17.7 0.9 copy-done.7
  18.7 1.0 copy-done.8
  19.7 0.8 copy-done.17
  20.5 1.3 shard_map.139
  21.8 0.7 copy-done.11
  22.5 0.0 collective-permute-start
  22.5 1.2 copy-done.6
  23.8 1.6 %shard_map.138 = (f32[2048,128]{1,0:T(8,128)S(1)}, f32[256,128]{1,0:T(8,128)S(1)}, f32[256,128]{1,0:T(8,128)S(1)}) custom-call(s32[3]{0:T(128)S(1)} %pad_add_fusion.spot_ref.refs_0_, f32[2048,128]{1,0:T(8,128)S(1)} %copy-done.5, f32[2048,128]{1,0:T(8,128)S(1)} %copy-done.6), custom_call_target="tpu_custom_call" | custom-call | tf_op jit(solution)/shard_map/pallas_call | solution.py:384
  25.4 0.6 copy-done.13
  26.0 0.6 copy-done.15
  26.7 3.4 %all-to-all-done.refs_0_ = f32[32,16,128]{2,1,0:T(8,128)S(1)} async-done(((f32[32,16,128]{2,1,0:T(8,128)}), f32[32,16,128]{2,1,0:T(8,128)S(1)}, u32[]{:S(2)}, u32[]{:S(2)}) %all-to-all-start) | async-done | bytes 262176 | tf_op jit(solution)/shard_map/all_to_all | solution.py:354
  30.1 2.7 %shard_map.140 = (f32[16,256,128]{2,1,0:T(8,128)S(1)}, f32[256,128]{1,0:T(8,128)}) custom-call(f32[32,16,128]{2,1,0:T(8,128)S(1)} %all-to-all-done.refs_0_, f32[2048,128]{1,0:T(8,128)S(1)} %get-tuple-element.34.refs_1_.refs_2_.table_ref, f32[5,64,256]{2,1,0:T(8,128)} %get-tuple-element.35.refs_2_), custom_call_target="tpu_custom_call" | custom-call | tf_op jit(solution)/shard_map/pallas_call | solution.py:395
  32.8 6.4 %all-to-all-start.1 = ((f32[32,8,128]{2,1,0:T(8,128)}), f32[32,8,128]{2,1,0:T(8,128)S(1)}, u32[]{:S(2)}, u32[]{:S(2)}) async-start(f32[32,8,128]{2,1,0:T(8,128)} %bitcast.5), calls=%async_computation.1 | async-start | bytes 262144 | tf_op jit(solution)/shard_map/all_to_all | solution.py:354
  39.2 0.9 copy-done.12
  40.1 1.8 %shard_map.141 = (f32[5,64,256]{2,1,0:T(8,128)}, f32[5,64,256]{2,1,0:T(8,128)S(1)}) custom-call(s32[3]{0:T(128)S(1)} %pad_add_fusion.spot_ref.refs_0_, f32[5,64,256]{2,1,0:T(8,128)} %collective-permute-done.refs_1_, f32[4,64,256]{2,1,0:T(8,128)S(1)} %copy-done.12, f32[64,128]{1,0:T(8,128)S(1)} %copy-done.18, f32[256,128]{1,0:T(8,128)} %get-tuple-element.36.refs_4_), custom_call_target="tpu_custom_call" | custom-call | tf_op jit(solution)/shard_map/pallas_call | solution.py:404
  41.9 0.7 copy-done.9
  42.6 0.5 collective-permute-start.1
  43.1 6.9 %all-to-all-done.1.refs_0_ = f32[32,8,128]{2,1,0:T(8,128)S(1)} async-done(((f32[32,8,128]{2,1,0:T(8,128)}), f32[32,8,128]{2,1,0:T(8,128)S(1)}, u32[]{:S(2)}, u32[]{:S(2)}) %all-to-all-start.1) | async-done | bytes 131104 | tf_op jit(solution)/shard_map/all_to_all | solution.py:354
  50.1 0.7 shard_map.142
  50.8 4.6 %all-to-all-start.2 = ((f32[32,8,128]{2,1,0:T(8,128)}), f32[32,8,128]{2,1,0:T(8,128)}, u32[]{:S(2)}, u32[]{:S(2)}) async-start(f32[32,8,128]{2,1,0:T(8,128)} %get-tuple-element.41.refs_3_), calls=%async_computation.2 | async-start | bytes 262144 | tf_op jit(solution)/shard_map/all_to_all | solution.py:354
  55.4 0.0 collective-permute-done.1.refs_1_
  55.4 1.0 copy-done.10
  56.4 1.8 %shard_map.143 = (f32[6,64,256]{2,1,0:T(8,128)}, f32[6,64,256]{2,1,0:T(8,128)S(1)}) custom-call(s32[3]{0:T(128)S(1)} %pad_add_fusion.spot_ref.refs_0_, f32[5,64,256]{2,1,0:T(8,128)} %collective-permute-done.1.refs_1_, f32[5,64,256]{2,1,0:T(8,128)S(1)} %copy-done.10, f32[32,8,128]{2,1,0:T(8,128)} %get-tuple-element.41.refs_3_), custom_call_target="tpu_custom_call" | custom-call | tf_op jit(solution)/shard_map/pallas_call | solution.py:421
  58.2 2.1 %collective-permute-start.2 = (f32[6,64,256]{2,1,0:T(8,128)}, f32[6,64,256]{2,1,0:T(8,128)}, u32[]{:S(2)}, u32[]{:S(2)}) collective-permute-start(f32[6,64,256]{2,1,0:T(8,128)} %get-tuple-element.44.refs_3_), channel_id=1, source_target_pairs={{0,4},{2,6},{4,0},{6,2},{1,5},{3,7},{5,1},{7,3},{8,12},{10,14},{12... | collective-permute-start | bytes 1179656 | tf_op jit(solution)/shard_map/ppermute | solution.py:408
  60.3 5.4 %all-to-all-done.2 = f32[32,8,128]{2,1,0:T(8,128)} async-done(((f32[32,8,128]{2,1,0:T(8,128)}), f32[32,8,128]{2,1,0:T(8,128)}, u32[]{:S(2)}, u32[]{:S(2)}) %all-to-all-start.2) | async-done | bytes 131104 | tf_op jit(solution)/shard_map/all_to_all | solution.py:354
  65.7 2.3 %shard_map.144.refs_3_ = f32[256,128]{1,0:T(8,128)S(1)} custom-call(f32[256,128]{1,0:T(8,128)} %bitcast.7.refs_0_, f32[16,256,128]{2,1,0:T(8,128)S(1)} %get-tuple-element.42.refs_1_.marks_ref, f32[2048,128]{1,0:T(8,128)S(1)} %get-tuple-element.34.refs_1_.refs_2_.table_ref, f32[6,64,256]{2,1,0:T(8,128)} %get-tuple-element.44.refs_3_), custom_call_target="tpu_custom_call" | custom-call | tf_op jit(solution)/shard_map/pallas_call | solution.py:424
  68.1 0.0 copy-start.3
  68.1 0.6 copy-done.3
  68.7 4.6 %all-to-all-start.3 = ((f32[32,8,128]{2,1,0:T(8,128)}), f32[32,8,128]{2,1,0:T(8,128)}, u32[]{:S(2)}, u32[]{:S(2)}) async-start(f32[32,8,128]{2,1,0:T(8,128)} %bitcast.11), calls=%async_computation.3 | async-start | bytes 262144 | tf_op jit(solution)/shard_map/all_to_all | solution.py:354
  73.3 0.0 copy-start.4
  73.4 0.9 copy-done.4
  74.3 0.9 copy-done.16
  75.2 1.7 %shard_map.145.refs_4_.scale_ref = f32[256,128]{1,0:T(8,128)S(1)} custom-call(f32[6,64,256]{2,1,0:T(8,128)S(1)} %get-tuple-element.47.refs_0_.held_ref, f32[6,64,256]{2,1,0:T(8,128)} %collective-permute-done.2.refs_1_.recv_ref, f32[256,128]{1,0:T(8,128)S(1)} %copy-done.16, f32[256,128]{1,0:T(8,128)S(1)} %copy-done.4), custom_call_target="tpu_custom_call" | custom-call | tf_op jit(solution)/shard_map/pallas_call | solution.py:409
  76.9 0.6 copy-done
  77.6 6.1 %all-to-all-done.3.refs_0_ = f32[32,8,128]{2,1,0:T(8,128)} async-done(((f32[32,8,128]{2,1,0:T(8,128)}), f32[32,8,128]{2,1,0:T(8,128)}, u32[]{:S(2)}, u32[]{:S(2)}) %all-to-all-start.3) | async-done | bytes 131104 | tf_op jit(solution)/shard_map/all_to_all | solution.py:354
  83.7 0.9 copy-done.1
  84.6 1.0 shard_map.146
  85.6 13.8 %all_to_all.45 = f32[32,8,128]{2,1,0:T(8,128)S(1)} all-to-all(f32[32,8,128]{2,1,0:T(8,128)S(1)} %get-tuple-element.49), channel_id=1, replica_groups=mesh['y'=4,'z'=8,'x'=4,'core'=2] {'y','z'}, dimensions={0} | all-to-all | bytes 262144 | tf_op jit(solution)/shard_map/all_to_all | solution.py:354
  99.4 3.1 %shard_map.147 = (f32[256,128]{1,0:T(8,128)S(1)}, f32[8,256,128]{2,1,0:T(8,128)S(1)}) custom-call(f32[256,128]{1,0:T(8,128)S(1)} %bitcast.12, f32[16,256,128]{2,1,0:T(8,128)S(1)} %get-tuple-element.42.refs_1_.marks_ref, f32[2048,128]{1,0:T(8,128)S(1)} %get-tuple-element.34.refs_1_.refs_2_.table_ref), custom_call_target="tpu_custom_call" | custom-call | tf_op jit(solution)/shard_map/pallas_call | solution.py:427
  102.5 19.3 %all_to_all.46.stats_ref = f32[8,256,128]{2,1,0:T(8,128)S(1)} all-to-all(f32[8,256,128]{2,1,0:T(8,128)S(1)} %get-tuple-element.50), channel_id=1, replica_groups=mesh['y'=4,'z'=8,'x'=4,'core'=2] {'x','core'}, dimensions={0} | all-to-all | bytes 2097152 | tf_op jit(solution)/shard_map/all_to_all | solution.py:354
  121.8 1.7 %shard_map.148 = (f32[256,128]{1,0:T(8,128)}, f32[8,64,128]{2,1,0:T(8,128)S(1)}) custom-call(s32[3]{0:T(128)S(1)} %pad_add_fusion.spot_ref.refs_0_, f32[8,256,128]{2,1,0:T(8,128)S(1)} %all_to_all.46.stats_ref, f32[256,128]{1,0:T(8,128)S(1)} %copy-done.14, f32[256,128]{1,0:T(8,128)S(1)} %copy-done.2, f32[6,64,256]{2,1,0:T(8,128)S(1)} %get-tuple-element.47.refs_0_.held_ref, ...), custom_call_target="tpu_custom_call" | custom-call | tf_op jit(solution)/shard_map/pallas_call | solution.py:431
  123.5 9.9 %all_to_all.47.grad_ref = f32[8,64,128]{2,1,0:T(8,128)S(1)} all-to-all(f32[8,64,128]{2,1,0:T(8,128)S(1)} %get-tuple-element.52), channel_id=1, replica_groups=mesh['y'=4,'z'=8,'x'=4,'core'=2] {'x','core'}, dimensions={0} | all-to-all | bytes 524288 | tf_op jit(solution)/shard_map/all_to_all | solution.py:354
  133.5 9.2 %all_to_all.48.recv_ref = f32[4,128,128]{2,1,0:T(8,128)S(1)} all-to-all(f32[4,128,128]{2,1,0:T(8,128)S(1)} %shard_map.149), channel_id=1, replica_groups=mesh['y'=4,'z'=8,'x'=4,'core'=2] {'y'}, dimensions={0} | all-to-all | bytes 524288 | tf_op jit(solution)/shard_map/all_to_all | solution.py:354
  142.7 13.6 %all_to_all.49.recv_ref = f32[8,72,128]{2,1,0:T(8,128)S(1)} all-to-all(f32[8,72,128]{2,1,0:T(8,128)S(1)} %shard_map.150), channel_id=1, replica_groups=mesh['y'=4,'z'=8,'x'=4,'core'=2] {'z'}, dimensions={0} | all-to-all | bytes 589824 | tf_op jit(solution)/shard_map/all_to_all | solution.py:354
  156.3 0.6 shard_map.151
  (31 shorter events, 0.1 us)
Async XLA Ops:
  0.6 21.9 %copy-start.5 = (f32[2048,128]{1,0:T(8,128)S(1)}, f32[2048,128]{1,0:T(8,128)}, u32[]{:S(2)}) copy-start(f32[2048,128]{1,0:T(8,128)} %shape_ref.1) | copy-start | bytes 3145732
  6.1 24.0 %all-to-all-start = ((f32[32,16,128]{2,1,0:T(8,128)}), f32[32,16,128]{2,1,0:T(8,128)S(1)}, u32[]{:S(2)}, u32[]{:S(2)}) async-start(f32[32,16,128]{2,1,0:T(8,128)} %get-tuple-element.33.refs_3_), calls=%async_computation | async-start | bytes 524288 | tf_op jit(solution)/shard_map/all_to_all | solution.py:354
  17.7 1.0 copy-start.7
  18.7 1.0 copy-start.8
  19.7 0.8 copy-start.17
  20.5 18.7 %copy-start.18 = (f32[64,128]{1,0:T(8,128)S(1)}, f32[64,128]{1,0:T(8,128)}, u32[]{:S(2)}) copy-start(f32[64,128]{1,0:T(8,128)} %refs_3_.1) | copy-start | bytes 98308
  21.8 0.7 copy-start.11
  22.5 16.6 %collective-permute-start = (f32[5,64,256]{2,1,0:T(8,128)}, f32[5,64,256]{2,1,0:T(8,128)}, u32[]{:S(2)}, u32[]{:S(2)}) collective-permute-start(f32[5,64,256]{2,1,0:T(8,128)} %get-tuple-element.35.refs_2_), channel_id=1, source_target_pairs={{0,1},{1,0},{2,3},{3,2},{4,5},{5,4},{6,7},{7,6},{8,9},{9,8},{10,11... | collective-permute-start | bytes 983048 | tf_op jit(solution)/shard_map/ppermute | solution.py:403
  22.5 1.2 copy-start.6
  23.7 26.3 %copy-start.19 = (f32[128]{0:T(128)S(1)}, f32[128]{0:T(128)}, u32[]{:S(2)}) copy-start(f32[128]{0:T(128)} %param.17) | copy-start | bytes 1540
  23.7 26.3 %copy-start.20 = (f32[8,128]{1,0:T(8,128)S(1)}, f32[8,128]{1,0:T(8,128)}, u32[]{:S(2)}) copy-start(f32[8,128]{1,0:T(8,128)} %get-tuple-element.37.refs_1_) | copy-start | bytes 12292
  23.8 26.3 %copy-start.21 = (f32[8,128]{1,0:T(8,128)S(1)}, f32[8,128]{1,0:T(8,128)}, u32[]{:S(2)}) copy-start(f32[8,128]{1,0:T(8,128)} %get-tuple-element.38.refs_2_) | copy-start | bytes 12292
  25.4 0.7 copy-start.13
  26.0 0.7 copy-start.15
  32.8 17.3 %all-to-all-start.1 = ((f32[32,8,128]{2,1,0:T(8,128)}), f32[32,8,128]{2,1,0:T(8,128)S(1)}, u32[]{:S(2)}, u32[]{:S(2)}) async-start(f32[32,8,128]{2,1,0:T(8,128)} %bitcast.5), calls=%async_computation.1 | async-start | bytes 262144 | tf_op jit(solution)/shard_map/all_to_all | solution.py:354
  39.2 1.0 copy-start.12
  41.9 0.7 copy-start.9
  42.6 12.8 %collective-permute-start.1 = (f32[5,64,256]{2,1,0:T(8,128)}, f32[5,64,256]{2,1,0:T(8,128)}, u32[]{:S(2)}, u32[]{:S(2)}) collective-permute-start(f32[5,64,256]{2,1,0:T(8,128)} %get-tuple-element.40.refs_4_), channel_id=1, source_target_pairs={{0,2},{2,0},{4,6},{6,4},{1,3},{3,1},{5,7},{7,5},{8,10},{10,8},{12,... | collective-permute-start | bytes 983048 | tf_op jit(solution)/shard_map/ppermute | solution.py:420
  50.8 14.9 %all-to-all-start.2 = ((f32[32,8,128]{2,1,0:T(8,128)}), f32[32,8,128]{2,1,0:T(8,128)}, u32[]{:S(2)}, u32[]{:S(2)}) async-start(f32[32,8,128]{2,1,0:T(8,128)} %get-tuple-element.41.refs_3_), calls=%async_computation.2 | async-start | bytes 262144 | tf_op jit(solution)/shard_map/all_to_all | solution.py:354
  55.4 1.0 copy-start.10
  58.2 15.2 %collective-permute-start.2 = (f32[6,64,256]{2,1,0:T(8,128)}, f32[6,64,256]{2,1,0:T(8,128)}, u32[]{:S(2)}, u32[]{:S(2)}) collective-permute-start(f32[6,64,256]{2,1,0:T(8,128)} %get-tuple-element.44.refs_3_), channel_id=1, source_target_pairs={{0,4},{2,6},{4,0},{6,2},{1,5},{3,7},{5,1},{7,3},{8,12},{10,14},{12... | collective-permute-start | bytes 1179656 | tf_op jit(solution)/shard_map/ppermute | solution.py:408
  68.1 0.7 copy-start.3
  68.7 14.9 %all-to-all-start.3 = ((f32[32,8,128]{2,1,0:T(8,128)}), f32[32,8,128]{2,1,0:T(8,128)}, u32[]{:S(2)}, u32[]{:S(2)}) async-start(f32[32,8,128]{2,1,0:T(8,128)} %bitcast.11), calls=%async_computation.3 | async-start | bytes 262144 | tf_op jit(solution)/shard_map/all_to_all | solution.py:354
  73.3 0.9 copy-start.4
  74.3 0.9 copy-start.16
  76.9 0.6 copy-start
  83.7 0.9 copy-start.1
  99.4 22.4 %copy-start.2 = (f32[256,128]{1,0:T(8,128)S(1)}, f32[256,128]{1,0:T(8,128)}, u32[]{:S(2)}) copy-start(f32[256,128]{1,0:T(8,128)} %copy-done) | copy-start | bytes 393220
  99.4 22.4 %copy-start.14 = (f32[256,128]{1,0:T(8,128)S(1)}, f32[256,128]{1,0:T(8,128)}, u32[]{:S(2)}) copy-start(f32[256,128]{1,0:T(8,128)} %copy-done.13) | copy-start | bytes 393220

commit v6 on v5

--- a/solution.py
+++ b/solution.py
@@ -59,6 +59,15 @@
 
 def shape_of(*dims):
     return jax.ShapeDtypeStruct(dims, F32)
+
+
+def split(x):
+    high = x.astype(BF16)
+    return high, (x - high.astype(F32)).astype(BF16)
+
+
+def dot(left, right, dims):
+    return lax.dot_general(left, right, dims, preferred_element_type=F32)
 
 
 def prep_kernel(
@@ -105,22 +114,28 @@
     before = jnp.where(before, 1.0, 0.0).astype(BF16)
     owner_iota = lax.broadcasted_iota(jnp.int32, (owners, width), 0)
     rank_iota = lax.broadcasted_iota(jnp.int32, (capacity, width), 0).astype(F32)
-    carry = jnp.zeros((owners, 1), F32)
-    lists = jnp.zeros((4 * owners, capacity), F32)
-    for chunk in range(rows // 2):
-        user = 2 * chunk // blocks
+    chunks = rows // 2
+    ids_of, marks_of = [], []
+    for chunk in range(chunks):
         ids = jnp.concatenate(
             [ids_ref[2 * chunk : 2 * chunk + 1, :], ids_ref[2 * chunk + 1 : 2 * chunk + 2, :]], axis=1
         )
+        ids_of.append(ids)
+        marks_of.append(jnp.where(owner_iota == (ids >> 11), 1.0, 0.0))
+    earlier_of = dot(jnp.concatenate([marks.astype(BF16) for marks in marks_of], axis=0), before, NN)
+    carry = jnp.zeros((owners, 1), F32)
+    lists = jnp.zeros((4 * owners, capacity), F32)
+    for chunk in range(chunks):
+        user = 2 * chunk // blocks
+        ids, marks = ids_of[chunk], marks_of[chunk]
         weights = []
         for row in (2 * chunk, 2 * chunk + 1):
             live = jnp.where(row % blocks < counts_ref[user], 1.0, 0.0)
             weights.append(clicks_ref[row : row + 1, :].astype(F32) * live)
         weight = jnp.concatenate(weights, axis=1)
-        marks = jnp.where(owner_iota == (ids >> 11), 1.0, 0.0)
-        earlier = lax.dot_general(marks.astype(BF16), before, NN, preferred_element_type=F32)
+        earlier = earlier_of[chunk * owners : (chunk + 1) * owners]
         rank = jnp.sum(marks * (earlier + carry), axis=0, keepdims=True)
-        carry = carry + jnp.sum(marks, axis=1, keepdims=True)
+        carry = carry + (earlier[:, width - 1 :] + marks[:, width - 1 :])
         place = jnp.where(rank_iota == rank, 1.0, 0.0).astype(BF16)
         high = ((ids >> 7) & 15).astype(F32)
         low = (ids & 127).astype(F32)
@@ -143,45 +158,39 @@
         send_ref[owner, 8:16, :] = theta
 
 
-def table_kernel(spot_ref, shape_ref, rate_ref, table_ref, shape_here_ref, rate_here_ref):
+def table_kernel(shape_ref, rate_ref, table_ref):
     table_ref[...] = exp_digamma_over(shape_ref[...], rate_ref[...])
-    share = shape_here_ref.shape[0]
-    here = pl.ds(pl.multiple_of(spot_ref[2] * share, share), share)
-    shape_here_ref[...] = shape_ref[here, :]
-    rate_here_ref[...] = rate_ref[here, :]
-
-
-def split(x):
-    high = x.astype(BF16)
-    return high, (x - high.astype(F32)).astype(BF16)
-
-
-def dot(left, right, dims):
-    return lax.dot_general(left, right, dims, preferred_element_type=F32)
-
-
-def ascend(theta, marks_ref, table_ref, stats_ref=None):
-    factors = theta.shape[1]
+
+
+def widen(table):
+    table_high, table_low = split(table)
+    twice = jnp.concatenate([table_high, table_high], axis=1)
+    return table_high, table_low, twice, jnp.concatenate([table_high, table_low], axis=1)
+
+
+def ascend_block(theta_high, theta_both, marks, table):
+    factors = table.shape[1]
+    table_high, table_low, twice, both = widen(table)
+    share = dot(theta_both, twice, NT) + dot(theta_high, table_low, NT)
+    ratio_high, ratio_low = split(marks / share)
+    wide = dot(ratio_high, both, NN)
+    part = wide[:, :factors] + wide[:, factors:] + dot(ratio_low, table_high, NN)
+    return ratio_high, ratio_low, part
+
+
+def split_theta(theta):
     theta_high, theta_low = split(theta)
-    theta_both = jnp.concatenate([theta_high, theta_low], axis=1)
+    return theta_high, jnp.concatenate([theta_high, theta_low], axis=1)
+
+
+def ascend(theta, marks_ref, table_ref):
+    theta_high, theta_both = split_theta(theta)
     total = jnp.zeros(theta.shape, F32)
     width = 2 * LANES
     for pair in range(marks_ref.shape[0] // 2):
-        rows = slice(pair * width, (pair + 1) * width)
-        table = table_ref[rows, :]
-        table_high, table_low = split(table)
-        share = dot(theta_both, jnp.concatenate([table_high, table_high], axis=1), NT) + dot(
-            theta_high, table_low, NT
-        )
         marks = jnp.concatenate([marks_ref[2 * pair], marks_ref[2 * pair + 1]], axis=1)
-        ratio = marks / share
-        ratio_high, ratio_low = split(ratio)
-        wide = dot(ratio_high, jnp.concatenate([table_high, table_low], axis=1), NN)
-        total = total + (wide[:, :factors] + wide[:, factors:]) + dot(ratio_low, table_high, NN)
-        if stats_ref is not None:
-            wide = dot(ratio_high, theta_both, TN)
-            spread = wide[:, :factors] + wide[:, factors:] + dot(ratio_low, theta_high, TN)
-            stats_ref[pair, :width, :] = table * spread
+        table = table_ref[pair * width : (pair + 1) * width, :]
+        total = total + ascend_block(theta_high, theta_both, marks, table)[2]
     return total
 
 
@@ -209,63 +218,88 @@
     partial_ref[...] = ascend(theta, marks_ref, table_ref)
 
 
-def ascend_kernel(theta_ref, marks_ref, table_ref, partial_ref):
-    partial_ref[...] = ascend(theta_ref[...], marks_ref, table_ref)
-
-
-def last_kernel(theta_ref, marks_ref, table_ref, partial_ref, stats_ref):
-    partial_ref[...] = ascend(theta_ref[...], marks_ref, table_ref, stats_ref)
-
-
-def core_kernel(spot_ref, cov_ref, weight_ref, send_ref, keep_ref):
-    pairs, _, width = keep_ref.shape
-    core = spot_ref[2] & 1
-    for pair in range(pairs):
-        other = pl.multiple_of((2 * pair + 1 - core) * width, width)
-        own = pl.multiple_of((2 * pair + core) * width, width)
-        send_ref[pair] = cov_ref[:, pl.ds(other, width)]
-        keep_ref[pair] = cov_ref[:, pl.ds(own, width)]
-    send_ref[pairs, :, :LANES] = weight_ref[...]
-    send_ref[pairs, :, LANES:] = weight_ref[...]
-
-
-def near_kernel(spot_ref, recv_ref, held_ref, weight_ref, send_ref, keep_ref):
-    low = (spot_ref[2] >> 1) & 1
-    for high in range(2):
-        other = 2 * high + 1 - low
-        own = 2 * high + low
-        send_ref[2 * high] = held_ref[other]
-        send_ref[2 * high + 1] = recv_ref[other]
-        keep_ref[2 * high] = held_ref[own]
-        keep_ref[2 * high + 1] = recv_ref[own]
-    for target in (send_ref, keep_ref):
-        target[4, :, :LANES] = weight_ref[...]
-        target[4, :, LANES:] = recv_ref[4, :, :LANES]
-
-
-def far_kernel(spot_ref, recv_ref, held_ref, send_ref, keep_ref):
-    high = spot_ref[2] >> 2
-    for core in range(2):
-        other = 2 * (1 - high) + core
-        own = 2 * high + core
-        send_ref[core] = held_ref[other]
-        send_ref[2 + core] = recv_ref[other]
-        keep_ref[core] = held_ref[own]
-        keep_ref[2 + core] = recv_ref[own]
-    for target in (send_ref, keep_ref):
-        target[4] = held_ref[4]
-        target[5] = recv_ref[4]
-
-
-def scale_kernel(held_ref, recv_ref, rate_ref, scale_ref):
-    total = jnp.zeros(rate_ref.shape, F32)
-    for source in (held_ref, recv_ref):
-        cov = jnp.concatenate([source[place] for place in range(4)], axis=0)
-        weight = jnp.concatenate(
-            [source[4 + place // 2, :, (place % 2) * LANES : (place % 2 + 1) * LANES] for place in range(4)], axis=0
+def ascend_kernel(theta_ref, marks_ref, table_ref, partial_ref, token_ref):
+    total = ascend(theta_ref[...], marks_ref, table_ref)
+    partial_ref[...] = total
+    token_ref[...] = total[: token_ref.shape[0]]
+
+
+def pack_kernel(cov_ref, weight_ref, own_ref):
+    items = cov_ref.shape[1]
+    own_ref[:, :items] = cov_ref[...]
+    own_ref[:, items:] = weight_ref[...]
+
+
+def prior_kernel(shards, *refs):
+    shard_refs, refs = refs[:shards], refs[shards:]
+    sum_ref, token_ref = refs[-2:]
+    items = sum_ref.shape[1]
+    width = 2 * LANES
+    weight = jnp.concatenate([shard[:, items:] for shard in shard_refs], axis=0)
+    for start in range(0, items, width):
+        cov = jnp.concatenate([shard[:, start : start + width] for shard in shard_refs], axis=0)
+        part = lax.dot_general(weight, cov, TN, precision=HIGHEST, preferred_element_type=F32)
+        if len(refs) > 2:
+            part = part + refs[0][:, start : start + width]
+        sum_ref[:, start : start + width] = part
+    token_ref[...] = weight[: token_ref.shape[0]]
+
+
+def scale_kernel(shard_ref, sum_ref, rate_ref, scale_ref):
+    items = scale_ref.shape[0]
+    width = 2 * LANES
+    weight = shard_ref[:, items:]
+    for start in range(0, items, width):
+        part = lax.dot_general(
+            weight, shard_ref[:, start : start + width], TN, precision=HIGHEST, preferred_element_type=F32
         )
-        total = total + lax.dot_general(cov, weight, TN, precision=HIGHEST, preferred_element_type=F32)
-    scale_ref[...] = jnp.exp(total) / rate_ref[...]
+        prior_log = (part + sum_ref[:, start : start + width]).T
+        scale_ref[start : start + width, :] = jnp.exp(prior_log) / rate_ref[start : start + width, :]
+
+
+def last_kernel(shards, spot_ref, theta_ref, marks_ref, table_ref, scale_ref, shape_ref, *refs):
+    shard_refs = refs[:shards]
+    partial_ref, base_ref, keep_ref, send_ref, grad_ref = refs[shards:]
+    spot = spot_ref[2]
+    theta = theta_ref[...]
+    factors = theta.shape[1]
+    theta_high, theta_both = split_theta(theta)
+    total = jnp.zeros(theta.shape, F32)
+    rows = grad_ref.shape[1]
+    grad = jnp.zeros((shards * rows, factors), F32)
+    width = 2 * LANES
+    for place in range(shards):
+        block = spot ^ place
+        here = pl.ds(pl.multiple_of(block * width, width), width)
+        table = table_ref[here, :]
+        marks = jnp.concatenate([marks_ref[2 * block], marks_ref[2 * block + 1]], axis=1)
+        ratio_high, ratio_low, part = ascend_block(theta_high, theta_both, marks, table)
+        total = total + part
+        wide = dot(ratio_high, theta_both, TN)
+        stats = table * (wide[:, :factors] + wide[:, factors:] + dot(ratio_low, theta_high, TN))
+        target = send_ref if place % 2 else keep_ref
+        target[place // 2] = stats
+        base = (1.0 - step_weight) * shape_ref[here, :] + step_weight * item_prior
+        if place == 0:
+            base_ref[...] = base
+        score = item_prior / shards - scale_ref[here, :] * (base / shards + step_weight * USER_RATIO * stats)
+        score_high, score_low = split(score)
+        cov_high, cov_low = split(jnp.concatenate([shard[:, here] for shard in shard_refs], axis=0))
+        wide = dot(cov_high, jnp.concatenate([score_high, score_low], axis=1), NN)
+        grad = grad + (wide[:, :factors] + wide[:, factors:] + dot(cov_low, score_high, NN))
+    partial_ref[...] = total
+    for place in range(shards):
+        grad_ref[spot ^ place] = grad[place * rows : (place + 1) * rows]
+
+
+def halve_kernel(held_ref, recv_ref, keep_ref, send_ref):
+    for place in range(held_ref.shape[0]):
+        target = send_ref if place % 2 else keep_ref
+        target[place // 2] = held_ref[place] + recv_ref[place]
+
+
+def close_kernel(held_ref, recv_ref, base_ref, new_ref):
+    new_ref[...] = base_ref[...] + step_weight * USER_RATIO * (held_ref[0] + recv_ref[0])
 
 
 def update_kernel(activity_shape, recv_ref, theta_ref, activity_ref, totals_ref, active_ref, next_ref, send_ref):
@@ -277,19 +311,6 @@
     theta = exp_digamma_over(shapes, rates)
     next_ref[...] = theta
     send_ref[...] = jnp.broadcast_to(theta[None], send_ref.shape)
-
-
-def score_kernel(spot_ref, stats_ref, shape_ref, scale_ref, held_ref, recv_ref, new_ref, grad_ref):
-    stats = jnp.sum(stats_ref[...], axis=0)
-    new_shape = (1.0 - step_weight) * shape_ref[...] + step_weight * (item_prior + USER_RATIO * stats)
-    new_ref[...] = new_shape
-    score = item_prior - scale_ref[...] * new_shape
-    rows = grad_ref.shape[1]
-    for part, source in enumerate((held_ref, recv_ref)):
-        cov = jnp.concatenate([source[place] for place in range(4)], axis=0)
-        grad = lax.dot_general(cov, score, NN, precision=HIGHEST, preferred_element_type=F32)
-        for place in range(4):
-            grad_ref[spot_ref[2] ^ (4 * part + place)] = grad[place * rows : (place + 1) * rows]
 
 
 def join_kernel(grad_ref, partial_ref, send_ref):
@@ -381,63 +402,87 @@
         user_rate0,
     )
     recv = exchange(send, user_axes)
-    table, shape_here, rate_here = kernel_call(
-        table_kernel, (shape_of(item_rows, factors), share, share), in_specs=[smem, vmem, vmem]
-    )(spot, item_shape, item_rate)
-
-    swap_core = [(place, place ^ 1) for place in range(lax.axis_size("core"))]
-    swap_near = [(place, place ^ 1) for place in range(lax.axis_size("x"))]
-    swap_far = [(place, place ^ 2) for place in range(lax.axis_size("x"))]
-    block = (cov_rows, share_rows)
-    moved, held = kernel_call(
-        behind(core_kernel, 3), (shape_of(5, *block), shape_of(4, *block)), in_specs=[smem, vmem, vmem, hbm]
-    )(spot, covariates, cov_weight, send)
+    table = kernel_call(table_kernel, shape_of(item_rows, factors))(item_shape, item_rate)
+
+    def swap(array, distance):
+        axis, bit = ("core", 1) if distance == 1 else ("x", distance // 2)
+        return lax.ppermute(array, axis, [(place, place ^ bit) for place in range(lax.axis_size(axis))])
+
+    shards = [None] * split_count
+    own = kernel_call(
+        behind(pack_kernel, 2), shape_of(cov_rows, item_rows + factors), in_specs=[vmem, vmem, hbm]
+    )(covariates, cov_weight, theta)
+    shards[0] = own
+    for distance in (1, 2, 6, 4):
+        shards[distance] = swap(own, distance)
+    for distance in (2, 6, 4):
+        shards[distance + 1] = swap(shards[distance], 1)
+
+    def add_prior(places, total, awaited):
+        inputs = [shards[place] for place in places] + ([] if total is None else [total])
+        return kernel_call(
+            behind(functools.partial(prior_kernel, len(places)), len(inputs)),
+            (shape_of(factors, item_rows), small),
+            in_specs=[vmem] * len(inputs) + [hbm],
+        )(*inputs, awaited)
+
     marks, partial = kernel_call(
         behind(build_kernel, 2),
         (shape_of(highs, everyone, LANES), shape_of(everyone, factors)),
         in_specs=[vmem, vmem, hbm],
-    )(recv, table, moved)
+    )(recv, table, own)
+    prior, token = add_prior((0, 1), None, partial)
     for iteration in range(ITERS - 1):
-        first = iteration == 0
-        if first:
-            moved = lax.ppermute(moved, "core", swap_core)
-            moved, held = kernel_call(
-                behind(near_kernel, 4), (shape_of(5, *block), shape_of(5, *block)), in_specs=[smem, vmem, vmem, vmem, hbm]
-            )(spot, moved, held, cov_weight, partial)
-        else:
-            moved = lax.ppermute(moved, "x", swap_far)
-            scale = kernel_call(behind(scale_kernel, 3), share, in_specs=[vmem, vmem, vmem, hbm])(
-                held, moved, rate_here, partial
-            )
         parts = exchange(partial.reshape(owners, users_here, factors), user_axes)
         active, theta, spread = kernel_call(
             behind(functools.partial(update_kernel, activity_shape), 4),
             (small, small, shape_of(owners, users_here, factors)),
             in_specs=[vmem] * 4 + [hbm],
-        )(parts, theta, active, totals, moved if first else scale)
+        )(parts, theta, active, totals, token)
         theta_all = exchange(spread, user_axes).reshape(everyone, factors)
-        if first:
-            moved = lax.ppermute(moved, "x", swap_near)
-            moved, held = kernel_call(
-                behind(far_kernel, 3), (shape_of(6, *block), shape_of(6, *block)), in_specs=[smem, vmem, vmem, hbm]
-            )(spot, moved, held, spread)
-            partial = kernel_call(
-                behind(ascend_kernel, 3), shape_of(everyone, factors), in_specs=[vmem, vmem, vmem, hbm]
-            )(theta_all, marks, table, moved)
-    partial, stats = kernel_call(
-        last_kernel, (shape_of(everyone, factors), shape_of(split_count, share_rows, factors))
-    )(theta_all, marks, table)
-    stats = exchange(stats, item_axes)
-    new_shape, grad = kernel_call(
-        score_kernel, (share, shape_of(split_count, cov_rows, factors)), in_specs=[smem] + [vmem] * 5
-    )(spot, stats, shape_here, scale, held, moved)
+        if iteration == 0:
+            prior, token = add_prior((2, 6), prior, spread)
+            partial, token = kernel_call(
+                behind(ascend_kernel, 3),
+                (shape_of(everyone, factors), small),
+                in_specs=[vmem, vmem, vmem, hbm],
+            )(theta_all, marks, table, token)
+            prior, token = add_prior((3, 7, 4), prior, token)
+        else:
+            scale = kernel_call(
+                behind(scale_kernel, 3), shape_of(item_rows, factors), in_specs=[vmem, vmem, vmem, hbm]
+            )(shards[5], prior, item_rate, spread)
+    half = split_count // 2
+    partial, base, held, moved, grad = kernel_call(
+        functools.partial(last_kernel, split_count),
+        (
+            shape_of(everyone, factors),
+            share,
+            shape_of(half, share_rows, factors),
+            shape_of(half, share_rows, factors),
+            shape_of(split_count, cov_rows, factors),
+        ),
+        in_specs=[smem] + [vmem] * (5 + split_count),
+    )(spot, theta_all, marks, table, scale, item_shape, *shards)
+
+    def halve(held, moved, distance):
+        half = held.shape[0] // 2
+        return kernel_call(halve_kernel, (shape_of(half, share_rows, factors),) * 2)(held, swap(moved, distance))
+
     grad = exchange(grad, item_axes)
-    both = kernel_call(join_kernel, shape_of(y_size, z_size * users_here + cov_rows, factors))(grad, partial)
+    held, moved = halve(held, moved, 1)
+    both = kernel_call(
+        behind(join_kernel, 2), shape_of(y_size, z_size * users_here + cov_rows, factors), in_specs=[vmem, vmem, hbm]
+    )(grad, partial, moved)
     both = exchange(both, ("y",))
+    held, moved = halve(held, moved, 2)
     both = kernel_call(
-        functools.partial(fan_kernel, users_here), shape_of(z_size, users_here + cov_rows, factors)
-    )(both)
+        behind(functools.partial(fan_kernel, users_here), 1),
+        shape_of(z_size, users_here + cov_rows, factors),
+        in_specs=[vmem, hbm],
+    )(both, moved)
     both = exchange(both, ("z",))
+    new_shape = kernel_call(close_kernel, share)(held, swap(moved, 4), base)
     user_shape, user_rate, active, cov_grad = kernel_call(
         functools.partial(finish_kernel, activity_shape, math.sqrt(item_rows * owners)),
         (small, small, shape_of(1, users_here), shape_of(cov_rows, factors)),

time: 158 us -> 147 us (0.930)
  blocking collectives: 65.8 us -> 0 us
  waiting for transfers between devices: 21.9 us -> 50.9 us
  starting transfers between devices: 29.7 us -> 47.8 us
  Pallas kernels: 26 us -> 31.7 us
    all_to_all x5 -> x0, blocking collectives: 65.8 us -> none  [exchange(): return lax.all_to_all(array, axes, split_axis=0, concat_axis=0, tiled=True)]
    all_to_all x4 -> x8, waiting for transfers between devices: 21.9 us -> 45.9 us  [exchange(): return lax.all_to_all(array, axes, split_axis=0, concat_axis=0, tiled=True)]
    all_to_all x4 -> x8, starting transfers between devices: 27 us -> 41.7 us  [exchange(): return lax.all_to_all(array, axes, split_axis=0, concat_axis=0, tiled=True)]
    pallas_call x10 -> x13, Pallas kernels: 15.5 us -> 23.6 us  [the longest x1 9.53 us: shards(): kernel_call(functools.partial(last_kernel, split_count), (shape_of(everyo...]
    ppermute x3 -> x10, waiting for transfers between devices: 0.01 us -> 5.04 us  [swap(): lax.ppermute(array, axis, [(place, place ^ bit) for place in range(lax.ax...]
    ppermute x3 -> x10, starting transfers between devices: 2.66 us -> 6.1 us  [swap(): lax.ppermute(array, axis, [(place, place ^ bit) for place in range(lax.ax...]
    pallas_call x1, Pallas kernels: 5.49 us -> 3.42 us  [shards(): kernel_call(functools.partial(prep_kernel, owners), (shape_of(owners, 16,...]
    unnamed x44 -> x38, local copies, waits for them, and re-layouts: 12.7 us -> 14.2 us
  transfers between devices with their start and end apart: 7 -> 18, of which waited for: 4 -> 9; matrix products, arithmetic and copies ran while one was open for 0% -> 0% of each run, Pallas kernels for 9% -> 12%
where the time goes in v6:
time: 147 us; the launch traced here: 146 us
  waiting for transfers between devices  50.9 us (35%)
  starting transfers between devices  47.8 us (33%)
  Pallas kernels  31.7 us (22%)
  local copies, waits for them, and re-layouts  14.2 us (10%)
    all_to_all x8, waiting for transfers between devices, exchange(): return lax.all_to_all(array, axes, split_axis=0, concat_axis=0, tiled=True)  45.9 us
    all_to_all x8, starting transfers between devices, exchange(): return lax.all_to_all(array, axes, split_axis=0, concat_axis=0, tiled=True)  41.7 us
    unnamed x38, local copies, waits for them, and re-layouts  14.2 us
    pallas_call x1, Pallas kernels, shards(): kernel_call(functools.partial(last_kernel, split_count), (shape_of(everyo...  9.53 us
    pallas_call x3, Pallas kernels, add_prior(): kernel_call(behind(functools.partial(prior_kernel, len(places)), len(inpu...  6.41 us
    ppermute x10, starting transfers between devices, swap(): lax.ppermute(array, axis, [(place, place ^ bit) for place in range(lax.ax...  6.1 us
    ppermute x10, waiting for transfers between devices, swap(): lax.ppermute(array, axis, [(place, place ^ bit) for place in range(lax.ax...  5.04 us
    pallas_call x1, Pallas kernels, shards(): kernel_call(functools.partial(prep_kernel, owners), (shape_of(owners, 16,...  3.42 us
  transfers between devices with their start and end apart: 18, of which 9 were waited for; matrix products, arithmetic and copies ran while one was open for 0% of the time, Pallas kernels for 12%

profile of v6, /device:TPU:2, one launch (start us, length us, event | category | flops | bytes accessed | tf_op | source)
XLA Modules:
  0.0 145.7 jit_solution(5411258567661636139)
XLA Ops:
  0.6 3.4 %shard_map.137 = (f32[32,16,128]{2,1,0:T(8,128)}, f32[8,128]{1,0:T(8,128)}, f32[8,128]{1,0:T(8,128)}) custom-call(s32[8]{0:T(128)} %counts_hbm.1, s32[64,128]{1,0:T(8,128)} %bitcast.16, s32[64,128]{1,0:T(8,128)} %bitcast.17, f32[8,128]{1,0:T(8,128)} %shape_hbm.1, f32[8,128]{1,0:T(8,128)} %rate_hbm.1), custom_call_target="tpu_custom_call" | custom-call | tf_op jit(solution)/shard_map/pallas_call | solution.py:384
  4.1 11.5 %all-to-all-start = ((f32[32,16,128]{2,1,0:T(8,128)}), f32[32,16,128]{2,1,0:T(8,128)S(1)}, u32[]{:S(2)}, u32[]{:S(2)}) async-start(f32[32,16,128]{2,1,0:T(8,128)} %get-tuple-element.37), calls=%async_computation | async-start | bytes 524288 | tf_op jit(solution)/shard_map/all_to_all | solution.py:375
  15.6 1.0 copy-done.13
  16.6 0.8 copy-done.14
  17.4 0.7 copy-done.15
  18.1 1.6 %collective-permute-start.2 = (f32[64,2176]{1,0:T(8,128)S(1)}, f32[64,2176]{1,0:T(8,128)S(1)}, u32[]{:S(2)}, u32[]{:S(2)}) collective-permute-start(f32[64,2176]{1,0:T(8,128)S(1)} %shard_map.139.refs_2_.refs_0_), channel_id=1, source_target_pairs={{0,6},{2,4},{4,2},{6,0},{1,7},{3,5},{5,3},{7,1},{8,14},{10,12},{12... | collective-permute-start | bytes 1671176 | tf_op jit(solution)/shard_map/ppermute | solution.py:409
  19.7 1.8 %collective-permute-start.1 = (f32[64,2176]{1,0:T(8,128)S(1)}, f32[64,2176]{1,0:T(8,128)}, u32[]{:S(2)}, u32[]{:S(2)}) collective-permute-start(f32[64,2176]{1,0:T(8,128)S(1)} %shard_map.139.refs_2_.refs_0_), channel_id=1, source_target_pairs={{0,2},{2,0},{4,6},{6,4},{1,3},{3,1},{5,7},{7,5},{8,10},{10,8},{12,... | collective-permute-start | bytes 1671176 | tf_op jit(solution)/shard_map/ppermute | solution.py:409
  21.7 1.2 copy-done.4
  22.9 1.1 shard_map.138.refs_1_.refs_2_.table_ref
  24.1 4.0 %all-to-all-done.refs_0_ = f32[32,16,128]{2,1,0:T(8,128)S(1)} async-done(((f32[32,16,128]{2,1,0:T(8,128)}), f32[32,16,128]{2,1,0:T(8,128)S(1)}, u32[]{:S(2)}, u32[]{:S(2)}) %all-to-all-start) | async-done | bytes 262176 | tf_op jit(solution)/shard_map/all_to_all | solution.py:375
  28.0 2.7 %shard_map.140 = (f32[16,256,128]{2,1,0:T(8,128)S(1)}, f32[256,128]{1,0:T(8,128)}) custom-call(f32[32,16,128]{2,1,0:T(8,128)S(1)} %all-to-all-done.refs_0_, f32[2048,128]{1,0:T(8,128)S(1)} %shard_map.138.refs_1_.refs_2_.table_ref, f32[64,2176]{1,0:T(8,128)S(1)} %shard_map.139.refs_2_.refs_0_), custom_call_target="tpu_custom_call" | custom-call | tf_op jit(solution)/shard_map/pallas_call | solution.py:429
  30.7 1.3 copy-done.1
  32.0 5.8 %all-to-all-start.1 = ((f32[32,8,128]{2,1,0:T(8,128)}), f32[32,8,128]{2,1,0:T(8,128)S(1)}, u32[]{:S(2)}, u32[]{:S(2)}) async-start(f32[32,8,128]{2,1,0:T(8,128)} %bitcast.5), calls=%async_computation.1 | async-start | bytes 262144 | tf_op jit(solution)/shard_map/all_to_all | solution.py:375
  38.5 2.1 %shard_map.141 = (f32[128,2048]{1,0:T(8,128)S(1)}, f32[8,128]{1,0:T(8,128)S(1)}) custom-call(f32[64,2176]{1,0:T(8,128)S(1)} %shard_map.139.refs_2_.refs_0_, f32[64,2176]{1,0:T(8,128)} %collective-permute-done.refs_1_, f32[256,128]{1,0:T(8,128)} %get-tuple-element.39.refs_2_), custom_call_target="tpu_custom_call" | custom-call | tf_op jit(solution)/shard_map/pallas_call | solution.py:423
  40.6 1.0 copy-done.7
  41.5 7.1 %all-to-all-done.1.refs_0_ = f32[32,8,128]{2,1,0:T(8,128)S(1)} async-done(((f32[32,8,128]{2,1,0:T(8,128)}), f32[32,8,128]{2,1,0:T(8,128)S(1)}, u32[]{:S(2)}, u32[]{:S(2)}) %all-to-all-start.1) | async-done | bytes 131104 | tf_op jit(solution)/shard_map/all_to_all | solution.py:375
  48.7 0.7 shard_map.142
  49.4 3.9 %all-to-all-start.2 = ((f32[32,8,128]{2,1,0:T(8,128)}), f32[32,8,128]{2,1,0:T(8,128)S(1)}, u32[]{:S(2)}, u32[]{:S(2)}) async-start(f32[32,8,128]{2,1,0:T(8,128)} %get-tuple-element.42.refs_3_), calls=%async_computation.2 | async-start | bytes 262144 | tf_op jit(solution)/shard_map/all_to_all | solution.py:375
  53.6 1.2 copy-done.8
  54.8 2.1 %shard_map.143 = (f32[128,2048]{1,0:T(8,128)S(1)}, f32[8,128]{1,0:T(8,128)S(1)}) custom-call(f32[64,2176]{1,0:T(8,128)} %collective-permute-done.1.refs_0_.refs_2_, f32[64,2176]{1,0:T(8,128)S(1)} %collective-permute-done.2.refs_1_.refs_6_, f32[128,2048]{1,0:T(8,128)S(1)} %copy-done.8, f32[32,8,128]{2,1,0:T(8,128)} %get-tuple-element.42.refs_3_), custom_call_target="tpu_custom_call" | custom-call | tf_op jit(solution)/shard_map/pallas_call | solution.py:423
  56.9 1.0 copy-done.9
  57.8 5.9 %all-to-all-done.2 = f32[32,8,128]{2,1,0:T(8,128)S(1)} async-done(((f32[32,8,128]{2,1,0:T(8,128)}), f32[32,8,128]{2,1,0:T(8,128)S(1)}, u32[]{:S(2)}, u32[]{:S(2)}) %all-to-all-start.2) | async-done | bytes 131104 | tf_op jit(solution)/shard_map/all_to_all | solution.py:375
  63.7 1.6 %copy-done.2 = f32[16,256,128]{2,1,0:T(8,128)S(1)} copy-done((f32[16,256,128]{2,1,0:T(8,128)S(1)}, f32[16,256,128]{2,1,0:T(8,128)}, u32[]{:S(2)}) %copy-start.2) | copy-done | bytes 2097176
  65.3 2.1 %shard_map.144 = (f32[256,128]{1,0:T(8,128)}, f32[8,128]{1,0:T(8,128)S(1)}) custom-call(f32[256,128]{1,0:T(8,128)S(1)} %bitcast.12, f32[16,256,128]{2,1,0:T(8,128)S(1)} %copy-done.2, f32[2048,128]{1,0:T(8,128)S(1)} %shard_map.138.refs_1_.refs_2_.table_ref, f32[8,128]{1,0:T(8,128)S(1)} %get-tuple-element.45.refs_3_), custom_call_target="tpu_custom_call" | custom-call | tf_op jit(solution)/shard_map/pallas_call | solution.py:445
  67.4 4.1 %all-to-all-start.3 = ((f32[32,8,128]{2,1,0:T(8,128)}), f32[32,8,128]{2,1,0:T(8,128)S(1)}, u32[]{:S(2)}, u32[]{:S(2)}) async-start(f32[32,8,128]{2,1,0:T(8,128)} %bitcast.8), calls=%async_computation.3 | async-start | bytes 262144 | tf_op jit(solution)/shard_map/all_to_all | solution.py:375
  71.5 1.2 copy-done.10
  72.7 2.3 %shard_map.145 = (f32[128,2048]{1,0:T(8,128)S(1)}, f32[8,128]{1,0:T(8,128)S(1)}) custom-call(f32[64,2176]{1,0:T(8,128)} %collective-permute-done.3.refs_0_.refs_3_, f32[64,2176]{1,0:T(8,128)S(1)} %collective-permute-done.4.refs_1_.refs_7_, f32[64,2176]{1,0:T(8,128)} %collective-permute-done.5.refs_2_.refs_4_, f32[128,2048]{1,0:T(8,128)S(1)} %copy-done.10, ...), custom_call_target="tpu_custom_call" | custom-call | tf_op jit(solution)/shard_map/pallas_call | solution.py:423
  75.0 1.0 copy-done.11
  76.0 6.4 %all-to-all-done.3.refs_0_ = f32[32,8,128]{2,1,0:T(8,128)S(1)} async-done(((f32[32,8,128]{2,1,0:T(8,128)}), f32[32,8,128]{2,1,0:T(8,128)S(1)}, u32[]{:S(2)}, u32[]{:S(2)}) %all-to-all-start.3) | async-done | bytes 131104 | tf_op jit(solution)/shard_map/all_to_all | solution.py:375
  82.4 0.7 shard_map.146
  83.1 3.9 %all-to-all-start.4 = ((f32[32,8,128]{2,1,0:T(8,128)}), f32[32,8,128]{2,1,0:T(8,128)S(1)}, u32[]{:S(2)}, u32[]{:S(2)}) async-start(f32[32,8,128]{2,1,0:T(8,128)} %get-tuple-element.52.refs_3_), calls=%async_computation.4 | async-start | bytes 262144 | tf_op jit(solution)/shard_map/all_to_all | solution.py:375
  87.1 1.2 copy-done.12
  88.3 2.2 %shard_map.147.scale_ref = f32[2048,128]{1,0:T(8,128)S(1)} custom-call(f32[64,2176]{1,0:T(8,128)} %collective-permute-done.6.refs_0_.refs_5_, f32[128,2048]{1,0:T(8,128)S(1)} %copy-done.12, f32[2048,128]{1,0:T(8,128)S(1)} %copy-done.5, f32[32,8,128]{2,1,0:T(8,128)} %get-tuple-element.52.refs_3_), custom_call_target="tpu_custom_call" | custom-call | tf_op jit(solution)/shard_map/pallas_call | solution.py:452
  90.5 1.0 copy-done.6
  91.5 5.9 %all-to-all-done.4 = f32[32,8,128]{2,1,0:T(8,128)S(1)} async-done(((f32[32,8,128]{2,1,0:T(8,128)}), f32[32,8,128]{2,1,0:T(8,128)S(1)}, u32[]{:S(2)}, u32[]{:S(2)}) %all-to-all-start.4) | async-done | bytes 131104 | tf_op jit(solution)/shard_map/all_to_all | solution.py:375
  97.3 9.5 %shard_map.148 = (f32[256,128]{1,0:T(8,128)S(1)}, f32[256,128]{1,0:T(8,128)S(1)}, f32[4,256,128]{2,1,0:T(8,128)S(1)}, f32[4,256,128]{2,1,0:T(8,128)}, f32[8,64,128]{2,1,0:T(8,128)}) custom-call(s32[3]{0:T(128)S(1)} %pad_add_fusion.spot_ref, f32[256,128]{1,0:T(8,128)S(1)} %bitcast.11, f32[16,256,128]{2,1,0:T(8,128)} %copy-done.1, f32[2048,128]{1,0:T(8,128)} %copy-done, ...), custom_call_target="tpu_custom_call" | custom-call | tf_op jit(solution)/shard_map/pallas_call | solution.py:456
  106.9 5.8 %all-to-all-start.5 = ((f32[8,64,128]{2,1,0:T(8,128)}), f32[8,64,128]{2,1,0:T(8,128)S(1)}, u32[]{:S(2)}, u32[]{:S(2)}) async-start(f32[8,64,128]{2,1,0:T(8,128)} %get-tuple-element.54), calls=%async_computation.5 | async-start | bytes 524288 | tf_op jit(solution)/shard_map/all_to_all | solution.py:375
  112.8 6.4 %all-to-all-done.5.refs_0_ = f32[8,64,128]{2,1,0:T(8,128)S(1)} async-done(((f32[8,64,128]{2,1,0:T(8,128)}), f32[8,64,128]{2,1,0:T(8,128)S(1)}, u32[]{:S(2)}, u32[]{:S(2)}) %all-to-all-start.5) | async-done | bytes 262176 | tf_op jit(solution)/shard_map/all_to_all | solution.py:375
  119.2 0.7 shard_map.150
  120.0 3.4 %all-to-all-start.6 = ((f32[4,128,128]{2,1,0:T(8,128)}), f32[4,128,128]{2,1,0:T(8,128)S(1)}, u32[]{:S(2)}, u32[]{:S(2)}) async-start(f32[4,128,128]{2,1,0:T(8,128)} %shard_map.150), calls=%async_computation.6 | async-start | bytes 524288 | tf_op jit(solution)/shard_map/all_to_all | solution.py:375
  123.4 6.6 %all-to-all-done.6.refs_0_ = f32[4,128,128]{2,1,0:T(8,128)S(1)} async-done(((f32[4,128,128]{2,1,0:T(8,128)}), f32[4,128,128]{2,1,0:T(8,128)S(1)}, u32[]{:S(2)}, u32[]{:S(2)}) %all-to-all-start.6) | async-done | bytes 262176 | tf_op jit(solution)/shard_map/all_to_all | solution.py:375
  130.0 0.7 shard_map.152
  130.8 3.4 %all-to-all-start.7 = ((f32[8,72,128]{2,1,0:T(8,128)}), f32[8,72,128]{2,1,0:T(8,128)S(1)}, u32[]{:S(2)}, u32[]{:S(2)}) async-start(f32[8,72,128]{2,1,0:T(8,128)} %shard_map.152), calls=%async_computation.7 | async-start | bytes 589824 | tf_op jit(solution)/shard_map/all_to_all | solution.py:375
  134.2 1.5 %collective-permute-start.9 = (f32[1,256,128]{2,1,0:T(8,128)S(1)}, f32[1,256,128]{2,1,0:T(8,128)S(1)}, u32[]{:S(2)}, u32[]{:S(2)}) collective-permute-start(f32[1,256,128]{2,1,0:T(8,128)S(1)} %get-tuple-element.60.refs_1_), channel_id=1, source_target_pairs={{0,4},{2,6},{4,0},{6,2},{1,5},{3,7},{5,1},{7,3},{8,12},{10,14},{12... | collective-permute-start | bytes 393224 | tf_op jit(solution)/shard_map/ppermute | solution.py:409
  135.7 5.0 %collective-permute-done.9.recv_ref = f32[1,256,128]{2,1,0:T(8,128)S(1)} collective-permute-done((f32[1,256,128]{2,1,0:T(8,128)S(1)}, f32[1,256,128]{2,1,0:T(8,128)S(1)}, u32[]{:S(2)}, u32[]{:S(2)}) %collective-permute-start.9) | collective-permute-done | bytes 131104 | tf_op jit(solution)/shard_map/ppermute | solution.py:409
  140.7 0.7 shard_map.154
  141.4 3.7 %all-to-all-done.7.recv_ref = f32[8,72,128]{2,1,0:T(8,128)S(1)} async-done(((f32[8,72,128]{2,1,0:T(8,128)}), f32[8,72,128]{2,1,0:T(8,128)S(1)}, u32[]{:S(2)}, u32[]{:S(2)}) %all-to-all-start.7) | async-done | bytes 294944 | tf_op jit(solution)/shard_map/all_to_all | solution.py:375
  145.1 0.6 shard_map.153
  (45 shorter events, 1.5 us)
Async XLA Ops:
  0.6 21.1 %copy-start.3 = (f32[2048,128]{1,0:T(8,128)S(1)}, f32[2048,128]{1,0:T(8,128)}, u32[]{:S(2)}) copy-start(f32[2048,128]{1,0:T(8,128)} %shape_ref.3) | copy-start | bytes 3145732
  4.1 24.0 %all-to-all-start = ((f32[32,16,128]{2,1,0:T(8,128)}), f32[32,16,128]{2,1,0:T(8,128)S(1)}, u32[]{:S(2)}, u32[]{:S(2)}) async-start(f32[32,16,128]{2,1,0:T(8,128)} %get-tuple-element.37), calls=%async_computation | async-start | bytes 524288 | tf_op jit(solution)/shard_map/all_to_all | solution.py:375
  15.6 1.0 copy-start.13
  16.6 0.8 copy-start.14
  17.4 0.7 copy-start.15
  18.1 19.8 %collective-permute-start.2 = (f32[64,2176]{1,0:T(8,128)S(1)}, f32[64,2176]{1,0:T(8,128)S(1)}, u32[]{:S(2)}, u32[]{:S(2)}) collective-permute-start(f32[64,2176]{1,0:T(8,128)S(1)} %shard_map.139.refs_2_.refs_0_), channel_id=1, source_target_pairs={{0,6},{2,4},{4,2},{6,0},{1,7},{3,5},{5,3},{7,1},{8,14},{10,12},{12... | collective-permute-start | bytes 1671176 | tf_op jit(solution)/shard_map/ppermute | solution.py:409
  19.7 18.3 %collective-permute-start.1 = (f32[64,2176]{1,0:T(8,128)S(1)}, f32[64,2176]{1,0:T(8,128)}, u32[]{:S(2)}, u32[]{:S(2)}) collective-permute-start(f32[64,2176]{1,0:T(8,128)S(1)} %shard_map.139.refs_2_.refs_0_), channel_id=1, source_target_pairs={{0,2},{2,0},{4,6},{6,4},{1,3},{3,1},{5,7},{7,5},{8,10},{10,8},{12,... | collective-permute-start | bytes 1671176 | tf_op jit(solution)/shard_map/ppermute | solution.py:409
  21.5 17.0 %collective-permute-start = (f32[64,2176]{1,0:T(8,128)S(1)}, f32[64,2176]{1,0:T(8,128)}, u32[]{:S(2)}, u32[]{:S(2)}) collective-permute-start(f32[64,2176]{1,0:T(8,128)S(1)} %shard_map.139.refs_2_.refs_0_), channel_id=1, source_target_pairs={{0,1},{1,0},{2,3},{3,2},{4,5},{5,4},{6,7},{7,6},{8,9},{9,8},{10,11... | collective-permute-start | bytes 1671176 | tf_op jit(solution)/shard_map/ppermute | solution.py:409
  21.5 31.8 %collective-permute-start.5 = (f32[64,2176]{1,0:T(8,128)S(1)}, f32[64,2176]{1,0:T(8,128)}, u32[]{:S(2)}, u32[]{:S(2)}) collective-permute-start(f32[64,2176]{1,0:T(8,128)S(1)} %shard_map.139.refs_2_.refs_0_), channel_id=1, source_target_pairs={{0,4},{2,6},{4,0},{6,2},{1,5},{3,7},{5,1},{7,3},{8,12},{10,14},{12... | collective-permute-start | bytes 1671176 | tf_op jit(solution)/shard_map/ppermute | solution.py:409
  21.7 1.2 copy-start.4
  24.0 39.7 %copy-start = (f32[2048,128]{1,0:T(8,128)}, f32[2048,128]{1,0:T(8,128)S(1)}, u32[]{:S(2)}) copy-start(f32[2048,128]{1,0:T(8,128)S(1)} %shard_map.138.refs_1_.refs_2_.table_ref) | copy-start | bytes 3145732
  24.0 24.6 %copy-start.16 = (f32[8,128]{1,0:T(8,128)S(1)}, f32[8,128]{1,0:T(8,128)}, u32[]{:S(2)}) copy-start(f32[8,128]{1,0:T(8,128)} %get-tuple-element.38.refs_2_.refs_1_) | copy-start | bytes 12292
  24.0 24.6 %copy-start.17 = (f32[128]{0:T(128)S(1)}, f32[128]{0:T(128)}, u32[]{:S(2)}) copy-start(f32[128]{0:T(128)} %param.17) | copy-start | bytes 1540
  24.0 24.6 %copy-start.18 = (f32[8,128]{1,0:T(8,128)S(1)}, f32[8,128]{1,0:T(8,128)}, u32[]{:S(2)}) copy-start(f32[8,128]{1,0:T(8,128)} %get-tuple-element.40.refs_2_) | copy-start | bytes 12292
  30.7 1.4 copy-start.1
  32.0 16.6 %all-to-all-start.1 = ((f32[32,8,128]{2,1,0:T(8,128)}), f32[32,8,128]{2,1,0:T(8,128)S(1)}, u32[]{:S(2)}, u32[]{:S(2)}) async-start(f32[32,8,128]{2,1,0:T(8,128)} %bitcast.5), calls=%async_computation.1 | async-start | bytes 262144 | tf_op jit(solution)/shard_map/all_to_all | solution.py:375
  37.9 33.6 %collective-permute-start.4 = (f32[64,2176]{1,0:T(8,128)S(1)}, f32[64,2176]{1,0:T(8,128)S(1)}, u32[]{:S(2)}, u32[]{:S(2)}) collective-permute-start(f32[64,2176]{1,0:T(8,128)S(1)} %collective-permute-done.2.refs_1_.refs_6_), channel_id=1, source_target_pairs={{0,1},{1,0},{2,3},{3,2},{4,5},{5,4},{6,7},{7,6},{8,9},{9,8},{10,11... | collective-permute-start | bytes 1671176 | tf_op jit(solution)/shard_map/ppermute | solution.py:409
  38.0 33.5 %collective-permute-start.3 = (f32[64,2176]{1,0:T(8,128)}, f32[64,2176]{1,0:T(8,128)}, u32[]{:S(2)}, u32[]{:S(2)}) collective-permute-start(f32[64,2176]{1,0:T(8,128)} %collective-permute-done.1.refs_0_.refs_2_), channel_id=1, source_target_pairs={{0,1},{1,0},{2,3},{3,2},{4,5},{5,4},{6,7},{7,6},{8,9},{9,8},{10,11... | collective-permute-start | bytes 1671176 | tf_op jit(solution)/shard_map/ppermute | solution.py:409
  40.6 1.0 copy-start.7
  49.4 14.3 %all-to-all-start.2 = ((f32[32,8,128]{2,1,0:T(8,128)}), f32[32,8,128]{2,1,0:T(8,128)S(1)}, u32[]{:S(2)}, u32[]{:S(2)}) async-start(f32[32,8,128]{2,1,0:T(8,128)} %get-tuple-element.42.refs_3_), calls=%async_computation.2 | async-start | bytes 262144 | tf_op jit(solution)/shard_map/all_to_all | solution.py:375
  53.3 33.8 %collective-permute-start.6 = (f32[64,2176]{1,0:T(8,128)}, f32[64,2176]{1,0:T(8,128)}, u32[]{:S(2)}, u32[]{:S(2)}) collective-permute-start(f32[64,2176]{1,0:T(8,128)} %collective-permute-done.5.refs_2_.refs_4_), channel_id=1, source_target_pairs={{0,1},{1,0},{2,3},{3,2},{4,5},{5,4},{6,7},{7,6},{8,9},{9,8},{10,11... | collective-permute-start | bytes 1671176 | tf_op jit(solution)/shard_map/ppermute | solution.py:409
  53.5 1.2 copy-start.8
  56.9 1.0 copy-start.9
  63.7 1.6 %copy-start.2 = (f32[16,256,128]{2,1,0:T(8,128)S(1)}, f32[16,256,128]{2,1,0:T(8,128)}, u32[]{:S(2)}) copy-start(f32[16,256,128]{2,1,0:T(8,128)} %copy-done.1) | copy-start | bytes 6291460
  67.4 19.7 %copy-start.5 = (f32[2048,128]{1,0:T(8,128)S(1)}, f32[2048,128]{1,0:T(8,128)}, u32[]{:S(2)}) copy-start(f32[2048,128]{1,0:T(8,128)} %refs_2_.1) | copy-start | bytes 3145732
  67.4 15.0 %all-to-all-start.3 = ((f32[32,8,128]{2,1,0:T(8,128)}), f32[32,8,128]{2,1,0:T(8,128)S(1)}, u32[]{:S(2)}, u32[]{:S(2)}) async-start(f32[32,8,128]{2,1,0:T(8,128)} %bitcast.8), calls=%async_computation.3 | async-start | bytes 262144 | tf_op jit(solution)/shard_map/all_to_all | solution.py:375
  71.5 1.2 copy-start.10
  75.0 1.0 copy-start.11
  83.1 14.2 %all-to-all-start.4 = ((f32[32,8,128]{2,1,0:T(8,128)}), f32[32,8,128]{2,1,0:T(8,128)S(1)}, u32[]{:S(2)}, u32[]{:S(2)}) async-start(f32[32,8,128]{2,1,0:T(8,128)} %get-tuple-element.52.refs_3_), calls=%async_computation.4 | async-start | bytes 262144 | tf_op jit(solution)/shard_map/all_to_all | solution.py:375
  87.1 1.2 copy-start.12
  90.5 1.0 copy-start.6
  106.9 5.8 %collective-permute-start.7 = (f32[4,256,128]{2,1,0:T(8,128)}, f32[4,256,128]{2,1,0:T(8,128)S(1)}, u32[]{:S(2)}, u32[]{:S(2)}) collective-permute-start(f32[4,256,128]{2,1,0:T(8,128)} %get-tuple-element.57), channel_id=1, source_target_pairs={{0,1},{1,0},{2,3},{3,2},{4,5},{5,4},{6,7},{7,6},{8,9},{9,8},{10,11... | collective-permute-start | bytes 1572872 | tf_op jit(solution)/shard_map/ppermute | solution.py:409
  106.9 12.4 %all-to-all-start.5 = ((f32[8,64,128]{2,1,0:T(8,128)}), f32[8,64,128]{2,1,0:T(8,128)S(1)}, u32[]{:S(2)}, u32[]{:S(2)}) async-start(f32[8,64,128]{2,1,0:T(8,128)} %get-tuple-element.54), calls=%async_computation.5 | async-start | bytes 524288 | tf_op jit(solution)/shard_map/all_to_all | solution.py:375
  112.7 10.6 %collective-permute-start.8 = (f32[2,256,128]{2,1,0:T(8,128)S(1)}, f32[2,256,128]{2,1,0:T(8,128)S(1)}, u32[]{:S(2)}, u32[]{:S(2)}) collective-permute-start(f32[2,256,128]{2,1,0:T(8,128)S(1)} %get-tuple-element.58.refs_2_), channel_id=1, source_target_pairs={{0,2},{2,0},{4,6},{6,4},{1,3},{3,1},{5,7},{7,5},{8,10},{10,8},{12,... | collective-permute-start | bytes 786440 | tf_op jit(solution)/shard_map/ppermute | solution.py:409
  120.0 10.1 %all-to-all-start.6 = ((f32[4,128,128]{2,1,0:T(8,128)}), f32[4,128,128]{2,1,0:T(8,128)S(1)}, u32[]{:S(2)}, u32[]{:S(2)}) async-start(f32[4,128,128]{2,1,0:T(8,128)} %shard_map.150), calls=%async_computation.6 | async-start | bytes 524288 | tf_op jit(solution)/shard_map/all_to_all | solution.py:375
  130.8 14.3 %all-to-all-start.7 = ((f32[8,72,128]{2,1,0:T(8,128)}), f32[8,72,128]{2,1,0:T(8,128)S(1)}, u32[]{:S(2)}, u32[]{:S(2)}) async-start(f32[8,72,128]{2,1,0:T(8,128)} %shard_map.152), calls=%async_computation.7 | async-start | bytes 589824 | tf_op jit(solution)/shard_map/all_to_all | solution.py:375
  134.2 6.6 %collective-permute-start.9 = (f32[1,256,128]{2,1,0:T(8,128)S(1)}, f32[1,256,128]{2,1,0:T(8,128)S(1)}, u32[]{:S(2)}, u32[]{:S(2)}) collective-permute-start(f32[1,256,128]{2,1,0:T(8,128)S(1)} %get-tuple-element.60.refs_1_), channel_id=1, source_target_pairs={{0,4},{2,6},{4,0},{6,2},{1,5},{3,7},{5,1},{7,3},{8,12},{10,14},{12... | collective-permute-start | bytes 393224 | tf_op jit(solution)/shard_map/ppermute | solution.py:409

commit v7 on v6

--- a/solution.py
+++ b/solution.py
@@ -25,7 +25,7 @@
 NN = (((1,), (0,)), ((), ()))
 TN = (((0,), (0,)), ((), ()))
 LANES = 128
-VMEM_LIMIT = 48 * 1024 * 1024
+VMEM_LIMIT = 24 * 1024 * 1024
 WHOLE_VMEM = 60 * 1024 * 1024
 
 
@@ -259,14 +259,12 @@
 
 def last_kernel(shards, spot_ref, theta_ref, marks_ref, table_ref, scale_ref, shape_ref, *refs):
     shard_refs = refs[:shards]
-    partial_ref, base_ref, keep_ref, send_ref, grad_ref = refs[shards:]
+    partial_ref, base_ref, keep_ref, send_ref, grad_ref, score_ref = refs[shards:]
     spot = spot_ref[2]
     theta = theta_ref[...]
     factors = theta.shape[1]
     theta_high, theta_both = split_theta(theta)
     total = jnp.zeros(theta.shape, F32)
-    rows = grad_ref.shape[1]
-    grad = jnp.zeros((shards * rows, factors), F32)
     width = 2 * LANES
     for place in range(shards):
         block = spot ^ place
@@ -283,13 +281,17 @@
         if place == 0:
             base_ref[...] = base
         score = item_prior / shards - scale_ref[here, :] * (base / shards + step_weight * USER_RATIO * stats)
-        score_high, score_low = split(score)
-        cov_high, cov_low = split(jnp.concatenate([shard[:, here] for shard in shard_refs], axis=0))
-        wide = dot(cov_high, jnp.concatenate([score_high, score_low], axis=1), NN)
-        grad = grad + (wide[:, :factors] + wide[:, factors:] + dot(cov_low, score_high, NN))
+        score_ref[here, :] = jnp.concatenate(split(score), axis=1)
     partial_ref[...] = total
-    for place in range(shards):
-        grad_ref[spot ^ place] = grad[place * rows : (place + 1) * rows]
+    rows = grad_ref.shape[1]
+    group = 4
+    for first in range(0, shards, group):
+        cov = jnp.concatenate([shard[:, : score_ref.shape[0]] for shard in shard_refs[first : first + group]], axis=0)
+        cov_high, cov_low = split(cov)
+        wide = dot(cov_high, score_ref[...], NN)
+        grad = wide[:, :factors] + wide[:, factors:] + dot(cov_low, score_ref[:, :factors], NN)
+        for place in range(group):
+            grad_ref[spot ^ (first + place)] = grad[place * rows : (place + 1) * rows]
 
 
 def halve_kernel(held_ref, recv_ref, keep_ref, send_ref):
@@ -463,6 +465,7 @@
             shape_of(split_count, cov_rows, factors),
         ),
         in_specs=[smem] + [vmem] * (5 + split_count),
+        scratch_shapes=[pltpu.VMEM((item_rows, 2 * factors), BF16)],
     )(spot, theta_all, marks, table, scale, item_shape, *shards)
 
     def halve(held, moved, distance):

time: 147 us -> 150 us (1.020)
  local copies, waits for them, and re-layouts: 14.2 us -> 23.1 us
  waiting for transfers between devices: 50.9 us -> 47.3 us
  Pallas kernels: 31.7 us -> 28.9 us
    unnamed x38 -> x54, local copies, waits for them, and re-layouts: 14.2 us -> 23.1 us
    all_to_all x8, waiting for transfers between devices: 45.9 us -> 42.2 us  [exchange(): return lax.all_to_all(array, axes, split_axis=0, concat_axis=0, tiled=True)]
    pallas_call x1, Pallas kernels: 9.53 us -> 7.05 us  [shards(): kernel_call(functools.partial(last_kernel, split_count), (shape_of(everyo...]
  transfers between devices with their start and end apart: 18 -> 18, of which waited for: 9 -> 9; matrix products, arithmetic and copies ran while one was open for 0% -> 0% of each run, Pallas kernels for 12% -> 11%
where the time goes in v7:
time: 150 us; the launch traced here: 148 us
  starting transfers between devices  47.9 us (32%)
  waiting for transfers between devices  47.3 us (32%)
  Pallas kernels  28.9 us (19%)
  local copies, waits for them, and re-layouts  23.1 us (15%)
    all_to_all x8, waiting for transfers between devices, exchange(): return lax.all_to_all(array, axes, split_axis=0, concat_axis=0, tiled=True)  42.2 us
    all_to_all x8, starting transfers between devices, exchange(): return lax.all_to_all(array, axes, split_axis=0, concat_axis=0, tiled=True)  41.8 us
    unnamed x54, local copies, waits for them, and re-layouts  23.1 us
    pallas_call x1, Pallas kernels, shards(): kernel_call(functools.partial(last_kernel, split_count), (shape_of(everyo...  7.05 us
    pallas_call x3, Pallas kernels, add_prior(): kernel_call(behind(functools.partial(prior_kernel, len(places)), len(inpu...  6.62 us
    ppermute x10, starting transfers between devices, swap(): lax.ppermute(array, axis, [(place, place ^ bit) for place in range(lax.ax...  6.09 us
    ppermute x10, waiting for transfers between devices, swap(): lax.ppermute(array, axis, [(place, place ^ bit) for place in range(lax.ax...  5.04 us
    pallas_call x1, Pallas kernels, shards(): kernel_call(functools.partial(prep_kernel, owners), (shape_of(owners, 16,...  3.43 us
  transfers between devices with their start and end apart: 18, of which 9 were waited for; matrix products, arithmetic and copies ran while one was open for 0% of the time, Pallas kernels for 11%

profile of v7, /device:TPU:2, one launch (start us, length us, event | category | flops | bytes accessed | tf_op | source)
XLA Modules:
  0.0 148.1 jit_solution(6228770302249672740)
XLA Ops:
  0.6 3.4 %shard_map.137 = (f32[32,16,128]{2,1,0:T(8,128)}, f32[8,128]{1,0:T(8,128)}, f32[8,128]{1,0:T(8,128)}) custom-call(s32[8]{0:T(128)} %counts_hbm.1, s32[64,128]{1,0:T(8,128)} %bitcast.17, s32[64,128]{1,0:T(8,128)} %bitcast.18, f32[8,128]{1,0:T(8,128)} %shape_hbm.1, f32[8,128]{1,0:T(8,128)} %rate_hbm.1), custom_call_target="tpu_custom_call" | custom-call | tf_op jit(solution)/shard_map/pallas_call | solution.py:386
  4.1 11.5 %all-to-all-start = ((f32[32,16,128]{2,1,0:T(8,128)}), f32[32,16,128]{2,1,0:T(8,128)S(1)}, u32[]{:S(2)}, u32[]{:S(2)}) async-start(f32[32,16,128]{2,1,0:T(8,128)} %get-tuple-element.37), calls=%async_computation | async-start | bytes 524288 | tf_op jit(solution)/shard_map/all_to_all | solution.py:377
  15.6 1.0 copy-done.16
  16.6 0.8 copy-done.22
  18.1 1.6 %collective-permute-start.2 = (f32[64,2176]{1,0:T(8,128)S(1)}, f32[64,2176]{1,0:T(8,128)S(1)}, u32[]{:S(2)}, u32[]{:S(2)}) collective-permute-start(f32[64,2176]{1,0:T(8,128)S(1)} %shard_map.139.refs_2_.refs_0_), channel_id=1, source_target_pairs={{0,6},{2,4},{4,2},{6,0},{1,7},{3,5},{5,3},{7,1},{8,14},{10,12},{12... | collective-permute-start | bytes 1671176 | tf_op jit(solution)/shard_map/ppermute | solution.py:411
  19.7 1.8 %collective-permute-start.1 = (f32[64,2176]{1,0:T(8,128)S(1)}, f32[64,2176]{1,0:T(8,128)}, u32[]{:S(2)}, u32[]{:S(2)}) collective-permute-start(f32[64,2176]{1,0:T(8,128)S(1)} %shard_map.139.refs_2_.refs_0_), channel_id=1, source_target_pairs={{0,2},{2,0},{4,6},{6,4},{1,3},{3,1},{5,7},{7,5},{8,10},{10,8},{12,... | collective-permute-start | bytes 1671176 | tf_op jit(solution)/shard_map/ppermute | solution.py:411
  21.7 1.2 copy-done.4
  22.9 1.1 shard_map.138.refs_1_.refs_2_.table_ref
  24.1 4.0 %all-to-all-done.refs_0_ = f32[32,16,128]{2,1,0:T(8,128)S(1)} async-done(((f32[32,16,128]{2,1,0:T(8,128)}), f32[32,16,128]{2,1,0:T(8,128)S(1)}, u32[]{:S(2)}, u32[]{:S(2)}) %all-to-all-start) | async-done | bytes 262176 | tf_op jit(solution)/shard_map/all_to_all | solution.py:377
  28.0 2.0 %shard_map.140 = (f32[16,256,128]{2,1,0:T(8,128)S(1)}, f32[256,128]{1,0:T(8,128)S(1)}) custom-call(f32[32,16,128]{2,1,0:T(8,128)S(1)} %all-to-all-done.refs_0_, f32[2048,128]{1,0:T(8,128)S(1)} %shard_map.138.refs_1_.refs_2_.table_ref, f32[64,2176]{1,0:T(8,128)S(1)} %shard_map.139.refs_2_.refs_0_), custom_call_target="tpu_custom_call" | custom-call | tf_op jit(solution)/shard_map/pallas_call | solution.py:431
  30.1 1.3 copy-done
  32.1 5.8 %all-to-all-start.1 = ((f32[32,8,128]{2,1,0:T(8,128)}), f32[32,8,128]{2,1,0:T(8,128)S(1)}, u32[]{:S(2)}, u32[]{:S(2)}) async-start(f32[32,8,128]{2,1,0:T(8,128)} %bitcast.12), calls=%async_computation.1 | async-start | bytes 262144 | tf_op jit(solution)/shard_map/all_to_all | solution.py:377
  38.5 0.9 copy-done.15
  39.4 2.1 %shard_map.141 = (f32[128,2048]{1,0:T(8,128)S(1)}, f32[8,128]{1,0:T(8,128)S(1)}) custom-call(f32[64,2176]{1,0:T(8,128)S(1)} %shard_map.139.refs_2_.refs_0_, f32[64,2176]{1,0:T(8,128)} %collective-permute-done.refs_1_, f32[256,128]{1,0:T(8,128)S(1)} %copy-done.15), custom_call_target="tpu_custom_call" | custom-call | tf_op jit(solution)/shard_map/pallas_call | solution.py:425
  41.5 1.0 copy-done.8
  42.5 6.2 %all-to-all-done.1.refs_0_ = f32[32,8,128]{2,1,0:T(8,128)S(1)} async-done(((f32[32,8,128]{2,1,0:T(8,128)}), f32[32,8,128]{2,1,0:T(8,128)S(1)}, u32[]{:S(2)}, u32[]{:S(2)}) %all-to-all-start.1) | async-done | bytes 131104 | tf_op jit(solution)/shard_map/all_to_all | solution.py:377
  49.4 3.9 %all-to-all-start.2 = ((f32[32,8,128]{2,1,0:T(8,128)}), f32[32,8,128]{2,1,0:T(8,128)S(1)}, u32[]{:S(2)}, u32[]{:S(2)}) async-start(f32[32,8,128]{2,1,0:T(8,128)} %get-tuple-element.42.refs_3_), calls=%async_computation.2 | async-start | bytes 262144 | tf_op jit(solution)/shard_map/all_to_all | solution.py:377
  53.6 1.2 copy-done.9
  54.8 2.1 %shard_map.143 = (f32[128,2048]{1,0:T(8,128)S(1)}, f32[8,128]{1,0:T(8,128)S(1)}) custom-call(f32[64,2176]{1,0:T(8,128)} %collective-permute-done.1.refs_0_.refs_2_, f32[64,2176]{1,0:T(8,128)S(1)} %collective-permute-done.2.refs_1_.refs_6_, f32[128,2048]{1,0:T(8,128)S(1)} %copy-done.9, f32[32,8,128]{2,1,0:T(8,128)} %get-tuple-element.42.refs_3_), custom_call_target="tpu_custom_call" | custom-call | tf_op jit(solution)/shard_map/pallas_call | solution.py:425
  56.9 1.0 copy-done.10
  57.9 5.7 %all-to-all-done.2 = f32[32,8,128]{2,1,0:T(8,128)S(1)} async-done(((f32[32,8,128]{2,1,0:T(8,128)}), f32[32,8,128]{2,1,0:T(8,128)S(1)}, u32[]{:S(2)}, u32[]{:S(2)}) %all-to-all-start.2) | async-done | bytes 131104 | tf_op jit(solution)/shard_map/all_to_all | solution.py:377
  63.5 1.6 %copy-done.1 = f32[16,256,128]{2,1,0:T(8,128)S(1)} copy-done((f32[16,256,128]{2,1,0:T(8,128)S(1)}, f32[16,256,128]{2,1,0:T(8,128)}, u32[]{:S(2)}) %copy-start.1) | copy-done | bytes 2097176
  65.1 2.1 %shard_map.144 = (f32[256,128]{1,0:T(8,128)}, f32[8,128]{1,0:T(8,128)S(1)}) custom-call(f32[256,128]{1,0:T(8,128)S(1)} %bitcast.13, f32[16,256,128]{2,1,0:T(8,128)S(1)} %copy-done.1, f32[2048,128]{1,0:T(8,128)S(1)} %shard_map.138.refs_1_.refs_2_.table_ref, f32[8,128]{1,0:T(8,128)S(1)} %get-tuple-element.45.refs_3_), custom_call_target="tpu_custom_call" | custom-call | tf_op jit(solution)/shard_map/pallas_call | solution.py:447
  67.2 4.1 %all-to-all-start.3 = ((f32[32,8,128]{2,1,0:T(8,128)}), f32[32,8,128]{2,1,0:T(8,128)S(1)}, u32[]{:S(2)}, u32[]{:S(2)}) async-start(f32[32,8,128]{2,1,0:T(8,128)} %bitcast.8), calls=%async_computation.3 | async-start | bytes 262144 | tf_op jit(solution)/shard_map/all_to_all | solution.py:377
  71.4 1.2 copy-done.11
  72.6 2.5 %shard_map.145 = (f32[128,2048]{1,0:T(8,128)S(1)}, f32[8,128]{1,0:T(8,128)S(1)}) custom-call(f32[64,2176]{1,0:T(8,128)} %collective-permute-done.3.refs_0_.refs_3_, f32[64,2176]{1,0:T(8,128)} %collective-permute-done.4.refs_1_.refs_7_, f32[64,2176]{1,0:T(8,128)} %collective-permute-done.5.refs_2_.refs_4_, f32[128,2048]{1,0:T(8,128)S(1)} %copy-done.11, ...), custom_call_target="tpu_custom_call" | custom-call | tf_op jit(solution)/shard_map/pallas_call | solution.py:425
  75.1 1.0 copy-done.12
  76.1 6.2 %all-to-all-done.3.refs_0_ = f32[32,8,128]{2,1,0:T(8,128)S(1)} async-done(((f32[32,8,128]{2,1,0:T(8,128)}), f32[32,8,128]{2,1,0:T(8,128)S(1)}, u32[]{:S(2)}, u32[]{:S(2)}) %all-to-all-start.3) | async-done | bytes 131104 | tf_op jit(solution)/shard_map/all_to_all | solution.py:377
  83.0 3.9 %all-to-all-start.4 = ((f32[32,8,128]{2,1,0:T(8,128)}), f32[32,8,128]{2,1,0:T(8,128)S(1)}, u32[]{:S(2)}, u32[]{:S(2)}) async-start(f32[32,8,128]{2,1,0:T(8,128)} %get-tuple-element.52.refs_3_), calls=%async_computation.4 | async-start | bytes 262144 | tf_op jit(solution)/shard_map/all_to_all | solution.py:377
  87.0 1.2 copy-done.5
  88.2 1.2 copy-done.13
  89.4 2.2 %shard_map.147.scale_ref = f32[2048,128]{1,0:T(8,128)S(1)} custom-call(f32[64,2176]{1,0:T(8,128)} %collective-permute-done.6.refs_0_.refs_5_, f32[128,2048]{1,0:T(8,128)S(1)} %copy-done.13, f32[2048,128]{1,0:T(8,128)S(1)} %copy-done.5, f32[32,8,128]{2,1,0:T(8,128)} %get-tuple-element.52.refs_3_), custom_call_target="tpu_custom_call" | custom-call | tf_op jit(solution)/shard_map/pallas_call | solution.py:454
  91.6 1.0 copy-done.6
  92.6 4.5 %all-to-all-done.4 = f32[32,8,128]{2,1,0:T(8,128)S(1)} async-done(((f32[32,8,128]{2,1,0:T(8,128)}), f32[32,8,128]{2,1,0:T(8,128)S(1)}, u32[]{:S(2)}, u32[]{:S(2)}) %all-to-all-start.4) | async-done | bytes 131104 | tf_op jit(solution)/shard_map/all_to_all | solution.py:377
  97.2 1.6 %copy-done.2 = f32[16,256,128]{2,1,0:T(8,128)S(1)} copy-done((f32[16,256,128]{2,1,0:T(8,128)S(1)}, f32[16,256,128]{2,1,0:T(8,128)}, u32[]{:S(2)}) %copy-start.2) | copy-done | bytes 2097176
  98.7 1.2 copy-done.7
  100.0 7.0 %shard_map.148 = (f32[256,128]{1,0:T(8,128)S(1)}, f32[256,128]{1,0:T(8,128)S(1)}, f32[4,256,128]{2,1,0:T(8,128)S(1)}, f32[4,256,128]{2,1,0:T(8,128)}, f32[8,64,128]{2,1,0:T(8,128)S(1)}) custom-call(s32[3]{0:T(128)S(1)} %pad_add_fusion.spot_ref, f32[256,128]{1,0:T(8,128)S(1)} %bitcast.11, f32[16,256,128]{2,1,0:T(8,128)S(1)} %copy-done.2, ...), custom_call_target="tpu_custom_call" | custom-call | tf_op jit(solution)/shard_map/pallas_call | solution.py:458
  107.0 0.8 copy-done.17
  109.2 5.8 %all-to-all-start.5 = ((f32[8,64,128]{2,1,0:T(8,128)}), f32[8,64,128]{2,1,0:T(8,128)S(1)}, u32[]{:S(2)}, u32[]{:S(2)}) async-start(f32[8,64,128]{2,1,0:T(8,128)} %copy-done.19), calls=%async_computation.5 | async-start | bytes 524288 | tf_op jit(solution)/shard_map/all_to_all | solution.py:377
  115.0 1.0 copy-done.18
  116.2 5.3 %all-to-all-done.5.refs_0_ = f32[8,64,128]{2,1,0:T(8,128)S(1)} async-done(((f32[8,64,128]{2,1,0:T(8,128)}), f32[8,64,128]{2,1,0:T(8,128)S(1)}, u32[]{:S(2)}, u32[]{:S(2)}) %all-to-all-start.5) | async-done | bytes 262176 | tf_op jit(solution)/shard_map/all_to_all | solution.py:377
  122.3 3.4 %all-to-all-start.6 = ((f32[4,128,128]{2,1,0:T(8,128)}), f32[4,128,128]{2,1,0:T(8,128)S(1)}, u32[]{:S(2)}, u32[]{:S(2)}) async-start(f32[4,128,128]{2,1,0:T(8,128)} %shard_map.150), calls=%async_computation.6 | async-start | bytes 524288 | tf_op jit(solution)/shard_map/all_to_all | solution.py:377
  125.8 6.6 %all-to-all-done.6.refs_0_ = f32[4,128,128]{2,1,0:T(8,128)S(1)} async-done(((f32[4,128,128]{2,1,0:T(8,128)}), f32[4,128,128]{2,1,0:T(8,128)S(1)}, u32[]{:S(2)}, u32[]{:S(2)}) %all-to-all-start.6) | async-done | bytes 262176 | tf_op jit(solution)/shard_map/all_to_all | solution.py:377
  132.4 0.7 shard_map.152
  133.1 3.4 %all-to-all-start.7 = ((f32[8,72,128]{2,1,0:T(8,128)}), f32[8,72,128]{2,1,0:T(8,128)S(1)}, u32[]{:S(2)}, u32[]{:S(2)}) async-start(f32[8,72,128]{2,1,0:T(8,128)} %shard_map.152), calls=%async_computation.7 | async-start | bytes 589824 | tf_op jit(solution)/shard_map/all_to_all | solution.py:377
  136.6 1.5 %collective-permute-start.9 = (f32[1,256,128]{2,1,0:T(8,128)S(1)}, f32[1,256,128]{2,1,0:T(8,128)S(1)}, u32[]{:S(2)}, u32[]{:S(2)}) collective-permute-start(f32[1,256,128]{2,1,0:T(8,128)S(1)} %get-tuple-element.60.refs_1_), channel_id=1, source_target_pairs={{0,4},{2,6},{4,0},{6,2},{1,5},{3,7},{5,1},{7,3},{8,12},{10,14},{12... | collective-permute-start | bytes 393224 | tf_op jit(solution)/shard_map/ppermute | solution.py:411
  138.1 5.0 %collective-permute-done.9.recv_ref = f32[1,256,128]{2,1,0:T(8,128)S(1)} collective-permute-done((f32[1,256,128]{2,1,0:T(8,128)S(1)}, f32[1,256,128]{2,1,0:T(8,128)S(1)}, u32[]{:S(2)}, u32[]{:S(2)}) %collective-permute-start.9) | collective-permute-done | bytes 131104 | tf_op jit(solution)/shard_map/ppermute | solution.py:411
  143.8 3.7 %all-to-all-done.7.recv_ref = f32[8,72,128]{2,1,0:T(8,128)S(1)} async-done(((f32[8,72,128]{2,1,0:T(8,128)}), f32[8,72,128]{2,1,0:T(8,128)S(1)}, u32[]{:S(2)}, u32[]{:S(2)}) %all-to-all-start.7) | async-done | bytes 294944 | tf_op jit(solution)/shard_map/all_to_all | solution.py:377
  (61 shorter events, 7.7 us)
Async XLA Ops:
  0.6 21.1 %copy-start.3 = (f32[2048,128]{1,0:T(8,128)S(1)}, f32[2048,128]{1,0:T(8,128)}, u32[]{:S(2)}) copy-start(f32[2048,128]{1,0:T(8,128)} %shape_ref.3) | copy-start | bytes 3145732
  4.1 24.0 %all-to-all-start = ((f32[32,16,128]{2,1,0:T(8,128)}), f32[32,16,128]{2,1,0:T(8,128)S(1)}, u32[]{:S(2)}, u32[]{:S(2)}) async-start(f32[32,16,128]{2,1,0:T(8,128)} %get-tuple-element.37), calls=%async_computation | async-start | bytes 524288 | tf_op jit(solution)/shard_map/all_to_all | solution.py:377
  15.6 1.0 copy-start.16
  16.6 0.8 copy-start.22
  17.4 0.7 copy-start.23
  18.1 19.8 %collective-permute-start.2 = (f32[64,2176]{1,0:T(8,128)S(1)}, f32[64,2176]{1,0:T(8,128)S(1)}, u32[]{:S(2)}, u32[]{:S(2)}) collective-permute-start(f32[64,2176]{1,0:T(8,128)S(1)} %shard_map.139.refs_2_.refs_0_), channel_id=1, source_target_pairs={{0,6},{2,4},{4,2},{6,0},{1,7},{3,5},{5,3},{7,1},{8,14},{10,12},{12... | collective-permute-start | bytes 1671176 | tf_op jit(solution)/shard_map/ppermute | solution.py:411
  19.7 18.3 %collective-permute-start.1 = (f32[64,2176]{1,0:T(8,128)S(1)}, f32[64,2176]{1,0:T(8,128)}, u32[]{:S(2)}, u32[]{:S(2)}) collective-permute-start(f32[64,2176]{1,0:T(8,128)S(1)} %shard_map.139.refs_2_.refs_0_), channel_id=1, source_target_pairs={{0,2},{2,0},{4,6},{6,4},{1,3},{3,1},{5,7},{7,5},{8,10},{10,8},{12,... | collective-permute-start | bytes 1671176 | tf_op jit(solution)/shard_map/ppermute | solution.py:411
  21.5 17.0 %collective-permute-start = (f32[64,2176]{1,0:T(8,128)S(1)}, f32[64,2176]{1,0:T(8,128)}, u32[]{:S(2)}, u32[]{:S(2)}) collective-permute-start(f32[64,2176]{1,0:T(8,128)S(1)} %shard_map.139.refs_2_.refs_0_), channel_id=1, source_target_pairs={{0,1},{1,0},{2,3},{3,2},{4,5},{5,4},{6,7},{7,6},{8,9},{9,8},{10,11... | collective-permute-start | bytes 1671176 | tf_op jit(solution)/shard_map/ppermute | solution.py:411
  21.5 31.8 %collective-permute-start.5 = (f32[64,2176]{1,0:T(8,128)S(1)}, f32[64,2176]{1,0:T(8,128)}, u32[]{:S(2)}, u32[]{:S(2)}) collective-permute-start(f32[64,2176]{1,0:T(8,128)S(1)} %shard_map.139.refs_2_.refs_0_), channel_id=1, source_target_pairs={{0,4},{2,6},{4,0},{6,2},{1,5},{3,7},{5,1},{7,3},{8,12},{10,14},{12... | collective-permute-start | bytes 1671176 | tf_op jit(solution)/shard_map/ppermute | solution.py:411
  21.7 1.2 copy-start.4
  24.0 24.6 %copy-start.24 = (f32[8,128]{1,0:T(8,128)S(1)}, f32[8,128]{1,0:T(8,128)}, u32[]{:S(2)}) copy-start(f32[8,128]{1,0:T(8,128)} %get-tuple-element.38.refs_2_.refs_1_) | copy-start | bytes 12292
  24.0 24.6 %copy-start.25 = (f32[128]{0:T(128)S(1)}, f32[128]{0:T(128)}, u32[]{:S(2)}) copy-start(f32[128]{0:T(128)} %param.17) | copy-start | bytes 1540
  24.0 24.6 %copy-start.26 = (f32[8,128]{1,0:T(8,128)S(1)}, f32[8,128]{1,0:T(8,128)}, u32[]{:S(2)}) copy-start(f32[8,128]{1,0:T(8,128)} %get-tuple-element.40.refs_2_) | copy-start | bytes 12292
  30.1 1.4 copy-start
  31.4 0.7 copy-start.14
  32.1 16.6 %all-to-all-start.1 = ((f32[32,8,128]{2,1,0:T(8,128)}), f32[32,8,128]{2,1,0:T(8,128)S(1)}, u32[]{:S(2)}, u32[]{:S(2)}) async-start(f32[32,8,128]{2,1,0:T(8,128)} %bitcast.12), calls=%async_computation.1 | async-start | bytes 262144 | tf_op jit(solution)/shard_map/all_to_all | solution.py:377
  37.9 33.5 %collective-permute-start.4 = (f32[64,2176]{1,0:T(8,128)S(1)}, f32[64,2176]{1,0:T(8,128)}, u32[]{:S(2)}, u32[]{:S(2)}) collective-permute-start(f32[64,2176]{1,0:T(8,128)S(1)} %collective-permute-done.2.refs_1_.refs_6_), channel_id=1, source_target_pairs={{0,1},{1,0},{2,3},{3,2},{4,5},{5,4},{6,7},{7,6},{8,9},{9,8},{10,11... | collective-permute-start | bytes 1671176 | tf_op jit(solution)/shard_map/ppermute | solution.py:411
  38.0 33.4 %collective-permute-start.3 = (f32[64,2176]{1,0:T(8,128)}, f32[64,2176]{1,0:T(8,128)}, u32[]{:S(2)}, u32[]{:S(2)}) collective-permute-start(f32[64,2176]{1,0:T(8,128)} %collective-permute-done.1.refs_0_.refs_2_), channel_id=1, source_target_pairs={{0,1},{1,0},{2,3},{3,2},{4,5},{5,4},{6,7},{7,6},{8,9},{9,8},{10,11... | collective-permute-start | bytes 1671176 | tf_op jit(solution)/shard_map/ppermute | solution.py:411
  38.5 0.9 copy-start.15
  41.5 1.0 copy-start.8
  49.4 14.1 %all-to-all-start.2 = ((f32[32,8,128]{2,1,0:T(8,128)}), f32[32,8,128]{2,1,0:T(8,128)S(1)}, u32[]{:S(2)}, u32[]{:S(2)}) async-start(f32[32,8,128]{2,1,0:T(8,128)} %get-tuple-element.42.refs_3_), calls=%async_computation.2 | async-start | bytes 262144 | tf_op jit(solution)/shard_map/all_to_all | solution.py:377
  53.3 33.7 %collective-permute-start.6 = (f32[64,2176]{1,0:T(8,128)}, f32[64,2176]{1,0:T(8,128)}, u32[]{:S(2)}, u32[]{:S(2)}) collective-permute-start(f32[64,2176]{1,0:T(8,128)} %collective-permute-done.5.refs_2_.refs_4_), channel_id=1, source_target_pairs={{0,1},{1,0},{2,3},{3,2},{4,5},{5,4},{6,7},{7,6},{8,9},{9,8},{10,11... | collective-permute-start | bytes 1671176 | tf_op jit(solution)/shard_map/ppermute | solution.py:411
  53.6 1.2 copy-start.9
  56.9 1.0 copy-start.10
  63.5 1.6 %copy-start.1 = (f32[16,256,128]{2,1,0:T(8,128)S(1)}, f32[16,256,128]{2,1,0:T(8,128)}, u32[]{:S(2)}) copy-start(f32[16,256,128]{2,1,0:T(8,128)} %copy-done) | copy-start | bytes 6291460
  67.2 15.0 %all-to-all-start.3 = ((f32[32,8,128]{2,1,0:T(8,128)}), f32[32,8,128]{2,1,0:T(8,128)S(1)}, u32[]{:S(2)}, u32[]{:S(2)}) async-start(f32[32,8,128]{2,1,0:T(8,128)} %bitcast.8), calls=%async_computation.3 | async-start | bytes 262144 | tf_op jit(solution)/shard_map/all_to_all | solution.py:377
  71.4 1.2 copy-start.11
  75.1 1.0 copy-start.12
  83.0 14.1 %all-to-all-start.4 = ((f32[32,8,128]{2,1,0:T(8,128)}), f32[32,8,128]{2,1,0:T(8,128)S(1)}, u32[]{:S(2)}, u32[]{:S(2)}) async-start(f32[32,8,128]{2,1,0:T(8,128)} %get-tuple-element.52.refs_3_), calls=%async_computation.4 | async-start | bytes 262144 | tf_op jit(solution)/shard_map/all_to_all | solution.py:377
  87.0 1.2 copy-start.5
  88.2 1.2 copy-start.13
  91.6 1.0 copy-start.6
  97.2 1.6 %copy-start.2 = (f32[16,256,128]{2,1,0:T(8,128)S(1)}, f32[16,256,128]{2,1,0:T(8,128)}, u32[]{:S(2)}) copy-start(f32[16,256,128]{2,1,0:T(8,128)} %copy-done) | copy-start | bytes 6291460
  98.7 1.2 copy-start.7
  107.0 0.8 copy-start.17
  107.8 0.7 copy-start.19
  108.6 0.7 copy-start.20
  109.2 5.8 %collective-permute-start.7 = (f32[4,256,128]{2,1,0:T(8,128)}, f32[4,256,128]{2,1,0:T(8,128)S(1)}, u32[]{:S(2)}, u32[]{:S(2)}) collective-permute-start(f32[4,256,128]{2,1,0:T(8,128)} %get-tuple-element.57), channel_id=1, source_target_pairs={{0,1},{1,0},{2,3},{3,2},{4,5},{5,4},{6,7},{7,6},{8,9},{9,8},{10,11... | collective-permute-start | bytes 1572872 | tf_op jit(solution)/shard_map/ppermute | solution.py:411
  109.2 12.4 %all-to-all-start.5 = ((f32[8,64,128]{2,1,0:T(8,128)}), f32[8,64,128]{2,1,0:T(8,128)S(1)}, u32[]{:S(2)}, u32[]{:S(2)}) async-start(f32[8,64,128]{2,1,0:T(8,128)} %copy-done.19), calls=%async_computation.5 | async-start | bytes 524288 | tf_op jit(solution)/shard_map/all_to_all | solution.py:377
  115.0 1.0 copy-start.18
  116.1 27.0 %copy-start.21 = (f32[256,128]{1,0:T(8,128)S(1)}, f32[256,128]{1,0:T(8,128)}, u32[]{:S(2)}) copy-start(f32[256,128]{1,0:T(8,128)} %copy-done.20) | copy-start | bytes 393220
  116.1 9.6 %collective-permute-start.8 = (f32[2,256,128]{2,1,0:T(8,128)S(1)}, f32[2,256,128]{2,1,0:T(8,128)S(1)}, u32[]{:S(2)}, u32[]{:S(2)}) collective-permute-start(f32[2,256,128]{2,1,0:T(8,128)S(1)} %get-tuple-element.58.refs_2_), channel_id=1, source_target_pairs={{0,2},{2,0},{4,6},{6,4},{1,3},{3,1},{5,7},{7,5},{8,10},{10,8},{12,... | collective-permute-start | bytes 786440 | tf_op jit(solution)/shard_map/ppermute | solution.py:411
  122.3 10.1 %all-to-all-start.6 = ((f32[4,128,128]{2,1,0:T(8,128)}), f32[4,128,128]{2,1,0:T(8,128)S(1)}, u32[]{:S(2)}, u32[]{:S(2)}) async-start(f32[4,128,128]{2,1,0:T(8,128)} %shard_map.150), calls=%async_computation.6 | async-start | bytes 524288 | tf_op jit(solution)/shard_map/all_to_all | solution.py:377
  133.1 14.3 %all-to-all-start.7 = ((f32[8,72,128]{2,1,0:T(8,128)}), f32[8,72,128]{2,1,0:T(8,128)S(1)}, u32[]{:S(2)}, u32[]{:S(2)}) async-start(f32[8,72,128]{2,1,0:T(8,128)} %shard_map.152), calls=%async_computation.7 | async-start | bytes 589824 | tf_op jit(solution)/shard_map/all_to_all | solution.py:377
  136.6 6.6 %collective-permute-start.9 = (f32[1,256,128]{2,1,0:T(8,128)S(1)}, f32[1,256,128]{2,1,0:T(8,128)S(1)}, u32[]{:S(2)}, u32[]{:S(2)}) collective-permute-start(f32[1,256,128]{2,1,0:T(8,128)S(1)} %get-tuple-element.60.refs_1_), channel_id=1, source_target_pairs={{0,4},{2,6},{4,0},{6,2},{1,5},{3,7},{5,1},{7,3},{8,12},{10,14},{12... | collective-permute-start | bytes 393224 | tf_op jit(solution)/shard_map/ppermute | solution.py:411

commit v8 on v7

--- a/solution.py
+++ b/solution.py
@@ -25,7 +25,7 @@
 NN = (((1,), (0,)), ((), ()))
 TN = (((0,), (0,)), ((), ()))
 LANES = 128
-VMEM_LIMIT = 24 * 1024 * 1024
+VMEM_LIMIT = 48 * 1024 * 1024
 WHOLE_VMEM = 60 * 1024 * 1024
 
 
@@ -230,63 +230,76 @@
     own_ref[:, items:] = weight_ref[...]
 
 
-def prior_kernel(shards, *refs):
-    shard_refs, refs = refs[:shards], refs[shards:]
-    sum_ref, token_ref = refs[-2:]
-    items = sum_ref.shape[1]
+def touch_kernel(weight_ref, token_ref):
+    token_ref[...] = weight_ref[: token_ref.shape[0], :]
+
+
+def scale_kernel(shards, *refs):
+    shard_refs = refs[:shards]
+    rate_ref, scale_ref = refs[shards:]
+    items = scale_ref.shape[0]
     width = 2 * LANES
     weight = jnp.concatenate([shard[:, items:] for shard in shard_refs], axis=0)
     for start in range(0, items, width):
         cov = jnp.concatenate([shard[:, start : start + width] for shard in shard_refs], axis=0)
-        part = lax.dot_general(weight, cov, TN, precision=HIGHEST, preferred_element_type=F32)
-        if len(refs) > 2:
-            part = part + refs[0][:, start : start + width]
-        sum_ref[:, start : start + width] = part
-    token_ref[...] = weight[: token_ref.shape[0]]
-
-
-def scale_kernel(shard_ref, sum_ref, rate_ref, scale_ref):
-    items = scale_ref.shape[0]
+        prior_log = lax.dot_general(weight, cov, TN, precision=HIGHEST, preferred_element_type=F32).T
+        scale_ref[start : start + width, :] = jnp.exp(prior_log) / rate_ref[start : start + width, :]
+
+
+def last_kernel(shards, spot_ref, theta_ref, marks_hbm, table_hbm, scale_hbm, shape_hbm, *refs):
+    shard_hbm, refs = refs[:shards], refs[shards:]
+    partial_ref, base_ref, keep_ref, send_ref, grad_ref = refs[:5]
+    marks_ref, table_ref, scale_ref, shape_ref, cov_ref, score_ref, block_sems, shard_sems = refs[5:]
+    spot = spot_ref[2]
     width = 2 * LANES
-    weight = shard_ref[:, items:]
-    for start in range(0, items, width):
-        part = lax.dot_general(
-            weight, shard_ref[:, start : start + width], TN, precision=HIGHEST, preferred_element_type=F32
+    copies = []
+    for place in range(shards):
+        block = spot ^ place
+        here = pl.ds(pl.multiple_of(block * width, width), width)
+        pairs = [(marks_hbm.at[pl.ds(2 * block, 2)], marks_ref.at[place])]
+        for source, target in ((table_hbm, table_ref), (scale_hbm, scale_ref), (shape_hbm, shape_ref)):
+            pairs.append((source.at[here], target.at[place]))
+        copies.append(
+            [
+                pltpu.make_async_copy(source, target, block_sems.at[place, index])
+                for index, (source, target) in enumerate(pairs)
+            ]
         )
-        prior_log = (part + sum_ref[:, start : start + width]).T
-        scale_ref[start : start + width, :] = jnp.exp(prior_log) / rate_ref[start : start + width, :]
-
-
-def last_kernel(shards, spot_ref, theta_ref, marks_ref, table_ref, scale_ref, shape_ref, *refs):
-    shard_refs = refs[:shards]
-    partial_ref, base_ref, keep_ref, send_ref, grad_ref, score_ref = refs[shards:]
-    spot = spot_ref[2]
+    shard_copies = [
+        pltpu.make_async_copy(source, cov_ref.at[place], shard_sems.at[place])
+        for place, source in enumerate(shard_hbm)
+    ]
+    for copy in [copy for group in copies for copy in group] + shard_copies:
+        copy.start()
     theta = theta_ref[...]
     factors = theta.shape[1]
     theta_high, theta_both = split_theta(theta)
     total = jnp.zeros(theta.shape, F32)
-    width = 2 * LANES
     for place in range(shards):
-        block = spot ^ place
-        here = pl.ds(pl.multiple_of(block * width, width), width)
-        table = table_ref[here, :]
-        marks = jnp.concatenate([marks_ref[2 * block], marks_ref[2 * block + 1]], axis=1)
+        for copy in copies[place]:
+            copy.wait()
+        table = table_ref[place]
+        marks = jnp.concatenate([marks_ref[place, 0], marks_ref[place, 1]], axis=1)
         ratio_high, ratio_low, part = ascend_block(theta_high, theta_both, marks, table)
         total = total + part
         wide = dot(ratio_high, theta_both, TN)
         stats = table * (wide[:, :factors] + wide[:, factors:] + dot(ratio_low, theta_high, TN))
         target = send_ref if place % 2 else keep_ref
         target[place // 2] = stats
-        base = (1.0 - step_weight) * shape_ref[here, :] + step_weight * item_prior
+        base = (1.0 - step_weight) * shape_ref[place] + step_weight * item_prior
         if place == 0:
             base_ref[...] = base
-        score = item_prior / shards - scale_ref[here, :] * (base / shards + step_weight * USER_RATIO * stats)
+        score = item_prior / shards - scale_ref[place] * (base / shards + step_weight * USER_RATIO * stats)
+        here = pl.ds(pl.multiple_of((spot ^ place) * width, width), width)
         score_ref[here, :] = jnp.concatenate(split(score), axis=1)
     partial_ref[...] = total
     rows = grad_ref.shape[1]
     group = 4
+    items = score_ref.shape[0]
     for first in range(0, shards, group):
-        cov = jnp.concatenate([shard[:, : score_ref.shape[0]] for shard in shard_refs[first : first + group]], axis=0)
+        for copy in shard_copies[first : first + group]:
+            copy.wait()
+        cov = jnp.concatenate([cov_ref[place, :, :items] for place in range(first, first + group)], axis=0)
         cov_high, cov_low = split(cov)
         wide = dot(cov_high, score_ref[...], NN)
         grad = wide[:, :factors] + wide[:, factors:] + dot(cov_low, score_ref[:, :factors], NN)
@@ -420,40 +433,39 @@
     for distance in (2, 6, 4):
         shards[distance + 1] = swap(shards[distance], 1)
 
-    def add_prior(places, total, awaited):
-        inputs = [shards[place] for place in places] + ([] if total is None else [total])
+    def touch(*awaited):
         return kernel_call(
-            behind(functools.partial(prior_kernel, len(places)), len(inputs)),
-            (shape_of(factors, item_rows), small),
-            in_specs=[vmem] * len(inputs) + [hbm],
-        )(*inputs, awaited)
+            behind(touch_kernel, 1, len(awaited)), small, in_specs=[vmem] + [hbm] * len(awaited)
+        )(cov_weight, *awaited)
 
     marks, partial = kernel_call(
         behind(build_kernel, 2),
         (shape_of(highs, everyone, LANES), shape_of(everyone, factors)),
         in_specs=[vmem, vmem, hbm],
     )(recv, table, own)
-    prior, token = add_prior((0, 1), None, partial)
+    token = touch(partial, marks, shards[1])
     for iteration in range(ITERS - 1):
         parts = exchange(partial.reshape(owners, users_here, factors), user_axes)
         active, theta, spread = kernel_call(
-            behind(functools.partial(update_kernel, activity_shape), 4),
+            behind(functools.partial(update_kernel, activity_shape), 4, 2),
             (small, small, shape_of(owners, users_here, factors)),
-            in_specs=[vmem] * 4 + [hbm],
-        )(parts, theta, active, totals, token)
+            in_specs=[vmem] * 4 + [hbm] * 2,
+        )(parts, theta, active, totals, token, marks)
         theta_all = exchange(spread, user_axes).reshape(everyone, factors)
         if iteration == 0:
-            prior, token = add_prior((2, 6), prior, spread)
+            token = touch(spread, marks, shards[2], shards[6])
             partial, token = kernel_call(
                 behind(ascend_kernel, 3),
                 (shape_of(everyone, factors), small),
                 in_specs=[vmem, vmem, vmem, hbm],
             )(theta_all, marks, table, token)
-            prior, token = add_prior((3, 7, 4), prior, token)
+            token = touch(token, marks, shards[3], shards[4], shards[7])
         else:
             scale = kernel_call(
-                behind(scale_kernel, 3), shape_of(item_rows, factors), in_specs=[vmem, vmem, vmem, hbm]
-            )(shards[5], prior, item_rate, spread)
+                behind(functools.partial(scale_kernel, split_count), split_count + 1, 2),
+                shape_of(item_rows, factors),
+                in_specs=[vmem] * (split_count + 1) + [hbm] * 2,
+            )(*shards, item_rate, spread, marks)
     half = split_count // 2
     partial, base, held, moved, grad = kernel_call(
         functools.partial(last_kernel, split_count),
@@ -464,8 +476,17 @@
             shape_of(half, share_rows, factors),
             shape_of(split_count, cov_rows, factors),
         ),
-        in_specs=[smem] + [vmem] * (5 + split_count),
-        scratch_shapes=[pltpu.VMEM((item_rows, 2 * factors), BF16)],
+        in_specs=[smem, vmem] + [hbm] * (4 + split_count),
+        scratch_shapes=[
+            pltpu.VMEM((split_count, highs // split_count, everyone, LANES), F32),
+            pltpu.VMEM((split_count, share_rows, factors), F32),
+            pltpu.VMEM((split_count, share_rows, factors), F32),
+            pltpu.VMEM((split_count, share_rows, factors), F32),
+            pltpu.VMEM((split_count, cov_rows, item_rows + factors), F32),
+            pltpu.VMEM((item_rows, 2 * factors), BF16),
+            pltpu.SemaphoreType.DMA((split_count, 4)),
+            pltpu.SemaphoreType.DMA((split_count,)),
+        ],
     )(spot, theta_all, marks, table, scale, item_shape, *shards)
 
     def halve(held, moved, distance):

time: 150 us -> 143 us (0.953)
  local copies, waits for them, and re-layouts: 23.1 us -> 4.72 us
  waiting for transfers between devices: 47.3 us -> 60.2 us
    unnamed x54 -> x24, local copies, waits for them, and re-layouts: 23.1 us -> 4.72 us
    all_to_all x8, waiting for transfers between devices: 42.2 us -> 55.2 us  [exchange(): return lax.all_to_all(array, axes, split_axis=0, concat_axis=0, tiled=True)]
    pallas_call x6, Pallas kernels: 10.3 us -> 6.2 us  [the longest x1 4.74 us: shards(): kernel_call(behind(functools.partial(scale_kernel, split_count), split_co...]
    pallas_call x1, Pallas kernels: 7.05 us -> 8.71 us  [shards(): kernel_call(functools.partial(last_kernel, split_count), (shape_of(everyo...]
  transfers between devices with their start and end apart: 18 -> 18, of which waited for: 9 -> 9; matrix products, arithmetic and copies ran while one was open for 0% -> 0% of each run, Pallas kernels for 11% -> 10%
where the time goes in v8:
time: 143 us; the launch traced here: 142 us
  waiting for transfers between devices  60.2 us (42%)
  starting transfers between devices  48.4 us (34%)
  Pallas kernels  28 us (20%)
  local copies, waits for them, and re-layouts  4.72 us (3%)
    all_to_all x8, waiting for transfers between devices, exchange(): return lax.all_to_all(array, axes, split_axis=0, concat_axis=0, tiled=True)  55.2 us
    all_to_all x8, starting transfers between devices, exchange(): return lax.all_to_all(array, axes, split_axis=0, concat_axis=0, tiled=True)  42.5 us
    pallas_call x1, Pallas kernels, shards(): kernel_call(functools.partial(last_kernel, split_count), (shape_of(everyo...  8.71 us
    ppermute x10, starting transfers between devices, swap(): lax.ppermute(array, axis, [(place, place ^ bit) for place in range(lax.ax...  5.92 us
    ppermute x10, waiting for transfers between devices, swap(): lax.ppermute(array, axis, [(place, place ^ bit) for place in range(lax.ax...  5.04 us
    pallas_call x1, Pallas kernels, shards(): kernel_call(behind(functools.partial(scale_kernel, split_count), split_co...  4.74 us
    unnamed x24, local copies, waits for them, and re-layouts  4.72 us
    pallas_call x1, Pallas kernels, shards(): kernel_call(functools.partial(prep_kernel, owners), (shape_of(owners, 16,...  3.46 us
  transfers between devices with their start and end apart: 18, of which 9 were waited for; matrix products, arithmetic and copies ran while one was open for 0% of the time, Pallas kernels for 10%

profile of v8, /device:TPU:2, one launch (start us, length us, event | category | flops | bytes accessed | tf_op | source)
XLA Modules:
  0.0 142.3 jit_solution(12058856341536023511)
XLA Ops:
  0.6 0.0 copy-start.2
  0.6 3.5 %shard_map.137 = (f32[32,16,128]{2,1,0:T(8,128)}, f32[8,128]{1,0:T(8,128)}, f32[8,128]{1,0:T(8,128)}) custom-call(s32[8]{0:T(128)} %counts_hbm.1, s32[64,128]{1,0:T(8,128)} %bitcast.16, s32[64,128]{1,0:T(8,128)} %bitcast.17, f32[8,128]{1,0:T(8,128)} %shape_hbm.2, f32[8,128]{1,0:T(8,128)} %rate_hbm.1), custom_call_target="tpu_custom_call" | custom-call | tf_op jit(solution)/shard_map/pallas_call | solution.py:399
  4.1 11.5 %all-to-all-start = ((f32[32,16,128]{2,1,0:T(8,128)}), f32[32,16,128]{2,1,0:T(8,128)S(1)}, u32[]{:S(2)}, u32[]{:S(2)}) async-start(f32[32,16,128]{2,1,0:T(8,128)} %get-tuple-element.31), calls=%async_computation | async-start | bytes 524288 | tf_op jit(solution)/shard_map/all_to_all | solution.py:390
  15.6 1.0 copy-done.5
  16.7 0.8 copy-done.6
  17.4 0.7 copy-done.8
  18.1 0.8 shard_map.139.refs_2_.refs_0_
  19.0 1.5 %collective-permute-start.2 = (f32[64,2176]{1,0:T(8,128)}, f32[64,2176]{1,0:T(8,128)}, u32[]{:S(2)}, u32[]{:S(2)}) collective-permute-start(f32[64,2176]{1,0:T(8,128)} %shard_map.139.refs_2_.refs_0_), channel_id=1, source_target_pairs={{0,6},{2,4},{4,2},{6,0},{1,7},{3,5},{5,3},{7,1},{8,14},{10,12},{12... | collective-permute-start | bytes 1671176 | tf_op jit(solution)/shard_map/ppermute | solution.py:424
  20.4 1.8 %collective-permute-start.1 = (f32[64,2176]{1,0:T(8,128)}, f32[64,2176]{1,0:T(8,128)}, u32[]{:S(2)}, u32[]{:S(2)}) collective-permute-start(f32[64,2176]{1,0:T(8,128)} %shard_map.139.refs_2_.refs_0_), channel_id=1, source_target_pairs={{0,2},{2,0},{4,6},{6,4},{1,3},{3,1},{5,7},{7,5},{8,10},{10,8},{12,... | collective-permute-start | bytes 1671176 | tf_op jit(solution)/shard_map/ppermute | solution.py:424
  22.3 0.2 collective-permute-start.4
  22.5 1.2 copy-done.3
  23.7 1.1 shard_map.138.refs_1_.refs_2_.table_hbm
  24.8 0.0 copy-start.10
  24.8 3.3 %all-to-all-done.refs_0_ = f32[32,16,128]{2,1,0:T(8,128)S(1)} async-done(((f32[32,16,128]{2,1,0:T(8,128)}), f32[32,16,128]{2,1,0:T(8,128)S(1)}, u32[]{:S(2)}, u32[]{:S(2)}) %all-to-all-start) | async-done | bytes 262176 | tf_op jit(solution)/shard_map/all_to_all | solution.py:390
  28.1 2.7 %shard_map.140 = (f32[16,256,128]{2,1,0:T(8,128)S(1)}, f32[256,128]{1,0:T(8,128)}) custom-call(f32[32,16,128]{2,1,0:T(8,128)S(1)} %all-to-all-done.refs_0_, f32[2048,128]{1,0:T(8,128)S(1)} %shard_map.138.refs_1_.refs_2_.table_hbm, f32[64,2176]{1,0:T(8,128)} %shard_map.139.refs_2_.refs_0_), custom_call_target="tpu_custom_call" | custom-call | tf_op jit(solution)/shard_map/pallas_call | solution.py:441
  30.7 6.5 %all-to-all-start.1 = ((f32[32,8,128]{2,1,0:T(8,128)}), f32[32,8,128]{2,1,0:T(8,128)S(1)}, u32[]{:S(2)}, u32[]{:S(2)}) async-start(f32[32,8,128]{2,1,0:T(8,128)} %bitcast.5), calls=%async_computation.1 | async-start | bytes 262144 | tf_op jit(solution)/shard_map/all_to_all | solution.py:390
  37.3 0.1 collective-permute-start.5
  37.4 0.5 collective-permute-start.3
  37.9 10.2 %all-to-all-done.1.refs_0_ = f32[32,8,128]{2,1,0:T(8,128)S(1)} async-done(((f32[32,8,128]{2,1,0:T(8,128)}), f32[32,8,128]{2,1,0:T(8,128)S(1)}, u32[]{:S(2)}, u32[]{:S(2)}) %all-to-all-start.1) | async-done | bytes 131104 | tf_op jit(solution)/shard_map/all_to_all | solution.py:390
  48.1 0.7 shard_map.142
  48.8 3.9 %all-to-all-start.2 = ((f32[32,8,128]{2,1,0:T(8,128)}), f32[32,8,128]{2,1,0:T(8,128)S(1)}, u32[]{:S(2)}, u32[]{:S(2)}) async-start(f32[32,8,128]{2,1,0:T(8,128)} %get-tuple-element.36.refs_1_), calls=%async_computation.2 | async-start | bytes 262144 | tf_op jit(solution)/shard_map/all_to_all | solution.py:390
  52.7 0.1 collective-permute-start.6
  52.8 10.3 %all-to-all-done.2 = f32[32,8,128]{2,1,0:T(8,128)S(1)} async-done(((f32[32,8,128]{2,1,0:T(8,128)}), f32[32,8,128]{2,1,0:T(8,128)S(1)}, u32[]{:S(2)}, u32[]{:S(2)}) %all-to-all-start.2) | async-done | bytes 131104 | tf_op jit(solution)/shard_map/all_to_all | solution.py:390
  63.1 2.1 %shard_map.144 = (f32[256,128]{1,0:T(8,128)}, f32[8,128]{1,0:T(8,128)S(1)}) custom-call(f32[256,128]{1,0:T(8,128)S(1)} %bitcast.12, f32[16,256,128]{2,1,0:T(8,128)S(1)} %get-tuple-element.35.refs_2_.refs_5_.refs_1_.refs_10_.marks_hbm, f32[2048,128]{1,0:T(8,128)S(1)} %shard_map.138.refs_1_.refs_2_.table_hbm, f32[8,128]{1,0:T(8,128)S(1)} %shard_map.143.refs_3_), custom_call_target="tpu_custom_call" | custom-call | tf_op jit(solution)/shard_map/pallas_call | solution.py:457
  65.2 4.0 %all-to-all-start.3 = ((f32[32,8,128]{2,1,0:T(8,128)}), f32[32,8,128]{2,1,0:T(8,128)S(1)}, u32[]{:S(2)}, u32[]{:S(2)}) async-start(f32[32,8,128]{2,1,0:T(8,128)} %bitcast.8), calls=%async_computation.3 | async-start | bytes 262144 | tf_op jit(solution)/shard_map/all_to_all | solution.py:390
  69.3 10.3 %all-to-all-done.3.refs_0_ = f32[32,8,128]{2,1,0:T(8,128)S(1)} async-done(((f32[32,8,128]{2,1,0:T(8,128)}), f32[32,8,128]{2,1,0:T(8,128)S(1)}, u32[]{:S(2)}, u32[]{:S(2)}) %all-to-all-start.3) | async-done | bytes 131104 | tf_op jit(solution)/shard_map/all_to_all | solution.py:390
  79.6 0.7 shard_map.146
  80.4 3.9 %all-to-all-start.4 = ((f32[32,8,128]{2,1,0:T(8,128)}), f32[32,8,128]{2,1,0:T(8,128)S(1)}, u32[]{:S(2)}, u32[]{:S(2)}) async-start(f32[32,8,128]{2,1,0:T(8,128)} %get-tuple-element.41.refs_9_), calls=%async_computation.4 | async-start | bytes 262144 | tf_op jit(solution)/shard_map/all_to_all | solution.py:390
  84.2 0.1 pad_add_fusion.spot_ref
  84.3 4.7 %shard_map.147.scale_hbm = f32[2048,128]{1,0:T(8,128)S(1)} custom-call(f32[64,2176]{1,0:T(8,128)} %shard_map.139.refs_2_.refs_0_, f32[64,2176]{1,0:T(8,128)} %collective-permute-done.refs_3_.refs_1_, f32[64,2176]{1,0:T(8,128)} %collective-permute-done.1.refs_3_.refs_2_, f32[64,2176]{1,0:T(8,128)} %collective-permute-done.3.refs_3_, ...), custom_call_target="tpu_custom_call" | custom-call | tf_op jit(solution)/shard_map/pallas_call | solution.py:464
  89.1 1.0 copy-done.4
  90.1 4.5 %all-to-all-done.4 = f32[32,8,128]{2,1,0:T(8,128)S(1)} async-done(((f32[32,8,128]{2,1,0:T(8,128)}), f32[32,8,128]{2,1,0:T(8,128)S(1)}, u32[]{:S(2)}, u32[]{:S(2)}) %all-to-all-start.4) | async-done | bytes 131104 | tf_op jit(solution)/shard_map/all_to_all | solution.py:390
  94.5 8.7 %shard_map.148 = (f32[256,128]{1,0:T(8,128)S(1)}, f32[256,128]{1,0:T(8,128)S(1)}, f32[4,256,128]{2,1,0:T(8,128)S(1)}, f32[4,256,128]{2,1,0:T(8,128)S(1)}, f32[8,64,128]{2,1,0:T(8,128)}) custom-call(s32[3]{0:T(128)S(1)} %pad_add_fusion.spot_ref, f32[256,128]{1,0:T(8,128)S(1)} %bitcast.11, f32[16,256,128]{2,1,0:T(8,128)} %copy-done, f32[2048,128]{1,0:T(8,128)} %copy-done.1, ...), custom_call_target="tpu_custom_call" | custom-call | tf_op jit(solution)/shard_map/pallas_call | solution.py:470
  103.2 0.1 collective-permute-start.7
  103.3 5.8 %all-to-all-start.5 = ((f32[8,64,128]{2,1,0:T(8,128)}), f32[8,64,128]{2,1,0:T(8,128)S(1)}, u32[]{:S(2)}, u32[]{:S(2)}) async-start(f32[8,64,128]{2,1,0:T(8,128)} %get-tuple-element.42), calls=%async_computation.5 | async-start | bytes 524288 | tf_op jit(solution)/shard_map/all_to_all | solution.py:390
  109.2 0.1 shard_map.149
  109.2 0.1 collective-permute-start.8
  109.3 6.4 %all-to-all-done.5.refs_0_ = f32[8,64,128]{2,1,0:T(8,128)S(1)} async-done(((f32[8,64,128]{2,1,0:T(8,128)}), f32[8,64,128]{2,1,0:T(8,128)S(1)}, u32[]{:S(2)}, u32[]{:S(2)}) %all-to-all-start.5) | async-done | bytes 262176 | tf_op jit(solution)/shard_map/all_to_all | solution.py:390
  115.7 0.7 shard_map.150
  116.5 3.4 %all-to-all-start.6 = ((f32[4,128,128]{2,1,0:T(8,128)}), f32[4,128,128]{2,1,0:T(8,128)S(1)}, u32[]{:S(2)}, u32[]{:S(2)}) async-start(f32[4,128,128]{2,1,0:T(8,128)} %shard_map.150), calls=%async_computation.6 | async-start | bytes 524288 | tf_op jit(solution)/shard_map/all_to_all | solution.py:390
  119.9 6.6 %all-to-all-done.6.refs_0_ = f32[4,128,128]{2,1,0:T(8,128)S(1)} async-done(((f32[4,128,128]{2,1,0:T(8,128)}), f32[4,128,128]{2,1,0:T(8,128)S(1)}, u32[]{:S(2)}, u32[]{:S(2)}) %all-to-all-start.6) | async-done | bytes 262176 | tf_op jit(solution)/shard_map/all_to_all | solution.py:390
  126.5 0.7 shard_map.152
  127.3 3.4 %all-to-all-start.7 = ((f32[8,72,128]{2,1,0:T(8,128)}), f32[8,72,128]{2,1,0:T(8,128)S(1)}, u32[]{:S(2)}, u32[]{:S(2)}) async-start(f32[8,72,128]{2,1,0:T(8,128)} %shard_map.152), calls=%async_computation.7 | async-start | bytes 589824 | tf_op jit(solution)/shard_map/all_to_all | solution.py:390
  130.7 1.5 %collective-permute-start.9 = (f32[1,256,128]{2,1,0:T(8,128)S(1)}, f32[1,256,128]{2,1,0:T(8,128)S(1)}, u32[]{:S(2)}, u32[]{:S(2)}) collective-permute-start(f32[1,256,128]{2,1,0:T(8,128)S(1)} %get-tuple-element.48.refs_1_), channel_id=1, source_target_pairs={{0,4},{2,6},{4,0},{6,2},{1,5},{3,7},{5,1},{7,3},{8,12},{10,14},{12... | collective-permute-start | bytes 393224 | tf_op jit(solution)/shard_map/ppermute | solution.py:424
  132.3 5.0 %collective-permute-done.9.recv_ref = f32[1,256,128]{2,1,0:T(8,128)S(1)} collective-permute-done((f32[1,256,128]{2,1,0:T(8,128)S(1)}, f32[1,256,128]{2,1,0:T(8,128)S(1)}, u32[]{:S(2)}, u32[]{:S(2)}) %collective-permute-start.9) | collective-permute-done | bytes 131104 | tf_op jit(solution)/shard_map/ppermute | solution.py:424
  137.3 0.7 shard_map.154
  137.9 3.7 %all-to-all-done.7.recv_ref = f32[8,72,128]{2,1,0:T(8,128)S(1)} async-done(((f32[8,72,128]{2,1,0:T(8,128)}), f32[8,72,128]{2,1,0:T(8,128)S(1)}, u32[]{:S(2)}, u32[]{:S(2)}) %all-to-all-start.7) | async-done | bytes 294944 | tf_op jit(solution)/shard_map/all_to_all | solution.py:390
  141.6 0.6 shard_map.153
  (31 shorter events, 0.1 us)
Async XLA Ops:
  0.6 21.8 %copy-start.2 = (f32[2048,128]{1,0:T(8,128)S(1)}, f32[2048,128]{1,0:T(8,128)}, u32[]{:S(2)}) copy-start(f32[2048,128]{1,0:T(8,128)} %refs_8_.1) | copy-start | bytes 3145732
  4.1 24.0 %all-to-all-start = ((f32[32,16,128]{2,1,0:T(8,128)}), f32[32,16,128]{2,1,0:T(8,128)S(1)}, u32[]{:S(2)}, u32[]{:S(2)}) async-start(f32[32,16,128]{2,1,0:T(8,128)} %get-tuple-element.31), calls=%async_computation | async-start | bytes 524288 | tf_op jit(solution)/shard_map/all_to_all | solution.py:390
  15.6 1.0 copy-start.5
  16.7 0.8 copy-start.6
  17.4 0.7 copy-start.8
  18.1 19.8 %copy-start.7 = (f32[64,128]{1,0:T(8,128)S(1)}, f32[64,128]{1,0:T(8,128)}, u32[]{:S(2)}) copy-start(f32[64,128]{1,0:T(8,128)} %refs_0_.7) | copy-start | bytes 98308
  19.0 18.3 %collective-permute-start.2 = (f32[64,2176]{1,0:T(8,128)}, f32[64,2176]{1,0:T(8,128)}, u32[]{:S(2)}, u32[]{:S(2)}) collective-permute-start(f32[64,2176]{1,0:T(8,128)} %shard_map.139.refs_2_.refs_0_), channel_id=1, source_target_pairs={{0,6},{2,4},{4,2},{6,0},{1,7},{3,5},{5,3},{7,1},{8,14},{10,12},{12... | collective-permute-start | bytes 1671176 | tf_op jit(solution)/shard_map/ppermute | solution.py:424
  20.4 17.0 %collective-permute-start.1 = (f32[64,2176]{1,0:T(8,128)}, f32[64,2176]{1,0:T(8,128)}, u32[]{:S(2)}, u32[]{:S(2)}) collective-permute-start(f32[64,2176]{1,0:T(8,128)} %shard_map.139.refs_2_.refs_0_), channel_id=1, source_target_pairs={{0,2},{2,0},{4,6},{6,4},{1,3},{3,1},{5,7},{7,5},{8,10},{10,8},{12,... | collective-permute-start | bytes 1671176 | tf_op jit(solution)/shard_map/ppermute | solution.py:424
  22.2 15.7 %collective-permute-start = (f32[64,2176]{1,0:T(8,128)}, f32[64,2176]{1,0:T(8,128)}, u32[]{:S(2)}, u32[]{:S(2)}) collective-permute-start(f32[64,2176]{1,0:T(8,128)} %shard_map.139.refs_2_.refs_0_), channel_id=1, source_target_pairs={{0,1},{1,0},{2,3},{3,2},{4,5},{5,4},{6,7},{7,6},{8,9},{9,8},{10,11... | collective-permute-start | bytes 1671176 | tf_op jit(solution)/shard_map/ppermute | solution.py:424
  22.3 30.4 %collective-permute-start.4 = (f32[64,2176]{1,0:T(8,128)}, f32[64,2176]{1,0:T(8,128)}, u32[]{:S(2)}, u32[]{:S(2)}) collective-permute-start(f32[64,2176]{1,0:T(8,128)} %shard_map.139.refs_2_.refs_0_), channel_id=1, source_target_pairs={{0,4},{2,6},{4,0},{6,2},{1,5},{3,7},{5,1},{7,3},{8,12},{10,14},{12... | collective-permute-start | bytes 1671176 | tf_op jit(solution)/shard_map/ppermute | solution.py:424
  22.5 1.2 copy-start.3
  24.8 38.4 %copy-start.1 = (f32[2048,128]{1,0:T(8,128)}, f32[2048,128]{1,0:T(8,128)S(1)}, u32[]{:S(2)}) copy-start(f32[2048,128]{1,0:T(8,128)S(1)} %shard_map.138.refs_1_.refs_2_.table_hbm) | copy-start | bytes 3145732
  24.8 23.3 %copy-start.9 = (f32[8,128]{1,0:T(8,128)S(1)}, f32[8,128]{1,0:T(8,128)}, u32[]{:S(2)}) copy-start(f32[8,128]{1,0:T(8,128)} %get-tuple-element.32.refs_2_.refs_1_) | copy-start | bytes 12292
  24.8 23.3 %copy-start.10 = (f32[128]{0:T(128)S(1)}, f32[128]{0:T(128)}, u32[]{:S(2)}) copy-start(f32[128]{0:T(128)} %param.17) | copy-start | bytes 1540
  24.8 23.3 %copy-start.11 = (f32[8,128]{1,0:T(8,128)S(1)}, f32[8,128]{1,0:T(8,128)}, u32[]{:S(2)}) copy-start(f32[8,128]{1,0:T(8,128)} %get-tuple-element.34.refs_2_) | copy-start | bytes 12292
  30.7 48.9 %copy-start = (f32[16,256,128]{2,1,0:T(8,128)}, f32[16,256,128]{2,1,0:T(8,128)S(1)}, u32[]{:S(2)}) copy-start(f32[16,256,128]{2,1,0:T(8,128)S(1)} %get-tuple-element.35.refs_2_.refs_5_.refs_1_.refs_10_.marks_hbm) | copy-start | bytes 6291460
  30.7 17.3 %all-to-all-start.1 = ((f32[32,8,128]{2,1,0:T(8,128)}), f32[32,8,128]{2,1,0:T(8,128)S(1)}, u32[]{:S(2)}, u32[]{:S(2)}) async-start(f32[32,8,128]{2,1,0:T(8,128)} %bitcast.5), calls=%async_computation.1 | async-start | bytes 262144 | tf_op jit(solution)/shard_map/all_to_all | solution.py:390
  37.3 32.0 %collective-permute-start.5 = (f32[64,2176]{1,0:T(8,128)}, f32[64,2176]{1,0:T(8,128)}, u32[]{:S(2)}, u32[]{:S(2)}) collective-permute-start(f32[64,2176]{1,0:T(8,128)} %collective-permute-done.2.refs_4_.refs_6_), channel_id=1, source_target_pairs={{0,1},{1,0},{2,3},{3,2},{4,5},{5,4},{6,7},{7,6},{8,9},{9,8},{10,11... | collective-permute-start | bytes 1671176 | tf_op jit(solution)/shard_map/ppermute | solution.py:424
  37.4 31.9 %collective-permute-start.3 = (f32[64,2176]{1,0:T(8,128)}, f32[64,2176]{1,0:T(8,128)}, u32[]{:S(2)}, u32[]{:S(2)}) collective-permute-start(f32[64,2176]{1,0:T(8,128)} %collective-permute-done.1.refs_3_.refs_2_), channel_id=1, source_target_pairs={{0,1},{1,0},{2,3},{3,2},{4,5},{5,4},{6,7},{7,6},{8,9},{9,8},{10,11... | collective-permute-start | bytes 1671176 | tf_op jit(solution)/shard_map/ppermute | solution.py:424
  48.8 14.3 %all-to-all-start.2 = ((f32[32,8,128]{2,1,0:T(8,128)}), f32[32,8,128]{2,1,0:T(8,128)S(1)}, u32[]{:S(2)}, u32[]{:S(2)}) async-start(f32[32,8,128]{2,1,0:T(8,128)} %get-tuple-element.36.refs_1_), calls=%async_computation.2 | async-start | bytes 262144 | tf_op jit(solution)/shard_map/all_to_all | solution.py:390
  52.7 31.6 %collective-permute-start.6 = (f32[64,2176]{1,0:T(8,128)}, f32[64,2176]{1,0:T(8,128)}, u32[]{:S(2)}, u32[]{:S(2)}) collective-permute-start(f32[64,2176]{1,0:T(8,128)} %collective-permute-done.4.refs_4_), channel_id=1, source_target_pairs={{0,1},{1,0},{2,3},{3,2},{4,5},{5,4},{6,7},{7,6},{8,9},{9,8},{10,11... | collective-permute-start | bytes 1671176 | tf_op jit(solution)/shard_map/ppermute | solution.py:424
  65.2 14.4 %all-to-all-start.3 = ((f32[32,8,128]{2,1,0:T(8,128)}), f32[32,8,128]{2,1,0:T(8,128)S(1)}, u32[]{:S(2)}, u32[]{:S(2)}) async-start(f32[32,8,128]{2,1,0:T(8,128)} %bitcast.8), calls=%async_computation.3 | async-start | bytes 262144 | tf_op jit(solution)/shard_map/all_to_all | solution.py:390
  80.4 14.2 %all-to-all-start.4 = ((f32[32,8,128]{2,1,0:T(8,128)}), f32[32,8,128]{2,1,0:T(8,128)S(1)}, u32[]{:S(2)}, u32[]{:S(2)}) async-start(f32[32,8,128]{2,1,0:T(8,128)} %get-tuple-element.41.refs_9_), calls=%async_computation.4 | async-start | bytes 262144 | tf_op jit(solution)/shard_map/all_to_all | solution.py:390
  89.1 1.0 copy-start.4
  103.2 5.9 %collective-permute-start.7 = (f32[4,256,128]{2,1,0:T(8,128)S(1)}, f32[4,256,128]{2,1,0:T(8,128)S(1)}, u32[]{:S(2)}, u32[]{:S(2)}) collective-permute-start(f32[4,256,128]{2,1,0:T(8,128)S(1)} %get-tuple-element.45), channel_id=1, source_target_pairs={{0,1},{1,0},{2,3},{3,2},{4,5},{5,4},{6,7},{7,6},{8,9},{9,8},{10,11... | collective-permute-start | bytes 1572872 | tf_op jit(solution)/shard_map/ppermute | solution.py:424
  103.3 12.4 %all-to-all-start.5 = ((f32[8,64,128]{2,1,0:T(8,128)}), f32[8,64,128]{2,1,0:T(8,128)S(1)}, u32[]{:S(2)}, u32[]{:S(2)}) async-start(f32[8,64,128]{2,1,0:T(8,128)} %get-tuple-element.42), calls=%async_computation.5 | async-start | bytes 524288 | tf_op jit(solution)/shard_map/all_to_all | solution.py:390
  109.2 10.7 %collective-permute-start.8 = (f32[2,256,128]{2,1,0:T(8,128)S(1)}, f32[2,256,128]{2,1,0:T(8,128)S(1)}, u32[]{:S(2)}, u32[]{:S(2)}) collective-permute-start(f32[2,256,128]{2,1,0:T(8,128)S(1)} %get-tuple-element.46.refs_2_), channel_id=1, source_target_pairs={{0,2},{2,0},{4,6},{6,4},{1,3},{3,1},{5,7},{7,5},{8,10},{10,8},{12,... | collective-permute-start | bytes 786440 | tf_op jit(solution)/shard_map/ppermute | solution.py:424
  116.5 10.1 %all-to-all-start.6 = ((f32[4,128,128]{2,1,0:T(8,128)}), f32[4,128,128]{2,1,0:T(8,128)S(1)}, u32[]{:S(2)}, u32[]{:S(2)}) async-start(f32[4,128,128]{2,1,0:T(8,128)} %shard_map.150), calls=%async_computation.6 | async-start | bytes 524288 | tf_op jit(solution)/shard_map/all_to_all | solution.py:390
  127.3 14.3 %all-to-all-start.7 = ((f32[8,72,128]{2,1,0:T(8,128)}), f32[8,72,128]{2,1,0:T(8,128)S(1)}, u32[]{:S(2)}, u32[]{:S(2)}) async-start(f32[8,72,128]{2,1,0:T(8,128)} %shard_map.152), calls=%async_computation.7 | async-start | bytes 589824 | tf_op jit(solution)/shard_map/all_to_all | solution.py:390
  130.7 6.6 %collective-permute-start.9 = (f32[1,256,128]{2,1,0:T(8,128)S(1)}, f32[1,256,128]{2,1,0:T(8,128)S(1)}, u32[]{:S(2)}, u32[]{:S(2)}) collective-permute-start(f32[1,256,128]{2,1,0:T(8,128)S(1)} %get-tuple-element.48.refs_1_), channel_id=1, source_target_pairs={{0,4},{2,6},{4,0},{6,2},{1,5},{3,7},{5,1},{7,3},{8,12},{10,14},{12... | collective-permute-start | bytes 393224 | tf_op jit(solution)/shard_map/ppermute | solution.py:424

commit v9 on v8

--- a/solution.py
+++ b/solution.py
@@ -77,9 +77,12 @@
     clicks_hbm,
     shape_hbm,
     rate_hbm,
+    cov_hbm,
+    weight_hbm,
     send_ref,
     theta_ref,
     active_ref,
+    own_hbm,
     counts_ref,
     ids_ref,
     clicks_ref,
@@ -99,7 +102,14 @@
             )
         )
     ]
-    for copy in copies:
+    items = cov_hbm.shape[1]
+    pack = [
+        pltpu.make_async_copy(cov_hbm, own_hbm.at[:, pl.ds(0, items)], sems.at[len(copies)]),
+        pltpu.make_async_copy(
+            weight_hbm, own_hbm.at[:, pl.ds(items, weight_hbm.shape[1])], sems.at[len(copies) + 1]
+        ),
+    ]
+    for copy in copies + pack:
         copy.start()
     for copy in copies:
         copy.wait()
@@ -156,6 +166,8 @@
             send_ref[owner, 2 * part + 1 : 2 * part + 2, :] = line[:, LANES:]
         send_ref[owner, 6:8, :] = jnp.zeros((2, LANES), F32)
         send_ref[owner, 8:16, :] = theta
+    for copy in pack:
+        copy.wait()
 
 
 def table_kernel(shape_ref, rate_ref, table_ref):
@@ -222,12 +234,6 @@
     total = ascend(theta_ref[...], marks_ref, table_ref)
     partial_ref[...] = total
     token_ref[...] = total[: token_ref.shape[0]]
-
-
-def pack_kernel(cov_ref, weight_ref, own_ref):
-    items = cov_ref.shape[1]
-    own_ref[:, :items] = cov_ref[...]
-    own_ref[:, items:] = weight_ref[...]
 
 
 def touch_kernel(weight_ref, token_ref):
@@ -269,7 +275,8 @@
         pltpu.make_async_copy(source, cov_ref.at[place], shard_sems.at[place])
         for place, source in enumerate(shard_hbm)
     ]
-    for copy in [copy for group in copies for copy in group] + shard_copies:
+    ahead = 2
+    for copy in [copy for group in copies[:ahead] for copy in group]:
         copy.start()
     theta = theta_ref[...]
     factors = theta.shape[1]
@@ -278,6 +285,8 @@
     for place in range(shards):
         for copy in copies[place]:
             copy.wait()
+        for copy in (copies[place + ahead] if place + ahead < shards else []) + [shard_copies[place]]:
+            copy.start()
         table = table_ref[place]
         marks = jnp.concatenate([marks_ref[place, 0], marks_ref[place, 1]], axis=1)
         ratio_high, ratio_low, part = ascend_block(theta_high, theta_both, marks, table)
@@ -396,18 +405,19 @@
     hbm = pl.BlockSpec(memory_space=pl.ANY)
     small = shape_of(users_here, factors)
     share = shape_of(share_rows, factors)
-    send, theta, active = kernel_call(
+    send, theta, active, own = kernel_call(
         functools.partial(prep_kernel, owners),
-        (shape_of(owners, 16, LANES), small, small),
+        (shape_of(owners, 16, LANES), small, small, shape_of(cov_rows, item_rows + factors)),
         vmem=WHOLE_VMEM,
-        in_specs=[hbm] * 5,
+        in_specs=[hbm] * 7,
+        out_specs=(vmem, vmem, vmem, hbm),
         scratch_shapes=[
             pltpu.SMEM((users_here,), jnp.int32),
             pltpu.VMEM((slot_rows, block_width), jnp.int32),
             pltpu.VMEM((slot_rows, block_width), jnp.int32),
             pltpu.VMEM((users_here, factors), F32),
             pltpu.VMEM((users_here, factors), F32),
-            pltpu.SemaphoreType.DMA((5,)),
+            pltpu.SemaphoreType.DMA((7,)),
         ],
     )(
         block_counts,
@@ -415,6 +425,8 @@
         clicks.reshape(slot_rows, block_width),
         user_shape0,
         user_rate0,
+        covariates,
+        cov_weight,
     )
     recv = exchange(send, user_axes)
     table = kernel_call(table_kernel, shape_of(item_rows, factors))(item_shape, item_rate)
@@ -424,9 +436,6 @@
         return lax.ppermute(array, axis, [(place, place ^ bit) for place in range(lax.axis_size(axis))])
 
     shards = [None] * split_count
-    own = kernel_call(
-        behind(pack_kernel, 2), shape_of(cov_rows, item_rows + factors), in_specs=[vmem, vmem, hbm]
-    )(covariates, cov_weight, theta)
     shards[0] = own
     for distance in (1, 2, 6, 4):
         shards[distance] = swap(own, distance)
@@ -439,18 +448,16 @@
         )(cov_weight, *awaited)
 
     marks, partial = kernel_call(
-        behind(build_kernel, 2),
-        (shape_of(highs, everyone, LANES), shape_of(everyone, factors)),
-        in_specs=[vmem, vmem, hbm],
-    )(recv, table, own)
-    token = touch(partial, marks, shards[1])
+        build_kernel, (shape_of(highs, everyone, LANES), shape_of(everyone, factors))
+    )(recv, table)
+    awaited = (marks,)
     for iteration in range(ITERS - 1):
         parts = exchange(partial.reshape(owners, users_here, factors), user_axes)
         active, theta, spread = kernel_call(
-            behind(functools.partial(update_kernel, activity_shape), 4, 2),
+            behind(functools.partial(update_kernel, activity_shape), 4, len(awaited)),
             (small, small, shape_of(owners, users_here, factors)),
-            in_specs=[vmem] * 4 + [hbm] * 2,
-        )(parts, theta, active, totals, token, marks)
+            in_specs=[vmem] * 4 + [hbm] * len(awaited),
+        )(parts, theta, active, totals, *awaited)
         theta_all = exchange(spread, user_axes).reshape(everyone, factors)
         if iteration == 0:
             token = touch(spread, marks, shards[2], shards[6])
@@ -459,7 +466,7 @@
                 (shape_of(everyone, factors), small),
                 in_specs=[vmem, vmem, vmem, hbm],
             )(theta_all, marks, table, token)
-            token = touch(token, marks, shards[3], shards[4], shards[7])
+            awaited = (touch(token, marks, shards[1], shards[3], shards[4], shards[7]), marks)
         else:
             scale = kernel_call(
                 behind(functools.partial(scale_kernel, split_count), split_count + 1, 2),

time: 143 us -> 156 us (1.091)
  Pallas kernels: 28 us -> 41.8 us
  starting transfers between devices: 48.4 us -> 46.6 us
    pallas_call x1, Pallas kernels: 3.46 us -> 18.7 us  [shards(): kernel_call(functools.partial(prep_kernel, owners), (shape_of(owners, 16,...]
    all_to_all x8, starting transfers between devices: 42.5 us -> 40.5 us  [exchange(): return lax.all_to_all(array, axes, split_axis=0, concat_axis=0, tiled=True)]
    pallas_call x4 -> x3, Pallas kernels: 4.96 us -> 3.45 us  [the longest x1 2 us: shards(): kernel_call(build_kernel, (shape_of(highs, everyone, LANES), shape_of(eve...]
    unnamed x24 -> x22, local copies, waits for them, and re-layouts: 4.72 us -> 4.1 us
  transfers between devices with their start and end apart: 18 -> 18, of which waited for: 9 -> 9; matrix products, arithmetic and copies ran while one was open for 0% -> 0% of each run, Pallas kernels for 10% -> 8%
where the time goes in v9:
time: 156 us; the launch traced here: 155 us
  waiting for transfers between devices  61.7 us (40%)
  starting transfers between devices  46.6 us (30%)
  Pallas kernels  41.8 us (27%)
  local copies, waits for them, and re-layouts  4.1 us (3%)
    all_to_all x8, waiting for transfers between devices, exchange(): return lax.all_to_all(array, axes, split_axis=0, concat_axis=0, tiled=True)  56.6 us
    all_to_all x8, starting transfers between devices, exchange(): return lax.all_to_all(array, axes, split_axis=0, concat_axis=0, tiled=True)  40.5 us
    pallas_call x1, Pallas kernels, shards(): kernel_call(functools.partial(prep_kernel, owners), (shape_of(owners, 16,...  18.7 us
    pallas_call x1, Pallas kernels, shards(): kernel_call(functools.partial(last_kernel, split_count), (shape_of(everyo...  8.9 us
    ppermute x10, starting transfers between devices, swap(): lax.ppermute(array, axis, [(place, place ^ bit) for place in range(lax.ax...  6.1 us
    ppermute x10, waiting for transfers between devices, swap(): lax.ppermute(array, axis, [(place, place ^ bit) for place in range(lax.ax...  5.04 us
    pallas_call x1, Pallas kernels, shards(): kernel_call(behind(functools.partial(scale_kernel, split_count), split_co...  4.58 us
    unnamed x22, local copies, waits for them, and re-layouts  4.1 us
  transfers between devices with their start and end apart: 18, of which 9 were waited for; matrix products, arithmetic and copies ran while one was open for 0% of the time, Pallas kernels for 8%

profile of v9, /device:TPU:2, one launch (start us, length us, event | category | flops | bytes accessed | tf_op | source)
XLA Modules:
  0.0 155.1 jit_solution(7011838484508211766)
XLA Ops:
  0.6 18.7 %shard_map.137 = (f32[32,16,128]{2,1,0:T(8,128)}, f32[8,128]{1,0:T(8,128)}, f32[8,128]{1,0:T(8,128)}, f32[64,2176]{1,0:T(8,128)}) custom-call(s32[8]{0:T(128)} %counts_hbm.1, s32[64,128]{1,0:T(8,128)} %bitcast.17, s32[64,128]{1,0:T(8,128)} %bitcast.18, f32[8,128]{1,0:T(8,128)} %shape_hbm.2, f32[8,128]{1,0:T(8,128)} %rate_hbm.1, f32[64,2048]{1,0:T(8,128)} %cov_hbm.1, ...), custom_call_target="tpu_custom_call" | custom-call | tf_op jit(solution)/shard_map/pallas_call | solution.py:408
  19.4 0.0 copy-start.10
  19.4 11.5 %all-to-all-start = ((f32[32,16,128]{2,1,0:T(8,128)}), f32[32,16,128]{2,1,0:T(8,128)S(1)}, u32[]{:S(2)}, u32[]{:S(2)}) async-start(f32[32,16,128]{2,1,0:T(8,128)} %get-tuple-element.32), calls=%async_computation | async-start | bytes 524288 | tf_op jit(solution)/shard_map/all_to_all | solution.py:399
  30.9 0.0 copy-start.8
  30.9 1.6 %collective-permute-start.1 = (f32[64,2176]{1,0:T(8,128)}, f32[64,2176]{1,0:T(8,128)}, u32[]{:S(2)}, u32[]{:S(2)}) collective-permute-start(f32[64,2176]{1,0:T(8,128)} %get-tuple-element.38.refs_0_), channel_id=1, source_target_pairs={{0,6},{2,4},{4,2},{6,0},{1,7},{3,5},{5,3},{7,1},{8,14},{10,12},{12... | collective-permute-start | bytes 1671176 | tf_op jit(solution)/shard_map/ppermute | solution.py:436
  32.5 1.8 %collective-permute-start = (f32[64,2176]{1,0:T(8,128)}, f32[64,2176]{1,0:T(8,128)}, u32[]{:S(2)}, u32[]{:S(2)}) collective-permute-start(f32[64,2176]{1,0:T(8,128)} %get-tuple-element.38.refs_0_), channel_id=1, source_target_pairs={{0,2},{2,0},{4,6},{6,4},{1,3},{3,1},{5,7},{7,5},{8,10},{10,8},{12,... | collective-permute-start | bytes 1671176 | tf_op jit(solution)/shard_map/ppermute | solution.py:436
  34.3 0.2 collective-permute-start.4
  34.5 1.2 copy-done.2
  35.7 1.2 copy-done.3
  37.0 1.1 shard_map.138.table_ref.refs_2_.table_hbm
  38.1 0.0 copy-start.6
  38.1 5.3 %all-to-all-done.recv_ref = f32[32,16,128]{2,1,0:T(8,128)S(1)} async-done(((f32[32,16,128]{2,1,0:T(8,128)}), f32[32,16,128]{2,1,0:T(8,128)S(1)}, u32[]{:S(2)}, u32[]{:S(2)}) %all-to-all-start) | async-done | bytes 262176 | tf_op jit(solution)/shard_map/all_to_all | solution.py:399
  43.4 2.0 %shard_map.139 = (f32[16,256,128]{2,1,0:T(8,128)S(1)}, f32[256,128]{1,0:T(8,128)S(1)}) custom-call(f32[32,16,128]{2,1,0:T(8,128)S(1)} %all-to-all-done.recv_ref, f32[2048,128]{1,0:T(8,128)S(1)} %shard_map.138.table_ref.refs_2_.table_hbm), custom_call_target="tpu_custom_call" | custom-call | tf_op jit(solution)/shard_map/pallas_call | solution.py:450
  45.4 0.6 copy-done.7
  46.0 4.5 %all-to-all-start.1 = ((f32[32,8,128]{2,1,0:T(8,128)}), f32[32,8,128]{2,1,0:T(8,128)S(1)}, u32[]{:S(2)}, u32[]{:S(2)}) async-start(f32[32,8,128]{2,1,0:T(8,128)} %bitcast.13), calls=%async_computation.1 | async-start | bytes 262144 | tf_op jit(solution)/shard_map/all_to_all | solution.py:399
  50.5 0.1 collective-permute-start.2
  50.7 0.5 collective-permute-start.5
  51.2 0.1 collective-permute-start.3
  51.3 9.6 %all-to-all-done.1.refs_0_ = f32[32,8,128]{2,1,0:T(8,128)S(1)} async-done(((f32[32,8,128]{2,1,0:T(8,128)}), f32[32,8,128]{2,1,0:T(8,128)S(1)}, u32[]{:S(2)}, u32[]{:S(2)}) %all-to-all-start.1) | async-done | bytes 131104 | tf_op jit(solution)/shard_map/all_to_all | solution.py:399
  60.9 0.7 shard_map.140
  61.6 3.9 %all-to-all-start.2 = ((f32[32,8,128]{2,1,0:T(8,128)}), f32[32,8,128]{2,1,0:T(8,128)S(1)}, u32[]{:S(2)}, u32[]{:S(2)}) async-start(f32[32,8,128]{2,1,0:T(8,128)} %get-tuple-element.37.refs_1_), calls=%async_computation.2 | async-start | bytes 262144 | tf_op jit(solution)/shard_map/all_to_all | solution.py:399
  65.5 0.1 collective-permute-start.6
  65.6 10.2 %all-to-all-done.2 = f32[32,8,128]{2,1,0:T(8,128)S(1)} async-done(((f32[32,8,128]{2,1,0:T(8,128)}), f32[32,8,128]{2,1,0:T(8,128)S(1)}, u32[]{:S(2)}, u32[]{:S(2)}) %all-to-all-start.2) | async-done | bytes 131104 | tf_op jit(solution)/shard_map/all_to_all | solution.py:399
  75.8 2.1 %shard_map.142 = (f32[256,128]{1,0:T(8,128)}, f32[8,128]{1,0:T(8,128)S(1)}) custom-call(f32[256,128]{1,0:T(8,128)S(1)} %bitcast.12, f32[16,256,128]{2,1,0:T(8,128)S(1)} %get-tuple-element.36.refs_4_.refs_2_.refs_1_.refs_5_.refs_10_.marks_hbm, f32[2048,128]{1,0:T(8,128)S(1)} %shard_map.138.table_ref.refs_2_.table_hbm, f32[8,128]{1,0:T(8,128)S(1)} %shard_map.141.refs_3_), custom_call_target="tpu_custom_call" | custom-call | tf_op jit(solution)/shard_map/pallas_call | solution.py:464
  77.9 4.0 %all-to-all-start.3 = ((f32[32,8,128]{2,1,0:T(8,128)}), f32[32,8,128]{2,1,0:T(8,128)S(1)}, u32[]{:S(2)}, u32[]{:S(2)}) async-start(f32[32,8,128]{2,1,0:T(8,128)} %bitcast.8), calls=%async_computation.3 | async-start | bytes 262144 | tf_op jit(solution)/shard_map/all_to_all | solution.py:399
  82.0 10.2 %all-to-all-done.3.refs_0_ = f32[32,8,128]{2,1,0:T(8,128)S(1)} async-done(((f32[32,8,128]{2,1,0:T(8,128)}), f32[32,8,128]{2,1,0:T(8,128)S(1)}, u32[]{:S(2)}, u32[]{:S(2)}) %all-to-all-start.3) | async-done | bytes 131104 | tf_op jit(solution)/shard_map/all_to_all | solution.py:399
  92.3 0.7 shard_map.144
  93.0 3.9 %all-to-all-start.4 = ((f32[32,8,128]{2,1,0:T(8,128)}), f32[32,8,128]{2,1,0:T(8,128)S(1)}, u32[]{:S(2)}, u32[]{:S(2)}) async-start(f32[32,8,128]{2,1,0:T(8,128)} %get-tuple-element.43.refs_9_), calls=%async_computation.4 | async-start | bytes 262144 | tf_op jit(solution)/shard_map/all_to_all | solution.py:399
  96.9 0.1 pad_add_fusion.spot_ref
  97.0 4.6 %shard_map.145.scale_hbm = f32[2048,128]{1,0:T(8,128)S(1)} custom-call(f32[64,2176]{1,0:T(8,128)S(1)} %copy-done.5, f32[64,2176]{1,0:T(8,128)} %collective-permute-done.2.refs_3_.refs_1_, f32[64,2176]{1,0:T(8,128)} %collective-permute-done.refs_3_.refs_2_, f32[64,2176]{1,0:T(8,128)} %collective-permute-done.3.refs_4_.refs_3_, ...), custom_call_target="tpu_custom_call" | custom-call | tf_op jit(solution)/shard_map/pallas_call | solution.py:471
  101.6 1.0 copy-done.4
  102.5 4.6 %all-to-all-done.4 = f32[32,8,128]{2,1,0:T(8,128)S(1)} async-done(((f32[32,8,128]{2,1,0:T(8,128)}), f32[32,8,128]{2,1,0:T(8,128)S(1)}, u32[]{:S(2)}, u32[]{:S(2)}) %all-to-all-start.4) | async-done | bytes 131104 | tf_op jit(solution)/shard_map/all_to_all | solution.py:399
  107.1 8.9 %shard_map.146 = (f32[256,128]{1,0:T(8,128)S(1)}, f32[256,128]{1,0:T(8,128)S(1)}, f32[4,256,128]{2,1,0:T(8,128)S(1)}, f32[4,256,128]{2,1,0:T(8,128)S(1)}, f32[8,64,128]{2,1,0:T(8,128)}) custom-call(s32[3]{0:T(128)S(1)} %pad_add_fusion.spot_ref, f32[256,128]{1,0:T(8,128)S(1)} %bitcast.11, f32[16,256,128]{2,1,0:T(8,128)} %copy-done, f32[2048,128]{1,0:T(8,128)} %copy-done.1, ...), custom_call_target="tpu_custom_call" | custom-call | tf_op jit(solution)/shard_map/pallas_call | solution.py:477
  116.1 0.1 collective-permute-start.7
  116.2 5.9 %all-to-all-start.5 = ((f32[8,64,128]{2,1,0:T(8,128)}), f32[8,64,128]{2,1,0:T(8,128)S(1)}, u32[]{:S(2)}, u32[]{:S(2)}) async-start(f32[8,64,128]{2,1,0:T(8,128)} %get-tuple-element.44), calls=%async_computation.5 | async-start | bytes 524288 | tf_op jit(solution)/shard_map/all_to_all | solution.py:399
  122.1 0.1 shard_map.147
  122.1 0.1 collective-permute-start.8
  122.2 6.4 %all-to-all-done.5.refs_0_ = f32[8,64,128]{2,1,0:T(8,128)S(1)} async-done(((f32[8,64,128]{2,1,0:T(8,128)}), f32[8,64,128]{2,1,0:T(8,128)S(1)}, u32[]{:S(2)}, u32[]{:S(2)}) %all-to-all-start.5) | async-done | bytes 262176 | tf_op jit(solution)/shard_map/all_to_all | solution.py:399
  128.6 0.7 shard_map.148
  129.4 3.4 %all-to-all-start.6 = ((f32[4,128,128]{2,1,0:T(8,128)}), f32[4,128,128]{2,1,0:T(8,128)S(1)}, u32[]{:S(2)}, u32[]{:S(2)}) async-start(f32[4,128,128]{2,1,0:T(8,128)} %shard_map.148), calls=%async_computation.6 | async-start | bytes 524288 | tf_op jit(solution)/shard_map/all_to_all | solution.py:399
  132.8 6.6 %all-to-all-done.6.refs_0_ = f32[4,128,128]{2,1,0:T(8,128)S(1)} async-done(((f32[4,128,128]{2,1,0:T(8,128)}), f32[4,128,128]{2,1,0:T(8,128)S(1)}, u32[]{:S(2)}, u32[]{:S(2)}) %all-to-all-start.6) | async-done | bytes 262176 | tf_op jit(solution)/shard_map/all_to_all | solution.py:399
  139.4 0.7 shard_map.150
  140.2 3.4 %all-to-all-start.7 = ((f32[8,72,128]{2,1,0:T(8,128)}), f32[8,72,128]{2,1,0:T(8,128)S(1)}, u32[]{:S(2)}, u32[]{:S(2)}) async-start(f32[8,72,128]{2,1,0:T(8,128)} %shard_map.150), calls=%async_computation.7 | async-start | bytes 589824 | tf_op jit(solution)/shard_map/all_to_all | solution.py:399
  143.6 1.5 collective-permute-start.9
  145.1 5.0 %collective-permute-done.9.recv_ref = f32[1,256,128]{2,1,0:T(8,128)S(1)} collective-permute-done((f32[1,256,128]{2,1,0:T(8,128)S(1)}, f32[1,256,128]{2,1,0:T(8,128)S(1)}, u32[]{:S(2)}, u32[]{:S(2)}) %collective-permute-start.9) | collective-permute-done | bytes 131104 | tf_op jit(solution)/shard_map/ppermute | solution.py:436
  150.1 0.7 shard_map.152
  150.8 3.7 %all-to-all-done.7.recv_ref = f32[8,72,128]{2,1,0:T(8,128)S(1)} async-done(((f32[8,72,128]{2,1,0:T(8,128)}), f32[8,72,128]{2,1,0:T(8,128)S(1)}, u32[]{:S(2)}, u32[]{:S(2)}) %all-to-all-start.7) | async-done | bytes 294944 | tf_op jit(solution)/shard_map/all_to_all | solution.py:399
  154.5 0.6 shard_map.151
  (27 shorter events, 0.1 us)
Async XLA Ops:
  19.4 41.5 %copy-start.9 = (f32[8,128]{1,0:T(8,128)S(1)}, f32[8,128]{1,0:T(8,128)}, u32[]{:S(2)}) copy-start(f32[8,128]{1,0:T(8,128)} %get-tuple-element.34.refs_1_) | copy-start | bytes 12292
  19.4 41.5 %copy-start.10 = (f32[8,128]{1,0:T(8,128)S(1)}, f32[8,128]{1,0:T(8,128)}, u32[]{:S(2)}) copy-start(f32[8,128]{1,0:T(8,128)} %get-tuple-element.35.refs_2_) | copy-start | bytes 12292
  19.4 24.0 %all-to-all-start = ((f32[32,16,128]{2,1,0:T(8,128)}), f32[32,16,128]{2,1,0:T(8,128)S(1)}, u32[]{:S(2)}, u32[]{:S(2)}) async-start(f32[32,16,128]{2,1,0:T(8,128)} %get-tuple-element.32), calls=%async_computation | async-start | bytes 524288 | tf_op jit(solution)/shard_map/all_to_all | solution.py:399
  30.9 30.0 %copy-start.8 = (f32[128]{0:T(128)S(1)}, f32[128]{0:T(128)}, u32[]{:S(2)}) copy-start(f32[128]{0:T(128)} %param.17) | copy-start | bytes 1540
  30.9 19.7 %collective-permute-start.1 = (f32[64,2176]{1,0:T(8,128)}, f32[64,2176]{1,0:T(8,128)}, u32[]{:S(2)}, u32[]{:S(2)}) collective-permute-start(f32[64,2176]{1,0:T(8,128)} %get-tuple-element.38.refs_0_), channel_id=1, source_target_pairs={{0,6},{2,4},{4,2},{6,0},{1,7},{3,5},{5,3},{7,1},{8,14},{10,12},{12... | collective-permute-start | bytes 1671176 | tf_op jit(solution)/shard_map/ppermute | solution.py:436
  32.5 18.6 %collective-permute-start = (f32[64,2176]{1,0:T(8,128)}, f32[64,2176]{1,0:T(8,128)}, u32[]{:S(2)}, u32[]{:S(2)}) collective-permute-start(f32[64,2176]{1,0:T(8,128)} %get-tuple-element.38.refs_0_), channel_id=1, source_target_pairs={{0,2},{2,0},{4,6},{6,4},{1,3},{3,1},{5,7},{7,5},{8,10},{10,8},{12,... | collective-permute-start | bytes 1671176 | tf_op jit(solution)/shard_map/ppermute | solution.py:436
  34.3 31.2 %collective-permute-start.4 = (f32[64,2176]{1,0:T(8,128)}, f32[64,2176]{1,0:T(8,128)}, u32[]{:S(2)}, u32[]{:S(2)}) collective-permute-start(f32[64,2176]{1,0:T(8,128)} %get-tuple-element.38.refs_0_), channel_id=1, source_target_pairs={{0,4},{2,6},{4,0},{6,2},{1,5},{3,7},{5,1},{7,3},{8,12},{10,14},{12... | collective-permute-start | bytes 1671176 | tf_op jit(solution)/shard_map/ppermute | solution.py:436
  34.5 1.2 copy-start.2
  35.7 1.2 copy-start.3
  38.1 37.8 %copy-start.1 = (f32[2048,128]{1,0:T(8,128)}, f32[2048,128]{1,0:T(8,128)S(1)}, u32[]{:S(2)}) copy-start(f32[2048,128]{1,0:T(8,128)S(1)} %shard_map.138.table_ref.refs_2_.table_hbm) | copy-start | bytes 3145732
  38.1 27.6 %copy-start.6 = (f32[64,128]{1,0:T(8,128)S(1)}, f32[64,128]{1,0:T(8,128)}, u32[]{:S(2)}) copy-start(f32[64,128]{1,0:T(8,128)} %refs_0_.3) | copy-start | bytes 98308
  45.4 0.7 copy-start.7
  46.0 46.2 %copy-start = (f32[16,256,128]{2,1,0:T(8,128)}, f32[16,256,128]{2,1,0:T(8,128)S(1)}, u32[]{:S(2)}) copy-start(f32[16,256,128]{2,1,0:T(8,128)S(1)} %get-tuple-element.36.refs_4_.refs_2_.refs_1_.refs_5_.refs_10_.marks_hbm) | copy-start | bytes 6291460
  46.0 14.9 %all-to-all-start.1 = ((f32[32,8,128]{2,1,0:T(8,128)}), f32[32,8,128]{2,1,0:T(8,128)S(1)}, u32[]{:S(2)}, u32[]{:S(2)}) async-start(f32[32,8,128]{2,1,0:T(8,128)} %bitcast.13), calls=%async_computation.1 | async-start | bytes 262144 | tf_op jit(solution)/shard_map/all_to_all | solution.py:399
  50.5 31.4 %collective-permute-start.2 = (f32[64,2176]{1,0:T(8,128)}, f32[64,2176]{1,0:T(8,128)}, u32[]{:S(2)}, u32[]{:S(2)}) collective-permute-start(f32[64,2176]{1,0:T(8,128)} %get-tuple-element.38.refs_0_), channel_id=1, source_target_pairs={{0,1},{1,0},{2,3},{3,2},{4,5},{5,4},{6,7},{7,6},{8,9},{9,8},{10,11... | collective-permute-start | bytes 1671176 | tf_op jit(solution)/shard_map/ppermute | solution.py:436
  50.7 31.3 %collective-permute-start.5 = (f32[64,2176]{1,0:T(8,128)}, f32[64,2176]{1,0:T(8,128)}, u32[]{:S(2)}, u32[]{:S(2)}) collective-permute-start(f32[64,2176]{1,0:T(8,128)} %collective-permute-done.1.refs_4_.refs_6_), channel_id=1, source_target_pairs={{0,1},{1,0},{2,3},{3,2},{4,5},{5,4},{6,7},{7,6},{8,9},{9,8},{10,11... | collective-permute-start | bytes 1671176 | tf_op jit(solution)/shard_map/ppermute | solution.py:436
  51.2 30.8 %collective-permute-start.3 = (f32[64,2176]{1,0:T(8,128)}, f32[64,2176]{1,0:T(8,128)}, u32[]{:S(2)}, u32[]{:S(2)}) collective-permute-start(f32[64,2176]{1,0:T(8,128)} %collective-permute-done.refs_3_.refs_2_), channel_id=1, source_target_pairs={{0,1},{1,0},{2,3},{3,2},{4,5},{5,4},{6,7},{7,6},{8,9},{9,8},{10,11... | collective-permute-start | bytes 1671176 | tf_op jit(solution)/shard_map/ppermute | solution.py:436
  61.6 14.2 %all-to-all-start.2 = ((f32[32,8,128]{2,1,0:T(8,128)}), f32[32,8,128]{2,1,0:T(8,128)S(1)}, u32[]{:S(2)}, u32[]{:S(2)}) async-start(f32[32,8,128]{2,1,0:T(8,128)} %get-tuple-element.37.refs_1_), calls=%async_computation.2 | async-start | bytes 262144 | tf_op jit(solution)/shard_map/all_to_all | solution.py:399
  65.5 31.4 %collective-permute-start.6 = (f32[64,2176]{1,0:T(8,128)}, f32[64,2176]{1,0:T(8,128)}, u32[]{:S(2)}, u32[]{:S(2)}) collective-permute-start(f32[64,2176]{1,0:T(8,128)} %collective-permute-done.4.refs_5_.refs_4_), channel_id=1, source_target_pairs={{0,1},{1,0},{2,3},{3,2},{4,5},{5,4},{6,7},{7,6},{8,9},{9,8},{10,11... | collective-permute-start | bytes 1671176 | tf_op jit(solution)/shard_map/ppermute | solution.py:436
  77.9 14.3 %all-to-all-start.3 = ((f32[32,8,128]{2,1,0:T(8,128)}), f32[32,8,128]{2,1,0:T(8,128)S(1)}, u32[]{:S(2)}, u32[]{:S(2)}) async-start(f32[32,8,128]{2,1,0:T(8,128)} %bitcast.8), calls=%async_computation.3 | async-start | bytes 262144 | tf_op jit(solution)/shard_map/all_to_all | solution.py:399
  82.0 14.9 %copy-start.5 = (f32[64,2176]{1,0:T(8,128)S(1)}, f32[64,2176]{1,0:T(8,128)}, u32[]{:S(2)}) copy-start(f32[64,2176]{1,0:T(8,128)} %get-tuple-element.38.refs_0_) | copy-start | bytes 1671172
  93.0 14.2 %all-to-all-start.4 = ((f32[32,8,128]{2,1,0:T(8,128)}), f32[32,8,128]{2,1,0:T(8,128)S(1)}, u32[]{:S(2)}, u32[]{:S(2)}) async-start(f32[32,8,128]{2,1,0:T(8,128)} %get-tuple-element.43.refs_9_), calls=%async_computation.4 | async-start | bytes 262144 | tf_op jit(solution)/shard_map/all_to_all | solution.py:399
  101.5 1.0 copy-start.4
  116.1 6.0 %collective-permute-start.7 = (f32[4,256,128]{2,1,0:T(8,128)S(1)}, f32[4,256,128]{2,1,0:T(8,128)S(1)}, u32[]{:S(2)}, u32[]{:S(2)}) collective-permute-start(f32[4,256,128]{2,1,0:T(8,128)S(1)} %get-tuple-element.47), channel_id=1, source_target_pairs={{0,1},{1,0},{2,3},{3,2},{4,5},{5,4},{6,7},{7,6},{8,9},{9,8},{10,11... | collective-permute-start | bytes 1572872 | tf_op jit(solution)/shard_map/ppermute | solution.py:436
  116.2 12.5 %all-to-all-start.5 = ((f32[8,64,128]{2,1,0:T(8,128)}), f32[8,64,128]{2,1,0:T(8,128)S(1)}, u32[]{:S(2)}, u32[]{:S(2)}) async-start(f32[8,64,128]{2,1,0:T(8,128)} %get-tuple-element.44), calls=%async_computation.5 | async-start | bytes 524288 | tf_op jit(solution)/shard_map/all_to_all | solution.py:399
  122.1 10.6 %collective-permute-start.8 = (f32[2,256,128]{2,1,0:T(8,128)S(1)}, f32[2,256,128]{2,1,0:T(8,128)S(1)}, u32[]{:S(2)}, u32[]{:S(2)}) collective-permute-start(f32[2,256,128]{2,1,0:T(8,128)S(1)} %get-tuple-element.48.refs_2_), channel_id=1, source_target_pairs={{0,2},{2,0},{4,6},{6,4},{1,3},{3,1},{5,7},{7,5},{8,10},{10,8},{12,... | collective-permute-start | bytes 786440 | tf_op jit(solution)/shard_map/ppermute | solution.py:436
  129.4 10.1 %all-to-all-start.6 = ((f32[4,128,128]{2,1,0:T(8,128)}), f32[4,128,128]{2,1,0:T(8,128)S(1)}, u32[]{:S(2)}, u32[]{:S(2)}) async-start(f32[4,128,128]{2,1,0:T(8,128)} %shard_map.148), calls=%async_computation.6 | async-start | bytes 524288 | tf_op jit(solution)/shard_map/all_to_all | solution.py:399
  140.2 14.3 %all-to-all-start.7 = ((f32[8,72,128]{2,1,0:T(8,128)}), f32[8,72,128]{2,1,0:T(8,128)S(1)}, u32[]{:S(2)}, u32[]{:S(2)}) async-start(f32[8,72,128]{2,1,0:T(8,128)} %shard_map.150), calls=%async_computation.7 | async-start | bytes 589824 | tf_op jit(solution)/shard_map/all_to_all | solution.py:399
  143.6 6.6 %collective-permute-start.9 = (f32[1,256,128]{2,1,0:T(8,128)S(1)}, f32[1,256,128]{2,1,0:T(8,128)S(1)}, u32[]{:S(2)}, u32[]{:S(2)}) collective-permute-start(f32[1,256,128]{2,1,0:T(8,128)S(1)} %get-tuple-element.50.refs_1_), channel_id=1, source_target_pairs={{0,4},{2,6},{4,0},{6,2},{1,5},{3,7},{5,1},{7,3},{8,12},{10,14},{12... | collective-permute-start | bytes 393224 | tf_op jit(solution)/shard_map/ppermute | solution.py:436

commit v10 on v9

--- a/solution.py
+++ b/solution.py
@@ -25,8 +25,7 @@
 NN = (((1,), (0,)), ((), ()))
 TN = (((0,), (0,)), ((), ()))
 LANES = 128
-VMEM_LIMIT = 48 * 1024 * 1024
-WHOLE_VMEM = 60 * 1024 * 1024
+VMEM_LIMIT = 32 * 1024 * 1024
 
 
 def exp_digamma_over(x, rate):
@@ -41,11 +40,11 @@
     return y * jnp.exp(-steps - tail) / rate
 
 
-def kernel_call(kernel, out_shape, vmem=VMEM_LIMIT, **specs):
+def kernel_call(kernel, out_shape, **specs):
     return pl.pallas_call(
         kernel,
         out_shape=out_shape,
-        compiler_params=pltpu.CompilerParams(vmem_limit_bytes=vmem),
+        compiler_params=pltpu.CompilerParams(vmem_limit_bytes=VMEM_LIMIT),
         **specs,
     )
 
@@ -59,6 +58,22 @@
 
 def shape_of(*dims):
     return jax.ShapeDtypeStruct(dims, F32)
+
+
+def on_chip(*dims):
+    return pltpu.VMEM(dims, F32)
+
+
+def off_chip(*dims):
+    return pltpu.HBM(dims, F32)
+
+
+def stay(array):
+    return pltpu.with_memory_space_constraint(array, pltpu.VMEM)
+
+
+def away(array):
+    return pltpu.with_memory_space_constraint(array, pltpu.HBM)
 
 
 def split(x):
@@ -82,7 +97,7 @@
     send_ref,
     theta_ref,
     active_ref,
-    own_hbm,
+    own_ref,
     counts_ref,
     ids_ref,
     clicks_ref,
@@ -104,9 +119,9 @@
     ]
     items = cov_hbm.shape[1]
     pack = [
-        pltpu.make_async_copy(cov_hbm, own_hbm.at[:, pl.ds(0, items)], sems.at[len(copies)]),
+        pltpu.make_async_copy(cov_hbm, own_ref.at[:, pl.ds(0, items)], sems.at[len(copies)]),
         pltpu.make_async_copy(
-            weight_hbm, own_hbm.at[:, pl.ds(items, weight_hbm.shape[1])], sems.at[len(copies) + 1]
+            weight_hbm, own_ref.at[:, pl.ds(items, weight_hbm.shape[1])], sems.at[len(copies) + 1]
         ),
     ]
     for copy in copies + pack:
@@ -170,8 +185,10 @@
         copy.wait()
 
 
-def table_kernel(shape_ref, rate_ref, table_ref):
-    table_ref[...] = exp_digamma_over(shape_ref[...], rate_ref[...])
+def table_kernel(shape_ref, rate_ref, table_ref, base_ref):
+    shapes = shape_ref[...]
+    table_ref[...] = exp_digamma_over(shapes, rate_ref[...])
+    base_ref[...] = (1.0 - step_weight) * shapes + step_weight * item_prior
 
 
 def widen(table):
@@ -252,56 +269,55 @@
         scale_ref[start : start + width, :] = jnp.exp(prior_log) / rate_ref[start : start + width, :]
 
 
-def last_kernel(shards, spot_ref, theta_ref, marks_hbm, table_hbm, scale_hbm, shape_hbm, *refs):
+def last_kernel(shards, spot_ref, theta_ref, marks_ref, table_ref, scale_hbm, base_hbm, *refs):
     shard_hbm, refs = refs[:shards], refs[shards:]
-    partial_ref, base_ref, keep_ref, send_ref, grad_ref = refs[:5]
-    marks_ref, table_ref, scale_ref, shape_ref, cov_ref, score_ref, block_sems, shard_sems = refs[5:]
+    partial_ref, here_ref, keep_hbm, send_hbm, grad_ref = refs[:5]
+    scale_ref, base_ref, cov_ref, stats_ref, score_ref, item_sems, shard_sems, stats_sems = refs[5:]
     spot = spot_ref[2]
-    width = 2 * LANES
-    copies = []
-    for place in range(shards):
-        block = spot ^ place
-        here = pl.ds(pl.multiple_of(block * width, width), width)
-        pairs = [(marks_hbm.at[pl.ds(2 * block, 2)], marks_ref.at[place])]
-        for source, target in ((table_hbm, table_ref), (scale_hbm, scale_ref), (shape_hbm, shape_ref)):
-            pairs.append((source.at[here], target.at[place]))
-        copies.append(
-            [
-                pltpu.make_async_copy(source, target, block_sems.at[place, index])
-                for index, (source, target) in enumerate(pairs)
-            ]
-        )
+    item_copies = [
+        pltpu.make_async_copy(source, target, item_sems.at[index])
+        for index, (source, target) in enumerate(((scale_hbm, scale_ref), (base_hbm, base_ref)))
+    ]
     shard_copies = [
         pltpu.make_async_copy(source, cov_ref.at[place], shard_sems.at[place])
         for place, source in enumerate(shard_hbm)
     ]
-    ahead = 2
-    for copy in [copy for group in copies[:ahead] for copy in group]:
+    stats_copies = [
+        pltpu.make_async_copy(
+            stats_ref.at[place], (send_hbm if place % 2 else keep_hbm).at[place // 2], stats_sems.at[place]
+        )
+        for place in range(shards)
+    ]
+    for copy in item_copies:
         copy.start()
     theta = theta_ref[...]
     factors = theta.shape[1]
     theta_high, theta_both = split_theta(theta)
     total = jnp.zeros(theta.shape, F32)
+    width = 2 * LANES
     for place in range(shards):
-        for copy in copies[place]:
-            copy.wait()
-        for copy in (copies[place + ahead] if place + ahead < shards else []) + [shard_copies[place]]:
-            copy.start()
-        table = table_ref[place]
-        marks = jnp.concatenate([marks_ref[place, 0], marks_ref[place, 1]], axis=1)
+        block = spot ^ place
+        here = pl.ds(pl.multiple_of(block * width, width), width)
+        table = table_ref[here, :]
+        marks = jnp.concatenate([marks_ref[2 * block], marks_ref[2 * block + 1]], axis=1)
         ratio_high, ratio_low, part = ascend_block(theta_high, theta_both, marks, table)
         total = total + part
         wide = dot(ratio_high, theta_both, TN)
-        stats = table * (wide[:, :factors] + wide[:, factors:] + dot(ratio_low, theta_high, TN))
-        target = send_ref if place % 2 else keep_ref
-        target[place // 2] = stats
-        base = (1.0 - step_weight) * shape_ref[place] + step_weight * item_prior
+        stats_ref[place] = table * (wide[:, :factors] + wide[:, factors:] + dot(ratio_low, theta_high, TN))
+        stats_copies[place].start()
+        shard_copies[place].start()
+    partial_ref[...] = total
+    for copy in item_copies:
+        copy.wait()
+    for place in range(shards):
+        here = pl.ds(pl.multiple_of((spot ^ place) * width, width), width)
+        base = base_ref[here, :]
         if place == 0:
-            base_ref[...] = base
-        score = item_prior / shards - scale_ref[place] * (base / shards + step_weight * USER_RATIO * stats)
-        here = pl.ds(pl.multiple_of((spot ^ place) * width, width), width)
+            here_ref[...] = base
+        score = item_prior / shards - scale_ref[here, :] * (
+            base / shards + step_weight * USER_RATIO * stats_ref[place]
+        )
         score_ref[here, :] = jnp.concatenate(split(score), axis=1)
-    partial_ref[...] = total
     rows = grad_ref.shape[1]
     group = 4
     items = score_ref.shape[0]
@@ -314,6 +330,8 @@
         grad = wide[:, :factors] + wide[:, factors:] + dot(cov_low, score_ref[:, :factors], NN)
         for place in range(group):
             grad_ref[spot ^ (first + place)] = grad[place * rows : (place + 1) * rows]
+    for copy in stats_copies:
+        copy.wait()
 
 
 def halve_kernel(held_ref, recv_ref, keep_ref, send_ref):
@@ -407,10 +425,8 @@
     share = shape_of(share_rows, factors)
     send, theta, active, own = kernel_call(
         functools.partial(prep_kernel, owners),
-        (shape_of(owners, 16, LANES), small, small, shape_of(cov_rows, item_rows + factors)),
-        vmem=WHOLE_VMEM,
+        (off_chip(owners, 16, LANES), small, small, off_chip(cov_rows, item_rows + factors)),
         in_specs=[hbm] * 7,
-        out_specs=(vmem, vmem, vmem, hbm),
         scratch_shapes=[
             pltpu.SMEM((users_here,), jnp.int32),
             pltpu.VMEM((slot_rows, block_width), jnp.int32),
@@ -420,23 +436,26 @@
             pltpu.SemaphoreType.DMA((7,)),
         ],
     )(
-        block_counts,
-        item_ids.reshape(slot_rows, block_width),
-        clicks.reshape(slot_rows, block_width),
-        user_shape0,
-        user_rate0,
-        covariates,
-        cov_weight,
+        away(block_counts),
+        away(item_ids.reshape(slot_rows, block_width)),
+        away(clicks.reshape(slot_rows, block_width)),
+        away(user_shape0),
+        away(user_rate0),
+        away(covariates),
+        away(cov_weight),
     )
     recv = exchange(send, user_axes)
-    table = kernel_call(table_kernel, shape_of(item_rows, factors))(item_shape, item_rate)
+    table, base = kernel_call(table_kernel, (on_chip(item_rows, factors), off_chip(item_rows, factors)))(
+        item_shape, item_rate
+    )
+    table = stay(table)
 
     def swap(array, distance):
         axis, bit = ("core", 1) if distance == 1 else ("x", distance // 2)
         return lax.ppermute(array, axis, [(place, place ^ bit) for place in range(lax.axis_size(axis))])
 
     shards = [None] * split_count
-    shards[0] = own
+    shards[0] = away(own)
     for distance in (1, 2, 6, 4):
         shards[distance] = swap(own, distance)
     for distance in (2, 6, 4):
@@ -448,53 +467,55 @@
         )(cov_weight, *awaited)
 
     marks, partial = kernel_call(
-        build_kernel, (shape_of(highs, everyone, LANES), shape_of(everyone, factors))
+        build_kernel, (on_chip(highs, everyone, LANES), off_chip(everyone, factors))
     )(recv, table)
-    awaited = (marks,)
+    marks = stay(marks)
+    awaited = ()
     for iteration in range(ITERS - 1):
         parts = exchange(partial.reshape(owners, users_here, factors), user_axes)
         active, theta, spread = kernel_call(
             behind(functools.partial(update_kernel, activity_shape), 4, len(awaited)),
-            (small, small, shape_of(owners, users_here, factors)),
+            (small, small, off_chip(owners, users_here, factors)),
             in_specs=[vmem] * 4 + [hbm] * len(awaited),
         )(parts, theta, active, totals, *awaited)
         theta_all = exchange(spread, user_axes).reshape(everyone, factors)
         if iteration == 0:
-            token = touch(spread, marks, shards[2], shards[6])
+            token = touch(away(spread), shards[2], shards[6])
             partial, token = kernel_call(
                 behind(ascend_kernel, 3),
-                (shape_of(everyone, factors), small),
+                (off_chip(everyone, factors), small),
                 in_specs=[vmem, vmem, vmem, hbm],
             )(theta_all, marks, table, token)
-            awaited = (touch(token, marks, shards[1], shards[3], shards[4], shards[7]), marks)
+            awaited = (touch(token, shards[1], shards[3], shards[4], shards[7]),)
         else:
             scale = kernel_call(
-                behind(functools.partial(scale_kernel, split_count), split_count + 1, 2),
-                shape_of(item_rows, factors),
-                in_specs=[vmem] * (split_count + 1) + [hbm] * 2,
-            )(*shards, item_rate, spread, marks)
+                behind(functools.partial(scale_kernel, split_count), split_count + 1),
+                off_chip(item_rows, factors),
+                in_specs=[vmem] * (split_count + 1) + [hbm],
+            )(*shards, item_rate, away(spread))
     half = split_count // 2
     partial, base, held, moved, grad = kernel_call(
         functools.partial(last_kernel, split_count),
         (
             shape_of(everyone, factors),
-            share,
-            shape_of(half, share_rows, factors),
-            shape_of(half, share_rows, factors),
-            shape_of(split_count, cov_rows, factors),
+            shape_of(share_rows, factors),
+            off_chip(half, share_rows, factors),
+            off_chip(half, share_rows, factors),
+            off_chip(split_count, cov_rows, factors),
         ),
-        in_specs=[smem, vmem] + [hbm] * (4 + split_count),
+        in_specs=[smem] + [vmem] * 3 + [hbm] * (2 + split_count),
+        out_specs=(vmem, vmem, hbm, hbm, vmem),
         scratch_shapes=[
-            pltpu.VMEM((split_count, highs // split_count, everyone, LANES), F32),
+            pltpu.VMEM((item_rows, factors), F32),
+            pltpu.VMEM((item_rows, factors), F32),
+            pltpu.VMEM((split_count, cov_rows, item_rows + factors), F32),
             pltpu.VMEM((split_count, share_rows, factors), F32),
-            pltpu.VMEM((split_count, share_rows, factors), F32),
-            pltpu.VMEM((split_count, share_rows, factors), F32),
-            pltpu.VMEM((split_count, cov_rows, item_rows + factors), F32),
             pltpu.VMEM((item_rows, 2 * factors), BF16),
-            pltpu.SemaphoreType.DMA((split_count, 4)),
+            pltpu.SemaphoreType.DMA((2,)),
+            pltpu.SemaphoreType.DMA((split_count,)),
             pltpu.SemaphoreType.DMA((split_count,)),
         ],
-    )(spot, theta_all, marks, table, scale, item_shape, *shards)
+    )(spot, theta_all, marks, table, away(scale), away(base), *shards)
 
     def halve(held, moved, distance):
         half = held.shape[0] // 2
@@ -503,13 +524,13 @@
     grad = exchange(grad, item_axes)
     held, moved = halve(held, moved, 1)
     both = kernel_call(
-        behind(join_kernel, 2), shape_of(y_size, z_size * users_here + cov_rows, factors), in_specs=[vmem, vmem, hbm]
+        behind(join_kernel, 2), off_chip(y_size, z_size * users_here + cov_rows, factors), in_specs=[vmem, vmem, hbm]
     )(grad, partial, moved)
     both = exchange(both, ("y",))
     held, moved = halve(held, moved, 2)
     both = kernel_call(
         behind(functools.partial(fan_kernel, users_here), 1),
-        shape_of(z_size, users_here + cov_rows, factors),
+        off_chip(z_size, users_here + cov_rows, factors),
         in_specs=[vmem, hbm],
     )(both, moved)
     both = exchange(both, ("z",))

time: 156 us -> 142 us (0.910)
  Pallas kernels: 41.8 us -> 28.4 us
  waiting for transfers between devices: 61.7 us -> 59.2 us
    pallas_call x6, Pallas kernels: 25.4 us -> 11.3 us  [the longest x1 3.56 us: shards(): kernel_call(functools.partial(prep_kernel, owners), (off_chip(owners, 16,...]
    all_to_all x8, waiting for transfers between devices: 56.6 us -> 54.1 us  [exchange(): return lax.all_to_all(array, axes, split_axis=0, concat_axis=0, tiled=True)]
    unnamed x22 -> x12, local copies, waits for them, and re-layouts: 4.1 us -> 4.73 us
  transfers between devices with their start and end apart: 18 -> 18, of which waited for: 9 -> 9; matrix products, arithmetic and copies ran while one was open for 0% -> 0% of each run, Pallas kernels for 8% -> 10%
where the time goes in v10:
time: 142 us; the launch traced here: 141 us
  waiting for transfers between devices  59.2 us (42%)
  starting transfers between devices  47.7 us (34%)
  Pallas kernels  28.4 us (20%)
  local copies, waits for them, and re-layouts  4.73 us (3%)
    all_to_all x8, waiting for transfers between devices, exchange(): return lax.all_to_all(array, axes, split_axis=0, concat_axis=0, tiled=True)  54.1 us
    all_to_all x8, starting transfers between devices, exchange(): return lax.all_to_all(array, axes, split_axis=0, concat_axis=0, tiled=True)  41.7 us
    pallas_call x1, Pallas kernels, shards(): kernel_call(functools.partial(last_kernel, split_count), (shape_of(everyo...  8.85 us
    ppermute x10, starting transfers between devices, swap(): lax.ppermute(array, axis, [(place, place ^ bit) for place in range(lax.ax...  6.01 us
    pallas_call x1, Pallas kernels, shards(): kernel_call(behind(functools.partial(scale_kernel, split_count), split_co...  5.39 us
    ppermute x10, waiting for transfers between devices, swap(): lax.ppermute(array, axis, [(place, place ^ bit) for place in range(lax.ax...  5.04 us
    unnamed x12, local copies, waits for them, and re-layouts  4.73 us
    pallas_call x1, Pallas kernels, shards(): kernel_call(functools.partial(prep_kernel, owners), (off_chip(owners, 16,...  3.56 us
  transfers between devices with their start and end apart: 18, of which 9 were waited for; matrix products, arithmetic and copies ran while one was open for 0% of the time, Pallas kernels for 10%

profile of v10, /device:TPU:2, one launch (start us, length us, event | category | flops | bytes accessed | tf_op | source)
XLA Modules:
  0.0 141.0 jit_solution(2042635254579726804)
XLA Ops:
  0.6 3.6 %shard_map.137 = (f32[32,16,128]{2,1,0:T(8,128)}, f32[8,128]{1,0:T(8,128)S(1)}, f32[8,128]{1,0:T(8,128)S(1)}, f32[64,2176]{1,0:T(8,128)}) custom-call(s32[8]{0:T(128)} %counts_hbm.1, s32[64,128]{1,0:T(8,128)} %bitcast.18, s32[64,128]{1,0:T(8,128)} %bitcast.19, f32[8,128]{1,0:T(8,128)} %shape_hbm.1, f32[8,128]{1,0:T(8,128)} %rate_hbm.1, f32[64,2048]{1,0:T(8,128)} %cov_hbm.1, ...), custom_call_target="tpu_custom_call" | custom-call | tf_op jit(solution)/shard_map/pallas_call | solution.py:426
  4.2 0.0 copy-start.5
  4.2 0.0 copy-start.4
  4.2 11.5 %all-to-all-start = ((f32[32,16,128]{2,1,0:T(8,128)}), f32[32,16,128]{2,1,0:T(8,128)S(1)}, u32[]{:S(2)}, u32[]{:S(2)}) async-start(f32[32,16,128]{2,1,0:T(8,128)} %get-tuple-element.34), calls=%async_computation | async-start | bytes 524288 | tf_op jit(solution)/shard_map/all_to_all | solution.py:417
  15.7 1.6 %collective-permute-start.1 = (f32[64,2176]{1,0:T(8,128)}, f32[64,2176]{1,0:T(8,128)}, u32[]{:S(2)}, u32[]{:S(2)}) collective-permute-start(f32[64,2176]{1,0:T(8,128)} %get-tuple-element.41.refs_0_), channel_id=1, source_target_pairs={{0,6},{2,4},{4,2},{6,0},{1,7},{3,5},{5,3},{7,1},{8,14},{10,12},{12... | collective-permute-start | bytes 1671176 | tf_op jit(solution)/shard_map/ppermute | solution.py:455
  17.3 1.8 %collective-permute-start = (f32[64,2176]{1,0:T(8,128)}, f32[64,2176]{1,0:T(8,128)}, u32[]{:S(2)}, u32[]{:S(2)}) collective-permute-start(f32[64,2176]{1,0:T(8,128)} %get-tuple-element.41.refs_0_), channel_id=1, source_target_pairs={{0,2},{2,0},{4,6},{6,4},{1,3},{3,1},{5,7},{7,5},{8,10},{10,8},{12,... | collective-permute-start | bytes 1671176 | tf_op jit(solution)/shard_map/ppermute | solution.py:455
  19.1 0.2 collective-permute-start.4
  19.3 1.2 copy-done
  20.5 1.2 copy-done.2
  21.8 1.5 %shard_map.138 = (f32[2048,128]{1,0:T(8,128)S(1)}, f32[2048,128]{1,0:T(8,128)}) custom-call(f32[2048,128]{1,0:T(8,128)S(1)} %copy-done.2, f32[2048,128]{1,0:T(8,128)S(1)} %copy-done), custom_call_target="tpu_custom_call" | custom-call | tf_op jit(solution)/shard_map/pallas_call | solution.py:448
  23.3 4.9 %all-to-all-done.recv_ref = f32[32,16,128]{2,1,0:T(8,128)S(1)} async-done(((f32[32,16,128]{2,1,0:T(8,128)}), f32[32,16,128]{2,1,0:T(8,128)S(1)}, u32[]{:S(2)}, u32[]{:S(2)}) %all-to-all-start) | async-done | bytes 262176 | tf_op jit(solution)/shard_map/all_to_all | solution.py:417
  28.2 2.7 %shard_map.139 = (f32[16,256,128]{2,1,0:T(8,128)S(1)}, f32[256,128]{1,0:T(8,128)}) custom-call(f32[32,16,128]{2,1,0:T(8,128)S(1)} %all-to-all-done.recv_ref, f32[2048,128]{1,0:T(8,128)S(1)} %get-tuple-element.35.table_ref.refs_2_), custom_call_target="tpu_custom_call" | custom-call | tf_op jit(solution)/shard_map/pallas_call | solution.py:469
  30.9 4.9 %all-to-all-start.1 = ((f32[32,8,128]{2,1,0:T(8,128)}), f32[32,8,128]{2,1,0:T(8,128)S(1)}, u32[]{:S(2)}, u32[]{:S(2)}) async-start(f32[32,8,128]{2,1,0:T(8,128)} %bitcast.16), calls=%async_computation.1 | async-start | bytes 262144 | tf_op jit(solution)/shard_map/all_to_all | solution.py:417
  35.8 0.1 collective-permute-start.2
  35.9 0.0 collective-permute-done.1.refs_3_.refs_6_
  35.9 0.5 collective-permute-start.5
  36.4 0.1 collective-permute-start.3
  36.5 9.6 %all-to-all-done.1.refs_0_ = f32[32,8,128]{2,1,0:T(8,128)S(1)} async-done(((f32[32,8,128]{2,1,0:T(8,128)}), f32[32,8,128]{2,1,0:T(8,128)S(1)}, u32[]{:S(2)}, u32[]{:S(2)}) %all-to-all-start.1) | async-done | bytes 131104 | tf_op jit(solution)/shard_map/all_to_all | solution.py:417
  46.1 0.7 shard_map.140
  46.8 3.9 %all-to-all-start.2 = ((f32[32,8,128]{2,1,0:T(8,128)}), f32[32,8,128]{2,1,0:T(8,128)S(1)}, u32[]{:S(2)}, u32[]{:S(2)}) async-start(f32[32,8,128]{2,1,0:T(8,128)} %get-tuple-element.39.refs_1_), calls=%async_computation.2 | async-start | bytes 262144 | tf_op jit(solution)/shard_map/all_to_all | solution.py:417
  50.7 0.1 collective-permute-start.6
  50.8 10.2 %all-to-all-done.2 = f32[32,8,128]{2,1,0:T(8,128)S(1)} async-done(((f32[32,8,128]{2,1,0:T(8,128)}), f32[32,8,128]{2,1,0:T(8,128)S(1)}, u32[]{:S(2)}, u32[]{:S(2)}) %all-to-all-start.2) | async-done | bytes 131104 | tf_op jit(solution)/shard_map/all_to_all | solution.py:417
  61.0 2.1 %shard_map.142 = (f32[256,128]{1,0:T(8,128)}, f32[8,128]{1,0:T(8,128)S(1)}) custom-call(f32[256,128]{1,0:T(8,128)S(1)} %bitcast.12, f32[16,256,128]{2,1,0:T(8,128)S(1)} %get-tuple-element.40.refs_1_.marks_ref, f32[2048,128]{1,0:T(8,128)S(1)} %get-tuple-element.35.table_ref.refs_2_, f32[8,128]{1,0:T(8,128)S(1)} %shard_map.141.refs_3_), custom_call_target="tpu_custom_call" | custom-call | tf_op jit(solution)/shard_map/pallas_call | solution.py:484
  63.1 4.0 %all-to-all-start.3 = ((f32[32,8,128]{2,1,0:T(8,128)}), f32[32,8,128]{2,1,0:T(8,128)S(1)}, u32[]{:S(2)}, u32[]{:S(2)}) async-start(f32[32,8,128]{2,1,0:T(8,128)} %bitcast.17), calls=%async_computation.3 | async-start | bytes 262144 | tf_op jit(solution)/shard_map/all_to_all | solution.py:417
  67.2 10.2 %all-to-all-done.3.refs_0_ = f32[32,8,128]{2,1,0:T(8,128)S(1)} async-done(((f32[32,8,128]{2,1,0:T(8,128)}), f32[32,8,128]{2,1,0:T(8,128)S(1)}, u32[]{:S(2)}, u32[]{:S(2)}) %all-to-all-start.3) | async-done | bytes 131104 | tf_op jit(solution)/shard_map/all_to_all | solution.py:417
  77.4 0.7 shard_map.144
  78.2 3.9 %all-to-all-start.4 = ((f32[32,8,128]{2,1,0:T(8,128)}), f32[32,8,128]{2,1,0:T(8,128)S(1)}, u32[]{:S(2)}, u32[]{:S(2)}) async-start(f32[32,8,128]{2,1,0:T(8,128)} %get-tuple-element.46.refs_9_), calls=%async_computation.4 | async-start | bytes 262144 | tf_op jit(solution)/shard_map/all_to_all | solution.py:417
  82.0 0.1 pad_add_fusion.spot_ref
  82.1 1.2 copy-done.1
  83.4 5.4 %shard_map.145.scale_hbm = f32[2048,128]{1,0:T(8,128)} custom-call(f32[64,2176]{1,0:T(8,128)} %get-tuple-element.41.refs_0_, f32[64,2176]{1,0:T(8,128)} %collective-permute-done.2.refs_2_.refs_1_, f32[64,2176]{1,0:T(8,128)} %collective-permute-done.refs_2_, f32[64,2176]{1,0:T(8,128)} %collective-permute-done.3.refs_3_, ...), custom_call_target="tpu_custom_call" | custom-call | tf_op jit(solution)/shard_map/pallas_call | solution.py:491
  88.7 3.6 %all-to-all-done.4 = f32[32,8,128]{2,1,0:T(8,128)S(1)} async-done(((f32[32,8,128]{2,1,0:T(8,128)}), f32[32,8,128]{2,1,0:T(8,128)S(1)}, u32[]{:S(2)}, u32[]{:S(2)}) %all-to-all-start.4) | async-done | bytes 131104 | tf_op jit(solution)/shard_map/all_to_all | solution.py:417
  92.3 8.9 %shard_map.146 = (f32[256,128]{1,0:T(8,128)S(1)}, f32[256,128]{1,0:T(8,128)S(1)}, f32[4,256,128]{2,1,0:T(8,128)}, f32[4,256,128]{2,1,0:T(8,128)}, f32[8,64,128]{2,1,0:T(8,128)}) custom-call(s32[3]{0:T(128)S(1)} %pad_add_fusion.spot_ref, f32[256,128]{1,0:T(8,128)S(1)} %bitcast.11, f32[16,256,128]{2,1,0:T(8,128)S(1)} %get-tuple-element.40.refs_1_.marks_ref, ...), custom_call_target="tpu_custom_call" | custom-call | tf_op jit(solution)/shard_map/pallas_call | solution.py:497
  101.2 0.1 collective-permute-start.7
  101.3 5.9 %all-to-all-start.5 = ((f32[8,64,128]{2,1,0:T(8,128)}), f32[8,64,128]{2,1,0:T(8,128)S(1)}, u32[]{:S(2)}, u32[]{:S(2)}) async-start(f32[8,64,128]{2,1,0:T(8,128)} %get-tuple-element.48), calls=%async_computation.5 | async-start | bytes 524288 | tf_op jit(solution)/shard_map/all_to_all | solution.py:417
  107.2 1.0 copy-done.3
  108.2 0.1 shard_map.147
  108.3 0.1 collective-permute-start.8
  108.4 5.3 %all-to-all-done.5.refs_0_ = f32[8,64,128]{2,1,0:T(8,128)S(1)} async-done(((f32[8,64,128]{2,1,0:T(8,128)}), f32[8,64,128]{2,1,0:T(8,128)S(1)}, u32[]{:S(2)}, u32[]{:S(2)}) %all-to-all-start.5) | async-done | bytes 262176 | tf_op jit(solution)/shard_map/all_to_all | solution.py:417
  113.8 0.7 shard_map.148
  114.5 3.4 %all-to-all-start.6 = ((f32[4,128,128]{2,1,0:T(8,128)}), f32[4,128,128]{2,1,0:T(8,128)S(1)}, u32[]{:S(2)}, u32[]{:S(2)}) async-start(f32[4,128,128]{2,1,0:T(8,128)} %shard_map.148), calls=%async_computation.6 | async-start | bytes 524288 | tf_op jit(solution)/shard_map/all_to_all | solution.py:417
  117.9 6.6 %all-to-all-done.6.refs_0_ = f32[4,128,128]{2,1,0:T(8,128)S(1)} async-done(((f32[4,128,128]{2,1,0:T(8,128)}), f32[4,128,128]{2,1,0:T(8,128)S(1)}, u32[]{:S(2)}, u32[]{:S(2)}) %all-to-all-start.6) | async-done | bytes 262176 | tf_op jit(solution)/shard_map/all_to_all | solution.py:417
  124.5 0.7 shard_map.150
  125.3 4.3 %all-to-all-start.7 = ((f32[8,72,128]{2,1,0:T(8,128)}), f32[8,72,128]{2,1,0:T(8,128)S(1)}, u32[]{:S(2)}, u32[]{:S(2)}) async-start(f32[8,72,128]{2,1,0:T(8,128)} %shard_map.150), calls=%async_computation.7 | async-start | bytes 589824 | tf_op jit(solution)/shard_map/all_to_all | solution.py:417
  129.5 1.5 %collective-permute-start.9 = (f32[1,256,128]{2,1,0:T(8,128)S(1)}, f32[1,256,128]{2,1,0:T(8,128)S(1)}, u32[]{:S(2)}, u32[]{:S(2)}) collective-permute-start(f32[1,256,128]{2,1,0:T(8,128)S(1)} %get-tuple-element.54.refs_1_), channel_id=1, source_target_pairs={{0,4},{2,6},{4,0},{6,2},{1,5},{3,7},{5,1},{7,3},{8,12},{10,14},{12... | collective-permute-start | bytes 393224 | tf_op jit(solution)/shard_map/ppermute | solution.py:455
  131.0 5.0 %collective-permute-done.9.recv_ref = f32[1,256,128]{2,1,0:T(8,128)S(1)} collective-permute-done((f32[1,256,128]{2,1,0:T(8,128)S(1)}, f32[1,256,128]{2,1,0:T(8,128)S(1)}, u32[]{:S(2)}, u32[]{:S(2)}) %collective-permute-start.9) | collective-permute-done | bytes 131104 | tf_op jit(solution)/shard_map/ppermute | solution.py:455
  136.0 0.7 shard_map.152
  136.7 3.7 %all-to-all-done.7.recv_ref = f32[8,72,128]{2,1,0:T(8,128)S(1)} async-done(((f32[8,72,128]{2,1,0:T(8,128)}), f32[8,72,128]{2,1,0:T(8,128)S(1)}, u32[]{:S(2)}, u32[]{:S(2)}) %all-to-all-start.7) | async-done | bytes 294944 | tf_op jit(solution)/shard_map/all_to_all | solution.py:417
  140.4 0.6 shard_map.151
  (17 shorter events, 0.1 us)
Async XLA Ops:
  4.2 41.9 %copy-start.5 = (f32[128]{0:T(128)S(1)}, f32[128]{0:T(128)}, u32[]{:S(2)}) copy-start(f32[128]{0:T(128)} %param.17) | copy-start | bytes 1540
  4.2 46.6 %copy-start.4 = (f32[64,128]{1,0:T(8,128)S(1)}, f32[64,128]{1,0:T(8,128)}, u32[]{:S(2)}) copy-start(f32[64,128]{1,0:T(8,128)} %refs_0_.3) | copy-start | bytes 98308
  4.2 24.0 %all-to-all-start = ((f32[32,16,128]{2,1,0:T(8,128)}), f32[32,16,128]{2,1,0:T(8,128)S(1)}, u32[]{:S(2)}, u32[]{:S(2)}) async-start(f32[32,16,128]{2,1,0:T(8,128)} %get-tuple-element.34), calls=%async_computation | async-start | bytes 524288 | tf_op jit(solution)/shard_map/all_to_all | solution.py:417
  15.7 20.1 %collective-permute-start.1 = (f32[64,2176]{1,0:T(8,128)}, f32[64,2176]{1,0:T(8,128)}, u32[]{:S(2)}, u32[]{:S(2)}) collective-permute-start(f32[64,2176]{1,0:T(8,128)} %get-tuple-element.41.refs_0_), channel_id=1, source_target_pairs={{0,6},{2,4},{4,2},{6,0},{1,7},{3,5},{5,3},{7,1},{8,14},{10,12},{12... | collective-permute-start | bytes 1671176 | tf_op jit(solution)/shard_map/ppermute | solution.py:455
  17.3 19.0 %collective-permute-start = (f32[64,2176]{1,0:T(8,128)}, f32[64,2176]{1,0:T(8,128)}, u32[]{:S(2)}, u32[]{:S(2)}) collective-permute-start(f32[64,2176]{1,0:T(8,128)} %get-tuple-element.41.refs_0_), channel_id=1, source_target_pairs={{0,2},{2,0},{4,6},{6,4},{1,3},{3,1},{5,7},{7,5},{8,10},{10,8},{12,... | collective-permute-start | bytes 1671176 | tf_op jit(solution)/shard_map/ppermute | solution.py:455
  19.1 31.6 %collective-permute-start.4 = (f32[64,2176]{1,0:T(8,128)}, f32[64,2176]{1,0:T(8,128)}, u32[]{:S(2)}, u32[]{:S(2)}) collective-permute-start(f32[64,2176]{1,0:T(8,128)} %get-tuple-element.41.refs_0_), channel_id=1, source_target_pairs={{0,4},{2,6},{4,0},{6,2},{1,5},{3,7},{5,1},{7,3},{8,12},{10,14},{12... | collective-permute-start | bytes 1671176 | tf_op jit(solution)/shard_map/ppermute | solution.py:455
  19.3 1.2 copy-start
  20.5 1.2 copy-start.2
  30.9 15.3 %all-to-all-start.1 = ((f32[32,8,128]{2,1,0:T(8,128)}), f32[32,8,128]{2,1,0:T(8,128)S(1)}, u32[]{:S(2)}, u32[]{:S(2)}) async-start(f32[32,8,128]{2,1,0:T(8,128)} %bitcast.16), calls=%async_computation.1 | async-start | bytes 262144 | tf_op jit(solution)/shard_map/all_to_all | solution.py:417
  35.8 31.4 %collective-permute-start.2 = (f32[64,2176]{1,0:T(8,128)}, f32[64,2176]{1,0:T(8,128)}, u32[]{:S(2)}, u32[]{:S(2)}) collective-permute-start(f32[64,2176]{1,0:T(8,128)} %get-tuple-element.41.refs_0_), channel_id=1, source_target_pairs={{0,1},{1,0},{2,3},{3,2},{4,5},{5,4},{6,7},{7,6},{8,9},{9,8},{10,11... | collective-permute-start | bytes 1671176 | tf_op jit(solution)/shard_map/ppermute | solution.py:455
  35.9 31.3 %collective-permute-start.5 = (f32[64,2176]{1,0:T(8,128)}, f32[64,2176]{1,0:T(8,128)}, u32[]{:S(2)}, u32[]{:S(2)}) collective-permute-start(f32[64,2176]{1,0:T(8,128)} %collective-permute-done.1.refs_3_.refs_6_), channel_id=1, source_target_pairs={{0,1},{1,0},{2,3},{3,2},{4,5},{5,4},{6,7},{7,6},{8,9},{9,8},{10,11... | collective-permute-start | bytes 1671176 | tf_op jit(solution)/shard_map/ppermute | solution.py:455
  36.4 30.8 %collective-permute-start.3 = (f32[64,2176]{1,0:T(8,128)}, f32[64,2176]{1,0:T(8,128)}, u32[]{:S(2)}, u32[]{:S(2)}) collective-permute-start(f32[64,2176]{1,0:T(8,128)} %collective-permute-done.refs_2_), channel_id=1, source_target_pairs={{0,1},{1,0},{2,3},{3,2},{4,5},{5,4},{6,7},{7,6},{8,9},{9,8},{10,11... | collective-permute-start | bytes 1671176 | tf_op jit(solution)/shard_map/ppermute | solution.py:455
  46.8 14.2 %all-to-all-start.2 = ((f32[32,8,128]{2,1,0:T(8,128)}), f32[32,8,128]{2,1,0:T(8,128)S(1)}, u32[]{:S(2)}, u32[]{:S(2)}) async-start(f32[32,8,128]{2,1,0:T(8,128)} %get-tuple-element.39.refs_1_), calls=%async_computation.2 | async-start | bytes 262144 | tf_op jit(solution)/shard_map/all_to_all | solution.py:417
  50.7 31.4 %collective-permute-start.6 = (f32[64,2176]{1,0:T(8,128)}, f32[64,2176]{1,0:T(8,128)}, u32[]{:S(2)}, u32[]{:S(2)}) collective-permute-start(f32[64,2176]{1,0:T(8,128)} %collective-permute-done.4.refs_4_), channel_id=1, source_target_pairs={{0,1},{1,0},{2,3},{3,2},{4,5},{5,4},{6,7},{7,6},{8,9},{9,8},{10,11... | collective-permute-start | bytes 1671176 | tf_op jit(solution)/shard_map/ppermute | solution.py:455
  63.1 14.3 %all-to-all-start.3 = ((f32[32,8,128]{2,1,0:T(8,128)}), f32[32,8,128]{2,1,0:T(8,128)S(1)}, u32[]{:S(2)}, u32[]{:S(2)}) async-start(f32[32,8,128]{2,1,0:T(8,128)} %bitcast.17), calls=%async_computation.3 | async-start | bytes 262144 | tf_op jit(solution)/shard_map/all_to_all | solution.py:417
  78.2 14.2 %all-to-all-start.4 = ((f32[32,8,128]{2,1,0:T(8,128)}), f32[32,8,128]{2,1,0:T(8,128)S(1)}, u32[]{:S(2)}, u32[]{:S(2)}) async-start(f32[32,8,128]{2,1,0:T(8,128)} %get-tuple-element.46.refs_9_), calls=%async_computation.4 | async-start | bytes 262144 | tf_op jit(solution)/shard_map/all_to_all | solution.py:417
  82.1 1.2 copy-start.1
  101.2 6.0 %collective-permute-start.7 = (f32[4,256,128]{2,1,0:T(8,128)}, f32[4,256,128]{2,1,0:T(8,128)S(1)}, u32[]{:S(2)}, u32[]{:S(2)}) collective-permute-start(f32[4,256,128]{2,1,0:T(8,128)} %get-tuple-element.51), channel_id=1, source_target_pairs={{0,1},{1,0},{2,3},{3,2},{4,5},{5,4},{6,7},{7,6},{8,9},{9,8},{10,11... | collective-permute-start | bytes 1572872 | tf_op jit(solution)/shard_map/ppermute | solution.py:455
  101.3 12.5 %all-to-all-start.5 = ((f32[8,64,128]{2,1,0:T(8,128)}), f32[8,64,128]{2,1,0:T(8,128)S(1)}, u32[]{:S(2)}, u32[]{:S(2)}) async-start(f32[8,64,128]{2,1,0:T(8,128)} %get-tuple-element.48), calls=%async_computation.5 | async-start | bytes 524288 | tf_op jit(solution)/shard_map/all_to_all | solution.py:417
  107.2 1.0 copy-start.3
  108.3 9.6 %collective-permute-start.8 = (f32[2,256,128]{2,1,0:T(8,128)S(1)}, f32[2,256,128]{2,1,0:T(8,128)S(1)}, u32[]{:S(2)}, u32[]{:S(2)}) collective-permute-start(f32[2,256,128]{2,1,0:T(8,128)S(1)} %get-tuple-element.52.refs_2_), channel_id=1, source_target_pairs={{0,2},{2,0},{4,6},{6,4},{1,3},{3,1},{5,7},{7,5},{8,10},{10,8},{12,... | collective-permute-start | bytes 786440 | tf_op jit(solution)/shard_map/ppermute | solution.py:455
  114.5 10.1 %all-to-all-start.6 = ((f32[4,128,128]{2,1,0:T(8,128)}), f32[4,128,128]{2,1,0:T(8,128)S(1)}, u32[]{:S(2)}, u32[]{:S(2)}) async-start(f32[4,128,128]{2,1,0:T(8,128)} %shard_map.148), calls=%async_computation.6 | async-start | bytes 524288 | tf_op jit(solution)/shard_map/all_to_all | solution.py:417
  125.3 15.1 %all-to-all-start.7 = ((f32[8,72,128]{2,1,0:T(8,128)}), f32[8,72,128]{2,1,0:T(8,128)S(1)}, u32[]{:S(2)}, u32[]{:S(2)}) async-start(f32[8,72,128]{2,1,0:T(8,128)} %shard_map.150), calls=%async_computation.7 | async-start | bytes 589824 | tf_op jit(solution)/shard_map/all_to_all | solution.py:417
  129.5 6.5 %collective-permute-start.9 = (f32[1,256,128]{2,1,0:T(8,128)S(1)}, f32[1,256,128]{2,1,0:T(8,128)S(1)}, u32[]{:S(2)}, u32[]{:S(2)}) collective-permute-start(f32[1,256,128]{2,1,0:T(8,128)S(1)} %get-tuple-element.54.refs_1_), channel_id=1, source_target_pairs={{0,4},{2,6},{4,0},{6,2},{1,5},{3,7},{5,1},{7,3},{8,12},{10,14},{12... | collective-permute-start | bytes 393224 | tf_op jit(solution)/shard_map/ppermute | solution.py:455

commit v11 on v10

--- a/solution.py
+++ b/solution.py
@@ -247,14 +247,8 @@
     partial_ref[...] = ascend(theta, marks_ref, table_ref)
 
 
-def ascend_kernel(theta_ref, marks_ref, table_ref, partial_ref, token_ref):
-    total = ascend(theta_ref[...], marks_ref, table_ref)
-    partial_ref[...] = total
-    token_ref[...] = total[: token_ref.shape[0]]
-
-
-def touch_kernel(weight_ref, token_ref):
-    token_ref[...] = weight_ref[: token_ref.shape[0], :]
+def ascend_kernel(theta_ref, marks_ref, table_ref, partial_ref):
+    partial_ref[...] = ascend(theta_ref[...], marks_ref, table_ref)
 
 
 def scale_kernel(shards, *refs):
@@ -269,27 +263,10 @@
         scale_ref[start : start + width, :] = jnp.exp(prior_log) / rate_ref[start : start + width, :]
 
 
-def last_kernel(shards, spot_ref, theta_ref, marks_ref, table_ref, scale_hbm, base_hbm, *refs):
-    shard_hbm, refs = refs[:shards], refs[shards:]
-    partial_ref, here_ref, keep_hbm, send_hbm, grad_ref = refs[:5]
-    scale_ref, base_ref, cov_ref, stats_ref, score_ref, item_sems, shard_sems, stats_sems = refs[5:]
+def last_kernel(shards, spot_ref, theta_ref, marks_ref, table_ref, scale_ref, base_ref, *refs):
+    shard_refs = refs[:shards]
+    partial_ref, here_ref, keep_ref, send_ref, grad_ref, score_ref = refs[shards:]
     spot = spot_ref[2]
-    item_copies = [
-        pltpu.make_async_copy(source, target, item_sems.at[index])
-        for index, (source, target) in enumerate(((scale_hbm, scale_ref), (base_hbm, base_ref)))
-    ]
-    shard_copies = [
-        pltpu.make_async_copy(source, cov_ref.at[place], shard_sems.at[place])
-        for place, source in enumerate(shard_hbm)
-    ]
-    stats_copies = [
-        pltpu.make_async_copy(
-            stats_ref.at[place], (send_hbm if place % 2 else keep_hbm).at[place // 2], stats_sems.at[place]
-        )
-        for place in range(shards)
-    ]
-    for copy in item_copies:
-        copy.start()
     theta = theta_ref[...]
     factors = theta.shape[1]
     theta_high, theta_both = split_theta(theta)
@@ -303,35 +280,24 @@
         ratio_high, ratio_low, part = ascend_block(theta_high, theta_both, marks, table)
         total = total + part
         wide = dot(ratio_high, theta_both, TN)
-        stats_ref[place] = table * (wide[:, :factors] + wide[:, factors:] + dot(ratio_low, theta_high, TN))
-        stats_copies[place].start()
-        shard_copies[place].start()
-    partial_ref[...] = total
-    for copy in item_copies:
-        copy.wait()
-    for place in range(shards):
-        here = pl.ds(pl.multiple_of((spot ^ place) * width, width), width)
+        stats = table * (wide[:, :factors] + wide[:, factors:] + dot(ratio_low, theta_high, TN))
+        (send_ref if place % 2 else keep_ref)[place // 2] = stats
         base = base_ref[here, :]
         if place == 0:
             here_ref[...] = base
-        score = item_prior / shards - scale_ref[here, :] * (
-            base / shards + step_weight * USER_RATIO * stats_ref[place]
-        )
+        score = item_prior / shards - scale_ref[here, :] * (base / shards + step_weight * USER_RATIO * stats)
         score_ref[here, :] = jnp.concatenate(split(score), axis=1)
+    partial_ref[...] = total
     rows = grad_ref.shape[1]
     group = 4
     items = score_ref.shape[0]
     for first in range(0, shards, group):
-        for copy in shard_copies[first : first + group]:
-            copy.wait()
-        cov = jnp.concatenate([cov_ref[place, :, :items] for place in range(first, first + group)], axis=0)
+        cov = jnp.concatenate([shard[:, :items] for shard in shard_refs[first : first + group]], axis=0)
         cov_high, cov_low = split(cov)
         wide = dot(cov_high, score_ref[...], NN)
         grad = wide[:, :factors] + wide[:, factors:] + dot(cov_low, score_ref[:, :factors], NN)
         for place in range(group):
             grad_ref[spot ^ (first + place)] = grad[place * rows : (place + 1) * rows]
-    for copy in stats_copies:
-        copy.wait()
 
 
 def halve_kernel(held_ref, recv_ref, keep_ref, send_ref):
@@ -455,19 +421,14 @@
         return lax.ppermute(array, axis, [(place, place ^ bit) for place in range(lax.axis_size(axis))])
 
     shards = [None] * split_count
-    shards[0] = away(own)
+    shards[0] = own
     for distance in (1, 2, 6, 4):
         shards[distance] = swap(own, distance)
     for distance in (2, 6, 4):
         shards[distance + 1] = swap(shards[distance], 1)
 
-    def touch(*awaited):
-        return kernel_call(
-            behind(touch_kernel, 1, len(awaited)), small, in_specs=[vmem] + [hbm] * len(awaited)
-        )(cov_weight, *awaited)
-
     marks, partial = kernel_call(
-        build_kernel, (on_chip(highs, everyone, LANES), off_chip(everyone, factors))
+        build_kernel, (on_chip(highs, everyone, LANES), shape_of(everyone, factors))
     )(recv, table)
     marks = stay(marks)
     awaited = ()
@@ -475,24 +436,23 @@
         parts = exchange(partial.reshape(owners, users_here, factors), user_axes)
         active, theta, spread = kernel_call(
             behind(functools.partial(update_kernel, activity_shape), 4, len(awaited)),
-            (small, small, off_chip(owners, users_here, factors)),
+            (small, small, shape_of(owners, users_here, factors)),
             in_specs=[vmem] * 4 + [hbm] * len(awaited),
         )(parts, theta, active, totals, *awaited)
         theta_all = exchange(spread, user_axes).reshape(everyone, factors)
         if iteration == 0:
-            token = touch(away(spread), shards[2], shards[6])
-            partial, token = kernel_call(
-                behind(ascend_kernel, 3),
-                (off_chip(everyone, factors), small),
-                in_specs=[vmem, vmem, vmem, hbm],
-            )(theta_all, marks, table, token)
-            awaited = (touch(token, shards[1], shards[3], shards[4], shards[7]),)
+            partial = kernel_call(
+                behind(ascend_kernel, 3, 2),
+                shape_of(everyone, factors),
+                in_specs=[vmem, vmem, vmem, hbm, hbm],
+            )(theta_all, marks, table, away(shards[2]), away(shards[6]))
+            awaited = [away(shards[place]) for place in (1, 3, 4, 7)]
         else:
             scale = kernel_call(
                 behind(functools.partial(scale_kernel, split_count), split_count + 1),
                 off_chip(item_rows, factors),
                 in_specs=[vmem] * (split_count + 1) + [hbm],
-            )(*shards, item_rate, away(spread))
+            )(*[away(shard) for shard in shards], away(item_rate), away(spread))
     half = split_count // 2
     partial, base, held, moved, grad = kernel_call(
         functools.partial(last_kernel, split_count),
@@ -503,19 +463,10 @@
             off_chip(half, share_rows, factors),
             off_chip(split_count, cov_rows, factors),
         ),
-        in_specs=[smem] + [vmem] * 3 + [hbm] * (2 + split_count),
-        out_specs=(vmem, vmem, hbm, hbm, vmem),
-        scratch_shapes=[
-            pltpu.VMEM((item_rows, factors), F32),
-            pltpu.VMEM((item_rows, factors), F32),
-            pltpu.VMEM((split_count, cov_rows, item_rows + factors), F32),
-            pltpu.VMEM((split_count, share_rows, factors), F32),
-            pltpu.VMEM((item_rows, 2 * factors), BF16),
-            pltpu.SemaphoreType.DMA((2,)),
-            pltpu.SemaphoreType.DMA((split_count,)),
-            pltpu.SemaphoreType.DMA((split_count,)),
-        ],
-    )(spot, theta_all, marks, table, away(scale), away(base), *shards)
+        in_specs=[smem] + [vmem] * (5 + split_count),
+        scratch_shapes=[pltpu.VMEM((item_rows, 2 * factors), BF16)],
+    )(spot, theta_all, marks, table, away(scale), away(base), *[away(shard) for shard in shards])
+    held = away(held)
 
     def halve(held, moved, distance):
         half = held.shape[0] // 2

time: 142 us -> 140 us (0.986)
  local copies, waits for them, and re-layouts: 4.73 us -> 2.45 us
    unnamed x12 -> x6, local copies, waits for them, and re-layouts: 4.73 us -> 2.45 us
    pallas_call x4 -> x2, Pallas kernels: 4.78 us -> 4.77 us  [the longest x1 2.66 us: shards(): kernel_call(build_kernel, (on_chip(highs, everyone, LANES), shape_of(ever...]
  transfers between devices with their start and end apart: 18 -> 18, of which waited for: 9 -> 9; matrix products, arithmetic and copies ran while one was open for 0% -> 0% of each run, Pallas kernels for 10% -> 11%
where the time goes in v11:
time: 140 us; the launch traced here: 139 us
  waiting for transfers between devices  60.1 us (43%)
  starting transfers between devices  46.9 us (34%)
  Pallas kernels  29 us (21%)
  local copies, waits for them, and re-layouts  2.45 us (2%)
    all_to_all x8, waiting for transfers between devices, exchange(): return lax.all_to_all(array, axes, split_axis=0, concat_axis=0, tiled=True)  55.1 us
    all_to_all x8, starting transfers between devices, exchange(): return lax.all_to_all(array, axes, split_axis=0, concat_axis=0, tiled=True)  40.9 us
    pallas_call x1, Pallas kernels, shards(): kernel_call(functools.partial(last_kernel, split_count), (shape_of(everyo...  8.1 us
    ppermute x10, starting transfers between devices, swap(): lax.ppermute(array, axis, [(place, place ^ bit) for place in range(lax.ax...  6 us
    pallas_call x1, Pallas kernels, shards(): kernel_call(behind(functools.partial(scale_kernel, split_count), split_co...  5.71 us
    ppermute x10, waiting for transfers between devices, swap(): lax.ppermute(array, axis, [(place, place ^ bit) for place in range(lax.ax...  5.04 us
    pallas_call x1, Pallas kernels, shards(): kernel_call(functools.partial(prep_kernel, owners), (off_chip(owners, 16,...  3.56 us
  transfers between devices with their start and end apart: 18, of which 9 were waited for; matrix products, arithmetic and copies ran while one was open for 0% of the time, Pallas kernels for 11%

profile of v11, /device:TPU:2, one launch (start us, length us, event | category | flops | bytes accessed | tf_op | source)
XLA Modules:
  0.0 139.4 jit_solution(7377361060909667456)
XLA Ops:
  0.6 3.6 %shard_map.137 = (f32[32,16,128]{2,1,0:T(8,128)}, f32[8,128]{1,0:T(8,128)S(1)}, f32[8,128]{1,0:T(8,128)S(1)}, f32[64,2176]{1,0:T(8,128)}) custom-call(s32[8]{0:T(128)} %counts_hbm.1, s32[64,128]{1,0:T(8,128)} %bitcast.16, s32[64,128]{1,0:T(8,128)} %bitcast.17, f32[8,128]{1,0:T(8,128)} %shape_hbm.1, f32[8,128]{1,0:T(8,128)} %rate_hbm.1, f32[64,2048]{1,0:T(8,128)} %cov_hbm.1, ...), custom_call_target="tpu_custom_call" | custom-call | tf_op jit(solution)/shard_map/pallas_call | solution.py:392
  4.2 0.0 copy-start.2
  4.2 11.5 %all-to-all-start = ((f32[32,16,128]{2,1,0:T(8,128)}), f32[32,16,128]{2,1,0:T(8,128)S(1)}, u32[]{:S(2)}, u32[]{:S(2)}) async-start(f32[32,16,128]{2,1,0:T(8,128)} %get-tuple-element.32), calls=%async_computation | async-start | bytes 524288 | tf_op jit(solution)/shard_map/all_to_all | solution.py:383
  15.7 1.6 %collective-permute-start.1 = (f32[64,2176]{1,0:T(8,128)}, f32[64,2176]{1,0:T(8,128)}, u32[]{:S(2)}, u32[]{:S(2)}) collective-permute-start(f32[64,2176]{1,0:T(8,128)} %get-tuple-element.39.refs_0_), channel_id=1, source_target_pairs={{0,6},{2,4},{4,2},{6,0},{1,7},{3,5},{5,3},{7,1},{8,14},{10,12},{12... | collective-permute-start | bytes 1671176 | tf_op jit(solution)/shard_map/ppermute | solution.py:421
  17.3 1.8 %collective-permute-start = (f32[64,2176]{1,0:T(8,128)}, f32[64,2176]{1,0:T(8,128)}, u32[]{:S(2)}, u32[]{:S(2)}) collective-permute-start(f32[64,2176]{1,0:T(8,128)} %get-tuple-element.39.refs_0_), channel_id=1, source_target_pairs={{0,2},{2,0},{4,6},{6,4},{1,3},{3,1},{5,7},{7,5},{8,10},{10,8},{12,... | collective-permute-start | bytes 1671176 | tf_op jit(solution)/shard_map/ppermute | solution.py:421
  19.1 0.2 collective-permute-start.4
  19.3 1.2 copy-done
  20.5 1.2 copy-done.1
  21.7 1.5 %shard_map.138 = (f32[2048,128]{1,0:T(8,128)S(1)}, f32[2048,128]{1,0:T(8,128)}) custom-call(f32[2048,128]{1,0:T(8,128)S(1)} %copy-done.1, f32[2048,128]{1,0:T(8,128)S(1)} %copy-done), custom_call_target="tpu_custom_call" | custom-call | tf_op jit(solution)/shard_map/pallas_call | solution.py:414
  23.3 4.9 %all-to-all-done.recv_ref = f32[32,16,128]{2,1,0:T(8,128)S(1)} async-done(((f32[32,16,128]{2,1,0:T(8,128)}), f32[32,16,128]{2,1,0:T(8,128)S(1)}, u32[]{:S(2)}, u32[]{:S(2)}) %all-to-all-start) | async-done | bytes 262176 | tf_op jit(solution)/shard_map/all_to_all | solution.py:383
  28.2 2.7 %shard_map.139 = (f32[16,256,128]{2,1,0:T(8,128)S(1)}, f32[256,128]{1,0:T(8,128)}) custom-call(f32[32,16,128]{2,1,0:T(8,128)S(1)} %all-to-all-done.recv_ref, f32[2048,128]{1,0:T(8,128)S(1)} %get-tuple-element.33.table_ref.refs_2_), custom_call_target="tpu_custom_call" | custom-call | tf_op jit(solution)/shard_map/pallas_call | solution.py:430
  30.8 4.9 %all-to-all-start.1 = ((f32[32,8,128]{2,1,0:T(8,128)}), f32[32,8,128]{2,1,0:T(8,128)S(1)}, u32[]{:S(2)}, u32[]{:S(2)}) async-start(f32[32,8,128]{2,1,0:T(8,128)} %bitcast.5), calls=%async_computation.1 | async-start | bytes 262144 | tf_op jit(solution)/shard_map/all_to_all | solution.py:383
  35.7 0.1 collective-permute-start.2
  35.8 0.0 collective-permute-done.1.refs_4_.refs_6_
  35.8 0.5 collective-permute-start.5
  36.3 0.0 collective-permute-done.refs_3_.refs_2_
  36.3 0.1 collective-permute-start.3
  36.4 9.6 %all-to-all-done.1.refs_0_ = f32[32,8,128]{2,1,0:T(8,128)S(1)} async-done(((f32[32,8,128]{2,1,0:T(8,128)}), f32[32,8,128]{2,1,0:T(8,128)S(1)}, u32[]{:S(2)}, u32[]{:S(2)}) %all-to-all-start.1) | async-done | bytes 131104 | tf_op jit(solution)/shard_map/all_to_all | solution.py:383
  46.1 0.7 shard_map.140
  46.8 3.9 %all-to-all-start.2 = ((f32[32,8,128]{2,1,0:T(8,128)}), f32[32,8,128]{2,1,0:T(8,128)S(1)}, u32[]{:S(2)}, u32[]{:S(2)}) async-start(f32[32,8,128]{2,1,0:T(8,128)} %get-tuple-element.37), calls=%async_computation.2 | async-start | bytes 262144 | tf_op jit(solution)/shard_map/all_to_all | solution.py:383
  50.7 0.0 collective-permute-done.4.refs_6_.refs_4_
  50.7 0.1 collective-permute-start.6
  50.8 10.2 %all-to-all-done.2 = f32[32,8,128]{2,1,0:T(8,128)S(1)} async-done(((f32[32,8,128]{2,1,0:T(8,128)}), f32[32,8,128]{2,1,0:T(8,128)S(1)}, u32[]{:S(2)}, u32[]{:S(2)}) %all-to-all-start.2) | async-done | bytes 131104 | tf_op jit(solution)/shard_map/all_to_all | solution.py:383
  61.0 2.1 %shard_map.141 = f32[256,128]{1,0:T(8,128)} custom-call(f32[256,128]{1,0:T(8,128)S(1)} %bitcast.12, f32[16,256,128]{2,1,0:T(8,128)S(1)} %get-tuple-element.38.refs_1_.marks_ref, f32[2048,128]{1,0:T(8,128)S(1)} %get-tuple-element.33.table_ref.refs_2_, f32[64,2176]{1,0:T(8,128)} %collective-permute-done.refs_3_.refs_2_, ...), custom_call_target="tpu_custom_call" | custom-call | tf_op jit(solution)/shard_map/pallas_call | solution.py:444
  63.1 4.0 %all-to-all-start.3 = ((f32[32,8,128]{2,1,0:T(8,128)}), f32[32,8,128]{2,1,0:T(8,128)S(1)}, u32[]{:S(2)}, u32[]{:S(2)}) async-start(f32[32,8,128]{2,1,0:T(8,128)} %bitcast.8), calls=%async_computation.3 | async-start | bytes 262144 | tf_op jit(solution)/shard_map/all_to_all | solution.py:383
  67.1 0.0 collective-permute-done.2.refs_4_.refs_1_
  67.1 0.0 collective-permute-done.5.refs_7_
  67.1 10.3 %all-to-all-done.3.refs_0_ = f32[32,8,128]{2,1,0:T(8,128)S(1)} async-done(((f32[32,8,128]{2,1,0:T(8,128)}), f32[32,8,128]{2,1,0:T(8,128)S(1)}, u32[]{:S(2)}, u32[]{:S(2)}) %all-to-all-start.3) | async-done | bytes 131104 | tf_op jit(solution)/shard_map/all_to_all | solution.py:383
  77.4 0.7 shard_map.142
  78.1 3.9 %all-to-all-start.4 = ((f32[32,8,128]{2,1,0:T(8,128)}), f32[32,8,128]{2,1,0:T(8,128)S(1)}, u32[]{:S(2)}, u32[]{:S(2)}) async-start(f32[32,8,128]{2,1,0:T(8,128)} %get-tuple-element.42.refs_9_), calls=%async_computation.4 | async-start | bytes 262144 | tf_op jit(solution)/shard_map/all_to_all | solution.py:383
  82.0 0.1 pad_add_fusion.spot_ref
  82.1 5.7 %shard_map.143.scale_ref = f32[2048,128]{1,0:T(8,128)} custom-call(f32[64,2176]{1,0:T(8,128)} %get-tuple-element.39.refs_0_, f32[64,2176]{1,0:T(8,128)} %collective-permute-done.2.refs_4_.refs_1_, f32[64,2176]{1,0:T(8,128)} %collective-permute-done.refs_3_.refs_2_, f32[64,2176]{1,0:T(8,128)} %collective-permute-done.3.refs_5_.refs_3_, ...), custom_call_target="tpu_custom_call" | custom-call | tf_op jit(solution)/shard_map/pallas_call | solution.py:451
  87.8 4.5 %all-to-all-done.4 = f32[32,8,128]{2,1,0:T(8,128)S(1)} async-done(((f32[32,8,128]{2,1,0:T(8,128)}), f32[32,8,128]{2,1,0:T(8,128)S(1)}, u32[]{:S(2)}, u32[]{:S(2)}) %all-to-all-start.4) | async-done | bytes 131104 | tf_op jit(solution)/shard_map/all_to_all | solution.py:383
  92.3 8.1 %shard_map.144 = (f32[256,128]{1,0:T(8,128)S(1)}, f32[256,128]{1,0:T(8,128)S(1)}, f32[4,256,128]{2,1,0:T(8,128)}, f32[4,256,128]{2,1,0:T(8,128)}, f32[8,64,128]{2,1,0:T(8,128)}) custom-call(s32[3]{0:T(128)S(1)} %pad_add_fusion.spot_ref, f32[256,128]{1,0:T(8,128)S(1)} %bitcast.11, f32[16,256,128]{2,1,0:T(8,128)S(1)} %get-tuple-element.38.refs_1_.marks_ref, ...), custom_call_target="tpu_custom_call" | custom-call | tf_op jit(solution)/shard_map/pallas_call | solution.py:457
  100.4 5.9 %all-to-all-start.5 = ((f32[8,64,128]{2,1,0:T(8,128)}), f32[8,64,128]{2,1,0:T(8,128)S(1)}, u32[]{:S(2)}, u32[]{:S(2)}) async-start(f32[8,64,128]{2,1,0:T(8,128)} %get-tuple-element.44), calls=%async_computation.5 | async-start | bytes 524288 | tf_op jit(solution)/shard_map/all_to_all | solution.py:383
  106.3 1.1 shard_map.145
  107.4 0.1 collective-permute-start.8
  107.5 5.4 %all-to-all-done.5.refs_0_ = f32[8,64,128]{2,1,0:T(8,128)S(1)} async-done(((f32[8,64,128]{2,1,0:T(8,128)}), f32[8,64,128]{2,1,0:T(8,128)S(1)}, u32[]{:S(2)}, u32[]{:S(2)}) %all-to-all-start.5) | async-done | bytes 262176 | tf_op jit(solution)/shard_map/all_to_all | solution.py:383
  112.9 0.7 shard_map.146
  113.6 3.4 %all-to-all-start.6 = ((f32[4,128,128]{2,1,0:T(8,128)}), f32[4,128,128]{2,1,0:T(8,128)S(1)}, u32[]{:S(2)}, u32[]{:S(2)}) async-start(f32[4,128,128]{2,1,0:T(8,128)} %shard_map.146), calls=%async_computation.6 | async-start | bytes 524288 | tf_op jit(solution)/shard_map/all_to_all | solution.py:383
  117.1 6.6 %all-to-all-done.6.refs_0_ = f32[4,128,128]{2,1,0:T(8,128)S(1)} async-done(((f32[4,128,128]{2,1,0:T(8,128)}), f32[4,128,128]{2,1,0:T(8,128)S(1)}, u32[]{:S(2)}, u32[]{:S(2)}) %all-to-all-start.6) | async-done | bytes 262176 | tf_op jit(solution)/shard_map/all_to_all | solution.py:383
  123.6 0.7 shard_map.148
  124.4 3.4 %all-to-all-start.7 = ((f32[8,72,128]{2,1,0:T(8,128)}), f32[8,72,128]{2,1,0:T(8,128)S(1)}, u32[]{:S(2)}, u32[]{:S(2)}) async-start(f32[8,72,128]{2,1,0:T(8,128)} %shard_map.148), calls=%async_computation.7 | async-start | bytes 589824 | tf_op jit(solution)/shard_map/all_to_all | solution.py:383
  127.8 1.5 %collective-permute-start.9 = (f32[1,256,128]{2,1,0:T(8,128)S(1)}, f32[1,256,128]{2,1,0:T(8,128)S(1)}, u32[]{:S(2)}, u32[]{:S(2)}) collective-permute-start(f32[1,256,128]{2,1,0:T(8,128)S(1)} %get-tuple-element.50.refs_1_), channel_id=1, source_target_pairs={{0,4},{2,6},{4,0},{6,2},{1,5},{3,7},{5,1},{7,3},{8,12},{10,14},{12... | collective-permute-start | bytes 393224 | tf_op jit(solution)/shard_map/ppermute | solution.py:421
  129.4 5.0 %collective-permute-done.9.recv_ref = f32[1,256,128]{2,1,0:T(8,128)S(1)} collective-permute-done((f32[1,256,128]{2,1,0:T(8,128)S(1)}, f32[1,256,128]{2,1,0:T(8,128)S(1)}, u32[]{:S(2)}, u32[]{:S(2)}) %collective-permute-start.9) | collective-permute-done | bytes 131104 | tf_op jit(solution)/shard_map/ppermute | solution.py:421
  134.4 0.7 shard_map.150
  135.1 3.7 %all-to-all-done.7.recv_ref = f32[8,72,128]{2,1,0:T(8,128)S(1)} async-done(((f32[8,72,128]{2,1,0:T(8,128)}), f32[8,72,128]{2,1,0:T(8,128)S(1)}, u32[]{:S(2)}, u32[]{:S(2)}) %all-to-all-start.7) | async-done | bytes 294944 | tf_op jit(solution)/shard_map/all_to_all | solution.py:383
  138.7 0.6 shard_map.149
  (9 shorter events, 0.0 us)
Async XLA Ops:
  4.2 41.9 %copy-start.2 = (f32[128]{0:T(128)S(1)}, f32[128]{0:T(128)}, u32[]{:S(2)}) copy-start(f32[128]{0:T(128)} %param.17) | copy-start | bytes 1540
  4.2 24.0 %all-to-all-start = ((f32[32,16,128]{2,1,0:T(8,128)}), f32[32,16,128]{2,1,0:T(8,128)S(1)}, u32[]{:S(2)}, u32[]{:S(2)}) async-start(f32[32,16,128]{2,1,0:T(8,128)} %get-tuple-element.32), calls=%async_computation | async-start | bytes 524288 | tf_op jit(solution)/shard_map/all_to_all | solution.py:383
  15.7 20.1 %collective-permute-start.1 = (f32[64,2176]{1,0:T(8,128)}, f32[64,2176]{1,0:T(8,128)}, u32[]{:S(2)}, u32[]{:S(2)}) collective-permute-start(f32[64,2176]{1,0:T(8,128)} %get-tuple-element.39.refs_0_), channel_id=1, source_target_pairs={{0,6},{2,4},{4,2},{6,0},{1,7},{3,5},{5,3},{7,1},{8,14},{10,12},{12... | collective-permute-start | bytes 1671176 | tf_op jit(solution)/shard_map/ppermute | solution.py:421
  17.3 19.0 %collective-permute-start = (f32[64,2176]{1,0:T(8,128)}, f32[64,2176]{1,0:T(8,128)}, u32[]{:S(2)}, u32[]{:S(2)}) collective-permute-start(f32[64,2176]{1,0:T(8,128)} %get-tuple-element.39.refs_0_), channel_id=1, source_target_pairs={{0,2},{2,0},{4,6},{6,4},{1,3},{3,1},{5,7},{7,5},{8,10},{10,8},{12,... | collective-permute-start | bytes 1671176 | tf_op jit(solution)/shard_map/ppermute | solution.py:421
  19.1 31.6 %collective-permute-start.4 = (f32[64,2176]{1,0:T(8,128)}, f32[64,2176]{1,0:T(8,128)}, u32[]{:S(2)}, u32[]{:S(2)}) collective-permute-start(f32[64,2176]{1,0:T(8,128)} %get-tuple-element.39.refs_0_), channel_id=1, source_target_pairs={{0,4},{2,6},{4,0},{6,2},{1,5},{3,7},{5,1},{7,3},{8,12},{10,14},{12... | collective-permute-start | bytes 1671176 | tf_op jit(solution)/shard_map/ppermute | solution.py:421
  19.3 1.2 copy-start
  20.5 1.2 copy-start.1
  30.8 15.2 %all-to-all-start.1 = ((f32[32,8,128]{2,1,0:T(8,128)}), f32[32,8,128]{2,1,0:T(8,128)S(1)}, u32[]{:S(2)}, u32[]{:S(2)}) async-start(f32[32,8,128]{2,1,0:T(8,128)} %bitcast.5), calls=%async_computation.1 | async-start | bytes 262144 | tf_op jit(solution)/shard_map/all_to_all | solution.py:383
  35.7 31.4 %collective-permute-start.2 = (f32[64,2176]{1,0:T(8,128)}, f32[64,2176]{1,0:T(8,128)}, u32[]{:S(2)}, u32[]{:S(2)}) collective-permute-start(f32[64,2176]{1,0:T(8,128)} %get-tuple-element.39.refs_0_), channel_id=1, source_target_pairs={{0,1},{1,0},{2,3},{3,2},{4,5},{5,4},{6,7},{7,6},{8,9},{9,8},{10,11... | collective-permute-start | bytes 1671176 | tf_op jit(solution)/shard_map/ppermute | solution.py:421
  35.8 31.3 %collective-permute-start.5 = (f32[64,2176]{1,0:T(8,128)}, f32[64,2176]{1,0:T(8,128)}, u32[]{:S(2)}, u32[]{:S(2)}) collective-permute-start(f32[64,2176]{1,0:T(8,128)} %collective-permute-done.1.refs_4_.refs_6_), channel_id=1, source_target_pairs={{0,1},{1,0},{2,3},{3,2},{4,5},{5,4},{6,7},{7,6},{8,9},{9,8},{10,11... | collective-permute-start | bytes 1671176 | tf_op jit(solution)/shard_map/ppermute | solution.py:421
  36.3 30.8 %collective-permute-start.3 = (f32[64,2176]{1,0:T(8,128)}, f32[64,2176]{1,0:T(8,128)}, u32[]{:S(2)}, u32[]{:S(2)}) collective-permute-start(f32[64,2176]{1,0:T(8,128)} %collective-permute-done.refs_3_.refs_2_), channel_id=1, source_target_pairs={{0,1},{1,0},{2,3},{3,2},{4,5},{5,4},{6,7},{7,6},{8,9},{9,8},{10,11... | collective-permute-start | bytes 1671176 | tf_op jit(solution)/shard_map/ppermute | solution.py:421
  46.8 14.2 %all-to-all-start.2 = ((f32[32,8,128]{2,1,0:T(8,128)}), f32[32,8,128]{2,1,0:T(8,128)S(1)}, u32[]{:S(2)}, u32[]{:S(2)}) async-start(f32[32,8,128]{2,1,0:T(8,128)} %get-tuple-element.37), calls=%async_computation.2 | async-start | bytes 262144 | tf_op jit(solution)/shard_map/all_to_all | solution.py:383
  50.7 31.4 %collective-permute-start.6 = (f32[64,2176]{1,0:T(8,128)}, f32[64,2176]{1,0:T(8,128)}, u32[]{:S(2)}, u32[]{:S(2)}) collective-permute-start(f32[64,2176]{1,0:T(8,128)} %collective-permute-done.4.refs_6_.refs_4_), channel_id=1, source_target_pairs={{0,1},{1,0},{2,3},{3,2},{4,5},{5,4},{6,7},{7,6},{8,9},{9,8},{10,11... | collective-permute-start | bytes 1671176 | tf_op jit(solution)/shard_map/ppermute | solution.py:421
  63.1 14.3 %all-to-all-start.3 = ((f32[32,8,128]{2,1,0:T(8,128)}), f32[32,8,128]{2,1,0:T(8,128)S(1)}, u32[]{:S(2)}, u32[]{:S(2)}) async-start(f32[32,8,128]{2,1,0:T(8,128)} %bitcast.8), calls=%async_computation.3 | async-start | bytes 262144 | tf_op jit(solution)/shard_map/all_to_all | solution.py:383
  78.1 14.2 %all-to-all-start.4 = ((f32[32,8,128]{2,1,0:T(8,128)}), f32[32,8,128]{2,1,0:T(8,128)S(1)}, u32[]{:S(2)}, u32[]{:S(2)}) async-start(f32[32,8,128]{2,1,0:T(8,128)} %get-tuple-element.42.refs_9_), calls=%async_computation.4 | async-start | bytes 262144 | tf_op jit(solution)/shard_map/all_to_all | solution.py:383
  100.4 5.9 %collective-permute-start.7 = (f32[4,256,128]{2,1,0:T(8,128)}, f32[4,256,128]{2,1,0:T(8,128)S(1)}, u32[]{:S(2)}, u32[]{:S(2)}) collective-permute-start(f32[4,256,128]{2,1,0:T(8,128)} %get-tuple-element.47), channel_id=1, source_target_pairs={{0,1},{1,0},{2,3},{3,2},{4,5},{5,4},{6,7},{7,6},{8,9},{9,8},{10,11... | collective-permute-start | bytes 1572872 | tf_op jit(solution)/shard_map/ppermute | solution.py:421
  100.4 12.5 %all-to-all-start.5 = ((f32[8,64,128]{2,1,0:T(8,128)}), f32[8,64,128]{2,1,0:T(8,128)S(1)}, u32[]{:S(2)}, u32[]{:S(2)}) async-start(f32[8,64,128]{2,1,0:T(8,128)} %get-tuple-element.44), calls=%async_computation.5 | async-start | bytes 524288 | tf_op jit(solution)/shard_map/all_to_all | solution.py:383
  107.4 9.6 %collective-permute-start.8 = (f32[2,256,128]{2,1,0:T(8,128)S(1)}, f32[2,256,128]{2,1,0:T(8,128)S(1)}, u32[]{:S(2)}, u32[]{:S(2)}) collective-permute-start(f32[2,256,128]{2,1,0:T(8,128)S(1)} %get-tuple-element.48.refs_2_), channel_id=1, source_target_pairs={{0,2},{2,0},{4,6},{6,4},{1,3},{3,1},{5,7},{7,5},{8,10},{10,8},{12,... | collective-permute-start | bytes 786440 | tf_op jit(solution)/shard_map/ppermute | solution.py:421
  113.6 10.1 %all-to-all-start.6 = ((f32[4,128,128]{2,1,0:T(8,128)}), f32[4,128,128]{2,1,0:T(8,128)S(1)}, u32[]{:S(2)}, u32[]{:S(2)}) async-start(f32[4,128,128]{2,1,0:T(8,128)} %shard_map.146), calls=%async_computation.6 | async-start | bytes 524288 | tf_op jit(solution)/shard_map/all_to_all | solution.py:383
  124.4 14.3 %all-to-all-start.7 = ((f32[8,72,128]{2,1,0:T(8,128)}), f32[8,72,128]{2,1,0:T(8,128)S(1)}, u32[]{:S(2)}, u32[]{:S(2)}) async-start(f32[8,72,128]{2,1,0:T(8,128)} %shard_map.148), calls=%async_computation.7 | async-start | bytes 589824 | tf_op jit(solution)/shard_map/all_to_all | solution.py:383
  127.8 6.6 %collective-permute-start.9 = (f32[1,256,128]{2,1,0:T(8,128)S(1)}, f32[1,256,128]{2,1,0:T(8,128)S(1)}, u32[]{:S(2)}, u32[]{:S(2)}) collective-permute-start(f32[1,256,128]{2,1,0:T(8,128)S(1)} %get-tuple-element.50.refs_1_), channel_id=1, source_target_pairs={{0,4},{2,6},{4,0},{6,2},{1,5},{3,7},{5,1},{7,3},{8,12},{10,14},{12... | collective-permute-start | bytes 393224 | tf_op jit(solution)/shard_map/ppermute | solution.py:421

commit v12 on v11

--- a/solution.py
+++ b/solution.py
@@ -441,12 +441,13 @@
         )(parts, theta, active, totals, *awaited)
         theta_all = exchange(spread, user_axes).reshape(everyone, factors)
         if iteration == 0:
+            awaited = [away(shards[place]) for place in (2, 6)]
             partial = kernel_call(
-                behind(ascend_kernel, 3, 2),
+                behind(ascend_kernel, 3, len(awaited)),
                 shape_of(everyone, factors),
-                in_specs=[vmem, vmem, vmem, hbm, hbm],
-            )(theta_all, marks, table, away(shards[2]), away(shards[6]))
-            awaited = [away(shards[place]) for place in (1, 3, 4, 7)]
+                in_specs=[vmem] * 3 + [hbm] * len(awaited),
+            )(theta_all, marks, table, *awaited)
+            awaited = [away(shards[place]) for place in ()]
         else:
             scale = kernel_call(
                 behind(functools.partial(scale_kernel, split_count), split_count + 1),

time: 140 us -> 138 us (0.986)
  blocking collectives: 0 us -> 30.2 us
  waiting for transfers between devices: 60.1 us -> 38 us
  starting transfers between devices: 46.9 us -> 38.5 us
    all_to_all x0 -> x2, blocking collectives: none -> 30.2 us  [exchange(): return lax.all_to_all(array, axes, split_axis=0, concat_axis=0, tiled=True)]
    all_to_all x8 -> x6, waiting for transfers between devices: 55.1 us -> 32.9 us  [exchange(): return lax.all_to_all(array, axes, split_axis=0, concat_axis=0, tiled=True)]
    all_to_all x8 -> x6, starting transfers between devices: 40.9 us -> 31 us  [exchange(): return lax.all_to_all(array, axes, split_axis=0, concat_axis=0, tiled=True)]
    ppermute x10, starting transfers between devices: 6 us -> 7.52 us  [swap(): lax.ppermute(array, axis, [(place, place ^ bit) for place in range(lax.ax...]
  transfers between devices with their start and end apart: 18 -> 16, of which waited for: 9 -> 7; matrix products, arithmetic and copies ran while one was open for 0% -> 0% of each run, Pallas kernels for 11% -> 11%
where the time goes in v12:
time: 138 us
  starting transfers between devices  38.5 us (28%)
  waiting for transfers between devices  38 us (28%)
  blocking collectives  30.2 us (22%)
  Pallas kernels  27.7 us (20%)
  local copies, waits for them, and re-layouts  2.45 us (2%)
    all_to_all x6, waiting for transfers between devices, exchange(): return lax.all_to_all(array, axes, split_axis=0, concat_axis=0, tiled=True)  32.9 us
    all_to_all x6, starting transfers between devices, exchange(): return lax.all_to_all(array, axes, split_axis=0, concat_axis=0, tiled=True)  31 us
    all_to_all x2, blocking collectives, exchange(): return lax.all_to_all(array, axes, split_axis=0, concat_axis=0, tiled=True)  30.2 us
    pallas_call x1, Pallas kernels, shards(): kernel_call(functools.partial(last_kernel, split_count), (shape_of(everyo...  8.06 us
    ppermute x10, starting transfers between devices, swap(): lax.ppermute(array, axis, [(place, place ^ bit) for place in range(lax.ax...  7.52 us
    pallas_call x1, Pallas kernels, shards(): kernel_call(behind(functools.partial(scale_kernel, split_count), split_co...  5.72 us
    ppermute x10, waiting for transfers between devices, swap(): lax.ppermute(array, axis, [(place, place ^ bit) for place in range(lax.ax...  5.04 us
    pallas_call x1, Pallas kernels, shards(): kernel_call(functools.partial(prep_kernel, owners), (off_chip(owners, 16,...  3.58 us
  transfers between devices with their start and end apart: 16, of which 7 were waited for; matrix products, arithmetic and copies ran while one was open for 0% of the time, Pallas kernels for 11%

profile of v12, /device:TPU:2, one launch (start us, length us, event | category | flops | bytes accessed | tf_op | source)
XLA Modules:
  0.0 137.6 jit_solution(6504280041882735523)
XLA Ops:
  0.6 3.6 %shard_map.137 = (f32[32,16,128]{2,1,0:T(8,128)}, f32[8,128]{1,0:T(8,128)S(1)}, f32[8,128]{1,0:T(8,128)S(1)}, f32[64,2176]{1,0:T(8,128)}) custom-call(s32[8]{0:T(128)} %counts_hbm.1, s32[64,128]{1,0:T(8,128)} %bitcast.18, s32[64,128]{1,0:T(8,128)} %bitcast.19, f32[8,128]{1,0:T(8,128)} %shape_hbm.1, f32[8,128]{1,0:T(8,128)} %rate_hbm.1, f32[64,2048]{1,0:T(8,128)} %cov_hbm.1, ...), custom_call_target="tpu_custom_call" | custom-call | tf_op jit(solution)/shard_map/pallas_call | solution.py:392
  4.2 0.0 copy-start.2
  4.2 11.5 %all-to-all-start = ((f32[32,16,128]{2,1,0:T(8,128)}), f32[32,16,128]{2,1,0:T(8,128)S(1)}, u32[]{:S(2)}, u32[]{:S(2)}) async-start(f32[32,16,128]{2,1,0:T(8,128)} %get-tuple-element.32), calls=%async_computation | async-start | bytes 524288 | tf_op jit(solution)/shard_map/all_to_all | solution.py:383
  15.7 2.2 %collective-permute-start.4 = (f32[64,2176]{1,0:T(8,128)}, f32[64,2176]{1,0:T(8,128)}, u32[]{:S(2)}, u32[]{:S(2)}) collective-permute-start(f32[64,2176]{1,0:T(8,128)} %get-tuple-element.39.refs_0_), channel_id=1, source_target_pairs={{0,4},{2,6},{4,0},{6,2},{1,5},{3,7},{5,1},{7,3},{8,12},{10,14},{12... | collective-permute-start | bytes 1671176 | tf_op jit(solution)/shard_map/ppermute | solution.py:421
  17.9 0.0 collective-permute-start.1
  18.0 2.6 %collective-permute-start = (f32[64,2176]{1,0:T(8,128)}, f32[64,2176]{1,0:T(8,128)}, u32[]{:S(2)}, u32[]{:S(2)}) collective-permute-start(f32[64,2176]{1,0:T(8,128)} %get-tuple-element.39.refs_0_), channel_id=1, source_target_pairs={{0,2},{2,0},{4,6},{6,4},{1,3},{3,1},{5,7},{7,5},{8,10},{10,8},{12,... | collective-permute-start | bytes 1671176 | tf_op jit(solution)/shard_map/ppermute | solution.py:421
  20.5 1.2 copy-done
  21.8 1.2 copy-done.1
  23.0 1.5 %shard_map.138 = (f32[2048,128]{1,0:T(8,128)S(1)}, f32[2048,128]{1,0:T(8,128)}) custom-call(f32[2048,128]{1,0:T(8,128)S(1)} %copy-done.1, f32[2048,128]{1,0:T(8,128)S(1)} %copy-done), custom_call_target="tpu_custom_call" | custom-call | tf_op jit(solution)/shard_map/pallas_call | solution.py:414
  24.5 3.7 %all-to-all-done.recv_ref = f32[32,16,128]{2,1,0:T(8,128)S(1)} async-done(((f32[32,16,128]{2,1,0:T(8,128)}), f32[32,16,128]{2,1,0:T(8,128)S(1)}, u32[]{:S(2)}, u32[]{:S(2)}) %all-to-all-start) | async-done | bytes 262176 | tf_op jit(solution)/shard_map/all_to_all | solution.py:383
  28.2 2.0 %shard_map.139 = (f32[16,256,128]{2,1,0:T(8,128)S(1)}, f32[256,128]{1,0:T(8,128)S(1)}) custom-call(f32[32,16,128]{2,1,0:T(8,128)S(1)} %all-to-all-done.recv_ref, f32[2048,128]{1,0:T(8,128)S(1)} %get-tuple-element.33.table_ref.refs_2_), custom_call_target="tpu_custom_call" | custom-call | tf_op jit(solution)/shard_map/pallas_call | solution.py:430
  30.2 16.3 %all_to_all.40.refs_0_ = f32[32,8,128]{2,1,0:T(8,128)S(1)} all-to-all(f32[32,8,128]{2,1,0:T(8,128)S(1)} %bitcast.14), channel_id=1, replica_groups=mesh['y'=4,'z'=8,'x'=4,'core'=2] {'y','z'}, dimensions={0} | all-to-all | bytes 262144 | tf_op jit(solution)/shard_map/all_to_all | solution.py:383
  46.5 0.7 shard_map.140
  47.2 3.9 %all-to-all-start.2 = ((f32[32,8,128]{2,1,0:T(8,128)}), f32[32,8,128]{2,1,0:T(8,128)S(1)}, u32[]{:S(2)}, u32[]{:S(2)}) async-start(f32[32,8,128]{2,1,0:T(8,128)} %get-tuple-element.37), calls=%async_computation.2 | async-start | bytes 262144 | tf_op jit(solution)/shard_map/all_to_all | solution.py:383
  51.1 0.1 collective-permute-start.2
  51.2 0.0 collective-permute-done.4.refs_4_
  51.2 0.5 collective-permute-start.5
  51.7 0.1 collective-permute-start.6
  51.8 0.4 collective-permute-start.3
  52.2 9.2 %all-to-all-done.2 = f32[32,8,128]{2,1,0:T(8,128)S(1)} async-done(((f32[32,8,128]{2,1,0:T(8,128)}), f32[32,8,128]{2,1,0:T(8,128)S(1)}, u32[]{:S(2)}, u32[]{:S(2)}) %all-to-all-start.2) | async-done | bytes 131104 | tf_op jit(solution)/shard_map/all_to_all | solution.py:383
  61.4 1.4 %shard_map.141 = f32[256,128]{1,0:T(8,128)S(1)} custom-call(f32[256,128]{1,0:T(8,128)S(1)} %bitcast.12, f32[16,256,128]{2,1,0:T(8,128)S(1)} %get-tuple-element.38.refs_1_.marks_ref, f32[2048,128]{1,0:T(8,128)S(1)} %get-tuple-element.33.table_ref.refs_2_, f32[64,2176]{1,0:T(8,128)} %collective-permute-done.refs_3_.refs_2_, ...), custom_call_target="tpu_custom_call" | custom-call | tf_op jit(solution)/shard_map/pallas_call | solution.py:445
  62.8 13.9 %all_to_all.41.refs_0_ = f32[32,8,128]{2,1,0:T(8,128)S(1)} all-to-all(f32[32,8,128]{2,1,0:T(8,128)S(1)} %bitcast.13), channel_id=1, replica_groups=mesh['y'=4,'z'=8,'x'=4,'core'=2] {'y','z'}, dimensions={0} | all-to-all | bytes 262144 | tf_op jit(solution)/shard_map/all_to_all | solution.py:383
  76.7 0.7 shard_map.142
  77.4 3.9 %all-to-all-start.4 = ((f32[32,8,128]{2,1,0:T(8,128)}), f32[32,8,128]{2,1,0:T(8,128)S(1)}, u32[]{:S(2)}, u32[]{:S(2)}) async-start(f32[32,8,128]{2,1,0:T(8,128)} %get-tuple-element.42.refs_9_), calls=%async_computation.4 | async-start | bytes 262144 | tf_op jit(solution)/shard_map/all_to_all | solution.py:383
  81.3 0.1 pad_add_fusion.spot_ref
  81.4 0.0 collective-permute-done.2.refs_1_
  81.4 0.0 collective-permute-done.5.refs_5_
  81.4 0.0 collective-permute-done.6.refs_7_
  81.4 0.0 collective-permute-done.3.refs_3_
  81.4 5.7 %shard_map.143.scale_ref = f32[2048,128]{1,0:T(8,128)} custom-call(f32[64,2176]{1,0:T(8,128)} %get-tuple-element.39.refs_0_, f32[64,2176]{1,0:T(8,128)} %collective-permute-done.2.refs_1_, f32[64,2176]{1,0:T(8,128)} %collective-permute-done.refs_3_.refs_2_, f32[64,2176]{1,0:T(8,128)} %collective-permute-done.3.refs_3_, ...), custom_call_target="tpu_custom_call" | custom-call | tf_op jit(solution)/shard_map/pallas_call | solution.py:452
  87.1 4.5 %all-to-all-done.4 = f32[32,8,128]{2,1,0:T(8,128)S(1)} async-done(((f32[32,8,128]{2,1,0:T(8,128)}), f32[32,8,128]{2,1,0:T(8,128)S(1)}, u32[]{:S(2)}, u32[]{:S(2)}) %all-to-all-start.4) | async-done | bytes 131104 | tf_op jit(solution)/shard_map/all_to_all | solution.py:383
  91.6 8.1 %shard_map.144 = (f32[256,128]{1,0:T(8,128)S(1)}, f32[256,128]{1,0:T(8,128)S(1)}, f32[4,256,128]{2,1,0:T(8,128)}, f32[4,256,128]{2,1,0:T(8,128)}, f32[8,64,128]{2,1,0:T(8,128)}) custom-call(s32[3]{0:T(128)S(1)} %pad_add_fusion.spot_ref, f32[256,128]{1,0:T(8,128)S(1)} %bitcast.11, f32[16,256,128]{2,1,0:T(8,128)S(1)} %get-tuple-element.38.refs_1_.marks_ref, ...), custom_call_target="tpu_custom_call" | custom-call | tf_op jit(solution)/shard_map/pallas_call | solution.py:458
  99.6 0.0 collective-permute-start.7
  99.6 4.9 %all-to-all-start.5 = ((f32[8,64,128]{2,1,0:T(8,128)}), f32[8,64,128]{2,1,0:T(8,128)S(1)}, u32[]{:S(2)}, u32[]{:S(2)}) async-start(f32[8,64,128]{2,1,0:T(8,128)} %get-tuple-element.44), calls=%async_computation.5 | async-start | bytes 524288 | tf_op jit(solution)/shard_map/all_to_all | solution.py:383
  104.6 1.1 shard_map.145
  105.7 0.1 collective-permute-start.8
  105.8 5.3 %all-to-all-done.5.refs_0_ = f32[8,64,128]{2,1,0:T(8,128)S(1)} async-done(((f32[8,64,128]{2,1,0:T(8,128)}), f32[8,64,128]{2,1,0:T(8,128)S(1)}, u32[]{:S(2)}, u32[]{:S(2)}) %all-to-all-start.5) | async-done | bytes 262176 | tf_op jit(solution)/shard_map/all_to_all | solution.py:383
  111.1 0.7 shard_map.146
  111.8 3.4 %all-to-all-start.6 = ((f32[4,128,128]{2,1,0:T(8,128)}), f32[4,128,128]{2,1,0:T(8,128)S(1)}, u32[]{:S(2)}, u32[]{:S(2)}) async-start(f32[4,128,128]{2,1,0:T(8,128)} %shard_map.146), calls=%async_computation.6 | async-start | bytes 524288 | tf_op jit(solution)/shard_map/all_to_all | solution.py:383
  115.3 0.0 collective-permute-done.8.recv_ref
  115.3 6.6 %all-to-all-done.6.refs_0_ = f32[4,128,128]{2,1,0:T(8,128)S(1)} async-done(((f32[4,128,128]{2,1,0:T(8,128)}), f32[4,128,128]{2,1,0:T(8,128)S(1)}, u32[]{:S(2)}, u32[]{:S(2)}) %all-to-all-start.6) | async-done | bytes 262176 | tf_op jit(solution)/shard_map/all_to_all | solution.py:383
  121.9 0.7 shard_map.148
  122.6 3.4 %all-to-all-start.7 = ((f32[8,72,128]{2,1,0:T(8,128)}), f32[8,72,128]{2,1,0:T(8,128)S(1)}, u32[]{:S(2)}, u32[]{:S(2)}) async-start(f32[8,72,128]{2,1,0:T(8,128)} %shard_map.148), calls=%async_computation.7 | async-start | bytes 589824 | tf_op jit(solution)/shard_map/all_to_all | solution.py:383
  126.1 1.5 %collective-permute-start.9 = (f32[1,256,128]{2,1,0:T(8,128)S(1)}, f32[1,256,128]{2,1,0:T(8,128)S(1)}, u32[]{:S(2)}, u32[]{:S(2)}) collective-permute-start(f32[1,256,128]{2,1,0:T(8,128)S(1)} %get-tuple-element.50.refs_1_), channel_id=1, source_target_pairs={{0,4},{2,6},{4,0},{6,2},{1,5},{3,7},{5,1},{7,3},{8,12},{10,14},{12... | collective-permute-start | bytes 393224 | tf_op jit(solution)/shard_map/ppermute | solution.py:421
  127.6 5.0 %collective-permute-done.9.recv_ref = f32[1,256,128]{2,1,0:T(8,128)S(1)} collective-permute-done((f32[1,256,128]{2,1,0:T(8,128)S(1)}, f32[1,256,128]{2,1,0:T(8,128)S(1)}, u32[]{:S(2)}, u32[]{:S(2)}) %collective-permute-start.9) | collective-permute-done | bytes 131104 | tf_op jit(solution)/shard_map/ppermute | solution.py:421
  132.6 0.7 shard_map.150
  133.3 3.7 %all-to-all-done.7.recv_ref = f32[8,72,128]{2,1,0:T(8,128)S(1)} async-done(((f32[8,72,128]{2,1,0:T(8,128)}), f32[8,72,128]{2,1,0:T(8,128)S(1)}, u32[]{:S(2)}, u32[]{:S(2)}) %all-to-all-start.7) | async-done | bytes 294944 | tf_op jit(solution)/shard_map/all_to_all | solution.py:383
  137.0 0.6 shard_map.149
  (7 shorter events, 0.0 us)
Async XLA Ops:
  4.2 42.3 %copy-start.2 = (f32[128]{0:T(128)S(1)}, f32[128]{0:T(128)}, u32[]{:S(2)}) copy-start(f32[128]{0:T(128)} %param.17) | copy-start | bytes 1540
  4.2 24.0 %all-to-all-start = ((f32[32,16,128]{2,1,0:T(8,128)}), f32[32,16,128]{2,1,0:T(8,128)S(1)}, u32[]{:S(2)}, u32[]{:S(2)}) async-start(f32[32,16,128]{2,1,0:T(8,128)} %get-tuple-element.32), calls=%async_computation | async-start | bytes 524288 | tf_op jit(solution)/shard_map/all_to_all | solution.py:383
  15.7 35.5 %collective-permute-start.4 = (f32[64,2176]{1,0:T(8,128)}, f32[64,2176]{1,0:T(8,128)}, u32[]{:S(2)}, u32[]{:S(2)}) collective-permute-start(f32[64,2176]{1,0:T(8,128)} %get-tuple-element.39.refs_0_), channel_id=1, source_target_pairs={{0,4},{2,6},{4,0},{6,2},{1,5},{3,7},{5,1},{7,3},{8,12},{10,14},{12... | collective-permute-start | bytes 1671176 | tf_op jit(solution)/shard_map/ppermute | solution.py:421
  17.9 33.7 %collective-permute-start.1 = (f32[64,2176]{1,0:T(8,128)}, f32[64,2176]{1,0:T(8,128)}, u32[]{:S(2)}, u32[]{:S(2)}) collective-permute-start(f32[64,2176]{1,0:T(8,128)} %get-tuple-element.39.refs_0_), channel_id=1, source_target_pairs={{0,6},{2,4},{4,2},{6,0},{1,7},{3,5},{5,3},{7,1},{8,14},{10,12},{12... | collective-permute-start | bytes 1671176 | tf_op jit(solution)/shard_map/ppermute | solution.py:421
  18.0 33.8 %collective-permute-start = (f32[64,2176]{1,0:T(8,128)}, f32[64,2176]{1,0:T(8,128)}, u32[]{:S(2)}, u32[]{:S(2)}) collective-permute-start(f32[64,2176]{1,0:T(8,128)} %get-tuple-element.39.refs_0_), channel_id=1, source_target_pairs={{0,2},{2,0},{4,6},{6,4},{1,3},{3,1},{5,7},{7,5},{8,10},{10,8},{12,... | collective-permute-start | bytes 1671176 | tf_op jit(solution)/shard_map/ppermute | solution.py:421
  20.5 1.2 copy-start
  21.7 1.2 copy-start.1
  47.2 14.2 %all-to-all-start.2 = ((f32[32,8,128]{2,1,0:T(8,128)}), f32[32,8,128]{2,1,0:T(8,128)S(1)}, u32[]{:S(2)}, u32[]{:S(2)}) async-start(f32[32,8,128]{2,1,0:T(8,128)} %get-tuple-element.37), calls=%async_computation.2 | async-start | bytes 262144 | tf_op jit(solution)/shard_map/all_to_all | solution.py:383
  51.1 30.3 %collective-permute-start.2 = (f32[64,2176]{1,0:T(8,128)}, f32[64,2176]{1,0:T(8,128)}, u32[]{:S(2)}, u32[]{:S(2)}) collective-permute-start(f32[64,2176]{1,0:T(8,128)} %get-tuple-element.39.refs_0_), channel_id=1, source_target_pairs={{0,1},{1,0},{2,3},{3,2},{4,5},{5,4},{6,7},{7,6},{8,9},{9,8},{10,11... | collective-permute-start | bytes 1671176 | tf_op jit(solution)/shard_map/ppermute | solution.py:421
  51.2 30.2 %collective-permute-start.5 = (f32[64,2176]{1,0:T(8,128)}, f32[64,2176]{1,0:T(8,128)}, u32[]{:S(2)}, u32[]{:S(2)}) collective-permute-start(f32[64,2176]{1,0:T(8,128)} %collective-permute-done.4.refs_4_), channel_id=1, source_target_pairs={{0,1},{1,0},{2,3},{3,2},{4,5},{5,4},{6,7},{7,6},{8,9},{9,8},{10,11... | collective-permute-start | bytes 1671176 | tf_op jit(solution)/shard_map/ppermute | solution.py:421
  51.7 29.7 %collective-permute-start.6 = (f32[64,2176]{1,0:T(8,128)}, f32[64,2176]{1,0:T(8,128)}, u32[]{:S(2)}, u32[]{:S(2)}) collective-permute-start(f32[64,2176]{1,0:T(8,128)} %collective-permute-done.1.refs_4_.refs_6_), channel_id=1, source_target_pairs={{0,1},{1,0},{2,3},{3,2},{4,5},{5,4},{6,7},{7,6},{8,9},{9,8},{10,11... | collective-permute-start | bytes 1671176 | tf_op jit(solution)/shard_map/ppermute | solution.py:421
  51.8 29.6 %collective-permute-start.3 = (f32[64,2176]{1,0:T(8,128)}, f32[64,2176]{1,0:T(8,128)}, u32[]{:S(2)}, u32[]{:S(2)}) collective-permute-start(f32[64,2176]{1,0:T(8,128)} %collective-permute-done.refs_3_.refs_2_), channel_id=1, source_target_pairs={{0,1},{1,0},{2,3},{3,2},{4,5},{5,4},{6,7},{7,6},{8,9},{9,8},{10,11... | collective-permute-start | bytes 1671176 | tf_op jit(solution)/shard_map/ppermute | solution.py:421
  77.4 14.2 %all-to-all-start.4 = ((f32[32,8,128]{2,1,0:T(8,128)}), f32[32,8,128]{2,1,0:T(8,128)S(1)}, u32[]{:S(2)}, u32[]{:S(2)}) async-start(f32[32,8,128]{2,1,0:T(8,128)} %get-tuple-element.42.refs_9_), calls=%async_computation.4 | async-start | bytes 262144 | tf_op jit(solution)/shard_map/all_to_all | solution.py:383
  99.6 4.9 %collective-permute-start.7 = (f32[4,256,128]{2,1,0:T(8,128)}, f32[4,256,128]{2,1,0:T(8,128)S(1)}, u32[]{:S(2)}, u32[]{:S(2)}) collective-permute-start(f32[4,256,128]{2,1,0:T(8,128)} %get-tuple-element.47), channel_id=1, source_target_pairs={{0,1},{1,0},{2,3},{3,2},{4,5},{5,4},{6,7},{7,6},{8,9},{9,8},{10,11... | collective-permute-start | bytes 1572872 | tf_op jit(solution)/shard_map/ppermute | solution.py:421
  99.6 11.5 %all-to-all-start.5 = ((f32[8,64,128]{2,1,0:T(8,128)}), f32[8,64,128]{2,1,0:T(8,128)S(1)}, u32[]{:S(2)}, u32[]{:S(2)}) async-start(f32[8,64,128]{2,1,0:T(8,128)} %get-tuple-element.44), calls=%async_computation.5 | async-start | bytes 524288 | tf_op jit(solution)/shard_map/all_to_all | solution.py:383
  105.7 9.6 %collective-permute-start.8 = (f32[2,256,128]{2,1,0:T(8,128)S(1)}, f32[2,256,128]{2,1,0:T(8,128)S(1)}, u32[]{:S(2)}, u32[]{:S(2)}) collective-permute-start(f32[2,256,128]{2,1,0:T(8,128)S(1)} %get-tuple-element.48.refs_2_), channel_id=1, source_target_pairs={{0,2},{2,0},{4,6},{6,4},{1,3},{3,1},{5,7},{7,5},{8,10},{10,8},{12,... | collective-permute-start | bytes 786440 | tf_op jit(solution)/shard_map/ppermute | solution.py:421
  111.8 10.1 %all-to-all-start.6 = ((f32[4,128,128]{2,1,0:T(8,128)}), f32[4,128,128]{2,1,0:T(8,128)S(1)}, u32[]{:S(2)}, u32[]{:S(2)}) async-start(f32[4,128,128]{2,1,0:T(8,128)} %shard_map.146), calls=%async_computation.6 | async-start | bytes 524288 | tf_op jit(solution)/shard_map/all_to_all | solution.py:383
  122.6 14.3 %all-to-all-start.7 = ((f32[8,72,128]{2,1,0:T(8,128)}), f32[8,72,128]{2,1,0:T(8,128)S(1)}, u32[]{:S(2)}, u32[]{:S(2)}) async-start(f32[8,72,128]{2,1,0:T(8,128)} %shard_map.148), calls=%async_computation.7 | async-start | bytes 589824 | tf_op jit(solution)/shard_map/all_to_all | solution.py:383
  126.1 6.6 %collective-permute-start.9 = (f32[1,256,128]{2,1,0:T(8,128)S(1)}, f32[1,256,128]{2,1,0:T(8,128)S(1)}, u32[]{:S(2)}, u32[]{:S(2)}) collective-permute-start(f32[1,256,128]{2,1,0:T(8,128)S(1)} %get-tuple-element.50.refs_1_), channel_id=1, source_target_pairs={{0,4},{2,6},{4,0},{6,2},{1,5},{3,7},{5,1},{7,3},{8,12},{10,14},{12... | collective-permute-start | bytes 393224 | tf_op jit(solution)/shard_map/ppermute | solution.py:421

commit v13 on v12

--- a/solution.py
+++ b/solution.py
@@ -469,22 +469,27 @@
     )(spot, theta_all, marks, table, away(scale), away(base), *[away(shard) for shard in shards])
     held = away(held)
 
-    def halve(held, moved, distance):
+    def halve(held, moved, *awaited):
         half = held.shape[0] // 2
-        return kernel_call(halve_kernel, (shape_of(half, share_rows, factors),) * 2)(held, swap(moved, distance))
+        return kernel_call(
+            behind(halve_kernel, 2, len(awaited)),
+            (shape_of(half, share_rows, factors),) * 2,
+            in_specs=[vmem] * 2 + [hbm] * len(awaited),
+        )(held, moved, *awaited)
 
     grad = exchange(grad, item_axes)
-    held, moved = halve(held, moved, 1)
+    held, moved = halve(held, swap(moved, 1))
     both = kernel_call(
-        behind(join_kernel, 2), off_chip(y_size, z_size * users_here + cov_rows, factors), in_specs=[vmem, vmem, hbm]
+        behind(join_kernel, 2), shape_of(y_size, z_size * users_here + cov_rows, factors), in_specs=[vmem, vmem, hbm]
     )(grad, partial, moved)
     both = exchange(both, ("y",))
-    held, moved = halve(held, moved, 2)
+    moved = swap(moved, 2)
     both = kernel_call(
         behind(functools.partial(fan_kernel, users_here), 1),
         off_chip(z_size, users_here + cov_rows, factors),
         in_specs=[vmem, hbm],
     )(both, moved)
+    held, moved = halve(held, moved, away(both))
     both = exchange(both, ("z",))
     new_shape = kernel_call(close_kernel, share)(held, swap(moved, 4), base)
     user_shape, user_rate, active, cov_grad = kernel_call(

time: 138 us -> 137 us (level)
  blocking collectives: 30.2 us -> 39.3 us
  waiting for transfers between devices: 38 us -> 31.3 us
  starting transfers between devices: 38.5 us -> 35.8 us
    all_to_all x2 -> x3, blocking collectives: 30.2 us -> 39.3 us  [exchange(): return lax.all_to_all(array, axes, split_axis=0, concat_axis=0, tiled=True)]
    all_to_all x6 -> x5, waiting for transfers between devices: 32.9 us -> 26.2 us  [exchange(): return lax.all_to_all(array, axes, split_axis=0, concat_axis=0, tiled=True)]
    all_to_all x6 -> x5, starting transfers between devices: 31 us -> 28.2 us  [exchange(): return lax.all_to_all(array, axes, split_axis=0, concat_axis=0, tiled=True)]
  transfers between devices with their start and end apart: 16 -> 15, of which waited for: 7 -> 6; matrix products, arithmetic and copies ran while one was open for 0% -> 0% of each run, Pallas kernels for 11% -> 10%
where the time goes in v13:
time: 137 us
  blocking collectives  39.3 us (29%)
  starting transfers between devices  35.8 us (26%)
  waiting for transfers between devices  31.3 us (23%)
  Pallas kernels  27 us (20%)
  local copies, waits for them, and re-layouts  2.45 us (2%)
    all_to_all x3, blocking collectives, exchange(): return lax.all_to_all(array, axes, split_axis=0, concat_axis=0, tiled=True)  39.3 us
    all_to_all x5, starting transfers between devices, exchange(): return lax.all_to_all(array, axes, split_axis=0, concat_axis=0, tiled=True)  28.2 us
    all_to_all x5, waiting for transfers between devices, exchange(): return lax.all_to_all(array, axes, split_axis=0, concat_axis=0, tiled=True)  26.2 us
    pallas_call x1, Pallas kernels, shards(): kernel_call(functools.partial(last_kernel, split_count), (shape_of(everyo...  8.05 us
    ppermute x10, starting transfers between devices, swap(): lax.ppermute(array, axis, [(place, place ^ bit) for place in range(lax.ax...  7.52 us
    pallas_call x1, Pallas kernels, shards(): kernel_call(behind(functools.partial(scale_kernel, split_count), split_co...  5.71 us
    ppermute x10, waiting for transfers between devices, swap(): lax.ppermute(array, axis, [(place, place ^ bit) for place in range(lax.ax...  5.04 us
    pallas_call x1, Pallas kernels, shards(): kernel_call(functools.partial(prep_kernel, owners), (off_chip(owners, 16,...  3.6 us
  transfers between devices with their start and end apart: 15, of which 6 were waited for; matrix products, arithmetic and copies ran while one was open for 0% of the time, Pallas kernels for 10%

profile of v13, /device:TPU:2, one launch (start us, length us, event | category | flops | bytes accessed | tf_op | source)
XLA Modules:
  0.0 136.6 jit_solution(17835991826250673416)
XLA Ops:
  0.6 3.6 %shard_map.137 = (f32[32,16,128]{2,1,0:T(8,128)}, f32[8,128]{1,0:T(8,128)S(1)}, f32[8,128]{1,0:T(8,128)S(1)}, f32[64,2176]{1,0:T(8,128)}) custom-call(s32[8]{0:T(128)} %counts_hbm.1, s32[64,128]{1,0:T(8,128)} %bitcast.18, s32[64,128]{1,0:T(8,128)} %bitcast.19, f32[8,128]{1,0:T(8,128)} %shape_hbm.1, f32[8,128]{1,0:T(8,128)} %rate_hbm.1, f32[64,2048]{1,0:T(8,128)} %cov_hbm.1, ...), custom_call_target="tpu_custom_call" | custom-call | tf_op jit(solution)/shard_map/pallas_call | solution.py:392
  4.2 0.0 copy-start.2
  4.3 11.5 %all-to-all-start = ((f32[32,16,128]{2,1,0:T(8,128)}), f32[32,16,128]{2,1,0:T(8,128)S(1)}, u32[]{:S(2)}, u32[]{:S(2)}) async-start(f32[32,16,128]{2,1,0:T(8,128)} %get-tuple-element.32), calls=%async_computation | async-start | bytes 524288 | tf_op jit(solution)/shard_map/all_to_all | solution.py:383
  15.8 2.2 %collective-permute-start.4 = (f32[64,2176]{1,0:T(8,128)}, f32[64,2176]{1,0:T(8,128)}, u32[]{:S(2)}, u32[]{:S(2)}) collective-permute-start(f32[64,2176]{1,0:T(8,128)} %get-tuple-element.39.refs_0_), channel_id=1, source_target_pairs={{0,4},{2,6},{4,0},{6,2},{1,5},{3,7},{5,1},{7,3},{8,12},{10,14},{12... | collective-permute-start | bytes 1671176 | tf_op jit(solution)/shard_map/ppermute | solution.py:421
  18.0 0.0 collective-permute-start.1
  18.0 2.6 %collective-permute-start = (f32[64,2176]{1,0:T(8,128)}, f32[64,2176]{1,0:T(8,128)}, u32[]{:S(2)}, u32[]{:S(2)}) collective-permute-start(f32[64,2176]{1,0:T(8,128)} %get-tuple-element.39.refs_0_), channel_id=1, source_target_pairs={{0,2},{2,0},{4,6},{6,4},{1,3},{3,1},{5,7},{7,5},{8,10},{10,8},{12,... | collective-permute-start | bytes 1671176 | tf_op jit(solution)/shard_map/ppermute | solution.py:421
  20.5 1.2 copy-done
  21.8 1.2 copy-done.1
  23.0 1.5 %shard_map.138 = (f32[2048,128]{1,0:T(8,128)S(1)}, f32[2048,128]{1,0:T(8,128)}) custom-call(f32[2048,128]{1,0:T(8,128)S(1)} %copy-done.1, f32[2048,128]{1,0:T(8,128)S(1)} %copy-done), custom_call_target="tpu_custom_call" | custom-call | tf_op jit(solution)/shard_map/pallas_call | solution.py:414
  24.5 3.7 %all-to-all-done.recv_ref = f32[32,16,128]{2,1,0:T(8,128)S(1)} async-done(((f32[32,16,128]{2,1,0:T(8,128)}), f32[32,16,128]{2,1,0:T(8,128)S(1)}, u32[]{:S(2)}, u32[]{:S(2)}) %all-to-all-start) | async-done | bytes 262176 | tf_op jit(solution)/shard_map/all_to_all | solution.py:383
  28.2 2.0 %shard_map.139 = (f32[16,256,128]{2,1,0:T(8,128)S(1)}, f32[256,128]{1,0:T(8,128)S(1)}) custom-call(f32[32,16,128]{2,1,0:T(8,128)S(1)} %all-to-all-done.recv_ref, f32[2048,128]{1,0:T(8,128)S(1)} %get-tuple-element.33.table_ref.refs_2_), custom_call_target="tpu_custom_call" | custom-call | tf_op jit(solution)/shard_map/pallas_call | solution.py:430
  30.2 16.3 %all_to_all.40.refs_0_ = f32[32,8,128]{2,1,0:T(8,128)S(1)} all-to-all(f32[32,8,128]{2,1,0:T(8,128)S(1)} %bitcast.14), channel_id=1, replica_groups=mesh['y'=4,'z'=8,'x'=4,'core'=2] {'y','z'}, dimensions={0} | all-to-all | bytes 262144 | tf_op jit(solution)/shard_map/all_to_all | solution.py:383
  46.5 0.7 shard_map.140
  47.2 3.9 %all-to-all-start.2 = ((f32[32,8,128]{2,1,0:T(8,128)}), f32[32,8,128]{2,1,0:T(8,128)S(1)}, u32[]{:S(2)}, u32[]{:S(2)}) async-start(f32[32,8,128]{2,1,0:T(8,128)} %get-tuple-element.37), calls=%async_computation.2 | async-start | bytes 262144 | tf_op jit(solution)/shard_map/all_to_all | solution.py:383
  51.1 0.1 collective-permute-start.2
  51.2 0.0 collective-permute-done.4.refs_4_
  51.2 0.5 collective-permute-start.5
  51.7 0.0 collective-permute-done.1.refs_4_.refs_6_
  51.7 0.1 collective-permute-start.6
  51.8 0.0 collective-permute-done.refs_3_.refs_2_
  51.8 0.4 collective-permute-start.3
  52.2 9.2 %all-to-all-done.2 = f32[32,8,128]{2,1,0:T(8,128)S(1)} async-done(((f32[32,8,128]{2,1,0:T(8,128)}), f32[32,8,128]{2,1,0:T(8,128)S(1)}, u32[]{:S(2)}, u32[]{:S(2)}) %all-to-all-start.2) | async-done | bytes 131104 | tf_op jit(solution)/shard_map/all_to_all | solution.py:383
  61.4 1.4 %shard_map.141 = f32[256,128]{1,0:T(8,128)S(1)} custom-call(f32[256,128]{1,0:T(8,128)S(1)} %bitcast.12, f32[16,256,128]{2,1,0:T(8,128)S(1)} %get-tuple-element.38.refs_1_.marks_ref, f32[2048,128]{1,0:T(8,128)S(1)} %get-tuple-element.33.table_ref.refs_2_, f32[64,2176]{1,0:T(8,128)} %collective-permute-done.refs_3_.refs_2_, ...), custom_call_target="tpu_custom_call" | custom-call | tf_op jit(solution)/shard_map/pallas_call | solution.py:445
  62.9 13.9 %all_to_all.41.refs_0_ = f32[32,8,128]{2,1,0:T(8,128)S(1)} all-to-all(f32[32,8,128]{2,1,0:T(8,128)S(1)} %bitcast.13), channel_id=1, replica_groups=mesh['y'=4,'z'=8,'x'=4,'core'=2] {'y','z'}, dimensions={0} | all-to-all | bytes 262144 | tf_op jit(solution)/shard_map/all_to_all | solution.py:383
  76.7 0.7 shard_map.142
  77.5 3.9 %all-to-all-start.4 = ((f32[32,8,128]{2,1,0:T(8,128)}), f32[32,8,128]{2,1,0:T(8,128)S(1)}, u32[]{:S(2)}, u32[]{:S(2)}) async-start(f32[32,8,128]{2,1,0:T(8,128)} %get-tuple-element.42.refs_9_), calls=%async_computation.4 | async-start | bytes 262144 | tf_op jit(solution)/shard_map/all_to_all | solution.py:383
  81.3 0.1 pad_add_fusion.spot_ref
  81.4 0.0 collective-permute-done.2.refs_1_
  81.4 0.0 collective-permute-done.5.refs_5_
  81.4 0.0 collective-permute-done.6.refs_7_
  81.4 0.0 collective-permute-done.3.refs_3_
  81.4 5.7 %shard_map.143.scale_ref = f32[2048,128]{1,0:T(8,128)} custom-call(f32[64,2176]{1,0:T(8,128)} %get-tuple-element.39.refs_0_, f32[64,2176]{1,0:T(8,128)} %collective-permute-done.2.refs_1_, f32[64,2176]{1,0:T(8,128)} %collective-permute-done.refs_3_.refs_2_, f32[64,2176]{1,0:T(8,128)} %collective-permute-done.3.refs_3_, ...), custom_call_target="tpu_custom_call" | custom-call | tf_op jit(solution)/shard_map/pallas_call | solution.py:452
  87.1 4.5 %all-to-all-done.4 = f32[32,8,128]{2,1,0:T(8,128)S(1)} async-done(((f32[32,8,128]{2,1,0:T(8,128)}), f32[32,8,128]{2,1,0:T(8,128)S(1)}, u32[]{:S(2)}, u32[]{:S(2)}) %all-to-all-start.4) | async-done | bytes 131104 | tf_op jit(solution)/shard_map/all_to_all | solution.py:383
  91.6 8.1 %shard_map.144 = (f32[256,128]{1,0:T(8,128)S(1)}, f32[256,128]{1,0:T(8,128)S(1)}, f32[4,256,128]{2,1,0:T(8,128)}, f32[4,256,128]{2,1,0:T(8,128)}, f32[8,64,128]{2,1,0:T(8,128)}) custom-call(s32[3]{0:T(128)S(1)} %pad_add_fusion.spot_ref, f32[256,128]{1,0:T(8,128)S(1)} %bitcast.11, f32[16,256,128]{2,1,0:T(8,128)S(1)} %get-tuple-element.38.refs_1_.marks_ref, ...), custom_call_target="tpu_custom_call" | custom-call | tf_op jit(solution)/shard_map/pallas_call | solution.py:458
  99.7 0.0 collective-permute-start.7
  99.7 4.9 %all-to-all-start.5 = ((f32[8,64,128]{2,1,0:T(8,128)}), f32[8,64,128]{2,1,0:T(8,128)S(1)}, u32[]{:S(2)}, u32[]{:S(2)}) async-start(f32[8,64,128]{2,1,0:T(8,128)} %get-tuple-element.44), calls=%async_computation.5 | async-start | bytes 524288 | tf_op jit(solution)/shard_map/all_to_all | solution.py:383
  104.6 0.0 collective-permute-done.7.refs_1_
  104.6 1.1 shard_map.145
  105.7 0.1 collective-permute-start.8
  105.8 5.3 %all-to-all-done.5.refs_0_ = f32[8,64,128]{2,1,0:T(8,128)S(1)} async-done(((f32[8,64,128]{2,1,0:T(8,128)}), f32[8,64,128]{2,1,0:T(8,128)S(1)}, u32[]{:S(2)}, u32[]{:S(2)}) %all-to-all-start.5) | async-done | bytes 262176 | tf_op jit(solution)/shard_map/all_to_all | solution.py:383
  111.2 9.2 %all_to_all.42.refs_0_ = f32[4,128,128]{2,1,0:T(8,128)S(1)} all-to-all(f32[4,128,128]{2,1,0:T(8,128)S(1)} %shard_map.146), channel_id=1, replica_groups=mesh['y'=4,'z'=8,'x'=4,'core'=2] {'y'}, dimensions={0} | all-to-all | bytes 524288 | tf_op jit(solution)/shard_map/all_to_all | solution.py:383
  120.4 0.7 shard_map.147.refs_2_
  121.1 4.1 %all-to-all-start.7 = ((f32[8,72,128]{2,1,0:T(8,128)}), f32[8,72,128]{2,1,0:T(8,128)S(1)}, u32[]{:S(2)}, u32[]{:S(2)}) async-start(f32[8,72,128]{2,1,0:T(8,128)} %shard_map.147.refs_2_), calls=%async_computation.7 | async-start | bytes 589824 | tf_op jit(solution)/shard_map/all_to_all | solution.py:383
  125.2 1.5 %collective-permute-start.9 = (f32[1,256,128]{2,1,0:T(8,128)S(1)}, f32[1,256,128]{2,1,0:T(8,128)S(1)}, u32[]{:S(2)}, u32[]{:S(2)}) collective-permute-start(f32[1,256,128]{2,1,0:T(8,128)S(1)} %get-tuple-element.56), channel_id=1, source_target_pairs={{0,4},{2,6},{4,0},{6,2},{1,5},{3,7},{5,1},{7,3},{8,12},{10,14},{12... | collective-permute-start | bytes 393224 | tf_op jit(solution)/shard_map/ppermute | solution.py:421
  126.8 5.0 %collective-permute-done.9.recv_ref = f32[1,256,128]{2,1,0:T(8,128)S(1)} collective-permute-done((f32[1,256,128]{2,1,0:T(8,128)S(1)}, f32[1,256,128]{2,1,0:T(8,128)S(1)}, u32[]{:S(2)}, u32[]{:S(2)}) %collective-permute-start.9) | collective-permute-done | bytes 131104 | tf_op jit(solution)/shard_map/ppermute | solution.py:421
  131.8 0.7 shard_map.150
  132.4 3.6 %all-to-all-done.7.recv_ref = f32[8,72,128]{2,1,0:T(8,128)S(1)} async-done(((f32[8,72,128]{2,1,0:T(8,128)}), f32[8,72,128]{2,1,0:T(8,128)S(1)}, u32[]{:S(2)}, u32[]{:S(2)}) %all-to-all-start.7) | async-done | bytes 294944 | tf_op jit(solution)/shard_map/all_to_all | solution.py:383
  136.0 0.6 shard_map.148
  (6 shorter events, 0.1 us)
Async XLA Ops:
  4.2 42.3 %copy-start.2 = (f32[128]{0:T(128)S(1)}, f32[128]{0:T(128)}, u32[]{:S(2)}) copy-start(f32[128]{0:T(128)} %param.17) | copy-start | bytes 1540
  4.3 24.0 %all-to-all-start = ((f32[32,16,128]{2,1,0:T(8,128)}), f32[32,16,128]{2,1,0:T(8,128)S(1)}, u32[]{:S(2)}, u32[]{:S(2)}) async-start(f32[32,16,128]{2,1,0:T(8,128)} %get-tuple-element.32), calls=%async_computation | async-start | bytes 524288 | tf_op jit(solution)/shard_map/all_to_all | solution.py:383
  15.8 35.5 %collective-permute-start.4 = (f32[64,2176]{1,0:T(8,128)}, f32[64,2176]{1,0:T(8,128)}, u32[]{:S(2)}, u32[]{:S(2)}) collective-permute-start(f32[64,2176]{1,0:T(8,128)} %get-tuple-element.39.refs_0_), channel_id=1, source_target_pairs={{0,4},{2,6},{4,0},{6,2},{1,5},{3,7},{5,1},{7,3},{8,12},{10,14},{12... | collective-permute-start | bytes 1671176 | tf_op jit(solution)/shard_map/ppermute | solution.py:421
  18.0 33.8 %collective-permute-start.1 = (f32[64,2176]{1,0:T(8,128)}, f32[64,2176]{1,0:T(8,128)}, u32[]{:S(2)}, u32[]{:S(2)}) collective-permute-start(f32[64,2176]{1,0:T(8,128)} %get-tuple-element.39.refs_0_), channel_id=1, source_target_pairs={{0,6},{2,4},{4,2},{6,0},{1,7},{3,5},{5,3},{7,1},{8,14},{10,12},{12... | collective-permute-start | bytes 1671176 | tf_op jit(solution)/shard_map/ppermute | solution.py:421
  18.0 33.9 %collective-permute-start = (f32[64,2176]{1,0:T(8,128)}, f32[64,2176]{1,0:T(8,128)}, u32[]{:S(2)}, u32[]{:S(2)}) collective-permute-start(f32[64,2176]{1,0:T(8,128)} %get-tuple-element.39.refs_0_), channel_id=1, source_target_pairs={{0,2},{2,0},{4,6},{6,4},{1,3},{3,1},{5,7},{7,5},{8,10},{10,8},{12,... | collective-permute-start | bytes 1671176 | tf_op jit(solution)/shard_map/ppermute | solution.py:421
  20.5 1.2 copy-start
  21.8 1.2 copy-start.1
  47.2 14.2 %all-to-all-start.2 = ((f32[32,8,128]{2,1,0:T(8,128)}), f32[32,8,128]{2,1,0:T(8,128)S(1)}, u32[]{:S(2)}, u32[]{:S(2)}) async-start(f32[32,8,128]{2,1,0:T(8,128)} %get-tuple-element.37), calls=%async_computation.2 | async-start | bytes 262144 | tf_op jit(solution)/shard_map/all_to_all | solution.py:383
  51.1 30.3 %collective-permute-start.2 = (f32[64,2176]{1,0:T(8,128)}, f32[64,2176]{1,0:T(8,128)}, u32[]{:S(2)}, u32[]{:S(2)}) collective-permute-start(f32[64,2176]{1,0:T(8,128)} %get-tuple-element.39.refs_0_), channel_id=1, source_target_pairs={{0,1},{1,0},{2,3},{3,2},{4,5},{5,4},{6,7},{7,6},{8,9},{9,8},{10,11... | collective-permute-start | bytes 1671176 | tf_op jit(solution)/shard_map/ppermute | solution.py:421
  51.2 30.2 %collective-permute-start.5 = (f32[64,2176]{1,0:T(8,128)}, f32[64,2176]{1,0:T(8,128)}, u32[]{:S(2)}, u32[]{:S(2)}) collective-permute-start(f32[64,2176]{1,0:T(8,128)} %collective-permute-done.4.refs_4_), channel_id=1, source_target_pairs={{0,1},{1,0},{2,3},{3,2},{4,5},{5,4},{6,7},{7,6},{8,9},{9,8},{10,11... | collective-permute-start | bytes 1671176 | tf_op jit(solution)/shard_map/ppermute | solution.py:421
  51.7 29.7 %collective-permute-start.6 = (f32[64,2176]{1,0:T(8,128)}, f32[64,2176]{1,0:T(8,128)}, u32[]{:S(2)}, u32[]{:S(2)}) collective-permute-start(f32[64,2176]{1,0:T(8,128)} %collective-permute-done.1.refs_4_.refs_6_), channel_id=1, source_target_pairs={{0,1},{1,0},{2,3},{3,2},{4,5},{5,4},{6,7},{7,6},{8,9},{9,8},{10,11... | collective-permute-start | bytes 1671176 | tf_op jit(solution)/shard_map/ppermute | solution.py:421
  51.8 29.6 %collective-permute-start.3 = (f32[64,2176]{1,0:T(8,128)}, f32[64,2176]{1,0:T(8,128)}, u32[]{:S(2)}, u32[]{:S(2)}) collective-permute-start(f32[64,2176]{1,0:T(8,128)} %collective-permute-done.refs_3_.refs_2_), channel_id=1, source_target_pairs={{0,1},{1,0},{2,3},{3,2},{4,5},{5,4},{6,7},{7,6},{8,9},{9,8},{10,11... | collective-permute-start | bytes 1671176 | tf_op jit(solution)/shard_map/ppermute | solution.py:421
  77.5 14.2 %all-to-all-start.4 = ((f32[32,8,128]{2,1,0:T(8,128)}), f32[32,8,128]{2,1,0:T(8,128)S(1)}, u32[]{:S(2)}, u32[]{:S(2)}) async-start(f32[32,8,128]{2,1,0:T(8,128)} %get-tuple-element.42.refs_9_), calls=%async_computation.4 | async-start | bytes 262144 | tf_op jit(solution)/shard_map/all_to_all | solution.py:383
  99.7 5.0 %collective-permute-start.7 = (f32[4,256,128]{2,1,0:T(8,128)}, f32[4,256,128]{2,1,0:T(8,128)S(1)}, u32[]{:S(2)}, u32[]{:S(2)}) collective-permute-start(f32[4,256,128]{2,1,0:T(8,128)} %get-tuple-element.47), channel_id=1, source_target_pairs={{0,1},{1,0},{2,3},{3,2},{4,5},{5,4},{6,7},{7,6},{8,9},{9,8},{10,11... | collective-permute-start | bytes 1572872 | tf_op jit(solution)/shard_map/ppermute | solution.py:421
  99.7 11.5 %all-to-all-start.5 = ((f32[8,64,128]{2,1,0:T(8,128)}), f32[8,64,128]{2,1,0:T(8,128)S(1)}, u32[]{:S(2)}, u32[]{:S(2)}) async-start(f32[8,64,128]{2,1,0:T(8,128)} %get-tuple-element.44), calls=%async_computation.5 | async-start | bytes 524288 | tf_op jit(solution)/shard_map/all_to_all | solution.py:383
  105.7 14.6 %collective-permute-start.8 = (f32[2,256,128]{2,1,0:T(8,128)S(1)}, f32[2,256,128]{2,1,0:T(8,128)S(1)}, u32[]{:S(2)}, u32[]{:S(2)}) collective-permute-start(f32[2,256,128]{2,1,0:T(8,128)S(1)} %get-tuple-element.48.refs_2_), channel_id=1, source_target_pairs={{0,2},{2,0},{4,6},{6,4},{1,3},{3,1},{5,7},{7,5},{8,10},{10,8},{12,... | collective-permute-start | bytes 786440 | tf_op jit(solution)/shard_map/ppermute | solution.py:421
  121.1 14.9 %all-to-all-start.7 = ((f32[8,72,128]{2,1,0:T(8,128)}), f32[8,72,128]{2,1,0:T(8,128)S(1)}, u32[]{:S(2)}, u32[]{:S(2)}) async-start(f32[8,72,128]{2,1,0:T(8,128)} %shard_map.147.refs_2_), calls=%async_computation.7 | async-start | bytes 589824 | tf_op jit(solution)/shard_map/all_to_all | solution.py:383
  125.2 6.6 %collective-permute-start.9 = (f32[1,256,128]{2,1,0:T(8,128)S(1)}, f32[1,256,128]{2,1,0:T(8,128)S(1)}, u32[]{:S(2)}, u32[]{:S(2)}) collective-permute-start(f32[1,256,128]{2,1,0:T(8,128)S(1)} %get-tuple-element.56), channel_id=1, source_target_pairs={{0,4},{2,6},{4,0},{6,2},{1,5},{3,7},{5,1},{7,3},{8,12},{10,14},{12... | collective-permute-start | bytes 393224 | tf_op jit(solution)/shard_map/ppermute | solution.py:421

commit v14 on v13

--- a/solution.py
+++ b/solution.py
@@ -185,10 +185,8 @@
         copy.wait()
 
 
-def table_kernel(shape_ref, rate_ref, table_ref, base_ref):
-    shapes = shape_ref[...]
-    table_ref[...] = exp_digamma_over(shapes, rate_ref[...])
-    base_ref[...] = (1.0 - step_weight) * shapes + step_weight * item_prior
+def table_kernel(shape_ref, rate_ref, table_ref):
+    table_ref[...] = exp_digamma_over(shape_ref[...], rate_ref[...])
 
 
 def widen(table):
@@ -263,7 +261,7 @@
         scale_ref[start : start + width, :] = jnp.exp(prior_log) / rate_ref[start : start + width, :]
 
 
-def last_kernel(shards, spot_ref, theta_ref, marks_ref, table_ref, scale_ref, base_ref, *refs):
+def last_kernel(shards, spot_ref, theta_ref, marks_ref, table_ref, scale_ref, shape_ref, *refs):
     shard_refs = refs[:shards]
     partial_ref, here_ref, keep_ref, send_ref, grad_ref, score_ref = refs[shards:]
     spot = spot_ref[2]
@@ -282,14 +280,14 @@
         wide = dot(ratio_high, theta_both, TN)
         stats = table * (wide[:, :factors] + wide[:, factors:] + dot(ratio_low, theta_high, TN))
         (send_ref if place % 2 else keep_ref)[place // 2] = stats
-        base = base_ref[here, :]
+        base = (1.0 - step_weight) * shape_ref[here, :] + step_weight * item_prior
         if place == 0:
             here_ref[...] = base
         score = item_prior / shards - scale_ref[here, :] * (base / shards + step_weight * USER_RATIO * stats)
         score_ref[here, :] = jnp.concatenate(split(score), axis=1)
     partial_ref[...] = total
     rows = grad_ref.shape[1]
-    group = 4
+    group = shards
     items = score_ref.shape[0]
     for first in range(0, shards, group):
         cov = jnp.concatenate([shard[:, :items] for shard in shard_refs[first : first + group]], axis=0)
@@ -411,9 +409,7 @@
         away(cov_weight),
     )
     recv = exchange(send, user_axes)
-    table, base = kernel_call(table_kernel, (on_chip(item_rows, factors), off_chip(item_rows, factors)))(
-        item_shape, item_rate
-    )
+    table = kernel_call(table_kernel, on_chip(item_rows, factors))(item_shape, item_rate)
     table = stay(table)
 
     def swap(array, distance):
@@ -466,7 +462,7 @@
         ),
         in_specs=[smem] + [vmem] * (5 + split_count),
         scratch_shapes=[pltpu.VMEM((item_rows, 2 * factors), BF16)],
-    )(spot, theta_all, marks, table, away(scale), away(base), *[away(shard) for shard in shards])
+    )(spot, theta_all, marks, table, away(scale), away(item_shape), *[away(shard) for shard in shards])
     held = away(held)
 
     def halve(held, moved, *awaited):

time: 137 us -> 137 us (level)
  no operation moved by 1% of the time
where the time goes in v14:
time: 137 us; the launch traced here: 136 us
  blocking collectives  38.9 us (28%)
  starting transfers between devices  35.8 us (26%)
  waiting for transfers between devices  31.7 us (23%)
  Pallas kernels  26.6 us (19%)
  local copies, waits for them, and re-layouts  2.45 us (2%)
    all_to_all x3, blocking collectives, exchange(): return lax.all_to_all(array, axes, split_axis=0, concat_axis=0, tiled=True)  38.9 us
    all_to_all x5, starting transfers between devices, exchange(): return lax.all_to_all(array, axes, split_axis=0, concat_axis=0, tiled=True)  28.2 us
    all_to_all x5, waiting for transfers between devices, exchange(): return lax.all_to_all(array, axes, split_axis=0, concat_axis=0, tiled=True)  26.6 us
    pallas_call x1, Pallas kernels, shards(): kernel_call(functools.partial(last_kernel, split_count), (shape_of(everyo...  8.09 us
    ppermute x10, starting transfers between devices, swap(): lax.ppermute(array, axis, [(place, place ^ bit) for place in range(lax.ax...  7.52 us
    pallas_call x1, Pallas kernels, shards(): kernel_call(behind(functools.partial(scale_kernel, split_count), split_co...  5.74 us
    ppermute x10, waiting for transfers between devices, swap(): lax.ppermute(array, axis, [(place, place ^ bit) for place in range(lax.ax...  5.04 us
    pallas_call x1, Pallas kernels, shards(): kernel_call(functools.partial(prep_kernel, owners), (off_chip(owners, 16,...  3.56 us
  transfers between devices with their start and end apart: 15, of which 6 were waited for; matrix products, arithmetic and copies ran while one was open for 0% of the time, Pallas kernels for 10%

profile of v14, /device:TPU:2, one launch (start us, length us, event | category | flops | bytes accessed | tf_op | source)
XLA Modules:
  0.0 136.2 jit_solution(10722767882345473199)
XLA Ops:
  0.6 3.6 %shard_map.137 = (f32[32,16,128]{2,1,0:T(8,128)}, f32[8,128]{1,0:T(8,128)S(1)}, f32[8,128]{1,0:T(8,128)S(1)}, f32[64,2176]{1,0:T(8,128)}) custom-call(s32[8]{0:T(128)} %counts_hbm.1, s32[64,128]{1,0:T(8,128)} %bitcast.18, s32[64,128]{1,0:T(8,128)} %bitcast.19, f32[8,128]{1,0:T(8,128)} %shape_hbm.1, f32[8,128]{1,0:T(8,128)} %rate_hbm.1, f32[64,2048]{1,0:T(8,128)} %cov_hbm.1, ...), custom_call_target="tpu_custom_call" | custom-call | tf_op jit(solution)/shard_map/pallas_call | solution.py:390
  4.2 11.5 %all-to-all-start = ((f32[32,16,128]{2,1,0:T(8,128)}), f32[32,16,128]{2,1,0:T(8,128)S(1)}, u32[]{:S(2)}, u32[]{:S(2)}) async-start(f32[32,16,128]{2,1,0:T(8,128)} %get-tuple-element.30), calls=%async_computation | async-start | bytes 524288 | tf_op jit(solution)/shard_map/all_to_all | solution.py:381
  15.7 0.0 copy-start.2
  15.7 2.2 %collective-permute-start.4 = (f32[64,2176]{1,0:T(8,128)}, f32[64,2176]{1,0:T(8,128)}, u32[]{:S(2)}, u32[]{:S(2)}) collective-permute-start(f32[64,2176]{1,0:T(8,128)} %get-tuple-element.36.refs_0_), channel_id=1, source_target_pairs={{0,4},{2,6},{4,0},{6,2},{1,5},{3,7},{5,1},{7,3},{8,12},{10,14},{12... | collective-permute-start | bytes 1671176 | tf_op jit(solution)/shard_map/ppermute | solution.py:417
  17.9 0.0 collective-permute-start.1
  17.9 2.6 %collective-permute-start = (f32[64,2176]{1,0:T(8,128)}, f32[64,2176]{1,0:T(8,128)}, u32[]{:S(2)}, u32[]{:S(2)}) collective-permute-start(f32[64,2176]{1,0:T(8,128)} %get-tuple-element.36.refs_0_), channel_id=1, source_target_pairs={{0,2},{2,0},{4,6},{6,4},{1,3},{3,1},{5,7},{7,5},{8,10},{10,8},{12,... | collective-permute-start | bytes 1671176 | tf_op jit(solution)/shard_map/ppermute | solution.py:417
  20.5 1.2 copy-done
  21.7 1.2 copy-done.1
  23.0 1.1 shard_map.138.table_ref.refs_2_
  24.0 4.1 %all-to-all-done.recv_ref = f32[32,16,128]{2,1,0:T(8,128)S(1)} async-done(((f32[32,16,128]{2,1,0:T(8,128)}), f32[32,16,128]{2,1,0:T(8,128)S(1)}, u32[]{:S(2)}, u32[]{:S(2)}) %all-to-all-start) | async-done | bytes 262176 | tf_op jit(solution)/shard_map/all_to_all | solution.py:381
  28.2 2.0 %shard_map.139 = (f32[16,256,128]{2,1,0:T(8,128)S(1)}, f32[256,128]{1,0:T(8,128)S(1)}) custom-call(f32[32,16,128]{2,1,0:T(8,128)S(1)} %all-to-all-done.recv_ref, f32[2048,128]{1,0:T(8,128)S(1)} %shard_map.138.table_ref.refs_2_), custom_call_target="tpu_custom_call" | custom-call | tf_op jit(solution)/shard_map/pallas_call | solution.py:426
  30.2 15.9 %all_to_all.40.refs_0_ = f32[32,8,128]{2,1,0:T(8,128)S(1)} all-to-all(f32[32,8,128]{2,1,0:T(8,128)S(1)} %bitcast.14), channel_id=1, replica_groups=mesh['y'=4,'z'=8,'x'=4,'core'=2] {'y','z'}, dimensions={0} | all-to-all | bytes 262144 | tf_op jit(solution)/shard_map/all_to_all | solution.py:381
  46.1 0.7 shard_map.140
  46.8 3.9 %all-to-all-start.2 = ((f32[32,8,128]{2,1,0:T(8,128)}), f32[32,8,128]{2,1,0:T(8,128)S(1)}, u32[]{:S(2)}, u32[]{:S(2)}) async-start(f32[32,8,128]{2,1,0:T(8,128)} %get-tuple-element.34), calls=%async_computation.2 | async-start | bytes 262144 | tf_op jit(solution)/shard_map/all_to_all | solution.py:381
  50.6 0.1 collective-permute-start.2
  50.7 0.0 collective-permute-done.4.refs_4_
  50.8 0.5 collective-permute-start.5
  51.2 0.0 collective-permute-done.1.refs_4_.refs_6_
  51.3 0.1 collective-permute-start.6
  51.4 0.0 collective-permute-done.refs_3_.refs_2_
  51.4 0.4 collective-permute-start.3
  51.8 9.2 %all-to-all-done.2 = f32[32,8,128]{2,1,0:T(8,128)S(1)} async-done(((f32[32,8,128]{2,1,0:T(8,128)}), f32[32,8,128]{2,1,0:T(8,128)S(1)}, u32[]{:S(2)}, u32[]{:S(2)}) %all-to-all-start.2) | async-done | bytes 131104 | tf_op jit(solution)/shard_map/all_to_all | solution.py:381
  60.9 1.4 %shard_map.141 = f32[256,128]{1,0:T(8,128)S(1)} custom-call(f32[256,128]{1,0:T(8,128)S(1)} %bitcast.12, f32[16,256,128]{2,1,0:T(8,128)S(1)} %get-tuple-element.35.refs_1_.marks_ref, f32[2048,128]{1,0:T(8,128)S(1)} %shard_map.138.table_ref.refs_2_, f32[64,2176]{1,0:T(8,128)} %collective-permute-done.refs_3_.refs_2_, ...), custom_call_target="tpu_custom_call" | custom-call | tf_op jit(solution)/shard_map/pallas_call | solution.py:441
  62.4 13.9 %all_to_all.41.refs_0_ = f32[32,8,128]{2,1,0:T(8,128)S(1)} all-to-all(f32[32,8,128]{2,1,0:T(8,128)S(1)} %bitcast.13), channel_id=1, replica_groups=mesh['y'=4,'z'=8,'x'=4,'core'=2] {'y','z'}, dimensions={0} | all-to-all | bytes 262144 | tf_op jit(solution)/shard_map/all_to_all | solution.py:381
  76.3 0.7 shard_map.142
  77.0 3.9 %all-to-all-start.4 = ((f32[32,8,128]{2,1,0:T(8,128)}), f32[32,8,128]{2,1,0:T(8,128)S(1)}, u32[]{:S(2)}, u32[]{:S(2)}) async-start(f32[32,8,128]{2,1,0:T(8,128)} %get-tuple-element.39.refs_9_), calls=%async_computation.4 | async-start | bytes 262144 | tf_op jit(solution)/shard_map/all_to_all | solution.py:381
  80.9 0.1 pad_add_fusion.spot_ref
  80.9 0.0 collective-permute-done.2.refs_1_
  80.9 0.0 collective-permute-done.5.refs_5_
  80.9 0.0 collective-permute-done.6.refs_7_
  80.9 0.0 collective-permute-done.3.refs_3_
  81.0 5.7 %shard_map.143.scale_ref = f32[2048,128]{1,0:T(8,128)} custom-call(f32[64,2176]{1,0:T(8,128)} %get-tuple-element.36.refs_0_, f32[64,2176]{1,0:T(8,128)} %collective-permute-done.2.refs_1_, f32[64,2176]{1,0:T(8,128)} %collective-permute-done.refs_3_.refs_2_, f32[64,2176]{1,0:T(8,128)} %collective-permute-done.3.refs_3_, ...), custom_call_target="tpu_custom_call" | custom-call | tf_op jit(solution)/shard_map/pallas_call | solution.py:448
  86.7 4.4 %all-to-all-done.4 = f32[32,8,128]{2,1,0:T(8,128)S(1)} async-done(((f32[32,8,128]{2,1,0:T(8,128)}), f32[32,8,128]{2,1,0:T(8,128)S(1)}, u32[]{:S(2)}, u32[]{:S(2)}) %all-to-all-start.4) | async-done | bytes 131104 | tf_op jit(solution)/shard_map/all_to_all | solution.py:381
  91.1 8.1 %shard_map.144 = (f32[256,128]{1,0:T(8,128)S(1)}, f32[256,128]{1,0:T(8,128)S(1)}, f32[4,256,128]{2,1,0:T(8,128)}, f32[4,256,128]{2,1,0:T(8,128)}, f32[8,64,128]{2,1,0:T(8,128)}) custom-call(s32[3]{0:T(128)S(1)} %pad_add_fusion.spot_ref, f32[256,128]{1,0:T(8,128)S(1)} %bitcast.11, f32[16,256,128]{2,1,0:T(8,128)S(1)} %get-tuple-element.35.refs_1_.marks_ref, ...), custom_call_target="tpu_custom_call" | custom-call | tf_op jit(solution)/shard_map/pallas_call | solution.py:454
  99.2 0.0 collective-permute-start.7
  99.2 4.9 %all-to-all-start.5 = ((f32[8,64,128]{2,1,0:T(8,128)}), f32[8,64,128]{2,1,0:T(8,128)S(1)}, u32[]{:S(2)}, u32[]{:S(2)}) async-start(f32[8,64,128]{2,1,0:T(8,128)} %get-tuple-element.40), calls=%async_computation.5 | async-start | bytes 524288 | tf_op jit(solution)/shard_map/all_to_all | solution.py:381
  104.2 0.0 collective-permute-done.7.refs_1_
  104.2 1.1 shard_map.145
  105.3 0.1 collective-permute-start.8
  105.4 5.3 %all-to-all-done.5.refs_0_ = f32[8,64,128]{2,1,0:T(8,128)S(1)} async-done(((f32[8,64,128]{2,1,0:T(8,128)}), f32[8,64,128]{2,1,0:T(8,128)S(1)}, u32[]{:S(2)}, u32[]{:S(2)}) %all-to-all-start.5) | async-done | bytes 262176 | tf_op jit(solution)/shard_map/all_to_all | solution.py:381
  110.7 9.2 %all_to_all.42.refs_0_ = f32[4,128,128]{2,1,0:T(8,128)S(1)} all-to-all(f32[4,128,128]{2,1,0:T(8,128)S(1)} %shard_map.146), channel_id=1, replica_groups=mesh['y'=4,'z'=8,'x'=4,'core'=2] {'y'}, dimensions={0} | all-to-all | bytes 524288 | tf_op jit(solution)/shard_map/all_to_all | solution.py:381
  119.9 0.7 shard_map.147.refs_2_
  120.7 4.1 %all-to-all-start.7 = ((f32[8,72,128]{2,1,0:T(8,128)}), f32[8,72,128]{2,1,0:T(8,128)S(1)}, u32[]{:S(2)}, u32[]{:S(2)}) async-start(f32[8,72,128]{2,1,0:T(8,128)} %shard_map.147.refs_2_), calls=%async_computation.7 | async-start | bytes 589824 | tf_op jit(solution)/shard_map/all_to_all | solution.py:381
  124.8 1.5 %collective-permute-start.9 = (f32[1,256,128]{2,1,0:T(8,128)S(1)}, f32[1,256,128]{2,1,0:T(8,128)S(1)}, u32[]{:S(2)}, u32[]{:S(2)}) collective-permute-start(f32[1,256,128]{2,1,0:T(8,128)S(1)} %get-tuple-element.52), channel_id=1, source_target_pairs={{0,4},{2,6},{4,0},{6,2},{1,5},{3,7},{5,1},{7,3},{8,12},{10,14},{12... | collective-permute-start | bytes 393224 | tf_op jit(solution)/shard_map/ppermute | solution.py:417
  126.3 5.0 %collective-permute-done.9.recv_ref = f32[1,256,128]{2,1,0:T(8,128)S(1)} collective-permute-done((f32[1,256,128]{2,1,0:T(8,128)S(1)}, f32[1,256,128]{2,1,0:T(8,128)S(1)}, u32[]{:S(2)}, u32[]{:S(2)}) %collective-permute-start.9) | collective-permute-done | bytes 131104 | tf_op jit(solution)/shard_map/ppermute | solution.py:417
  131.3 0.7 shard_map.150
  132.0 3.6 %all-to-all-done.7.recv_ref = f32[8,72,128]{2,1,0:T(8,128)S(1)} async-done(((f32[8,72,128]{2,1,0:T(8,128)}), f32[8,72,128]{2,1,0:T(8,128)S(1)}, u32[]{:S(2)}, u32[]{:S(2)}) %all-to-all-start.7) | async-done | bytes 294944 | tf_op jit(solution)/shard_map/all_to_all | solution.py:381
  135.6 0.6 shard_map.148
  (6 shorter events, 0.1 us)
Async XLA Ops:
  4.2 24.0 %all-to-all-start = ((f32[32,16,128]{2,1,0:T(8,128)}), f32[32,16,128]{2,1,0:T(8,128)S(1)}, u32[]{:S(2)}, u32[]{:S(2)}) async-start(f32[32,16,128]{2,1,0:T(8,128)} %get-tuple-element.30), calls=%async_computation | async-start | bytes 524288 | tf_op jit(solution)/shard_map/all_to_all | solution.py:381
  15.7 30.4 %copy-start.2 = (f32[128]{0:T(128)S(1)}, f32[128]{0:T(128)}, u32[]{:S(2)}) copy-start(f32[128]{0:T(128)} %param.17) | copy-start | bytes 1540
  15.7 35.0 %collective-permute-start.4 = (f32[64,2176]{1,0:T(8,128)}, f32[64,2176]{1,0:T(8,128)}, u32[]{:S(2)}, u32[]{:S(2)}) collective-permute-start(f32[64,2176]{1,0:T(8,128)} %get-tuple-element.36.refs_0_), channel_id=1, source_target_pairs={{0,4},{2,6},{4,0},{6,2},{1,5},{3,7},{5,1},{7,3},{8,12},{10,14},{12... | collective-permute-start | bytes 1671176 | tf_op jit(solution)/shard_map/ppermute | solution.py:417
  17.9 33.3 %collective-permute-start.1 = (f32[64,2176]{1,0:T(8,128)}, f32[64,2176]{1,0:T(8,128)}, u32[]{:S(2)}, u32[]{:S(2)}) collective-permute-start(f32[64,2176]{1,0:T(8,128)} %get-tuple-element.36.refs_0_), channel_id=1, source_target_pairs={{0,6},{2,4},{4,2},{6,0},{1,7},{3,5},{5,3},{7,1},{8,14},{10,12},{12... | collective-permute-start | bytes 1671176 | tf_op jit(solution)/shard_map/ppermute | solution.py:417
  17.9 33.4 %collective-permute-start = (f32[64,2176]{1,0:T(8,128)}, f32[64,2176]{1,0:T(8,128)}, u32[]{:S(2)}, u32[]{:S(2)}) collective-permute-start(f32[64,2176]{1,0:T(8,128)} %get-tuple-element.36.refs_0_), channel_id=1, source_target_pairs={{0,2},{2,0},{4,6},{6,4},{1,3},{3,1},{5,7},{7,5},{8,10},{10,8},{12,... | collective-permute-start | bytes 1671176 | tf_op jit(solution)/shard_map/ppermute | solution.py:417
  20.5 1.2 copy-start
  21.7 1.2 copy-start.1
  46.8 14.2 %all-to-all-start.2 = ((f32[32,8,128]{2,1,0:T(8,128)}), f32[32,8,128]{2,1,0:T(8,128)S(1)}, u32[]{:S(2)}, u32[]{:S(2)}) async-start(f32[32,8,128]{2,1,0:T(8,128)} %get-tuple-element.34), calls=%async_computation.2 | async-start | bytes 262144 | tf_op jit(solution)/shard_map/all_to_all | solution.py:381
  50.6 30.3 %collective-permute-start.2 = (f32[64,2176]{1,0:T(8,128)}, f32[64,2176]{1,0:T(8,128)}, u32[]{:S(2)}, u32[]{:S(2)}) collective-permute-start(f32[64,2176]{1,0:T(8,128)} %get-tuple-element.36.refs_0_), channel_id=1, source_target_pairs={{0,1},{1,0},{2,3},{3,2},{4,5},{5,4},{6,7},{7,6},{8,9},{9,8},{10,11... | collective-permute-start | bytes 1671176 | tf_op jit(solution)/shard_map/ppermute | solution.py:417
  50.8 30.2 %collective-permute-start.5 = (f32[64,2176]{1,0:T(8,128)}, f32[64,2176]{1,0:T(8,128)}, u32[]{:S(2)}, u32[]{:S(2)}) collective-permute-start(f32[64,2176]{1,0:T(8,128)} %collective-permute-done.4.refs_4_), channel_id=1, source_target_pairs={{0,1},{1,0},{2,3},{3,2},{4,5},{5,4},{6,7},{7,6},{8,9},{9,8},{10,11... | collective-permute-start | bytes 1671176 | tf_op jit(solution)/shard_map/ppermute | solution.py:417
  51.3 29.7 %collective-permute-start.6 = (f32[64,2176]{1,0:T(8,128)}, f32[64,2176]{1,0:T(8,128)}, u32[]{:S(2)}, u32[]{:S(2)}) collective-permute-start(f32[64,2176]{1,0:T(8,128)} %collective-permute-done.1.refs_4_.refs_6_), channel_id=1, source_target_pairs={{0,1},{1,0},{2,3},{3,2},{4,5},{5,4},{6,7},{7,6},{8,9},{9,8},{10,11... | collective-permute-start | bytes 1671176 | tf_op jit(solution)/shard_map/ppermute | solution.py:417
  51.4 29.6 %collective-permute-start.3 = (f32[64,2176]{1,0:T(8,128)}, f32[64,2176]{1,0:T(8,128)}, u32[]{:S(2)}, u32[]{:S(2)}) collective-permute-start(f32[64,2176]{1,0:T(8,128)} %collective-permute-done.refs_3_.refs_2_), channel_id=1, source_target_pairs={{0,1},{1,0},{2,3},{3,2},{4,5},{5,4},{6,7},{7,6},{8,9},{9,8},{10,11... | collective-permute-start | bytes 1671176 | tf_op jit(solution)/shard_map/ppermute | solution.py:417
  77.0 14.2 %all-to-all-start.4 = ((f32[32,8,128]{2,1,0:T(8,128)}), f32[32,8,128]{2,1,0:T(8,128)S(1)}, u32[]{:S(2)}, u32[]{:S(2)}) async-start(f32[32,8,128]{2,1,0:T(8,128)} %get-tuple-element.39.refs_9_), calls=%async_computation.4 | async-start | bytes 262144 | tf_op jit(solution)/shard_map/all_to_all | solution.py:381
  99.2 4.9 %collective-permute-start.7 = (f32[4,256,128]{2,1,0:T(8,128)}, f32[4,256,128]{2,1,0:T(8,128)S(1)}, u32[]{:S(2)}, u32[]{:S(2)}) collective-permute-start(f32[4,256,128]{2,1,0:T(8,128)} %get-tuple-element.43), channel_id=1, source_target_pairs={{0,1},{1,0},{2,3},{3,2},{4,5},{5,4},{6,7},{7,6},{8,9},{9,8},{10,11... | collective-permute-start | bytes 1572872 | tf_op jit(solution)/shard_map/ppermute | solution.py:417
  99.2 11.5 %all-to-all-start.5 = ((f32[8,64,128]{2,1,0:T(8,128)}), f32[8,64,128]{2,1,0:T(8,128)S(1)}, u32[]{:S(2)}, u32[]{:S(2)}) async-start(f32[8,64,128]{2,1,0:T(8,128)} %get-tuple-element.40), calls=%async_computation.5 | async-start | bytes 524288 | tf_op jit(solution)/shard_map/all_to_all | solution.py:381
  105.3 14.7 %collective-permute-start.8 = (f32[2,256,128]{2,1,0:T(8,128)S(1)}, f32[2,256,128]{2,1,0:T(8,128)S(1)}, u32[]{:S(2)}, u32[]{:S(2)}) collective-permute-start(f32[2,256,128]{2,1,0:T(8,128)S(1)} %get-tuple-element.44.refs_2_), channel_id=1, source_target_pairs={{0,2},{2,0},{4,6},{6,4},{1,3},{3,1},{5,7},{7,5},{8,10},{10,8},{12,... | collective-permute-start | bytes 786440 | tf_op jit(solution)/shard_map/ppermute | solution.py:417
  120.7 14.9 %all-to-all-start.7 = ((f32[8,72,128]{2,1,0:T(8,128)}), f32[8,72,128]{2,1,0:T(8,128)S(1)}, u32[]{:S(2)}, u32[]{:S(2)}) async-start(f32[8,72,128]{2,1,0:T(8,128)} %shard_map.147.refs_2_), calls=%async_computation.7 | async-start | bytes 589824 | tf_op jit(solution)/shard_map/all_to_all | solution.py:381
  124.8 6.6 %collective-permute-start.9 = (f32[1,256,128]{2,1,0:T(8,128)S(1)}, f32[1,256,128]{2,1,0:T(8,128)S(1)}, u32[]{:S(2)}, u32[]{:S(2)}) collective-permute-start(f32[1,256,128]{2,1,0:T(8,128)S(1)} %get-tuple-element.52), channel_id=1, source_target_pairs={{0,4},{2,6},{4,0},{6,2},{1,5},{3,7},{5,1},{7,3},{8,12},{10,14},{12... | collective-permute-start | bytes 393224 | tf_op jit(solution)/shard_map/ppermute | solution.py:417
